TPU v7x, 128 devices: a whole 4x4x4 slice. The times are simulated.
128 devices in a mesh: group: 8 (over x_hi, z), helper: 16 (over y, x_lo, core).
Axes of the slice: x: 4 (x_hi: 2, x_lo: 2; x = x_hi * 2 + x_lo), y: 4, z: 4, core: 2. Of those that a mesh axis runs over, the one named last changes fastest.
Arguments:
- embeddings: float32 [8, 8192, 1024], P('group', 'helper'), may hold values from -420 to 420
- sizes: int32 [8], replicated, may hold values from 4096 to 8192, as said below
- ranks: int32 [8, 8192], P('group', 'helper'), may hold values from 0 to 8191, each once within a row
Outputs:
- within: float32 [8, 8192], P('group', 'helper')
- adjacent: float32 [8, 8192], P('group', 'helper')
Inputs may be any that keep to these rules, and one draw needn't show every extreme that they name: `sizes`: real rows fill the leading positions of a cluster; at least one cluster is full. Each cluster's ranks are a permutation.
All inputs are finite; a program needn't handle non-finite values.
Results may differ from a plain program's by a relative error of at most 0.00046.
Values may be sent and summed in bfloat16 or wider, within the bound.
No kernel may reach another device: no remote copies, remote signals or barrier semaphores. Data moves between devices by JAX's collectives and lax.ppermute only.
A program may use at most 128 MiB of HBM per device.

v0:
```python
import math

import jax
import jax.numpy as jnp
from jax import lax
from jax.sharding import PartitionSpec as P

D = 1024


def passed_along(value, axis, steps):
    count = lax.axis_size(axis)
    pairs = [(source, (source + steps) % count) for source in range(count)]
    return lax.ppermute(value, axis, pairs)


def normalize(values):
    scale = lax.rsqrt(jnp.mean(values * values, axis=-1, keepdims=True) + 1e-06) / math.sqrt(D)
    return (values * scale).astype(jnp.bfloat16)


def inner(queries, keys):
    return lax.dot_general(
        queries, keys, (((1,), (1,)), ((), ())), preferred_element_type=jnp.float32
    )


def pick_count(sizes, which):
    return jnp.sum(jnp.where(jnp.arange(sizes.shape[0]) == which, sizes, 0))


def nearest_fold(queries, limit, best, piece):
    scores = inner(queries, piece)
    key_pos = jnp.arange(piece.shape[0], dtype=jnp.int32)
    scores = jnp.where((key_pos < limit)[None, :], scores, -1.0)
    return jnp.maximum(best, jnp.max(scores, axis=1))


def on_device(embeddings, sizes, ranks):
    rows = embeddings.shape[1]
    clusters = lax.axis_size("group")
    group_index = lax.axis_index("group")
    helper_index = lax.axis_index("helper")
    unit = normalize(embeddings[0])
    own_rank = ranks[0]
    count = pick_count(sizes, group_index)
    own_pos = helper_index * rows + jnp.arange(rows, dtype=jnp.int32)
    own_real = own_pos < count
    start_best = jnp.full((rows,), -1.0, jnp.float32)
    keys = lax.all_gather(unit, "helper", axis=0, tiled=True)
    key_rank = lax.all_gather(own_rank, "helper", axis=0, tiled=True)
    scores = inner(unit, keys)
    key_pos = jnp.arange(keys.shape[0], dtype=jnp.int32)
    usable = (key_rank[None, :] < own_rank[:, None]) & (key_pos < count)[None, :]
    within = jnp.maximum(start_best, jnp.max(jnp.where(usable, scores, -1.0), axis=1))
    next_count = pick_count(sizes, (group_index + 1) % clusters)
    next_rows = passed_along(unit, "group", -1)
    adjacent = nearest_fold(
        unit, next_count, start_best, lax.all_gather(next_rows, "helper", axis=0, tiled=True)
    )
    within = jnp.where(own_real, within, 0.0)
    adjacent = jnp.where(own_real, adjacent, 0.0)
    return (within[None, :], adjacent[None, :])


def solution(mesh):
    in_specs = (P("group", "helper", None), P(), P("group", "helper"))
    out_specs = (P("group", "helper"), P("group", "helper"))
    return jax.shard_map(
        on_device, mesh=mesh, in_specs=in_specs, out_specs=out_specs, check_vma=False
    )
```

profile of v0, /device:TPU:0, one launch (start us, length us, event | category | flops | bytes accessed | tf_op | source)
XLA Modules:
  0.0 234.7 jit_solution(5556733850312664523)
XLA Ops:
  7.2 0.0 all-gather.4.cloned.1.call-start
  7.2 1.8 fusion
  9.0 2.8 %fusion.1 = bf16[512,1024]{1,0:T(8,128)(2,1)} fusion(f32[1,512,1024]{2,1,0:T(8,128)} %param.3, f32[512]{0:T(512)S(1)} %rsqrt_multiply_fusion), kind=kLoop, calls=%fused_computation.5 | loop fusion | flops 1048576 | bytes 3147776 | tf_op jit(solution)/shard_map/convert_element_type | solution.py:19
  11.8 0.0 all-gather.4.cloned.1.call-update
  11.8 0.0 all-gather.6.cloned.1.call-start
  11.9 6.6 %collective-permute-start = (bf16[512,1024]{1,0:T(8,128)(2,1)}, bf16[512,1024]{1,0:T(8,128)(2,1)S(1)}, u32[]{:S(2)}, u32[]{:S(2)}) collective-permute-start(bf16[512,1024]{1,0:T(8,128)(2,1)} %fusion.1), channel_id=1, source_target_pairs={{0,112},{16,0},{32,16},{48,32},{64,48},{80,64},{96,80},{112,96},{1... | collective-permute-start | bytes 3145736 | tf_op jit(solution)/shard_map/ppermute | solution.py:14
  18.5 41.6 %collective-permute-done = bf16[512,1024]{1,0:T(8,128)(2,1)S(1)} collective-permute-done((bf16[512,1024]{1,0:T(8,128)(2,1)}, bf16[512,1024]{1,0:T(8,128)(2,1)S(1)}, u32[]{:S(2)}, u32[]{:S(2)}) %collective-permute-start) | collective-permute-done | bytes 1048608 | tf_op jit(solution)/shard_map/ppermute | solution.py:14
  60.1 0.0 copy-start.1
  60.1 1.0 copy-done.1
  61.1 0.0 all-gather.6.cloned.1.call-update
  61.1 18.6 %all-gather = s32[1,8192]{1,0:T(1,128)S(1)} all-gather(s32[1,512]{1,0:T(1,128)} %param.5), channel_id=2, replica_groups=mesh['group'=8,'helper'=16] {'helper'}, dimensions={1}, use_global_device_ids=true | all-gather | bytes 34816 | tf_op jit(solution)/shard_map/all_gather | solution.py:51
  79.7 1.3 fusion.3
  81.0 0.7 iota_compare_fusion
  81.7 0.6 iota_compare_fusion.1
  82.2 40.6 %all-gather.4.cloned.1.call-done = bf16[8192,1024]{1,0:T(8,128)(2,1)} async-done(((bf16[512,1024]{1,0:T(8,128)(2,1)}), bf16[8192,1024]{1,0:T(8,128)(2,1)}) %all-gather.4.cloned.1.call-update) | async-done | bytes 16777232 | tf_op jit(solution)/shard_map/all_gather | solution.py:50
  122.9 0.0 copy-start
  122.9 15.6 %select_reduce_fusion.1 = f32[512]{0:T(512)S(1)} fusion(bf16[512,1024]{1,0:T(8,128)(2,1)} %fusion.1, bf16[8192,1024]{1,0:T(8,128)(2,1)} %all-gather.4.cloned.1.call-done, s32[8192]{0:T(1024)S(1)} %bitcast.15, s32[512]{0:T(512)} %bitcast.18, pred[8192]{0:T(1024)(128)(4,1)S(1)} %iota_compare_fusion.1), kind=kOutput, calls=%fused_computation.1 | convolution fusion | flops 8606711808 | bytes 17870848 | tf_op jit(solution)/shard_map/dot_general | solution.py:23
  138.5 75.6 %all-gather.6.cloned.1.call-done = bf16[8192,1024]{1,0:T(8,128)(2,1)} async-done(((bf16[512,1024]{1,0:T(8,128)(2,1)}), bf16[8192,1024]{1,0:T(8,128)(2,1)}) %all-gather.6.cloned.1.call-update) | async-done | bytes 16777232 | tf_op jit(solution)/shard_map/all_gather | solution.py:59
  214.1 0.0 copy-done
  214.1 12.6 %select_reduce_fusion = f32[512]{0:T(512)S(1)} fusion(bf16[512,1024]{1,0:T(8,128)(2,1)S(1)} %copy-done, bf16[8192,1024]{1,0:T(8,128)(2,1)} %all-gather.6.cloned.1.call-done, pred[8192]{0:T(1024)(128)(4,1)S(1)} %iota_compare_fusion), kind=kOutput, calls=%fused_computation | convolution fusion | flops 8598323200 | bytes 17836032 | tf_op jit(solution)/shard_map/dot_general | solution.py:23
  226.7 1.2 compare_select_fusion
  (3 shorter events, 0.0 us)
Async XLA Ops:
  7.2 115.7 %all-gather.4.cloned.1.call-start = ((), (), s32[]{:S(2)}) async-start(), calls=%async_computation | async-start | bytes 17825792 | tf_op jit(solution)/shard_map/all_gather | solution.py:50
  11.8 202.3 %all-gather.6.cloned.1.call-start = ((), (), s32[]{:S(2)}) async-start(), calls=%async_computation.1 | async-start | bytes 17825792 | tf_op jit(solution)/shard_map/all_gather | solution.py:59
  11.9 48.2 %collective-permute-start = (bf16[512,1024]{1,0:T(8,128)(2,1)}, bf16[512,1024]{1,0:T(8,128)(2,1)S(1)}, u32[]{:S(2)}, u32[]{:S(2)}) collective-permute-start(bf16[512,1024]{1,0:T(8,128)(2,1)} %fusion.1), channel_id=1, source_target_pairs={{0,112},{16,0},{32,16},{48,32},{64,48},{80,64},{96,80},{112,96},{1... | collective-permute-start | bytes 3145736 | tf_op jit(solution)/shard_map/ppermute | solution.py:14
  60.1 1.0 copy-start.1
  122.9 91.2 %copy-start = (bf16[512,1024]{1,0:T(8,128)(2,1)S(1)}, bf16[512,1024]{1,0:T(8,128)(2,1)}, u32[]{:S(2)}) copy-start(bf16[512,1024]{1,0:T(8,128)(2,1)} %fusion.1) | copy-start | bytes 3145732
Sparse Core Ops, SparseCore 0:
  11.9 110.8 all-gather.3
  124.6 89.4 all-gather.5
where the time goes:
time: 236 us; the launch traced here: 235 us
  waiting for transfers between devices  158 us (67%)
  matrix products  28.3 us (12%)
  blocking collectives  18.6 us (8%)
  between operations  14.1 us (6%)
  other arithmetic  8.28 us (4%)
  starting transfers between devices  6.73 us (3%)
    all_gather x1, waiting for transfers between devices, on_device(): lax.all_gather(next_rows, 'helper', axis=0, tiled=True)  75.6 us
    ppermute x1, waiting for transfers between devices, passed_along(): return lax.ppermute(value, axis, pairs)  41.6 us
    all_gather x1, waiting for transfers between devices, on_device(): keys = lax.all_gather(unit, 'helper', axis=0, tiled=True)  40.6 us
    dot_general x2, matrix products, inner(): lax.dot_general(queries, keys, (((1,), (1,)), ((), ())), preferred_elemen...  28.3 us
    all_gather x1, blocking collectives, on_device(): key_rank = lax.all_gather(own_rank, 'helper', axis=0, tiled=True)  18.6 us
    ppermute x1, starting transfers between devices, passed_along(): return lax.ppermute(value, axis, pairs)  6.65 us
  transfers between devices with their start and end apart: 3, of which 3 were waited for; matrix products, arithmetic and copies ran while one was open for 8% of the time, Pallas kernels for 0%

commit v1 on v0

v1 whole, which is shorter than its diff:
```python
import functools
import math

import jax
import jax.numpy as jnp
from jax import lax
from jax.experimental import pallas as pl
from jax.experimental.pallas import tpu as pltpu
from jax.sharding import PartitionSpec as P

D = 1024
HALF = 256
EXTRA = 8
PAY = HALF + EXTRA
BASE = 64
FAR = 8192.0
LOW = -4.0
AXES = ("group", "helper")
VMEM = pl.BlockSpec(memory_space=pltpu.VMEM)


def place(index):
    group, helper = divmod(index, 16)
    return {
        "part": group // 4,
        "z": group % 4,
        "row": helper // 4,
        "col": (helper // 2) % 2,
        "core": helper % 2,
    }


def number(at):
    return (at["part"] * 4 + at["z"]) * 16 + at["row"] * 4 + at["col"] * 2 + at["core"]


def pairs(col=0, row=0, core=0, cluster=0):
    out = []
    for source in range(128):
        at = place(source)
        step = at["part"] * 4 + at["z"] + cluster
        flip = 1 if step // 4 != at["part"] else 0
        at["part"], at["z"] = (step // 4) % 2, step % 4
        at["col"] = (at["col"] + col + flip) % 2
        at["row"] = (at["row"] + row) % 4
        at["core"] = (at["core"] + core) % 2
        out.append((source, number(at)))
    return out


def send(value, **shift):
    return lax.ppermute(value, AXES, pairs(**shift))


def inner(keys, queries):
    return lax.dot_general(
        keys, queries, (((1,), (1,)), ((), ())), preferred_element_type=jnp.float32
    )


def pack_kernel(left_ref, rows_ref, rank_ref, pay_ref):
    half = pl.program_id(0)
    rows = rows_ref[...]
    scale = lax.rsqrt(jnp.mean(rows * rows, axis=-1, keepdims=True) + 1e-06) / math.sqrt(D)
    pay_ref[0, :HALF, :] = (rows * scale).astype(jnp.bfloat16)
    rank = rank_ref[...]
    position = lax.broadcasted_iota(jnp.int32, (1, HALF), 1) + half * HALF
    real = position < left_ref[0]
    high = jnp.where(real, rank // BASE, int(FAR) // BASE).astype(jnp.float32)
    low = jnp.where(real, rank % BASE, 0).astype(jnp.float32)
    both = jnp.concatenate([high, low, jnp.zeros((1, D - 2 * HALF), jnp.float32)], axis=1)
    pay_ref[0, HALF:, :] = jnp.broadcast_to(both, (EXTRA, D)).astype(jnp.bfloat16)


def packed(rows, ranks, left):
    return pl.pallas_call(
        pack_kernel,
        grid=(2,),
        in_specs=[
            pl.BlockSpec(memory_space=pltpu.SMEM),
            pl.BlockSpec((HALF, D), lambda i: (i, 0)),
            pl.BlockSpec((1, HALF), lambda i: (0, i)),
        ],
        out_specs=pl.BlockSpec((1, PAY, D), lambda i: (i, 0, 0)),
        out_shape=jax.ShapeDtypeStruct((2, PAY, D), jnp.bfloat16),
        name="pack",
        compiler_params=pltpu.CompilerParams(vmem_limit_bytes=16 * 2**20),
        cost_estimate=pl.CostEstimate(flops=4 * 512 * D, bytes_accessed=3 * 2**20, transcendentals=512),
    )(left, rows, ranks)


def rank_row(tail):
    tail = tail[0:1, :].astype(jnp.float32)
    return tail[:, :HALF] * BASE + tail[:, HALF:]


def rank_column(tail):
    return jnp.transpose(jnp.broadcast_to(rank_row(tail), (128, HALF)))


def score_kernel(jobs, row_of, key_of, count, *refs):
    ins, row_ref, key_ref = refs[:count], refs[count], refs[count + 1]

    def halves(index):
        ref = ins[index]
        if len(ref.shape) == 2:
            return [ref]
        return [ref.at[0], ref.at[1]]

    rows = [jnp.full((1, HALF), LOW, jnp.float32) for _ in range(row_ref.shape[0])]
    for job, (kind, keys, queries) in enumerate(jobs):
        views = [view for q in queries for view in halves(q)]
        if kind != "next":
            q_rank = [rank_row(view[HALF:, : 2 * HALF]) for view in views]

        def tile(view, slot, best, kind=kind, views=views):
            best = list(best)
            key = view[:HALF, :]
            if kind != "prev":
                k_rank = rank_column(view[HALF:, : 2 * HALF])
            side = jnp.full((HALF, 128), LOW, jnp.float32)
            for i, query in enumerate(views):
                scores = inner(key, query[:HALF, :])
                parts = []
                for c in range(0, HALF, 128):
                    piece = scores[:, c : c + 128]
                    if kind == "next":
                        parts.append(jnp.where(k_rank < FAR, piece, LOW))
                    elif kind == "prev":
                        side = jnp.maximum(side, jnp.where(q_rank[i][:, c : c + 128] < FAR, piece, LOW))
                    else:
                        earlier = k_rank < q_rank[i][:, c : c + 128]
                        parts.append(jnp.where(earlier, piece, LOW))
                        if kind == "pair":
                            side = jnp.maximum(side, jnp.where(earlier, LOW, piece))
                if parts:
                    top = [jnp.max(part, axis=0, keepdims=True) for part in parts]
                    best[i] = jnp.maximum(best[i], jnp.concatenate(top, axis=1))
            if slot is not None:
                key_ref[slot] = jnp.max(jnp.transpose(side), axis=0, keepdims=True)
            return best

        places = [row_of(job, i) for i in range(len(views))]
        best = [rows[p] if p is not None else jnp.zeros((1, HALF), jnp.float32) for p in places]
        first = key_of(job)
        flat = [k for k in keys if len(ins[k].shape) == 2]
        deep = [k for k in keys if len(ins[k].shape) == 3]
        for n, k in enumerate(flat):
            best = tile(ins[k], None if first is None else first + n, best)
        if deep:

            def step(h, best):
                for n, k in enumerate(deep):
                    slot = None if first is None else first + 2 * n + h
                    best = tile(ins[k].at[h], slot, best)
                return tuple(best)

            best = lax.fori_loop(0, 2, step, tuple(best))
        for p, value in zip(places, best):
            if p is not None:
                rows[p] = value
    for p, value in enumerate(rows):
        row_ref[p : p + 1, :] = value


def score(name, arrays, jobs, n_rows, row_of, n_keys, key_of):
    dots = 0
    size = lambda k: HALF * (2 if arrays[k].ndim == 3 else 1)
    for _, keys, queries in jobs:
        dots += 2 * D * sum(size(k) for k in keys) * sum(size(q) for q in queries)
    return pl.pallas_call(
        functools.partial(score_kernel, jobs, row_of, key_of, len(arrays)),
        in_specs=[VMEM] * len(arrays),
        out_specs=[VMEM, VMEM],
        out_shape=[
            jax.ShapeDtypeStruct((max(n_rows, 1), HALF), jnp.float32),
            jax.ShapeDtypeStruct((max(n_keys, 1), 1, HALF), jnp.float32),
        ],
        name=name,
        compiler_params=pltpu.CompilerParams(vmem_limit_bytes=32 * 2**20),
        cost_estimate=pl.CostEstimate(
            flops=dots, bytes_accessed=sum(2 * a.size for a in arrays), transcendentals=0
        ),
    )(*arrays)


def pick_count(sizes, which):
    return jnp.sum(jnp.where(jnp.arange(sizes.shape[0]) == which, sizes, 0))


def on_device(embeddings, sizes, ranks):
    rows = embeddings.shape[1]
    clusters = lax.axis_size("group")
    group_index = lax.axis_index("group")
    helper_index = lax.axis_index("helper")
    count = pick_count(sizes, group_index)
    left = count - helper_index * rows
    own = packed(embeddings[0], ranks, left[None])

    ownx = send(own, core=1)
    b03 = send(own, row=1)
    b10 = send(own, col=1)
    nxt = send(own, cluster=-1)
    b01a = send(own[0], row=-1)
    b01b = send(own[1], row=-1)
    prva = send(b01a, cluster=1)
    b13a = send(b03[0], col=1)
    b13b = send(b10[1], row=1)
    prvb = send(b01b, cluster=1)
    b01ax = send(b01a, core=1)
    b01bx = send(b01b, core=1)
    nxtx = send(nxt, core=1)
    prvax = send(prva, core=1)
    prvbx = send(prvb, core=1)

    row_self, _ = score("self", [own, ownx], [("self", [0, 1], [0])], 2, lambda j, i: i, 0, lambda j: None)
    row_own, key_own = score(
        "own", [own, ownx, b01a, b01b, b10], [("pair", [0, 1], [2, 3, 4])], 4, lambda j, i: i, 4, lambda j: 0
    )
    row_nxt, _ = score(
        "next", [nxt, nxtx, own, b01a, b01b, b03, b10], [("next", [0, 1], [2, 3, 4, 5, 6])],
        8, lambda j, i: i, 0, lambda j: None,
    )
    row_one, key_one = score(
        "one", [b01a, b01b, b01ax, b01bx, b03], [("pair", [0, 1, 2, 3], [4])], 2, lambda j, i: i, 4, lambda j: 0
    )
    _, key_prv = score(
        "prev", [prva, prvax, b03, b10], [("prev", [0, 1], [2, 3])], 0, lambda j, i: None, 2, lambda j: 0
    )
    row_last, key_last = score(
        "last",
        [own, ownx, b01a, b01b, b01ax, b01bx, nxt, nxtx, prva, prvax, b13a, b13b],
        [
            ("pair", [0, 1], [10, 11]),
            ("pair", [2, 3, 4, 5], [10, 11]),
            ("next", [6, 7], [10, 11]),
            ("prev", [8, 9], [10, 11]),
        ],
        4, lambda j, i: (i, i, 2 + i, None)[j], 10, lambda j: (0, 4, None, 8)[j],
    )
    _, key_end = score(
        "end", [prvb, prvbx, b03, b10, b13a, b13b], [("prev", [0, 1], [2, 3, 4, 5])],
        0, lambda j, i: None, 2, lambda j: 0,
    )

    key_own, key_one, key_prv = key_own[:, 0], key_one[:, 0], key_prv[:, 0]
    key_last, key_end = key_last[:, 0], key_end[:, 0]
    key_own = jnp.maximum(key_own, key_last[:4])
    key_one = jnp.maximum(key_one, key_last[4:8])
    key_prv = jnp.maximum(key_prv, key_last[8:10])

    back_01 = send(jnp.concatenate([row_own[:2], row_nxt[2:4]]), row=1)
    back_03 = send(jnp.concatenate([row_one, row_nxt[4:6]]), row=-1)
    back_10 = send(jnp.concatenate([row_own[2:4], row_nxt[6:8]]), col=1)
    back_13 = send(row_last, col=1, row=-1)
    back_own = send(key_own[2:], core=1)
    back_one = send(key_one[:2], row=1)
    back_onex = send(key_one[2:], row=1, core=1)
    back_prv = send(jnp.concatenate([key_prv[:1], key_end[:1]]), cluster=-1, row=1)
    back_prvx = send(jnp.concatenate([key_prv[1:], key_end[1:]]), cluster=-1, row=1, core=1)

    def largest(*values):
        return functools.reduce(jnp.maximum, values).reshape(1, rows)

    within = largest(
        row_self, key_own[:2], back_own, back_01[:2], back_03[:2], back_10[:2], back_13[:2], back_one, back_onex
    )
    adjacent = largest(row_nxt[:2], back_01[2:], back_03[2:], back_10[2:], back_13[2:], back_prv, back_prvx)
    next_count = pick_count(sizes, (group_index + 1) % clusters)
    adjacent = jnp.where(next_count < rows * lax.axis_size("helper"), jnp.maximum(adjacent, -1.0), adjacent)
    real = (jnp.arange(rows, dtype=jnp.int32) < left)[None, :]
    within = jnp.where(real, jnp.maximum(within, -1.0), 0.0)
    return (within, jnp.where(real, adjacent, 0.0))


def solution(mesh):
    in_specs = (P("group", "helper", None), P(), P("group", "helper"))
    out_specs = (P("group", "helper"), P("group", "helper"))
    return jax.shard_map(
        on_device, mesh=mesh, in_specs=in_specs, out_specs=out_specs, check_vma=False
    )
```

time: 236 us -> 102 us (0.43)
  waiting for transfers between devices: 158 us -> 39.7 us
  Pallas kernels: 0 us -> 30.3 us
  matrix products: 28.3 us -> 0 us
  blocking collectives: 18.6 us -> 0 us
  starting transfers between devices: 6.73 us -> 24.1 us
  between operations: 14.1 us -> 2.27 us
  other arithmetic: 8.28 us -> 1.97 us
    all_gather x2 -> x0, waiting for transfers between devices: 116 us -> none  [the longest x1 75.6 us: on_device(): lax.all_gather(next_rows, 'helper', axis=0, tiled=True)]
    pallas_call x0 -> x8, Pallas kernels: none -> 30.3 us  [the longest x7 29.9 us: score(): pl.pallas_call(functools.partial(score_kernel, jobs, row_of, key_of, len(...]
    dot_general x2 -> x0, matrix products: 28.3 us -> none  [inner(): lax.dot_general(queries, keys, (((1,), (1,)), ((), ())), preferred_elemen...]
    all_gather x1 -> x0, blocking collectives: 18.6 us -> none  [on_device(): key_rank = lax.all_gather(own_rank, 'helper', axis=0, tiled=True)]
    ppermute x1 -> x24, starting transfers between devices: 6.65 us -> 24.1 us  [send(): return lax.ppermute(value, AXES, pairs(**shift))]
    convert_element_type x1 -> x0, other arithmetic: 2.76 us -> none  [normalize(): return (values * scale).astype(jnp.bfloat16)]
    ppermute x1 -> x24, waiting for transfers between devices: 41.6 us -> 39.7 us  [send(): return lax.ppermute(value, AXES, pairs(**shift))]
  transfers between devices with their start and end apart: 3 -> 24, of which waited for: 3 -> 8; matrix products, arithmetic and copies ran while one was open for 8% -> 0% of each run, Pallas kernels for 0% -> 22%
where the time goes in v1:
time: 102 us; the launch traced here: 101 us
  waiting for transfers between devices  39.7 us (39%)
  Pallas kernels  30.3 us (30%)
  starting transfers between devices  24.1 us (24%)
  local copies, waits for them, and re-layouts  3.13 us (3%)
  between operations  2.27 us (2%)
  other arithmetic  1.97 us (2%)
    ppermute x24, waiting for transfers between devices, send(): return lax.ppermute(value, AXES, pairs(**shift))  39.7 us
    pallas_call x7, Pallas kernels, score(): pl.pallas_call(functools.partial(score_kernel, jobs, row_of, key_of, len(...  29.9 us
    ppermute x24, starting transfers between devices, send(): return lax.ppermute(value, AXES, pairs(**shift))  24.1 us
    unnamed x12, local copies, waits for them, and re-layouts  2.96 us
  transfers between devices with their start and end apart: 24, of which 8 were waited for; matrix products, arithmetic and copies ran while one was open for 0% of the time, Pallas kernels for 22%

profile of v1, /device:TPU:0, one launch (start us, length us, event | category | flops | bytes accessed | tf_op | source)
XLA Modules:
  0.0 101.4 jit_solution(10935157440407434851)
XLA Ops:
  0.6 1.3 %fusion.10 = (s32[]{:T(128)}, s32[]{:T(128)}) fusion(s32[8]{0:T(128)} %param.4, s32[]{:T(128)S(6)} %select_n.55, s32[]{:T(128)S(6)} %axis_index.23), kind=kLoop, calls=%fused_computation.43 | loop fusion | flops 46 | bytes 48 | tf_op jit(solution)/shard_map/reduce_sum | solution.py:188
  2.6 1.6 %copy-done = f32[1,512,1024]{2,1,0:T(8,128)S(1)} copy-done((f32[1,512,1024]{2,1,0:T(8,128)S(1)}, f32[1,512,1024]{2,1,0:T(8,128)}, u32[]{:S(2)}) %copy-start) | copy-done | bytes 2097176
  5.3 3.2 %collective-permute-start.2 = (bf16[264,1024]{1,0:T(8,128)(2,1)S(1)}, bf16[264,1024]{1,0:T(8,128)(2,1)}, u32[]{:S(2)}, u32[]{:S(2)}) collective-permute-start(bf16[264,1024]{1,0:T(8,128)(2,1)S(1)} %get-tuple-element.24), channel_id=1, source_target_pairs={{0,12},{1,13},{2,14},{3,15},{4,0},{5,1},{6,2},{7,3},{8,4},{9,5},{1... | collective-permute-start | bytes 1622024 | tf_op jit(solution)/shard_map/ppermute | solution.py:52
  9.2 1.3 %collective-permute-start.10 = (bf16[2,264,1024]{2,1,0:T(8,128)(2,1)S(1)}, bf16[2,264,1024]{2,1,0:T(8,128)(2,1)S(1)}, u32[]{:S(2)}, u32[]{:S(2)}) collective-permute-start(bf16[2,264,1024]{2,1,0:T(8,128)(2,1)S(1)} %pack.1.refs_0_.refs_2_), channel_id=1, source_target_pairs={{0,4},{1,5},{2,6},{3,7},{4,8},{5,9},{6,10},{7,11},{8,12},{9,13},{1... | collective-permute-start | bytes 3244040 | tf_op jit(solution)/shard_map/ppermute | solution.py:52
  10.5 1.5 %collective-permute-start.3 = (bf16[2,264,1024]{2,1,0:T(8,128)(2,1)S(1)}, bf16[2,264,1024]{2,1,0:T(8,128)(2,1)S(1)}, u32[]{:S(2)}, u32[]{:S(2)}) collective-permute-start(bf16[2,264,1024]{2,1,0:T(8,128)(2,1)S(1)} %pack.1.refs_0_.refs_2_), channel_id=1, source_target_pairs={{0,2},{1,3},{2,0},{3,1},{4,6},{5,7},{6,4},{7,5},{8,10},{9,11},{10,... | collective-permute-start | bytes 3244040 | tf_op jit(solution)/shard_map/ppermute | solution.py:52
  12.0 9.2 %collective-permute-done.2.refs_3_.refs_4_.refs_1_ = bf16[264,1024]{1,0:T(8,128)(2,1)} collective-permute-done((bf16[264,1024]{1,0:T(8,128)(2,1)S(1)}, bf16[264,1024]{1,0:T(8,128)(2,1)}, u32[]{:S(2)}, u32[]{:S(2)}) %collective-permute-start.2) | collective-permute-done | bytes 540704 | tf_op jit(solution)/shard_map/ppermute | solution.py:52
  21.2 1.9 %collective-permute-start.20 = (bf16[264,1024]{1,0:T(8,128)(2,1)}, bf16[264,1024]{1,0:T(8,128)(2,1)S(1)}, u32[]{:S(2)}, u32[]{:S(2)}) collective-permute-start(bf16[264,1024]{1,0:T(8,128)(2,1)} %collective-permute-done.2.refs_3_.refs_4_.refs_1_), channel_id=1, source_target_pairs={{0,16},{1,17},{2,18},{3,19},{4,20},{5,21},{6,22},{7,23},{8,24},{9,... | collective-permute-start | bytes 1622024 | tf_op jit(solution)/shard_map/ppermute | solution.py:52
  23.1 4.3 %collective-permute-start.6 = (bf16[2,264,1024]{2,1,0:T(8,128)(2,1)S(1)}, bf16[2,264,1024]{2,1,0:T(8,128)(2,1)}, u32[]{:S(2)}, u32[]{:S(2)}) collective-permute-start(bf16[2,264,1024]{2,1,0:T(8,128)(2,1)S(1)} %pack.1.refs_0_.refs_2_), channel_id=1, source_target_pairs={{0,114},{1,115},{2,112},{3,113},{4,118},{5,119},{6,116},{7,117},{8... | collective-permute-start | bytes 3244040 | tf_op jit(solution)/shard_map/ppermute | solution.py:52
  27.4 4.2 %collective-permute-done.1.refs_2_.refs_3_.refs_0_ = bf16[264,1024]{1,0:T(8,128)(2,1)} collective-permute-done((bf16[264,1024]{1,0:T(8,128)(2,1)S(1)}, bf16[264,1024]{1,0:T(8,128)(2,1)}, u32[]{:S(2)}, u32[]{:S(2)}) %collective-permute-start.1) | collective-permute-done | bytes 540704 | tf_op jit(solution)/shard_map/ppermute | solution.py:52
  31.6 6.3 %collective-permute-done.20.refs_0_ = bf16[264,1024]{1,0:T(8,128)(2,1)S(1)} collective-permute-done((bf16[264,1024]{1,0:T(8,128)(2,1)}, bf16[264,1024]{1,0:T(8,128)(2,1)S(1)}, u32[]{:S(2)}, u32[]{:S(2)}) %collective-permute-start.20) | collective-permute-done | bytes 540704 | tf_op jit(solution)/shard_map/ppermute | solution.py:52
  39.4 13.5 %collective-permute-done.8.refs_8_.refs_0_ = bf16[264,1024]{1,0:T(8,128)(2,1)} collective-permute-done((bf16[264,1024]{1,0:T(8,128)(2,1)}, bf16[264,1024]{1,0:T(8,128)(2,1)}, u32[]{:S(2)}, u32[]{:S(2)}) %collective-permute-start.8) | collective-permute-done | bytes 540704 | tf_op jit(solution)/shard_map/ppermute | solution.py:52
  53.5 1.2 %collective-permute-start.12 = (bf16[264,1024]{1,0:T(8,128)(2,1)S(1)}, bf16[264,1024]{1,0:T(8,128)(2,1)S(1)}, u32[]{:S(2)}, u32[]{:S(2)}) collective-permute-start(bf16[264,1024]{1,0:T(8,128)(2,1)S(1)} %slice_bitcast_fusion), channel_id=1, source_target_pairs={{0,4},{1,5},{2,6},{3,7},{4,8},{5,9},{6,10},{7,11},{8,12},{9,13},{1... | collective-permute-start | bytes 1622024 | tf_op jit(solution)/shard_map/ppermute | solution.py:52
  54.8 3.0 %one.1 = (f32[2,256]{1,0:T(2,128)S(1)}, f32[4,1,256]{2,1,0:T(1,128)S(1)}) custom-call(bf16[264,1024]{1,0:T(8,128)(2,1)} %collective-permute-done.1.refs_2_.refs_3_.refs_0_, bf16[264,1024]{1,0:T(8,128)(2,1)} %collective-permute-done.2.refs_3_.refs_4_.refs_1_, bf16[264,1024]{1,0:T(8,128)(2,1)} %collective-permute-done.4.refs_4_.refs_2_, ...), custom_call_target="tpu_custom_call" | custom-call | flops 1073741824 | bytes 3244032 | tf_op jit(solution)/shard_map/one/pallas_call | solution.py:171
  57.8 4.5 %own.1 = (f32[4,256]{1,0:T(4,128)S(1)}, f32[4,1,256]{2,1,0:T(1,128)S(1)}) custom-call(bf16[2,264,1024]{2,1,0:T(8,128)(2,1)S(1)} %pack.1.refs_0_.refs_2_, bf16[2,264,1024]{2,1,0:T(8,128)(2,1)} %collective-permute-done.refs_1_, bf16[264,1024]{1,0:T(8,128)(2,1)} %collective-permute-done.1.refs_2_.refs_3_.refs_0_, ...), custom_call_target="tpu_custom_call" | custom-call | flops 2147483648 | bytes 4325376 | tf_op jit(solution)/shard_map/own/pallas_call | solution.py:171
  62.3 2.9 %prev.1 = (f32[1,256]{1,0:T(1,128)}, f32[2,1,256]{2,1,0:T(1,128)S(1)}) custom-call(bf16[264,1024]{1,0:T(8,128)(2,1)} %collective-permute-done.8.refs_8_.refs_0_, bf16[264,1024]{1,0:T(8,128)(2,1)S(1)} %collective-permute-done.9.refs_9_.refs_1_, bf16[2,264,1024]{2,1,0:T(8,128)(2,1)S(1)} %collective-permute-done.10.refs_5_.refs_4_.refs_2_, ...), custom_call_target="tpu_custom_call" | custom-call | flops 1073741824 | bytes 3244032 | tf_op jit(solution)/shard_map/prev/pallas_call | solution.py:171
  65.1 2.5 %collective-permute-done.11.refs_10_.refs_4_ = bf16[264,1024]{1,0:T(8,128)(2,1)S(1)} collective-permute-done((bf16[264,1024]{1,0:T(8,128)(2,1)S(1)}, bf16[264,1024]{1,0:T(8,128)(2,1)S(1)}, u32[]{:S(2)}, u32[]{:S(2)}) %collective-permute-start.11) | collective-permute-done | bytes 540704 | tf_op jit(solution)/shard_map/ppermute | solution.py:52
  67.7 2.1 %collective-permute-done.12.refs_11_.refs_5_ = bf16[264,1024]{1,0:T(8,128)(2,1)S(1)} collective-permute-done((bf16[264,1024]{1,0:T(8,128)(2,1)S(1)}, bf16[264,1024]{1,0:T(8,128)(2,1)S(1)}, u32[]{:S(2)}, u32[]{:S(2)}) %collective-permute-start.12) | collective-permute-done | bytes 540704 | tf_op jit(solution)/shard_map/ppermute | solution.py:52
  69.8 2.4 %end.1 = (f32[1,256]{1,0:T(1,128)}, f32[2,1,256]{2,1,0:T(1,128)S(1)}) custom-call(bf16[264,1024]{1,0:T(8,128)(2,1)S(1)} %copy-done.3, bf16[264,1024]{1,0:T(8,128)(2,1)S(1)} %collective-permute-done.21.refs_1_, bf16[2,264,1024]{2,1,0:T(8,128)(2,1)S(1)} %collective-permute-done.10.refs_5_.refs_4_.refs_2_, ...), custom_call_target="tpu_custom_call" | custom-call | flops 1610612736 | bytes 4325376 | tf_op jit(solution)/shard_map/end/pallas_call | solution.py:171
  72.3 7.9 %last.1 = (f32[4,256]{1,0:T(4,128)S(1)}, f32[10,1,256]{2,1,0:T(1,128)S(1)}) custom-call(bf16[2,264,1024]{2,1,0:T(8,128)(2,1)S(1)} %pack.1.refs_0_.refs_2_, bf16[2,264,1024]{2,1,0:T(8,128)(2,1)} %collective-permute-done.refs_1_, bf16[264,1024]{1,0:T(8,128)(2,1)} %collective-permute-done.1.refs_2_.refs_3_.refs_0_, ...), custom_call_target="tpu_custom_call" | custom-call | flops 3758096384 | bytes 8650752 | tf_op jit(solution)/shard_map/last/pallas_call | solution.py:171
  80.5 4.6 %collective-permute-start.17 = (f32[4,256]{1,0:T(4,128)S(1)}, f32[4,256]{1,0:T(4,128)S(1)}, u32[]{:S(2)}, u32[]{:S(2)}) collective-permute-start(f32[4,256]{1,0:T(4,128)S(1)} %get-tuple-element.18), channel_id=1, source_target_pairs={{0,14},{1,15},{2,12},{3,13},{4,2},{5,3},{6,0},{7,1},{8,6},{9,7},{1... | collective-permute-start | bytes 12296 | tf_op jit(solution)/shard_map/ppermute | solution.py:52
  85.1 6.3 %next.1 = (f32[8,256]{1,0:T(8,128)S(1)}, f32[1,1,256]{2,1,0:T(1,128)}) custom-call(bf16[2,264,1024]{2,1,0:T(8,128)(2,1)} %collective-permute-done.6.refs_6_.refs_0_, bf16[2,264,1024]{2,1,0:T(8,128)(2,1)S(1)} %collective-permute-done.7.refs_7_.refs_1_, bf16[2,264,1024]{2,1,0:T(8,128)(2,1)S(1)} %pack.1.refs_0_.refs_2_, ...), custom_call_target="tpu_custom_call" | custom-call | flops 4294967296 | bytes 6488064 | tf_op jit(solution)/shard_map/next/pallas_call | solution.py:171
  92.8 3.2 %collective-permute-start.15 = (f32[4,256]{1,0:T(4,128)S(1)}, f32[4,256]{1,0:T(4,128)S(1)}, u32[]{:S(2)}, u32[]{:S(2)}) collective-permute-start(f32[4,256]{1,0:T(4,128)S(1)} %pad_maximum_fusion.1), channel_id=1, source_target_pairs={{0,12},{1,13},{2,14},{3,15},{4,0},{5,1},{6,2},{7,3},{8,4},{9,5},{1... | collective-permute-start | bytes 12296 | tf_op jit(solution)/shard_map/ppermute | solution.py:52
  96.4 2.9 %self.1 = (f32[2,256]{1,0:T(2,128)S(1)}, f32[1,1,256]{2,1,0:T(1,128)}) custom-call(bf16[2,264,1024]{2,1,0:T(8,128)(2,1)S(1)} %pack.1.refs_0_.refs_2_, bf16[2,264,1024]{2,1,0:T(8,128)(2,1)} %collective-permute-done.refs_1_), custom_call_target="tpu_custom_call" | custom-call | flops 1073741824 | bytes 2162688 | tf_op jit(solution)/shard_map/self/pallas_call | solution.py:171
  99.3 1.5 %collective-permute-done.14 = f32[4,256]{1,0:T(4,128)S(1)} collective-permute-done((f32[4,256]{1,0:T(4,128)S(1)}, f32[4,256]{1,0:T(4,128)S(1)}, u32[]{:S(2)}, u32[]{:S(2)}) %collective-permute-start.14) | collective-permute-done | bytes 4128 | tf_op jit(solution)/shard_map/ppermute | solution.py:52
  (65 shorter events, 5.9 us)
Async XLA Ops:
  5.3 15.8 %collective-permute-start.2 = (bf16[264,1024]{1,0:T(8,128)(2,1)S(1)}, bf16[264,1024]{1,0:T(8,128)(2,1)}, u32[]{:S(2)}, u32[]{:S(2)}) collective-permute-start(bf16[264,1024]{1,0:T(8,128)(2,1)S(1)} %get-tuple-element.24), channel_id=1, source_target_pairs={{0,12},{1,13},{2,14},{3,15},{4,0},{5,1},{6,2},{7,3},{8,4},{9,5},{1... | collective-permute-start | bytes 1622024 | tf_op jit(solution)/shard_map/ppermute | solution.py:52
  8.5 23.1 %collective-permute-start.1 = (bf16[264,1024]{1,0:T(8,128)(2,1)S(1)}, bf16[264,1024]{1,0:T(8,128)(2,1)}, u32[]{:S(2)}, u32[]{:S(2)}) collective-permute-start(bf16[264,1024]{1,0:T(8,128)(2,1)S(1)} %get-tuple-element.25), channel_id=1, source_target_pairs={{0,12},{1,13},{2,14},{3,15},{4,0},{5,1},{6,2},{7,3},{8,4},{9,5},{1... | collective-permute-start | bytes 1622024 | tf_op jit(solution)/shard_map/ppermute | solution.py:52
  9.2 28.6 %collective-permute-start.10 = (bf16[2,264,1024]{2,1,0:T(8,128)(2,1)S(1)}, bf16[2,264,1024]{2,1,0:T(8,128)(2,1)S(1)}, u32[]{:S(2)}, u32[]{:S(2)}) collective-permute-start(bf16[2,264,1024]{2,1,0:T(8,128)(2,1)S(1)} %pack.1.refs_0_.refs_2_), channel_id=1, source_target_pairs={{0,4},{1,5},{2,6},{3,7},{4,8},{5,9},{6,10},{7,11},{8,12},{9,13},{1... | collective-permute-start | bytes 3244040 | tf_op jit(solution)/shard_map/ppermute | solution.py:52
  10.5 27.5 %collective-permute-start.3 = (bf16[2,264,1024]{2,1,0:T(8,128)(2,1)S(1)}, bf16[2,264,1024]{2,1,0:T(8,128)(2,1)S(1)}, u32[]{:S(2)}, u32[]{:S(2)}) collective-permute-start(bf16[2,264,1024]{2,1,0:T(8,128)(2,1)S(1)} %pack.1.refs_0_.refs_2_), channel_id=1, source_target_pairs={{0,2},{1,3},{2,0},{3,1},{4,6},{5,7},{6,4},{7,5},{8,10},{9,11},{10,... | collective-permute-start | bytes 3244040 | tf_op jit(solution)/shard_map/ppermute | solution.py:52
  21.2 16.7 %collective-permute-start.20 = (bf16[264,1024]{1,0:T(8,128)(2,1)}, bf16[264,1024]{1,0:T(8,128)(2,1)S(1)}, u32[]{:S(2)}, u32[]{:S(2)}) collective-permute-start(bf16[264,1024]{1,0:T(8,128)(2,1)} %collective-permute-done.2.refs_3_.refs_4_.refs_1_), channel_id=1, source_target_pairs={{0,16},{1,17},{2,18},{3,19},{4,20},{5,21},{6,22},{7,23},{8,24},{9,... | collective-permute-start | bytes 1622024 | tf_op jit(solution)/shard_map/ppermute | solution.py:52
  23.1 29.8 %collective-permute-start.6 = (bf16[2,264,1024]{2,1,0:T(8,128)(2,1)S(1)}, bf16[2,264,1024]{2,1,0:T(8,128)(2,1)}, u32[]{:S(2)}, u32[]{:S(2)}) collective-permute-start(bf16[2,264,1024]{2,1,0:T(8,128)(2,1)S(1)} %pack.1.refs_0_.refs_2_), channel_id=1, source_target_pairs={{0,114},{1,115},{2,112},{3,113},{4,118},{5,119},{6,116},{7,117},{8... | collective-permute-start | bytes 3244040 | tf_op jit(solution)/shard_map/ppermute | solution.py:52
  31.6 21.8 %collective-permute-start = (bf16[2,264,1024]{2,1,0:T(8,128)(2,1)S(1)}, bf16[2,264,1024]{2,1,0:T(8,128)(2,1)}, u32[]{:S(2)}, u32[]{:S(2)}) collective-permute-start(bf16[2,264,1024]{2,1,0:T(8,128)(2,1)S(1)} %pack.1.refs_0_.refs_2_), channel_id=1, source_target_pairs={{0,1},{1,0},{2,3},{3,2},{4,5},{5,4},{6,7},{7,6},{8,9},{9,8},{10,11... | collective-permute-start | bytes 3244040 | tf_op jit(solution)/shard_map/ppermute | solution.py:52
  37.9 15.0 %collective-permute-start.8 = (bf16[264,1024]{1,0:T(8,128)(2,1)}, bf16[264,1024]{1,0:T(8,128)(2,1)}, u32[]{:S(2)}, u32[]{:S(2)}) collective-permute-start(bf16[264,1024]{1,0:T(8,128)(2,1)} %collective-permute-done.1.refs_2_.refs_3_.refs_0_), channel_id=1, source_target_pairs={{0,16},{1,17},{2,18},{3,19},{4,20},{5,21},{6,22},{7,23},{8,24},{9,... | collective-permute-start | bytes 1622024 | tf_op jit(solution)/shard_map/ppermute | solution.py:52
  37.9 15.6 %collective-permute-start.4 = (bf16[264,1024]{1,0:T(8,128)(2,1)}, bf16[264,1024]{1,0:T(8,128)(2,1)}, u32[]{:S(2)}, u32[]{:S(2)}) collective-permute-start(bf16[264,1024]{1,0:T(8,128)(2,1)} %collective-permute-done.1.refs_2_.refs_3_.refs_0_), channel_id=1, source_target_pairs={{0,1},{1,0},{2,3},{3,2},{4,5},{5,4},{6,7},{7,6},{8,9},{9,8},{10,11... | collective-permute-start | bytes 1622024 | tf_op jit(solution)/shard_map/ppermute | solution.py:52
  38.7 16.1 %collective-permute-start.5 = (bf16[264,1024]{1,0:T(8,128)(2,1)}, bf16[264,1024]{1,0:T(8,128)(2,1)}, u32[]{:S(2)}, u32[]{:S(2)}) collective-permute-start(bf16[264,1024]{1,0:T(8,128)(2,1)} %collective-permute-done.2.refs_3_.refs_4_.refs_1_), channel_id=1, source_target_pairs={{0,1},{1,0},{2,3},{3,2},{4,5},{5,4},{6,7},{7,6},{8,9},{9,8},{10,11... | collective-permute-start | bytes 1622024 | tf_op jit(solution)/shard_map/ppermute | solution.py:52
  52.9 9.4 %collective-permute-start.9 = (bf16[264,1024]{1,0:T(8,128)(2,1)}, bf16[264,1024]{1,0:T(8,128)(2,1)S(1)}, u32[]{:S(2)}, u32[]{:S(2)}) collective-permute-start(bf16[264,1024]{1,0:T(8,128)(2,1)} %collective-permute-done.8.refs_8_.refs_0_), channel_id=1, source_target_pairs={{0,1},{1,0},{2,3},{3,2},{4,5},{5,4},{6,7},{7,6},{8,9},{9,8},{10,11... | collective-permute-start | bytes 1622024 | tf_op jit(solution)/shard_map/ppermute | solution.py:52
  52.9 19.4 %collective-permute-start.7 = (bf16[2,264,1024]{2,1,0:T(8,128)(2,1)}, bf16[2,264,1024]{2,1,0:T(8,128)(2,1)S(1)}, u32[]{:S(2)}, u32[]{:S(2)}) collective-permute-start(bf16[2,264,1024]{2,1,0:T(8,128)(2,1)} %collective-permute-done.6.refs_6_.refs_0_), channel_id=1, source_target_pairs={{0,1},{1,0},{2,3},{3,2},{4,5},{5,4},{6,7},{7,6},{8,9},{9,8},{10,11... | collective-permute-start | bytes 3244040 | tf_op jit(solution)/shard_map/ppermute | solution.py:52
  53.4 14.3 %collective-permute-start.11 = (bf16[264,1024]{1,0:T(8,128)(2,1)S(1)}, bf16[264,1024]{1,0:T(8,128)(2,1)S(1)}, u32[]{:S(2)}, u32[]{:S(2)}) collective-permute-start(bf16[264,1024]{1,0:T(8,128)(2,1)S(1)} %slice_bitcast_fusion.1), channel_id=1, source_target_pairs={{0,2},{1,3},{2,0},{3,1},{4,6},{5,7},{6,4},{7,5},{8,10},{9,11},{10,... | collective-permute-start | bytes 1622024 | tf_op jit(solution)/shard_map/ppermute | solution.py:52
  53.5 16.3 %collective-permute-start.12 = (bf16[264,1024]{1,0:T(8,128)(2,1)S(1)}, bf16[264,1024]{1,0:T(8,128)(2,1)S(1)}, u32[]{:S(2)}, u32[]{:S(2)}) collective-permute-start(bf16[264,1024]{1,0:T(8,128)(2,1)S(1)} %slice_bitcast_fusion), channel_id=1, source_target_pairs={{0,4},{1,5},{2,6},{3,7},{4,8},{5,9},{6,10},{7,11},{8,12},{9,13},{1... | collective-permute-start | bytes 1622024 | tf_op jit(solution)/shard_map/ppermute | solution.py:52
  54.7 10.4 %collective-permute-start.21 = (bf16[264,1024]{1,0:T(8,128)(2,1)S(1)}, bf16[264,1024]{1,0:T(8,128)(2,1)S(1)}, u32[]{:S(2)}, u32[]{:S(2)}) collective-permute-start(bf16[264,1024]{1,0:T(8,128)(2,1)S(1)} %copy-done.3), channel_id=1, source_target_pairs={{0,1},{1,0},{2,3},{3,2},{4,5},{5,4},{6,7},{7,6},{8,9},{9,8},{10,11... | collective-permute-start | bytes 1622024 | tf_op jit(solution)/shard_map/ppermute | solution.py:52
  80.2 11.5 %collective-permute-start.23 = (f32[2,256]{1,0:T(2,128)S(1)}, f32[2,256]{1,0:T(2,128)S(1)}, u32[]{:S(2)}, u32[]{:S(2)}) collective-permute-start(f32[2,256]{1,0:T(2,128)S(1)} %pad_maximum_fusion.4), channel_id=1, source_target_pairs={{0,119},{1,118},{2,117},{3,116},{4,123},{5,122},{6,121},{7,120},{8... | collective-permute-start | bytes 6152 | tf_op jit(solution)/shard_map/ppermute | solution.py:52
  80.3 12.5 %collective-permute-start.22 = (f32[2,256]{1,0:T(2,128)S(1)}, f32[2,256]{1,0:T(2,128)S(1)}, u32[]{:S(2)}, u32[]{:S(2)}) collective-permute-start(f32[2,256]{1,0:T(2,128)S(1)} %pad_maximum_fusion.3), channel_id=1, source_target_pairs={{0,118},{1,119},{2,116},{3,117},{4,122},{5,123},{6,120},{7,121},{8... | collective-permute-start | bytes 6152 | tf_op jit(solution)/shard_map/ppermute | solution.py:52
  80.5 18.9 %collective-permute-start.17 = (f32[4,256]{1,0:T(4,128)S(1)}, f32[4,256]{1,0:T(4,128)S(1)}, u32[]{:S(2)}, u32[]{:S(2)}) collective-permute-start(f32[4,256]{1,0:T(4,128)S(1)} %get-tuple-element.18), channel_id=1, source_target_pairs={{0,14},{1,15},{2,12},{3,13},{4,2},{5,3},{6,0},{7,1},{8,6},{9,7},{1... | collective-permute-start | bytes 12296 | tf_op jit(solution)/shard_map/ppermute | solution.py:52
  91.5 4.5 %collective-permute-start.19 = (f32[2,256]{1,0:T(2,128)S(1)}, f32[2,256]{1,0:T(2,128)S(1)}, u32[]{:S(2)}, u32[]{:S(2)}) collective-permute-start(f32[2,256]{1,0:T(2,128)S(1)} %bitcast.48), channel_id=1, source_target_pairs={{0,5},{1,4},{2,7},{3,6},{4,9},{5,8},{6,11},{7,10},{8,13},{9,12},{1... | collective-permute-start | bytes 6152 | tf_op jit(solution)/shard_map/ppermute | solution.py:52
  91.6 4.9 %collective-permute-start.18 = (f32[2,256]{1,0:T(2,128)S(1)}, f32[2,256]{1,0:T(2,128)S(1)}, u32[]{:S(2)}, u32[]{:S(2)}) collective-permute-start(f32[2,256]{1,0:T(2,128)S(1)} %bitcast.47), channel_id=1, source_target_pairs={{0,4},{1,5},{2,6},{3,7},{4,8},{5,9},{6,10},{7,11},{8,12},{9,13},{1... | collective-permute-start | bytes 6152 | tf_op jit(solution)/shard_map/ppermute | solution.py:52
  91.7 7.6 %collective-permute-start.16 = (f32[4,256]{1,0:T(4,128)S(1)}, f32[4,256]{1,0:T(4,128)S(1)}, u32[]{:S(2)}, u32[]{:S(2)}) collective-permute-start(f32[4,256]{1,0:T(4,128)S(1)} %pad_maximum_fusion.2), channel_id=1, source_target_pairs={{0,2},{1,3},{2,0},{3,1},{4,6},{5,7},{6,4},{7,5},{8,10},{9,11},{10,... | collective-permute-start | bytes 12296 | tf_op jit(solution)/shard_map/ppermute | solution.py:52
  92.8 6.6 %collective-permute-start.15 = (f32[4,256]{1,0:T(4,128)S(1)}, f32[4,256]{1,0:T(4,128)S(1)}, u32[]{:S(2)}, u32[]{:S(2)}) collective-permute-start(f32[4,256]{1,0:T(4,128)S(1)} %pad_maximum_fusion.1), channel_id=1, source_target_pairs={{0,12},{1,13},{2,14},{3,15},{4,0},{5,1},{6,2},{7,3},{8,4},{9,5},{1... | collective-permute-start | bytes 12296 | tf_op jit(solution)/shard_map/ppermute | solution.py:52
  96.0 4.8 %collective-permute-start.14 = (f32[4,256]{1,0:T(4,128)S(1)}, f32[4,256]{1,0:T(4,128)S(1)}, u32[]{:S(2)}, u32[]{:S(2)}) collective-permute-start(f32[4,256]{1,0:T(4,128)S(1)} %pad_maximum_fusion), channel_id=1, source_target_pairs={{0,4},{1,5},{2,6},{3,7},{4,8},{5,9},{6,10},{7,11},{8,12},{9,13},{1... | collective-permute-start | bytes 12296 | tf_op jit(solution)/shard_map/ppermute | solution.py:52
  96.4 2.9 %collective-permute-start.13 = (f32[2,256]{1,0:T(2,128)S(1)}, f32[2,256]{1,0:T(2,128)S(1)}, u32[]{:S(2)}, u32[]{:S(2)}) collective-permute-start(f32[2,256]{1,0:T(2,128)S(1)} %slice_bitcast_fusion.4), channel_id=1, source_target_pairs={{0,1},{1,0},{2,3},{3,2},{4,5},{5,4},{6,7},{7,6},{8,9},{9,8},{10,11... | collective-permute-start | bytes 6152 | tf_op jit(solution)/shard_map/ppermute | solution.py:52
  (4 other events, 18.5 us)

commit v2 on v0

v2 whole, which is shorter than its diff:
```python
import functools
import math

import jax
import jax.numpy as jnp
from jax import lax
from jax.experimental import pallas as pl
from jax.experimental.pallas import tpu as pltpu
from jax.sharding import PartitionSpec as P

D = 1024
HALF = 256
EXTRA = 8
PAY = HALF + EXTRA
BASE = 64
FAR = 8192.0
LOW = -4.0
AXES = ("group", "helper")
VMEM = pl.BlockSpec(memory_space=pltpu.VMEM)
SMEM = pl.BlockSpec(memory_space=pltpu.SMEM)


def place(index):
    group, helper = divmod(index, 16)
    return {
        "part": group // 4,
        "z": group % 4,
        "row": helper // 4,
        "col": (helper // 2) % 2,
        "core": helper % 2,
    }


def number(at):
    return (at["part"] * 4 + at["z"]) * 16 + at["row"] * 4 + at["col"] * 2 + at["core"]


def pairs(col=0, row=0, core=0, cluster=0):
    out = []
    for source in range(128):
        at = place(source)
        step = at["part"] * 4 + at["z"] + cluster
        flip = 1 if step // 4 != at["part"] else 0
        at["part"], at["z"] = (step // 4) % 2, step % 4
        at["col"] = (at["col"] + col + flip) % 2
        at["row"] = (at["row"] + row) % 4
        at["core"] = (at["core"] + core) % 2
        out.append((source, number(at)))
    return out


def send(name, value, **shift):
    with jax.named_scope(name):
        return lax.ppermute(value, AXES, pairs(**shift))


def after(value, *others):
    return lax.optimization_barrier((value, *others))[0]


def inner(keys, queries):
    return lax.dot_general(
        keys, queries, (((1,), (1,)), ((), ())), preferred_element_type=jnp.float32
    )


PARTS = 4


def own_count(sizes_ref, step=0):
    return sizes_ref[lax.rem(lax.axis_index("group") + step, lax.axis_size("group"))]


def pack_kernel(sizes_ref, rows_hbm, rank_ref, pay_ref, a_ref, b_ref, rows_ref, sem):
    part = 2 * HALF // PARTS
    copies = [
        pltpu.make_async_copy(rows_hbm.at[pl.ds(i * part, part)], rows_ref.at[pl.ds(i * part, part)], sem.at[i])
        for i in range(PARTS)
    ]
    for copy in copies:
        copy.start()
    left = own_count(sizes_ref) - lax.axis_index("helper") * 2 * HALF
    for half, half_ref in enumerate((a_ref, b_ref)):
        rank = rank_ref[:, half * HALF : (half + 1) * HALF]
        position = lax.broadcasted_iota(jnp.int32, (1, HALF), 1) + half * HALF
        real = position < left
        high = jnp.where(real, rank // BASE, int(FAR) // BASE).astype(jnp.float32)
        low = jnp.where(real, rank % BASE, 0).astype(jnp.float32)
        both = jnp.concatenate([high, low, jnp.zeros((1, D - 2 * HALF), jnp.float32)], axis=1)
        tail = jnp.broadcast_to(both, (EXTRA, D)).astype(jnp.bfloat16)
        pay_ref[half, HALF:, :] = tail
        half_ref[HALF:, :] = tail
    for i, copy in enumerate(copies):
        copy.wait()
        half, at = divmod(i * part, HALF)
        rows = rows_ref[i * part : (i + 1) * part, :]
        scale = lax.rsqrt(jnp.mean(rows * rows, axis=-1, keepdims=True) + 1e-06) / math.sqrt(D)
        unit = (rows * scale).astype(jnp.bfloat16)
        pay_ref[half, at : at + part, :] = unit
        (a_ref, b_ref)[half][at : at + part, :] = unit


def packed(rows, ranks, sizes):
    half = jax.ShapeDtypeStruct((PAY, D), jnp.bfloat16)
    return pl.pallas_call(
        pack_kernel,
        in_specs=[SMEM, pl.BlockSpec(memory_space=pltpu.HBM), VMEM],
        out_specs=[VMEM] * 3,
        out_shape=[jax.ShapeDtypeStruct((2, PAY, D), jnp.bfloat16), half, half],
        scratch_shapes=[pltpu.VMEM((2 * HALF, D), jnp.float32), pltpu.SemaphoreType.DMA((PARTS,))],
        name="pack",
        compiler_params=pltpu.CompilerParams(vmem_limit_bytes=16 * 2**20),
        cost_estimate=pl.CostEstimate(flops=4 * 512 * D, bytes_accessed=4 * 2**20, transcendentals=512),
    )(sizes, rows, ranks)


def rank_row(tail):
    tail = tail[0:1, :].astype(jnp.float32)
    return tail[:, :HALF] * BASE + tail[:, HALF:]


def rank_column(tail):
    return jnp.transpose(jnp.broadcast_to(rank_row(tail), (128, HALF)))


def split(ref):
    return [ref.at[0], ref.at[1]]


def tops(scores):
    return jnp.max(scores.reshape(HALF // 8, 8, 128), axis=0)


def pieces(scores):
    return [scores[:, c : c + 128] for c in range(0, HALF, 128)]


def keep(row_ref, places, best):
    for at, value in zip(places, best):
        value = jnp.max(value, axis=0, keepdims=True)
        row_ref[at : at + 1, :] = jnp.maximum(row_ref[at : at + 1, :], value)


def lowest(queries):
    return [jnp.full((8, HALF), LOW, jnp.float32) for _ in queries]


def pair_job(row_ref, ranks, keys, queries, q_at, k_at):
    q_rank = [rank_row(query[HALF:, : 2 * HALF]) for query in queries]
    best, sides = lowest(queries), []
    for n, key_ref in enumerate(keys):
        key, k_rank, side = key_ref[:HALF, :], ranks[n][...], None
        for i, query in enumerate(queries):
            parts = []
            for c, piece in enumerate(pieces(inner(key, query[:HALF, :]))):
                earlier = k_rank < q_rank[i][:, c * 128 : c * 128 + 128]
                parts.append(tops(jnp.where(earlier, piece, LOW)))
                if k_at is not None:
                    other = jnp.where(earlier, LOW, piece)
                    side = other if side is None else jnp.maximum(side, other)
            best[i] = jnp.maximum(best[i], jnp.concatenate(parts, axis=1))
        sides.append(side)
    keep(row_ref, q_at, best)
    if k_at is not None:
        keep(row_ref, k_at, [jnp.transpose(side) for side in sides])


def real_job(row_ref, limits, keys, queries, q_at):
    best = lowest(queries)
    for n, key_ref in enumerate(keys):
        key = key_ref[:HALF, :]
        real = lax.broadcasted_iota(jnp.int32, (HALF, 128), 0) < limits[n]
        for i, query in enumerate(queries):
            parts = [tops(jnp.where(real, piece, LOW)) for piece in pieces(inner(key, query[:HALF, :]))]
            best[i] = jnp.maximum(best[i], jnp.concatenate(parts, axis=1))
    keep(row_ref, q_at, best)


def put_ranks(rank_ref, halves):
    for n, half in enumerate(halves):
        rank_ref[n] = rank_column(half[HALF:, : 2 * HALF])


def rank_shape(halves):
    return jax.ShapeDtypeStruct((halves, HALF, 128), jnp.float32)


def kernel_call(name, body, tasks, rows, sizes, arrays, extra_out=()):
    n = len(arrays)

    def kernel(*refs):
        sizes_ref, rows_in, ins = refs[0], refs[1], refs[2 : 2 + n]
        row_ref, extra = refs[2 + n], refs[3 + n :]
        row_ref[...] = rows_in[...]
        body(row_ref, sizes_ref, *ins, *extra)

    out = pl.pallas_call(
        kernel,
        in_specs=[SMEM, VMEM] + [VMEM] * n,
        out_specs=[VMEM] * (1 + len(extra_out)),
        out_shape=[jax.ShapeDtypeStruct((N_ROWS, HALF), jnp.float32), *extra_out],
        name=name,
        compiler_params=pltpu.CompilerParams(vmem_limit_bytes=14 * 2**20),
        cost_estimate=pl.CostEstimate(flops=int(tasks * 1024), bytes_accessed=1024, transcendentals=0),
    )(sizes, rows, *arrays)
    return out if extra_out else out[0]


W00, A00, KOWN, W03, A03, W10, A10 = 0, 2, 4, 6, 8, 10, 12
W13, A13, W01, A01, K01, PRV, KOWNX, K01X, PRVX = 14, 16, 18, 20, 22, 24, 26, 28, 30
N_ROWS = 32


def both(at):
    return [at, at + 1]


def real_rows(sizes_ref, col, row, other=0, cluster=0):
    helper = lax.axis_index("helper")
    flip = jnp.where(lax.axis_index("group") % 4 == 3, cluster, 0)
    row = (helper // 4 + row) % 4
    col = (helper // 2 + col + flip) % 2
    start = own_count(sizes_ref, cluster) - (row * 4 + col * 2 + (helper + other) % 2) * 2 * HALF
    return [start, start - HALF]


def self_kernel(row_ref, sizes_ref, own, ownx, ranks):
    keys = split(own) + split(ownx)
    put_ranks(ranks, keys)
    row_ref[...] = jnp.full(row_ref.shape, LOW, jnp.float32)
    pair_job(row_ref, [ranks.at[n] for n in range(4)], keys, split(own), both(W00), None)


def own_job(row_ref, own, ownx, ranks, queries, places):
    keys = split(own) + split(ownx)
    pair_job(row_ref, [ranks.at[n] for n in range(4)], keys, queries, places, both(KOWN) + both(KOWNX))


def first_kernel(row_ref, sizes_ref, own, ownx, ranks, b01a):
    own_job(row_ref, own, ownx, ranks, [b01a], [W01])


def bundle_kernel(b01a, b01b, nxt, prva, bundle):
    for n, half in enumerate([nxt.at[0], nxt.at[1], b01a, b01b, prva]):
        bundle[n] = half[...]


def middle_job(row_ref, sizes_ref, own, b01a, b01b, b03, b10, nxt, one, prv, ranks, core):
    queries = [*split(own), b01a, b01b, *split(b03), *split(b10)]
    real_job(
        row_ref, real_rows(sizes_ref, 0, 0, core, 1), nxt, queries, both(A00) + both(A01) + both(A03) + both(A10)
    )
    put_ranks(ranks, one)
    pair_job(row_ref, [ranks.at[0], ranks.at[1]], one, split(b03), both(W03), both((K01, K01X)[core]))
    limits = real_rows(sizes_ref, 0, -1) + real_rows(sizes_ref, 1, 0)
    real_job(row_ref, limits, split(b03) + split(b10), [prv], [(PRV, PRVX)[core]])


def same_kernel(row_ref, sizes_ref, own, ownx, own_ranks, b01a, b01b, b03, b10, nxt, prva, ranks):
    own_job(row_ref, own, ownx, own_ranks, [b01b, *split(b10)], [W01 + 1, W10, W10 + 1])
    middle_job(row_ref, sizes_ref, own, b01a, b01b, b03, b10, split(nxt), [b01a, b01b], prva, ranks, 0)


def cross_kernel(row_ref, sizes_ref, own, b01a, b01b, b03, b10, cross, ranks):
    nxt, one = [cross.at[0], cross.at[1]], [cross.at[2], cross.at[3]]
    middle_job(row_ref, sizes_ref, own, b01a, b01b, b03, b10, nxt, one, cross.at[4], ranks, 1)


def last_kernel(row_ref, sizes_ref, own, ownx, ranks, b01a, b01b, ranks1, ranks1x, nxt, prva, cross, b13a, b13b):
    b13 = [b13a, b13b]
    own_job(row_ref, own, ownx, ranks, b13, both(W13))
    one_ranks = [ranks1.at[0], ranks1.at[1], ranks1x.at[0], ranks1x.at[1]]
    keys = [b01a, b01b, cross.at[2], cross.at[3]]
    pair_job(row_ref, one_ranks, keys, b13, both(W13), both(K01) + both(K01X))
    limits = real_rows(sizes_ref, 0, 0, 0, 1) + real_rows(sizes_ref, 0, 0, 1, 1)
    real_job(row_ref, limits, [*split(nxt), cross.at[0], cross.at[1]], b13, both(A13))
    real_job(row_ref, real_rows(sizes_ref, 1, -1), b13, [prva, cross.at[4]], [PRV, PRVX])


def end_kernel(row_ref, sizes_ref, b03, b10, b13a, b13b, prvb, prvbx):
    limits = real_rows(sizes_ref, 1, -1) + real_rows(sizes_ref, 0, -1) + real_rows(sizes_ref, 1, 0)
    real_job(row_ref, limits, [b13a, b13b, *split(b03), *split(b10)], [prvb, prvbx], [PRV + 1, PRVX + 1])


def gather_kernel(rows_ref, swapped_ref, side_ref, own_ref, to03_ref, to01_ref, prv_ref):
    own_ref[...] = rows_ref[W00 : W00 + 6, :]
    own_ref[KOWN : KOWN + 2, :] = jnp.maximum(rows_ref[KOWN : KOWN + 2, :], swapped_ref[0:2, :])
    to03_ref[...] = jnp.maximum(rows_ref[W03 : W03 + 4, :], side_ref[4:8, :])
    to01_ref[...] = rows_ref[W01 : W01 + 6, :]
    to01_ref[4:6, :] = jnp.maximum(rows_ref[K01 : K01 + 2, :], swapped_ref[2:4, :])
    prv_ref[...] = jnp.maximum(rows_ref[PRV : PRV + 2, :], swapped_ref[4:6, :])


def final_kernel(sizes_ref, own, side, b03, b01, bprv, within_ref, adjacent_ref):
    left = own_count(sizes_ref) - lax.axis_index("helper") * 2 * HALF
    next_full = own_count(sizes_ref, 1) >= 2 * HALF * lax.axis_size("helper")
    for h in range(2):
        row = lambda ref, at: ref[at + h : at + h + 1, :]
        within = [row(own, W00), row(own, KOWN), row(side, 0), row(b03, 0), row(b01, 0), row(b01, 4)]
        adjacent = [row(own, A00), row(side, 2), row(b03, 2), row(b01, 2), row(bprv, 0)]
        within = functools.reduce(jnp.maximum, within)
        adjacent = functools.reduce(jnp.maximum, adjacent)
        adjacent = jnp.maximum(adjacent, jnp.where(next_full, LOW, -1.0))
        real = lax.broadcasted_iota(jnp.int32, (1, HALF), 1) + h * HALF < left
        within_ref[:, h * HALF : (h + 1) * HALF] = jnp.where(real, jnp.maximum(within, -1.0), 0.0)
        adjacent_ref[:, h * HALF : (h + 1) * HALF] = jnp.where(real, adjacent, 0.0)


def small_call(name, body, shapes, smem, arrays):
    return pl.pallas_call(
        body,
        in_specs=[SMEM] * smem + [VMEM] * (len(arrays) - smem),
        out_specs=[VMEM] * len(shapes),
        out_shape=[jax.ShapeDtypeStruct(shape, jnp.float32) for shape in shapes],
        name=name,
        compiler_params=pltpu.CompilerParams(vmem_limit_bytes=2 * 2**20),
    )(*arrays)


def on_device(embeddings, sizes, ranks):
    rows = embeddings.shape[1]
    own, own_a, own_b = packed(embeddings[0], ranks, sizes)

    b01a = send("b01a", own_a, row=-1)
    b10 = send("b10", own, col=1)
    b03 = send("b03", own, row=1)
    nxt = send("nxt", own, cluster=-1)
    ownx = send("ownx", own, core=1)
    b01b = send("b01b", after(own_b, ownx), row=-1)
    empty = jnp.zeros((N_ROWS, HALF), jnp.float32)
    state, own_ranks = kernel_call("self", self_kernel, 1, empty, sizes, [own, ownx], [rank_shape(4)])
    prva = send("prva", after(b01a, state), cluster=1)
    state = kernel_call("first", first_kernel, 0.5, state, sizes, [own, ownx, own_ranks, b01a])

    b03, b10, nxt, b01b, prva, state = lax.optimization_barrier((b03, b10, nxt, b01b, prva, state))
    b13a = send("b13a", b03[0], col=1)
    b13b = send("b13b", b10[1], row=1)
    prvb = send("prvb", b01b, cluster=1)
    bundle = pl.pallas_call(
        bundle_kernel,
        in_specs=[VMEM] * 4,
        out_specs=VMEM,
        out_shape=jax.ShapeDtypeStruct((5, PAY, D), jnp.bfloat16),
        name="bundle",
        compiler_params=pltpu.CompilerParams(vmem_limit_bytes=8 * 2**20),
    )(b01a, b01b, nxt, prva)
    cross = send("cross", bundle, core=1)
    state, ranks1 = kernel_call(
        "same", same_kernel, 4.5, state, sizes,
        [own, ownx, own_ranks, b01a, b01b, b03, b10, nxt, prva], [rank_shape(2)],
    )
    state, ranks1x = kernel_call(
        "cross", cross_kernel, 3, state, sizes, [own, b01a, b01b, b03, b10, cross], [rank_shape(2)]
    )
    prvbx = send("prvbx", after(prvb, state), core=1)
    state = kernel_call(
        "last", last_kernel, 3.5, state, sizes,
        [own, ownx, own_ranks, b01a, b01b, ranks1, ranks1x, nxt, prva, cross, b13a, b13b],
    )
    state = kernel_call("end", end_kernel, 1.5, state, sizes, [b03, b10, b13a, b13b, prvb, prvbx])

    swapped = send("swapped", state[KOWNX : KOWNX + 6], core=1)
    side = send("side", state[W10 : W10 + 8], col=1)
    shapes = [(6, HALF), (4, HALF), (6, HALF), (2, HALF)]
    kept, to_03, to_01, to_prv = small_call("gather", gather_kernel, shapes, 0, [state, swapped, side])
    back_03 = send("back_03", to_03, row=-1)
    back_01 = send("back_01", to_01, row=1)
    back_prv = send("back_prv", to_prv, cluster=-1, row=1)
    return tuple(
        small_call("final", final_kernel, [(1, rows)] * 2, 1, [sizes, kept, side, back_03, back_01, back_prv])
    )


def solution(mesh):
    in_specs = (P("group", "helper", None), P(), P("group", "helper"))
    out_specs = (P("group", "helper"), P("group", "helper"))
    return jax.shard_map(
        on_device, mesh=mesh, in_specs=in_specs, out_specs=out_specs, check_vma=False
    )
```

time: 236 us -> 80.3 us (0.34)
  the two profiles are of different devices: /device:TPU:0 before, /device:TPU:96 now
where the time goes in v2:
time: 80.3 us; the launch traced here: 80.2 us
  waiting for transfers between devices  36.9 us (46%)
  Pallas kernels  23 us (29%)
  starting transfers between devices  16.6 us (21%)
  local copies, waits for them, and re-layouts  3 us (4%)
    ppermute x17, waiting for transfers between devices, send(): return lax.ppermute(value, AXES, pairs(**shift))  36.9 us
    pallas_call x6, Pallas kernels, kernel_call(): pl.pallas_call(kernel, in_specs=[SMEM, VMEM] + [VMEM] * n, out_specs=[VME...  20.3 us
    ppermute x17, starting transfers between devices, send(): return lax.ppermute(value, AXES, pairs(**shift))  16.6 us
    unnamed x6, local copies, waits for them, and re-layouts  2.92 us
  transfers between devices with their start and end apart: 17, of which 9 were waited for; matrix products, arithmetic and copies ran while one was open for 0% of the time, Pallas kernels for 22%

profile of v2, /device:TPU:96, one launch (start us, length us, event | category | flops | bytes accessed | tf_op | source)
XLA Modules:
  0.0 80.2 jit_solution(8816653241492076200)
XLA Ops:
  0.6 1.6 %copy-done = f32[1,512,1024]{2,1,0:T(8,128)S(1)} copy-done((f32[1,512,1024]{2,1,0:T(8,128)S(1)}, f32[1,512,1024]{2,1,0:T(8,128)}, u32[]{:S(2)}) %copy-start) | copy-done | bytes 2097176
  3.6 1.3 %pack.1 = (bf16[2,264,1024]{2,1,0:T(8,128)(2,1)S(1)}, bf16[264,1024]{1,0:T(8,128)(2,1)S(1)}, bf16[264,1024]{1,0:T(8,128)(2,1)S(1)}) custom-call(s32[8]{0:T(128)S(1)} %copy-done.1, f32[512,1024]{1,0:T(8,128)S(1)} %bitcast.5, s32[1,512]{1,0:T(1,128)S(1)} %copy-done.2), custom_call_target="tpu_custom_call" | custom-call | flops 2097152 | bytes 4194304 | tf_op jit(solution)/shard_map/pack/pallas_call | solution.py:105
  5.0 3.1 %collective-permute-start.5 = (bf16[264,1024]{1,0:T(8,128)(2,1)S(1)}, bf16[264,1024]{1,0:T(8,128)(2,1)S(1)}, u32[]{:S(2)}, u32[]{:S(2)}) collective-permute-start(bf16[264,1024]{1,0:T(8,128)(2,1)S(1)} %get-tuple-element.27), channel_id=1, source_target_pairs={{0,12},{1,13},{2,14},{3,15},{4,0},{5,1},{6,2},{7,3},{8,4},{9,5},{1... | collective-permute-start | bytes 1622024 | tf_op jit(solution)/shard_map/b01a/ppermute | solution.py:54
  8.0 1.5 %collective-permute-start.1 = (bf16[2,264,1024]{2,1,0:T(8,128)(2,1)S(1)}, bf16[2,264,1024]{2,1,0:T(8,128)(2,1)S(1)}, u32[]{:S(2)}, u32[]{:S(2)}) collective-permute-start(bf16[2,264,1024]{2,1,0:T(8,128)(2,1)S(1)} %get-tuple-element.24.refs_2_), channel_id=1, source_target_pairs={{0,2},{1,3},{2,0},{3,1},{4,6},{5,7},{6,4},{7,5},{8,10},{9,11},{10,... | collective-permute-start | bytes 3244040 | tf_op jit(solution)/shard_map/b10/ppermute | solution.py:54
  9.9 3.2 %collective-permute-start.4 = (bf16[264,1024]{1,0:T(8,128)(2,1)S(1)}, bf16[264,1024]{1,0:T(8,128)(2,1)S(1)}, u32[]{:S(2)}, u32[]{:S(2)}) collective-permute-start(bf16[264,1024]{1,0:T(8,128)(2,1)S(1)} %get-tuple-element.26), channel_id=1, source_target_pairs={{0,12},{1,13},{2,14},{3,15},{4,0},{5,1},{6,2},{7,3},{8,4},{9,5},{1... | collective-permute-start | bytes 1622024 | tf_op jit(solution)/shard_map/b01b/ppermute | solution.py:54
  13.2 1.9 %self.1 = (f32[32,256]{1,0:T(8,128)S(1)}, f32[4,256,128]{2,1,0:T(8,128)S(1)}) custom-call(s32[8]{0:T(128)S(1)} %copy-done.1, f32[32,256]{1,0:T(8,128)S(1)} %broadcast_in_dim.3.refs_1_, bf16[2,264,1024]{2,1,0:T(8,128)(2,1)S(1)} %get-tuple-element.24.refs_2_, bf16[2,264,1024]{2,1,0:T(8,128)(2,1)S(1)} %collective-permute-done.3.refs_3_), custom_call_target="tpu_custom_call" | custom-call | flops 1024 | bytes 1024 | tf_op jit(solution)/shard_map/self/pallas_call | solution.py:197
  15.0 5.6 %collective-permute-done.5.refs_5_.b01a.refs_3_ = bf16[264,1024]{1,0:T(8,128)(2,1)S(1)} collective-permute-done((bf16[264,1024]{1,0:T(8,128)(2,1)S(1)}, bf16[264,1024]{1,0:T(8,128)(2,1)S(1)}, u32[]{:S(2)}, u32[]{:S(2)}) %collective-permute-start.5) | collective-permute-done | bytes 540704 | tf_op jit(solution)/shard_map/b01a/ppermute | solution.py:54
  20.6 1.4 %collective-permute-start.6 = (bf16[264,1024]{1,0:T(8,128)(2,1)S(1)}, bf16[264,1024]{1,0:T(8,128)(2,1)S(1)}, u32[]{:S(2)}, u32[]{:S(2)}) collective-permute-start(bf16[264,1024]{1,0:T(8,128)(2,1)S(1)} %collective-permute-done.5.refs_5_.b01a.refs_3_), channel_id=1, source_target_pairs={{0,16},{1,17},{2,18},{3,19},{4,20},{5,21},{6,22},{7,23},{8,24},{9,... | collective-permute-start | bytes 1622024 | tf_op jit(solution)/shard_map/prva/ppermute | solution.py:54
  22.0 1.4 %first.1.refs_1_ = f32[32,256]{1,0:T(8,128)S(1)} custom-call(s32[8]{0:T(128)S(1)} %copy-done.1, f32[32,256]{1,0:T(8,128)S(1)} %get-tuple-element.28.refs_1_, bf16[2,264,1024]{2,1,0:T(8,128)(2,1)S(1)} %get-tuple-element.24.refs_2_, bf16[2,264,1024]{2,1,0:T(8,128)(2,1)S(1)} %collective-permute-done.3.refs_3_, f32[4,256,128]{2,1,0:T(8,128)S(1)} %get-tuple-element.30.refs_4_, ...), custom_call_target="tpu_custom_call" | custom-call | flops 512 | bytes 1024 | tf_op jit(solution)/shard_map/first/pallas_call | solution.py:197
  23.5 11.7 %collective-permute-done.refs_7_.refs_5_.refs_2_ = bf16[2,264,1024]{2,1,0:T(8,128)(2,1)S(1)} collective-permute-done((bf16[2,264,1024]{2,1,0:T(8,128)(2,1)S(1)}, bf16[2,264,1024]{2,1,0:T(8,128)(2,1)S(1)}, u32[]{:S(2)}, u32[]{:S(2)}) %collective-permute-start) | collective-permute-done | bytes 1081376 | tf_op jit(solution)/shard_map/b03/ppermute | solution.py:54
  35.2 3.3 %collective-permute-done.2.refs_9_.nxt = bf16[2,264,1024]{2,1,0:T(8,128)(2,1)S(1)} collective-permute-done((bf16[2,264,1024]{2,1,0:T(8,128)(2,1)S(1)}, bf16[2,264,1024]{2,1,0:T(8,128)(2,1)S(1)}, u32[]{:S(2)}, u32[]{:S(2)}) %collective-permute-start.2) | collective-permute-done | bytes 1081376 | tf_op jit(solution)/shard_map/nxt/ppermute | solution.py:54
  39.2 1.3 %collective-permute-start.9 = (bf16[264,1024]{1,0:T(8,128)(2,1)S(1)}, bf16[264,1024]{1,0:T(8,128)(2,1)S(1)}, u32[]{:S(2)}, u32[]{:S(2)}) collective-permute-start(bf16[264,1024]{1,0:T(8,128)(2,1)S(1)} %slice_bitcast_fusion), channel_id=1, source_target_pairs={{0,4},{1,5},{2,6},{3,7},{4,8},{5,9},{6,10},{7,11},{8,12},{9,13},{1... | collective-permute-start | bytes 1622024 | tf_op jit(solution)/shard_map/b13b/ppermute | solution.py:54
  40.5 5.9 %same.1 = (f32[32,256]{1,0:T(8,128)S(1)}, f32[2,256,128]{2,1,0:T(8,128)S(1)}) custom-call(s32[8]{0:T(128)S(1)} %copy-done.1, f32[32,256]{1,0:T(8,128)S(1)} %first.1.refs_1_, bf16[2,264,1024]{2,1,0:T(8,128)(2,1)S(1)} %get-tuple-element.24.refs_2_, bf16[2,264,1024]{2,1,0:T(8,128)(2,1)S(1)} %collective-permute-done.3.refs_3_, ...), custom_call_target="tpu_custom_call" | custom-call | flops 4608 | bytes 1024 | tf_op jit(solution)/shard_map/same/pallas_call | solution.py:197
  46.4 4.1 %cross.1 = (f32[32,256]{1,0:T(8,128)S(1)}, f32[2,256,128]{2,1,0:T(8,128)S(1)}) custom-call(s32[8]{0:T(128)S(1)} %copy-done.1, f32[32,256]{1,0:T(8,128)S(1)} %get-tuple-element.37.refs_1_, bf16[2,264,1024]{2,1,0:T(8,128)(2,1)S(1)} %get-tuple-element.24.refs_2_, bf16[264,1024]{1,0:T(8,128)(2,1)S(1)} %collective-permute-done.5.refs_5_.b01a.refs_3_, ...), custom_call_target="tpu_custom_call" | custom-call | flops 3072 | bytes 1024 | tf_op jit(solution)/shard_map/cross/pallas_call | solution.py:197
  50.5 3.0 %collective-permute-done.10.refs_6_ = bf16[264,1024]{1,0:T(8,128)(2,1)S(1)} collective-permute-done((bf16[264,1024]{1,0:T(8,128)(2,1)S(1)}, bf16[264,1024]{1,0:T(8,128)(2,1)S(1)}, u32[]{:S(2)}, u32[]{:S(2)}) %collective-permute-start.10) | collective-permute-done | bytes 540704 | tf_op jit(solution)/shard_map/prvb/ppermute | solution.py:54
  53.6 2.2 %collective-permute-done.9.refs_13_.refs_5_ = bf16[264,1024]{1,0:T(8,128)(2,1)S(1)} collective-permute-done((bf16[264,1024]{1,0:T(8,128)(2,1)S(1)}, bf16[264,1024]{1,0:T(8,128)(2,1)S(1)}, u32[]{:S(2)}, u32[]{:S(2)}) %collective-permute-start.9) | collective-permute-done | bytes 540704 | tf_op jit(solution)/shard_map/b13b/ppermute | solution.py:54
  55.8 4.7 %last.1.refs_1_ = f32[32,256]{1,0:T(8,128)S(1)} custom-call(s32[8]{0:T(128)S(1)} %copy-done.1, f32[32,256]{1,0:T(8,128)S(1)} %get-tuple-element.38.refs_1_, bf16[2,264,1024]{2,1,0:T(8,128)(2,1)S(1)} %get-tuple-element.24.refs_2_, bf16[2,264,1024]{2,1,0:T(8,128)(2,1)S(1)} %collective-permute-done.3.refs_3_, f32[4,256,128]{2,1,0:T(8,128)S(1)} %get-tuple-element.30.refs_4_, ...), custom_call_target="tpu_custom_call" | custom-call | flops 3584 | bytes 1024 | tf_op jit(solution)/shard_map/last/pallas_call | solution.py:197
  60.5 2.4 %end.1.rows_ref = f32[32,256]{1,0:T(8,128)S(1)} custom-call(s32[8]{0:T(128)S(1)} %copy-done.1, f32[32,256]{1,0:T(8,128)S(1)} %last.1.refs_1_, bf16[2,264,1024]{2,1,0:T(8,128)(2,1)S(1)} %collective-permute-done.refs_7_.refs_5_.refs_2_, bf16[2,264,1024]{2,1,0:T(8,128)(2,1)S(1)} %collective-permute-done.1.refs_8_.refs_6_.refs_3_, ...), custom_call_target="tpu_custom_call" | custom-call | flops 1536 | bytes 1024 | tf_op jit(solution)/shard_map/end/pallas_call | solution.py:197
  62.9 1.8 %collective-permute-start.13 = (f32[8,256]{1,0:T(8,128)S(1)}, f32[8,256]{1,0:T(8,128)S(1)}, u32[]{:S(2)}, u32[]{:S(2)}) collective-permute-start(f32[8,256]{1,0:T(8,128)S(1)} %slice.17), channel_id=1, source_target_pairs={{0,2},{1,3},{2,0},{3,1},{4,6},{5,7},{6,4},{7,5},{8,10},{9,11},{10,... | collective-permute-start | bytes 24584 | tf_op jit(solution)/shard_map/side/ppermute | solution.py:54
  64.8 1.2 %collective-permute-done.12.swapped_ref = f32[6,256]{1,0:T(8,128)S(1)} collective-permute-done((f32[6,256]{1,0:T(8,128)S(1)}, f32[6,256]{1,0:T(8,128)S(1)}, u32[]{:S(2)}, u32[]{:S(2)}) %collective-permute-start.12) | collective-permute-done | bytes 6176 | tf_op jit(solution)/shard_map/swapped/ppermute | solution.py:54
  65.9 0.7 collective-permute-done.13.side_ref.side
  66.8 3.2 %collective-permute-start.14 = (f32[4,256]{1,0:T(4,128)S(1)}, f32[4,256]{1,0:T(4,128)S(1)}, u32[]{:S(2)}, u32[]{:S(2)}) collective-permute-start(f32[4,256]{1,0:T(4,128)S(1)} %get-tuple-element.43), channel_id=1, source_target_pairs={{0,12},{1,13},{2,14},{3,15},{4,0},{5,1},{6,2},{7,3},{8,4},{9,5},{1... | collective-permute-start | bytes 12296 | tf_op jit(solution)/shard_map/back_03/ppermute | solution.py:54
  70.0 9.0 %collective-permute-done.16.bprv = f32[2,256]{1,0:T(2,128)S(1)} collective-permute-done((f32[2,256]{1,0:T(2,128)S(1)}, f32[2,256]{1,0:T(2,128)S(1)}, u32[]{:S(2)}, u32[]{:S(2)}) %collective-permute-start.16) | collective-permute-done | bytes 2080 | tf_op jit(solution)/shard_map/back_prv/ppermute | solution.py:54
  79.0 1.1 %final.1 = (f32[1,512]{1,0:T(1,128)}, f32[1,512]{1,0:T(1,128)}) custom-call(s32[8]{0:T(128)S(1)} %copy-done.1, f32[6,256]{1,0:T(8,128)S(1)} %get-tuple-element.42.own, f32[8,256]{1,0:T(8,128)S(1)} %collective-permute-done.13.side_ref.side, f32[4,256]{1,0:T(4,128)S(1)} %collective-permute-done.14.b03, f32[6,256]{1,0:T(8,128)S(1)} %collective-permute-done.15.b01, ...), custom_call_target="tpu_custom_call" | custom-call | tf_op jit(solution)/shard_map/final/pallas_call | solution.py:310
  (31 shorter events, 2.8 us)
Async XLA Ops:
  0.6 1.6 %copy-start = (f32[1,512,1024]{2,1,0:T(8,128)S(1)}, f32[1,512,1024]{2,1,0:T(8,128)}, u32[]{:S(2)}) copy-start(f32[1,512,1024]{2,1,0:T(8,128)} %param.3) | copy-start | bytes 6291460
  2.2 0.7 copy-start.1
  2.9 0.7 copy-start.2
  4.9 5.1 %collective-permute-start.3 = (bf16[2,264,1024]{2,1,0:T(8,128)(2,1)S(1)}, bf16[2,264,1024]{2,1,0:T(8,128)(2,1)S(1)}, u32[]{:S(2)}, u32[]{:S(2)}) collective-permute-start(bf16[2,264,1024]{2,1,0:T(8,128)(2,1)S(1)} %get-tuple-element.24.refs_2_), channel_id=1, source_target_pairs={{0,1},{1,0},{2,3},{3,2},{4,5},{5,4},{6,7},{7,6},{8,9},{9,8},{10,11... | collective-permute-start | bytes 3244040 | tf_op jit(solution)/shard_map/ownx/ppermute | solution.py:54
  5.0 15.7 %collective-permute-start.5 = (bf16[264,1024]{1,0:T(8,128)(2,1)S(1)}, bf16[264,1024]{1,0:T(8,128)(2,1)S(1)}, u32[]{:S(2)}, u32[]{:S(2)}) collective-permute-start(bf16[264,1024]{1,0:T(8,128)(2,1)S(1)} %get-tuple-element.27), channel_id=1, source_target_pairs={{0,12},{1,13},{2,14},{3,15},{4,0},{5,1},{6,2},{7,3},{8,4},{9,5},{1... | collective-permute-start | bytes 1622024 | tf_op jit(solution)/shard_map/b01a/ppermute | solution.py:54
  8.0 27.1 %collective-permute-start = (bf16[2,264,1024]{2,1,0:T(8,128)(2,1)S(1)}, bf16[2,264,1024]{2,1,0:T(8,128)(2,1)S(1)}, u32[]{:S(2)}, u32[]{:S(2)}) collective-permute-start(bf16[2,264,1024]{2,1,0:T(8,128)(2,1)S(1)} %get-tuple-element.24.refs_2_), channel_id=1, source_target_pairs={{0,4},{1,5},{2,6},{3,7},{4,8},{5,9},{6,10},{7,11},{8,12},{9,13},{1... | collective-permute-start | bytes 3244040 | tf_op jit(solution)/shard_map/b03/ppermute | solution.py:54
  8.0 27.1 %collective-permute-start.1 = (bf16[2,264,1024]{2,1,0:T(8,128)(2,1)S(1)}, bf16[2,264,1024]{2,1,0:T(8,128)(2,1)S(1)}, u32[]{:S(2)}, u32[]{:S(2)}) collective-permute-start(bf16[2,264,1024]{2,1,0:T(8,128)(2,1)S(1)} %get-tuple-element.24.refs_2_), channel_id=1, source_target_pairs={{0,2},{1,3},{2,0},{3,1},{4,6},{5,7},{6,4},{7,5},{8,10},{9,11},{10,... | collective-permute-start | bytes 3244040 | tf_op jit(solution)/shard_map/b10/ppermute | solution.py:54
  9.5 29.0 %collective-permute-start.2 = (bf16[2,264,1024]{2,1,0:T(8,128)(2,1)S(1)}, bf16[2,264,1024]{2,1,0:T(8,128)(2,1)S(1)}, u32[]{:S(2)}, u32[]{:S(2)}) collective-permute-start(bf16[2,264,1024]{2,1,0:T(8,128)(2,1)S(1)} %get-tuple-element.24.refs_2_), channel_id=1, source_target_pairs={{0,114},{1,115},{2,112},{3,113},{4,118},{5,119},{6,116},{7,117},{8... | collective-permute-start | bytes 3244040 | tf_op jit(solution)/shard_map/nxt/ppermute | solution.py:54
  9.9 28.6 %collective-permute-start.4 = (bf16[264,1024]{1,0:T(8,128)(2,1)S(1)}, bf16[264,1024]{1,0:T(8,128)(2,1)S(1)}, u32[]{:S(2)}, u32[]{:S(2)}) collective-permute-start(bf16[264,1024]{1,0:T(8,128)(2,1)S(1)} %get-tuple-element.26), channel_id=1, source_target_pairs={{0,12},{1,13},{2,14},{3,15},{4,0},{5,1},{6,2},{7,3},{8,4},{9,5},{1... | collective-permute-start | bytes 1622024 | tf_op jit(solution)/shard_map/b01b/ppermute | solution.py:54
  20.6 17.9 %collective-permute-start.6 = (bf16[264,1024]{1,0:T(8,128)(2,1)S(1)}, bf16[264,1024]{1,0:T(8,128)(2,1)S(1)}, u32[]{:S(2)}, u32[]{:S(2)}) collective-permute-start(bf16[264,1024]{1,0:T(8,128)(2,1)S(1)} %collective-permute-done.5.refs_5_.b01a.refs_3_), channel_id=1, source_target_pairs={{0,16},{1,17},{2,18},{3,19},{4,20},{5,21},{6,22},{7,23},{8,24},{9,... | collective-permute-start | bytes 1622024 | tf_op jit(solution)/shard_map/prva/ppermute | solution.py:54
  38.7 7.7 %collective-permute-start.7 = (bf16[5,264,1024]{2,1,0:T(8,128)(2,1)S(1)}, bf16[5,264,1024]{2,1,0:T(8,128)(2,1)S(1)}, u32[]{:S(2)}, u32[]{:S(2)}) collective-permute-start(bf16[5,264,1024]{2,1,0:T(8,128)(2,1)S(1)} %bundle.1), channel_id=1, source_target_pairs={{0,1},{1,0},{2,3},{3,2},{4,5},{5,4},{6,7},{7,6},{8,9},{9,8},{10,11... | collective-permute-start | bytes 8110088 | tf_op jit(solution)/shard_map/cross/ppermute | solution.py:54
  38.8 14.7 %collective-permute-start.10 = (bf16[264,1024]{1,0:T(8,128)(2,1)S(1)}, bf16[264,1024]{1,0:T(8,128)(2,1)S(1)}, u32[]{:S(2)}, u32[]{:S(2)}) collective-permute-start(bf16[264,1024]{1,0:T(8,128)(2,1)S(1)} %collective-permute-done.4.refs_6_.b01b.refs_4_), channel_id=1, source_target_pairs={{0,16},{1,17},{2,18},{3,19},{4,20},{5,21},{6,22},{7,23},{8,24},{9,... | collective-permute-start | bytes 1622024 | tf_op jit(solution)/shard_map/prvb/ppermute | solution.py:54
  39.1 14.5 %collective-permute-start.8 = (bf16[264,1024]{1,0:T(8,128)(2,1)S(1)}, bf16[264,1024]{1,0:T(8,128)(2,1)S(1)}, u32[]{:S(2)}, u32[]{:S(2)}) collective-permute-start(bf16[264,1024]{1,0:T(8,128)(2,1)S(1)} %slice_bitcast_fusion.1), channel_id=1, source_target_pairs={{0,2},{1,3},{2,0},{3,1},{4,6},{5,7},{6,4},{7,5},{8,10},{9,11},{10,... | collective-permute-start | bytes 1622024 | tf_op jit(solution)/shard_map/b13a/ppermute | solution.py:54
  39.2 16.5 %collective-permute-start.9 = (bf16[264,1024]{1,0:T(8,128)(2,1)S(1)}, bf16[264,1024]{1,0:T(8,128)(2,1)S(1)}, u32[]{:S(2)}, u32[]{:S(2)}) collective-permute-start(bf16[264,1024]{1,0:T(8,128)(2,1)S(1)} %slice_bitcast_fusion), channel_id=1, source_target_pairs={{0,4},{1,5},{2,6},{3,7},{4,8},{5,9},{6,10},{7,11},{8,12},{9,13},{1... | collective-permute-start | bytes 1622024 | tf_op jit(solution)/shard_map/b13b/ppermute | solution.py:54
  53.5 7.0 %collective-permute-start.11 = (bf16[264,1024]{1,0:T(8,128)(2,1)S(1)}, bf16[264,1024]{1,0:T(8,128)(2,1)S(1)}, u32[]{:S(2)}, u32[]{:S(2)}) collective-permute-start(bf16[264,1024]{1,0:T(8,128)(2,1)S(1)} %collective-permute-done.10.refs_6_), channel_id=1, source_target_pairs={{0,1},{1,0},{2,3},{3,2},{4,5},{5,4},{6,7},{7,6},{8,9},{9,8},{10,11... | collective-permute-start | bytes 1622024 | tf_op jit(solution)/shard_map/prvbx/ppermute | solution.py:54
  62.9 3.7 %collective-permute-start.13 = (f32[8,256]{1,0:T(8,128)S(1)}, f32[8,256]{1,0:T(8,128)S(1)}, u32[]{:S(2)}, u32[]{:S(2)}) collective-permute-start(f32[8,256]{1,0:T(8,128)S(1)} %slice.17), channel_id=1, source_target_pairs={{0,2},{1,3},{2,0},{3,1},{4,6},{5,7},{6,4},{7,5},{8,10},{9,11},{10,... | collective-permute-start | bytes 24584 | tf_op jit(solution)/shard_map/side/ppermute | solution.py:54
  64.8 1.2 %collective-permute-start.12 = (f32[6,256]{1,0:T(8,128)S(1)}, f32[6,256]{1,0:T(8,128)S(1)}, u32[]{:S(2)}, u32[]{:S(2)}) collective-permute-start(f32[6,256]{1,0:T(8,128)S(1)} %slice.16), channel_id=1, source_target_pairs={{0,1},{1,0},{2,3},{3,2},{4,5},{5,4},{6,7},{7,6},{8,9},{9,8},{10,11... | collective-permute-start | bytes 18440 | tf_op jit(solution)/shard_map/swapped/ppermute | solution.py:54
  66.7 12.3 %collective-permute-start.15 = (f32[6,256]{1,0:T(8,128)S(1)}, f32[6,256]{1,0:T(8,128)S(1)}, u32[]{:S(2)}, u32[]{:S(2)}) collective-permute-start(f32[6,256]{1,0:T(8,128)S(1)} %get-tuple-element.44), channel_id=1, source_target_pairs={{0,4},{1,5},{2,6},{3,7},{4,8},{5,9},{6,10},{7,11},{8,12},{9,13},{1... | collective-permute-start | bytes 18440 | tf_op jit(solution)/shard_map/back_01/ppermute | solution.py:54
  66.8 12.2 %collective-permute-start.14 = (f32[4,256]{1,0:T(4,128)S(1)}, f32[4,256]{1,0:T(4,128)S(1)}, u32[]{:S(2)}, u32[]{:S(2)}) collective-permute-start(f32[4,256]{1,0:T(4,128)S(1)} %get-tuple-element.43), channel_id=1, source_target_pairs={{0,12},{1,13},{2,14},{3,15},{4,0},{5,1},{6,2},{7,3},{8,4},{9,5},{1... | collective-permute-start | bytes 12296 | tf_op jit(solution)/shard_map/back_03/ppermute | solution.py:54
  70.0 9.0 %collective-permute-start.16 = (f32[2,256]{1,0:T(2,128)S(1)}, f32[2,256]{1,0:T(2,128)S(1)}, u32[]{:S(2)}, u32[]{:S(2)}) collective-permute-start(f32[2,256]{1,0:T(2,128)S(1)} %get-tuple-element.45), channel_id=1, source_target_pairs={{0,118},{1,119},{2,116},{3,117},{4,122},{5,123},{6,120},{7,121},{8... | collective-permute-start | bytes 6152 | tf_op jit(solution)/shard_map/back_prv/ppermute | solution.py:54

commit v3 on v2

--- a/solution.py
+++ b/solution.py
@@ -65,20 +65,34 @@
 
 
 PARTS = 4
+PACK_MIB = 60
+LONG = 10**8
 
 
 def own_count(sizes_ref, step=0):
     return sizes_ref[lax.rem(lax.axis_index("group") + step, lax.axis_size("group"))]
 
 
-def pack_kernel(sizes_ref, rows_hbm, rank_ref, pay_ref, a_ref, b_ref, rows_ref, sem):
+def pack_kernel(sizes_hbm, rows_hbm, rank_hbm, pay_ref, a_ref, b_ref, rows_ref, rank_ref, sizes_ref, sem):
     part = 2 * HALF // PARTS
     copies = [
         pltpu.make_async_copy(rows_hbm.at[pl.ds(i * part, part)], rows_ref.at[pl.ds(i * part, part)], sem.at[i])
         for i in range(PARTS)
     ]
-    for copy in copies:
+    rank_copy = pltpu.make_async_copy(rank_hbm, rank_ref, sem.at[PARTS])
+    sizes_copy = pltpu.make_async_copy(sizes_hbm, sizes_ref, sem.at[PARTS + 1])
+    for copy in [*copies, rank_copy, sizes_copy]:
         copy.start()
+    for i, copy in enumerate(copies):
+        copy.wait()
+        half, at = divmod(i * part, HALF)
+        rows = rows_ref[i * part : (i + 1) * part, :]
+        scale = lax.rsqrt(jnp.mean(rows * rows, axis=-1, keepdims=True) + 1e-06) / math.sqrt(D)
+        unit = (rows * scale).astype(jnp.bfloat16)
+        pay_ref[half, at : at + part, :] = unit
+        (a_ref, b_ref)[half][at : at + part, :] = unit
+    rank_copy.wait()
+    sizes_copy.wait()
     left = own_count(sizes_ref) - lax.axis_index("helper") * 2 * HALF
     for half, half_ref in enumerate((a_ref, b_ref)):
         rank = rank_ref[:, half * HALF : (half + 1) * HALF]
@@ -90,26 +104,23 @@
         tail = jnp.broadcast_to(both, (EXTRA, D)).astype(jnp.bfloat16)
         pay_ref[half, HALF:, :] = tail
         half_ref[HALF:, :] = tail
-    for i, copy in enumerate(copies):
-        copy.wait()
-        half, at = divmod(i * part, HALF)
-        rows = rows_ref[i * part : (i + 1) * part, :]
-        scale = lax.rsqrt(jnp.mean(rows * rows, axis=-1, keepdims=True) + 1e-06) / math.sqrt(D)
-        unit = (rows * scale).astype(jnp.bfloat16)
-        pay_ref[half, at : at + part, :] = unit
-        (a_ref, b_ref)[half][at : at + part, :] = unit
 
 
 def packed(rows, ranks, sizes):
     half = jax.ShapeDtypeStruct((PAY, D), jnp.bfloat16)
     return pl.pallas_call(
         pack_kernel,
-        in_specs=[SMEM, pl.BlockSpec(memory_space=pltpu.HBM), VMEM],
+        in_specs=[pl.BlockSpec(memory_space=pltpu.HBM)] * 3,
         out_specs=[VMEM] * 3,
         out_shape=[jax.ShapeDtypeStruct((2, PAY, D), jnp.bfloat16), half, half],
-        scratch_shapes=[pltpu.VMEM((2 * HALF, D), jnp.float32), pltpu.SemaphoreType.DMA((PARTS,))],
+        scratch_shapes=[
+            pltpu.VMEM((2 * HALF, D), jnp.float32),
+            pltpu.VMEM((1, 2 * HALF), jnp.int32),
+            pltpu.SMEM(sizes.shape, jnp.int32),
+            pltpu.SemaphoreType.DMA((PARTS + 2,)),
+        ],
         name="pack",
-        compiler_params=pltpu.CompilerParams(vmem_limit_bytes=16 * 2**20),
+        compiler_params=pltpu.CompilerParams(vmem_limit_bytes=PACK_MIB * 2**20),
         cost_estimate=pl.CostEstimate(flops=4 * 512 * D, bytes_accessed=4 * 2**20, transcendentals=512),
     )(sizes, rows, ranks)
 
@@ -145,12 +156,18 @@
     return [jnp.full((8, HALF), LOW, jnp.float32) for _ in queries]
 
 
-def pair_job(row_ref, ranks, keys, queries, q_at, k_at):
+ALL = lambda k, q: True
+SHARE = {(0, 0), (1, 0), (1, 1), (2, 0), (2, 1), (3, 1)}
+
+
+def pair_job(row_ref, ranks, keys, queries, q_at, k_at, wanted=ALL):
     q_rank = [rank_row(query[HALF:, : 2 * HALF]) for query in queries]
     best, sides = lowest(queries), []
     for n, key_ref in enumerate(keys):
         key, k_rank, side = key_ref[:HALF, :], ranks[n][...], None
         for i, query in enumerate(queries):
+            if not wanted(n, i):
+                continue
             parts = []
             for c, piece in enumerate(pieces(inner(key, query[:HALF, :]))):
                 earlier = k_rank < q_rank[i][:, c * 128 : c * 128 + 128]
@@ -208,7 +225,7 @@
 
 W00, A00, KOWN, W03, A03, W10, A10 = 0, 2, 4, 6, 8, 10, 12
 W13, A13, W01, A01, K01, PRV, KOWNX, K01X, PRVX = 14, 16, 18, 20, 22, 24, 26, 28, 30
-N_ROWS = 32
+N_ROWS = 40
 
 
 def both(at):
@@ -231,9 +248,9 @@
     pair_job(row_ref, [ranks.at[n] for n in range(4)], keys, split(own), both(W00), None)
 
 
-def own_job(row_ref, own, ownx, ranks, queries, places):
+def own_job(row_ref, own, ownx, ranks, queries, places, wanted=ALL):
     keys = split(own) + split(ownx)
-    pair_job(row_ref, [ranks.at[n] for n in range(4)], keys, queries, places, both(KOWN) + both(KOWNX))
+    pair_job(row_ref, [ranks.at[n] for n in range(4)], keys, queries, places, both(KOWN) + both(KOWNX), wanted)
 
 
 def first_kernel(row_ref, sizes_ref, own, ownx, ranks, b01a):
@@ -245,36 +262,44 @@
         bundle[n] = half[...]
 
 
-def middle_job(row_ref, sizes_ref, own, b01a, b01b, b03, b10, nxt, one, prv, ranks, core):
+def same_kernel(row_ref, sizes_ref, own, ownx, own_ranks, b01a, b01b, b03, b10, nxt, prva, ranks):
+    places = [W01 + 1, W10, W10 + 1]
+    own_job(row_ref, own, ownx, own_ranks, [b01b, *split(b10)], places, lambda k, q: q == 0 or (k, q - 1) in SHARE)
     queries = [*split(own), b01a, b01b, *split(b03), *split(b10)]
-    real_job(
-        row_ref, real_rows(sizes_ref, 0, 0, core, 1), nxt, queries, both(A00) + both(A01) + both(A03) + both(A10)
-    )
-    put_ranks(ranks, one)
-    pair_job(row_ref, [ranks.at[0], ranks.at[1]], one, split(b03), both(W03), both((K01, K01X)[core]))
+    places = both(A00) + both(A01) + both(A03) + both(A10)
+    real_job(row_ref, real_rows(sizes_ref, 0, 0, 0, 1), split(nxt), queries, places)
+    put_ranks(ranks, [b01a, b01b])
+    pair_job(
+        row_ref, [ranks.at[0], ranks.at[1]], [b01a, b01b], split(b03), both(W03), both(K01),
+        lambda k, q: (k, q) in SHARE,
+    )
     limits = real_rows(sizes_ref, 0, -1) + real_rows(sizes_ref, 1, 0)
-    real_job(row_ref, limits, split(b03) + split(b10), [prv], [(PRV, PRVX)[core]])
-
-
-def same_kernel(row_ref, sizes_ref, own, ownx, own_ranks, b01a, b01b, b03, b10, nxt, prva, ranks):
-    own_job(row_ref, own, ownx, own_ranks, [b01b, *split(b10)], [W01 + 1, W10, W10 + 1])
-    middle_job(row_ref, sizes_ref, own, b01a, b01b, b03, b10, split(nxt), [b01a, b01b], prva, ranks, 0)
-
-
-def cross_kernel(row_ref, sizes_ref, own, b01a, b01b, b03, b10, cross, ranks):
-    nxt, one = [cross.at[0], cross.at[1]], [cross.at[2], cross.at[3]]
-    middle_job(row_ref, sizes_ref, own, b01a, b01b, b03, b10, nxt, one, cross.at[4], ranks, 1)
-
-
-def last_kernel(row_ref, sizes_ref, own, ownx, ranks, b01a, b01b, ranks1, ranks1x, nxt, prva, cross, b13a, b13b):
+    real_job(row_ref, limits, split(b03) + split(b10), [prva], [PRV])
+
+
+def last_kernel(row_ref, sizes_ref, own, ownx, ranks, b01a, b01b, ranks1, nxt, prva, b13a, b13b):
     b13 = [b13a, b13b]
     own_job(row_ref, own, ownx, ranks, b13, both(W13))
-    one_ranks = [ranks1.at[0], ranks1.at[1], ranks1x.at[0], ranks1x.at[1]]
-    keys = [b01a, b01b, cross.at[2], cross.at[3]]
-    pair_job(row_ref, one_ranks, keys, b13, both(W13), both(K01) + both(K01X))
-    limits = real_rows(sizes_ref, 0, 0, 0, 1) + real_rows(sizes_ref, 0, 0, 1, 1)
-    real_job(row_ref, limits, [*split(nxt), cross.at[0], cross.at[1]], b13, both(A13))
-    real_job(row_ref, real_rows(sizes_ref, 1, -1), b13, [prva, cross.at[4]], [PRV, PRVX])
+    pair_job(
+        row_ref, [ranks1.at[0], ranks1.at[1]], [b01a, b01b], b13, both(W13), both(K01), lambda k, q: (k, q) in SHARE
+    )
+    real_job(row_ref, real_rows(sizes_ref, 0, 0, 0, 1), split(nxt), b13, both(A13))
+    real_job(row_ref, real_rows(sizes_ref, 1, -1), b13, [prva], [PRV])
+
+
+def cross_kernel(row_ref, sizes_ref, own, b01a, b01b, b03, b10, b13a, b13b, cross):
+    b13 = [b13a, b13b]
+    queries = [*split(own), b01a, b01b, *split(b03), *split(b10), *b13]
+    places = both(A00) + both(A01) + both(A03) + both(A10) + both(A13)
+    real_job(row_ref, real_rows(sizes_ref, 0, 0, 1, 1), [cross.at[0], cross.at[1]], queries, places)
+    one = [cross.at[2], cross.at[3]]
+    ranks = [rank_column(half[HALF:, : 2 * HALF]) for half in one]
+    queries = split(b03) + b13
+    pair_job(
+        row_ref, ranks, one, queries, both(W03) + both(W13), both(K01X), lambda k, q: (2 + k, q % 2) in SHARE
+    )
+    limits = real_rows(sizes_ref, 0, -1) + real_rows(sizes_ref, 1, 0) + real_rows(sizes_ref, 1, -1)
+    real_job(row_ref, limits, split(b03) + split(b10) + b13, [cross.at[4]], [PRVX])
 
 
 def end_kernel(row_ref, sizes_ref, b03, b10, b13a, b13b, prvb, prvbx):
@@ -282,28 +307,33 @@
     real_job(row_ref, limits, [b13a, b13b, *split(b03), *split(b10)], [prvb, prvbx], [PRV + 1, PRVX + 1])
 
 
-def gather_kernel(rows_ref, swapped_ref, side_ref, own_ref, to03_ref, to01_ref, prv_ref):
-    own_ref[...] = rows_ref[W00 : W00 + 6, :]
-    own_ref[KOWN : KOWN + 2, :] = jnp.maximum(rows_ref[KOWN : KOWN + 2, :], swapped_ref[0:2, :])
+def gather_kernel(sizes_ref, rows_ref, swapped_ref, side_ref, kept_ref, to03_ref, to01_ref):
+    left = own_count(sizes_ref) - lax.axis_index("helper") * 2 * HALF
+    floor = jnp.where(own_count(sizes_ref, 1) >= 2 * HALF * lax.axis_size("helper"), LOW, -1.0)
+    for h in range(2):
+        row = lambda ref, at: ref[at + h : at + h + 1, :]
+        real = lax.broadcasted_iota(jnp.int32, (1, HALF), 1) + h * HALF < left
+        within = jnp.maximum(row(rows_ref, W00), row(rows_ref, KOWN))
+        within = jnp.maximum(jnp.maximum(within, row(swapped_ref, 0)), jnp.maximum(row(side_ref, 0), -1.0))
+        adjacent = jnp.maximum(jnp.maximum(row(rows_ref, A00), row(side_ref, 2)), floor)
+        kept_ref[h : h + 1, :] = within
+        kept_ref[2 + h : 3 + h, :] = adjacent
+        kept_ref[4 + h : 5 + h, :] = jnp.where(real, 1.0, 0.0)
+    kept_ref[6:8, :] = jnp.zeros((2, HALF), jnp.float32)
     to03_ref[...] = jnp.maximum(rows_ref[W03 : W03 + 4, :], side_ref[4:8, :])
     to01_ref[...] = rows_ref[W01 : W01 + 6, :]
     to01_ref[4:6, :] = jnp.maximum(rows_ref[K01 : K01 + 2, :], swapped_ref[2:4, :])
-    prv_ref[...] = jnp.maximum(rows_ref[PRV : PRV + 2, :], swapped_ref[4:6, :])
-
-
-def final_kernel(sizes_ref, own, side, b03, b01, bprv, within_ref, adjacent_ref):
-    left = own_count(sizes_ref) - lax.axis_index("helper") * 2 * HALF
-    next_full = own_count(sizes_ref, 1) >= 2 * HALF * lax.axis_size("helper")
+
+
+def final_kernel(kept, b03, b01, bprv, bprvx, within_ref, adjacent_ref):
     for h in range(2):
         row = lambda ref, at: ref[at + h : at + h + 1, :]
-        within = [row(own, W00), row(own, KOWN), row(side, 0), row(b03, 0), row(b01, 0), row(b01, 4)]
-        adjacent = [row(own, A00), row(side, 2), row(b03, 2), row(b01, 2), row(bprv, 0)]
-        within = functools.reduce(jnp.maximum, within)
-        adjacent = functools.reduce(jnp.maximum, adjacent)
-        adjacent = jnp.maximum(adjacent, jnp.where(next_full, LOW, -1.0))
-        real = lax.broadcasted_iota(jnp.int32, (1, HALF), 1) + h * HALF < left
-        within_ref[:, h * HALF : (h + 1) * HALF] = jnp.where(real, jnp.maximum(within, -1.0), 0.0)
-        adjacent_ref[:, h * HALF : (h + 1) * HALF] = jnp.where(real, adjacent, 0.0)
+        within = [row(kept, 0), row(b03, 0), row(b01, 0), row(b01, 4)]
+        adjacent = [row(kept, 2), row(b03, 2), row(b01, 2), row(bprv, 0), row(bprvx, 0)]
+        real = row(kept, 4) > 0
+        place = slice(h * HALF, (h + 1) * HALF)
+        within_ref[:, place] = jnp.where(real, functools.reduce(jnp.maximum, within), 0.0)
+        adjacent_ref[:, place] = jnp.where(real, functools.reduce(jnp.maximum, adjacent), 0.0)
 
 
 def small_call(name, body, shapes, smem, arrays):
@@ -322,9 +352,9 @@
     own, own_a, own_b = packed(embeddings[0], ranks, sizes)
 
     b01a = send("b01a", own_a, row=-1)
-    b10 = send("b10", own, col=1)
     b03 = send("b03", own, row=1)
     nxt = send("nxt", own, cluster=-1)
+    b10 = send("b10", own, col=1)
     ownx = send("ownx", own, core=1)
     b01b = send("b01b", after(own_b, ownx), row=-1)
     empty = jnp.zeros((N_ROWS, HALF), jnp.float32)
@@ -332,7 +362,8 @@
     prva = send("prva", after(b01a, state), cluster=1)
     state = kernel_call("first", first_kernel, 0.5, state, sizes, [own, ownx, own_ranks, b01a])
 
-    b03, b10, nxt, b01b, prva, state = lax.optimization_barrier((b03, b10, nxt, b01b, prva, state))
+    b03, b10, state = lax.optimization_barrier((b03, b10, state))
+    nxt, b01b, prva, state = lax.optimization_barrier((nxt, b01b, prva, state))
     b13a = send("b13a", b03[0], col=1)
     b13b = send("b13b", b10[1], row=1)
     prvb = send("prvb", b01b, cluster=1)
@@ -349,26 +380,26 @@
         "same", same_kernel, 4.5, state, sizes,
         [own, ownx, own_ranks, b01a, b01b, b03, b10, nxt, prva], [rank_shape(2)],
     )
-    state, ranks1x = kernel_call(
-        "cross", cross_kernel, 3, state, sizes, [own, b01a, b01b, b03, b10, cross], [rank_shape(2)]
+    state = kernel_call(
+        "last", last_kernel, LONG, state, sizes,
+        [own, ownx, own_ranks, b01a, b01b, ranks1, nxt, prva, b13a, b13b],
     )
     prvbx = send("prvbx", after(prvb, state), core=1)
     state = kernel_call(
-        "last", last_kernel, 3.5, state, sizes,
-        [own, ownx, own_ranks, b01a, b01b, ranks1, ranks1x, nxt, prva, cross, b13a, b13b],
-    )
+        "cross", cross_kernel, 4, state, sizes, [own, b01a, b01b, b03, b10, b13a, b13b, cross]
+    )
+
+    swapped = send("swapped", state[KOWNX : KOWNX + 4], core=1)
+    side = send("side", state[W10 : W10 + 8], col=1)
     state = kernel_call("end", end_kernel, 1.5, state, sizes, [b03, b10, b13a, b13b, prvb, prvbx])
-
-    swapped = send("swapped", state[KOWNX : KOWNX + 6], core=1)
-    side = send("side", state[W10 : W10 + 8], col=1)
-    shapes = [(6, HALF), (4, HALF), (6, HALF), (2, HALF)]
-    kept, to_03, to_01, to_prv = small_call("gather", gather_kernel, shapes, 0, [state, swapped, side])
+    shapes = [(8, HALF), (4, HALF), (6, HALF)]
+    kept, to_03, to_01 = small_call("gather", gather_kernel, shapes, 1, [sizes, state, swapped, side])
     back_03 = send("back_03", to_03, row=-1)
     back_01 = send("back_01", to_01, row=1)
-    back_prv = send("back_prv", to_prv, cluster=-1, row=1)
-    return tuple(
-        small_call("final", final_kernel, [(1, rows)] * 2, 1, [sizes, kept, side, back_03, back_01, back_prv])
-    )
+    back_prv = send("back_prv", state[PRV : PRV + 8], cluster=-1, row=1)
+    back_prvx = send("back_prvx", state[PRVX : PRVX + 8], cluster=-1, row=1, core=1)
+    arrays = [kept, back_03, back_01, back_prv, back_prvx]
+    return tuple(small_call("final", final_kernel, [(1, rows)] * 2, 0, arrays))
 
 
 def solution(mesh):

time: 80.3 us -> 73.7 us (0.918)
  the two profiles are of different devices: /device:TPU:96 before, /device:TPU:0 now
where the time goes in v3:
time: 73.7 us; the launch traced here: 72.7 us
  starting transfers between devices  25.5 us (35%)
  Pallas kernels  23.9 us (32%)
  waiting for transfers between devices  21.2 us (29%)
  local copies, waits for them, and re-layouts  1.33 us (2%)
  between operations  0.76 us (1%)
    ppermute x18, starting transfers between devices, send(): return lax.ppermute(value, AXES, pairs(**shift))  25.5 us
    ppermute x18, waiting for transfers between devices, send(): return lax.ppermute(value, AXES, pairs(**shift))  21.2 us
    pallas_call x6, Pallas kernels, kernel_call(): pl.pallas_call(kernel, in_specs=[SMEM, VMEM] + [VMEM] * n, out_specs=[VME...  19.5 us
    pallas_call x1, Pallas kernels, packed(): pl.pallas_call(pack_kernel, in_specs=[pl.BlockSpec(memory_space=pltpu.HBM...  3.09 us
  transfers between devices with their start and end apart: 18, of which 9 were waited for; matrix products, arithmetic and copies ran while one was open for 0% of the time, Pallas kernels for 28%

profile of v3, /device:TPU:0, one launch (start us, length us, event | category | flops | bytes accessed | tf_op | source)
XLA Modules:
  0.0 72.7 jit_solution(3599119358363145601)
XLA Ops:
  0.6 3.1 %pack.1 = (bf16[2,264,1024]{2,1,0:T(8,128)(2,1)}, bf16[264,1024]{1,0:T(8,128)(2,1)}, bf16[264,1024]{1,0:T(8,128)(2,1)}) custom-call(s32[8]{0:T(128)} %sizes_ref.1, f32[512,1024]{1,0:T(8,128)} %bitcast.5, s32[1,512]{1,0:T(1,128)} %rank_hbm.1), custom_call_target="tpu_custom_call" | custom-call | flops 2097152 | bytes 4194304 | tf_op jit(solution)/shard_map/pack/pallas_call | solution.py:111
  3.8 1.7 %collective-permute-start.5 = (bf16[2,264,1024]{2,1,0:T(8,128)(2,1)}, bf16[2,264,1024]{2,1,0:T(8,128)(2,1)S(1)}, u32[]{:S(2)}, u32[]{:S(2)}) collective-permute-start(bf16[2,264,1024]{2,1,0:T(8,128)(2,1)} %get-tuple-element.22.refs_2_), channel_id=1, source_target_pairs={{0,4},{1,5},{2,6},{3,7},{4,8},{5,9},{6,10},{7,11},{8,12},{9,13},{1... | collective-permute-start | bytes 3244040 | tf_op jit(solution)/shard_map/b03/ppermute | solution.py:54
  5.6 1.5 %collective-permute-start.6 = (bf16[2,264,1024]{2,1,0:T(8,128)(2,1)}, bf16[2,264,1024]{2,1,0:T(8,128)(2,1)S(1)}, u32[]{:S(2)}, u32[]{:S(2)}) collective-permute-start(bf16[2,264,1024]{2,1,0:T(8,128)(2,1)} %get-tuple-element.22.refs_2_), channel_id=1, source_target_pairs={{0,2},{1,3},{2,0},{3,1},{4,6},{5,7},{6,4},{7,5},{8,10},{9,11},{10,... | collective-permute-start | bytes 3244040 | tf_op jit(solution)/shard_map/b10/ppermute | solution.py:54
  7.0 1.7 %collective-permute-start.3 = (bf16[264,1024]{1,0:T(8,128)(2,1)}, bf16[264,1024]{1,0:T(8,128)(2,1)S(1)}, u32[]{:S(2)}, u32[]{:S(2)}) collective-permute-start(bf16[264,1024]{1,0:T(8,128)(2,1)} %get-tuple-element.25), channel_id=1, source_target_pairs={{0,12},{1,13},{2,14},{3,15},{4,0},{5,1},{6,2},{7,3},{8,4},{9,5},{1... | collective-permute-start | bytes 1622024 | tf_op jit(solution)/shard_map/b01a/ppermute | solution.py:54
  8.7 5.6 %collective-permute-start = (bf16[2,264,1024]{2,1,0:T(8,128)(2,1)}, bf16[2,264,1024]{2,1,0:T(8,128)(2,1)S(1)}, u32[]{:S(2)}, u32[]{:S(2)}) collective-permute-start(bf16[2,264,1024]{2,1,0:T(8,128)(2,1)} %get-tuple-element.22.refs_2_), channel_id=1, source_target_pairs={{0,114},{1,115},{2,112},{3,113},{4,118},{5,119},{6,116},{7,117},{8... | collective-permute-start | bytes 3244040 | tf_op jit(solution)/shard_map/nxt/ppermute | solution.py:54
  14.3 1.8 %collective-permute-start.2 = (bf16[264,1024]{1,0:T(8,128)(2,1)}, bf16[264,1024]{1,0:T(8,128)(2,1)S(1)}, u32[]{:S(2)}, u32[]{:S(2)}) collective-permute-start(bf16[264,1024]{1,0:T(8,128)(2,1)} %get-tuple-element.24), channel_id=1, source_target_pairs={{0,12},{1,13},{2,14},{3,15},{4,0},{5,1},{6,2},{7,3},{8,4},{9,5},{1... | collective-permute-start | bytes 1622024 | tf_op jit(solution)/shard_map/b01b/ppermute | solution.py:54
  16.1 1.2 %copy-done = bf16[2,264,1024]{2,1,0:T(8,128)(2,1)S(1)} copy-done((bf16[2,264,1024]{2,1,0:T(8,128)(2,1)S(1)}, bf16[2,264,1024]{2,1,0:T(8,128)(2,1)}, u32[]{:S(2)}) %copy-start) | copy-done | bytes 1081368
  17.3 1.9 %self.1 = (f32[40,256]{1,0:T(8,128)S(1)}, f32[4,256,128]{2,1,0:T(8,128)S(1)}) custom-call(s32[8]{0:T(128)S(1)} %copy-done.1, f32[40,256]{1,0:T(8,128)S(1)} %broadcast_in_dim.3.refs_1_, bf16[2,264,1024]{2,1,0:T(8,128)(2,1)S(1)} %copy-done, bf16[2,264,1024]{2,1,0:T(8,128)(2,1)S(1)} %collective-permute-done.1.refs_3_), custom_call_target="tpu_custom_call" | custom-call | flops 1024 | bytes 1024 | tf_op jit(solution)/shard_map/self/pallas_call | solution.py:214
  19.2 3.2 %collective-permute-done.3.refs_5_.b01a.refs_3_ = bf16[264,1024]{1,0:T(8,128)(2,1)S(1)} collective-permute-done((bf16[264,1024]{1,0:T(8,128)(2,1)}, bf16[264,1024]{1,0:T(8,128)(2,1)S(1)}, u32[]{:S(2)}, u32[]{:S(2)}) %collective-permute-start.3) | collective-permute-done | bytes 540704 | tf_op jit(solution)/shard_map/b01a/ppermute | solution.py:54
  22.4 1.9 %collective-permute-start.4 = (bf16[264,1024]{1,0:T(8,128)(2,1)S(1)}, bf16[264,1024]{1,0:T(8,128)(2,1)S(1)}, u32[]{:S(2)}, u32[]{:S(2)}) collective-permute-start(bf16[264,1024]{1,0:T(8,128)(2,1)S(1)} %collective-permute-done.3.refs_5_.b01a.refs_3_), channel_id=1, source_target_pairs={{0,16},{1,17},{2,18},{3,19},{4,20},{5,21},{6,22},{7,23},{8,24},{9,... | collective-permute-start | bytes 1622024 | tf_op jit(solution)/shard_map/prva/ppermute | solution.py:54
  24.3 1.4 %first.1.refs_1_ = f32[40,256]{1,0:T(8,128)S(1)} custom-call(s32[8]{0:T(128)S(1)} %copy-done.1, f32[40,256]{1,0:T(8,128)S(1)} %get-tuple-element.26.refs_1_, bf16[2,264,1024]{2,1,0:T(8,128)(2,1)S(1)} %copy-done, bf16[2,264,1024]{2,1,0:T(8,128)(2,1)S(1)} %collective-permute-done.1.refs_3_, f32[4,256,128]{2,1,0:T(8,128)S(1)} %get-tuple-element.28.refs_4_, ...), custom_call_target="tpu_custom_call" | custom-call | flops 512 | bytes 1024 | tf_op jit(solution)/shard_map/first/pallas_call | solution.py:214
  25.8 5.9 %collective-permute-done.5.refs_7_.refs_5_.refs_2_ = bf16[2,264,1024]{2,1,0:T(8,128)(2,1)S(1)} collective-permute-done((bf16[2,264,1024]{2,1,0:T(8,128)(2,1)}, bf16[2,264,1024]{2,1,0:T(8,128)(2,1)S(1)}, u32[]{:S(2)}, u32[]{:S(2)}) %collective-permute-start.5) | collective-permute-done | bytes 1081376 | tf_op jit(solution)/shard_map/b03/ppermute | solution.py:54
  31.7 1.6 %collective-permute-start.7 = (bf16[264,1024]{1,0:T(8,128)(2,1)S(1)}, bf16[264,1024]{1,0:T(8,128)(2,1)S(1)}, u32[]{:S(2)}, u32[]{:S(2)}) collective-permute-start(bf16[264,1024]{1,0:T(8,128)(2,1)S(1)} %slice_bitcast_fusion.1), channel_id=1, source_target_pairs={{0,2},{1,3},{2,0},{3,1},{4,6},{5,7},{6,4},{7,5},{8,10},{9,11},{10,... | collective-permute-start | bytes 1622024 | tf_op jit(solution)/shard_map/b13a/ppermute | solution.py:54
  33.3 1.6 %collective-permute-start.8 = (bf16[264,1024]{1,0:T(8,128)(2,1)S(1)}, bf16[264,1024]{1,0:T(8,128)(2,1)S(1)}, u32[]{:S(2)}, u32[]{:S(2)}) collective-permute-start(bf16[264,1024]{1,0:T(8,128)(2,1)S(1)} %slice_bitcast_fusion), channel_id=1, source_target_pairs={{0,4},{1,5},{2,6},{3,7},{4,8},{5,9},{6,10},{7,11},{8,12},{9,13},{1... | collective-permute-start | bytes 1622024 | tf_op jit(solution)/shard_map/b13b/ppermute | solution.py:54
  35.0 2.5 %collective-permute-done.refs_9_.refs_8_.nxt = bf16[2,264,1024]{2,1,0:T(8,128)(2,1)S(1)} collective-permute-done((bf16[2,264,1024]{2,1,0:T(8,128)(2,1)}, bf16[2,264,1024]{2,1,0:T(8,128)(2,1)S(1)}, u32[]{:S(2)}, u32[]{:S(2)}) %collective-permute-start) | collective-permute-done | bytes 1081376 | tf_op jit(solution)/shard_map/nxt/ppermute | solution.py:54
  38.8 5.4 %same.1 = (f32[40,256]{1,0:T(8,128)S(1)}, f32[2,256,128]{2,1,0:T(8,128)S(1)}) custom-call(s32[8]{0:T(128)S(1)} %copy-done.1, f32[40,256]{1,0:T(8,128)S(1)} %first.1.refs_1_, bf16[2,264,1024]{2,1,0:T(8,128)(2,1)S(1)} %copy-done, bf16[2,264,1024]{2,1,0:T(8,128)(2,1)S(1)} %collective-permute-done.1.refs_3_, f32[4,256,128]{2,1,0:T(8,128)S(1)} %get-tuple-element.28.refs_4_, ...), custom_call_target="tpu_custom_call" | custom-call | flops 4608 | bytes 1024 | tf_op jit(solution)/shard_map/same/pallas_call | solution.py:214
  44.2 1.5 %collective-permute-done.7.refs_10_.refs_7_.refs_4_ = bf16[264,1024]{1,0:T(8,128)(2,1)S(1)} collective-permute-done((bf16[264,1024]{1,0:T(8,128)(2,1)S(1)}, bf16[264,1024]{1,0:T(8,128)(2,1)S(1)}, u32[]{:S(2)}, u32[]{:S(2)}) %collective-permute-start.7) | collective-permute-done | bytes 540704 | tf_op jit(solution)/shard_map/b13a/ppermute | solution.py:54
  45.8 2.4 %collective-permute-done.8.refs_11_.refs_8_.refs_5_ = bf16[264,1024]{1,0:T(8,128)(2,1)S(1)} collective-permute-done((bf16[264,1024]{1,0:T(8,128)(2,1)S(1)}, bf16[264,1024]{1,0:T(8,128)(2,1)S(1)}, u32[]{:S(2)}, u32[]{:S(2)}) %collective-permute-start.8) | collective-permute-done | bytes 540704 | tf_op jit(solution)/shard_map/b13b/ppermute | solution.py:54
  48.2 3.2 %last.1.refs_1_ = f32[40,256]{1,0:T(8,128)S(1)} custom-call(s32[8]{0:T(128)S(1)} %copy-done.1, f32[40,256]{1,0:T(8,128)S(1)} %get-tuple-element.36.refs_1_, bf16[2,264,1024]{2,1,0:T(8,128)(2,1)S(1)} %copy-done, bf16[2,264,1024]{2,1,0:T(8,128)(2,1)S(1)} %collective-permute-done.1.refs_3_, f32[4,256,128]{2,1,0:T(8,128)S(1)} %get-tuple-element.28.refs_4_, ...), custom_call_target="tpu_custom_call" | custom-call | flops 102400000000 | bytes 1024 | tf_op jit(solution)/shard_map/last/pallas_call | solution.py:214
  51.4 3.0 %collective-permute-done.10.refs_6_ = bf16[264,1024]{1,0:T(8,128)(2,1)S(1)} collective-permute-done((bf16[264,1024]{1,0:T(8,128)(2,1)S(1)}, bf16[264,1024]{1,0:T(8,128)(2,1)S(1)}, u32[]{:S(2)}, u32[]{:S(2)}) %collective-permute-start.10) | collective-permute-done | bytes 540704 | tf_op jit(solution)/shard_map/prvb/ppermute | solution.py:54
  54.4 5.2 %cross.1.refs_1_ = f32[40,256]{1,0:T(8,128)S(1)} custom-call(s32[8]{0:T(128)S(1)} %copy-done.1, f32[40,256]{1,0:T(8,128)S(1)} %last.1.refs_1_, bf16[2,264,1024]{2,1,0:T(8,128)(2,1)S(1)} %copy-done, bf16[264,1024]{1,0:T(8,128)(2,1)S(1)} %collective-permute-done.3.refs_5_.b01a.refs_3_, bf16[264,1024]{1,0:T(8,128)(2,1)S(1)} %collective-permute-done.2.refs_6_.b01b.refs_4_, ...), custom_call_target="tpu_custom_call" | custom-call | flops 4096 | bytes 1024 | tf_op jit(solution)/shard_map/cross/pallas_call | solution.py:214
  60.2 2.4 %end.1.rows_ref = f32[40,256]{1,0:T(8,128)S(1)} custom-call(s32[8]{0:T(128)S(1)} %copy-done.1, f32[40,256]{1,0:T(8,128)S(1)} %cross.1.refs_1_, bf16[2,264,1024]{2,1,0:T(8,128)(2,1)S(1)} %collective-permute-done.5.refs_7_.refs_5_.refs_2_, bf16[2,264,1024]{2,1,0:T(8,128)(2,1)S(1)} %collective-permute-done.6.refs_8_.refs_6_.refs_3_, ...), custom_call_target="tpu_custom_call" | custom-call | flops 1536 | bytes 1024 | tf_op jit(solution)/shard_map/end/pallas_call | solution.py:214
  62.7 3.4 %collective-permute-start.16 = (f32[8,256]{1,0:T(8,128)S(1)}, f32[8,256]{1,0:T(8,128)S(1)}, u32[]{:S(2)}, u32[]{:S(2)}) collective-permute-start(f32[8,256]{1,0:T(8,128)S(1)} %get-tuple-element.43), channel_id=1, source_target_pairs={{0,118},{1,119},{2,116},{3,117},{4,122},{5,123},{6,120},{7,121},{8... | collective-permute-start | bytes 24584 | tf_op jit(solution)/shard_map/back_prv/ppermute | solution.py:54
  68.0 2.4 %collective-permute-start.14 = (f32[4,256]{1,0:T(4,128)S(1)}, f32[4,256]{1,0:T(4,128)S(1)}, u32[]{:S(2)}, u32[]{:S(2)}) collective-permute-start(f32[4,256]{1,0:T(4,128)S(1)} %get-tuple-element.40), channel_id=1, source_target_pairs={{0,12},{1,13},{2,14},{3,15},{4,0},{5,1},{6,2},{7,3},{8,4},{9,5},{1... | collective-permute-start | bytes 12296 | tf_op jit(solution)/shard_map/back_03/ppermute | solution.py:54
  (32 shorter events, 6.3 us)
Async XLA Ops:
  0.6 15.5 %copy-start.1 = (s32[8]{0:T(128)S(1)}, s32[8]{0:T(128)}, u32[]{:S(2)}) copy-start(s32[8]{0:T(128)} %sizes_ref.1) | copy-start | bytes 100
  3.7 10.5 %collective-permute-start.1 = (bf16[2,264,1024]{2,1,0:T(8,128)(2,1)}, bf16[2,264,1024]{2,1,0:T(8,128)(2,1)S(1)}, u32[]{:S(2)}, u32[]{:S(2)}) collective-permute-start(bf16[2,264,1024]{2,1,0:T(8,128)(2,1)} %get-tuple-element.22.refs_2_), channel_id=1, source_target_pairs={{0,1},{1,0},{2,3},{3,2},{4,5},{5,4},{6,7},{7,6},{8,9},{9,8},{10,11... | collective-permute-start | bytes 3244040 | tf_op jit(solution)/shard_map/ownx/ppermute | solution.py:54
  3.8 27.8 %collective-permute-start.5 = (bf16[2,264,1024]{2,1,0:T(8,128)(2,1)}, bf16[2,264,1024]{2,1,0:T(8,128)(2,1)S(1)}, u32[]{:S(2)}, u32[]{:S(2)}) collective-permute-start(bf16[2,264,1024]{2,1,0:T(8,128)(2,1)} %get-tuple-element.22.refs_2_), channel_id=1, source_target_pairs={{0,4},{1,5},{2,6},{3,7},{4,8},{5,9},{6,10},{7,11},{8,12},{9,13},{1... | collective-permute-start | bytes 3244040 | tf_op jit(solution)/shard_map/b03/ppermute | solution.py:54
  5.6 26.1 %collective-permute-start.6 = (bf16[2,264,1024]{2,1,0:T(8,128)(2,1)}, bf16[2,264,1024]{2,1,0:T(8,128)(2,1)S(1)}, u32[]{:S(2)}, u32[]{:S(2)}) collective-permute-start(bf16[2,264,1024]{2,1,0:T(8,128)(2,1)} %get-tuple-element.22.refs_2_), channel_id=1, source_target_pairs={{0,2},{1,3},{2,0},{3,1},{4,6},{5,7},{6,4},{7,5},{8,10},{9,11},{10,... | collective-permute-start | bytes 3244040 | tf_op jit(solution)/shard_map/b10/ppermute | solution.py:54
  7.0 15.4 %collective-permute-start.3 = (bf16[264,1024]{1,0:T(8,128)(2,1)}, bf16[264,1024]{1,0:T(8,128)(2,1)S(1)}, u32[]{:S(2)}, u32[]{:S(2)}) collective-permute-start(bf16[264,1024]{1,0:T(8,128)(2,1)} %get-tuple-element.25), channel_id=1, source_target_pairs={{0,12},{1,13},{2,14},{3,15},{4,0},{5,1},{6,2},{7,3},{8,4},{9,5},{1... | collective-permute-start | bytes 1622024 | tf_op jit(solution)/shard_map/b01a/ppermute | solution.py:54
  8.7 28.8 %collective-permute-start = (bf16[2,264,1024]{2,1,0:T(8,128)(2,1)}, bf16[2,264,1024]{2,1,0:T(8,128)(2,1)S(1)}, u32[]{:S(2)}, u32[]{:S(2)}) collective-permute-start(bf16[2,264,1024]{2,1,0:T(8,128)(2,1)} %get-tuple-element.22.refs_2_), channel_id=1, source_target_pairs={{0,114},{1,115},{2,112},{3,113},{4,118},{5,119},{6,116},{7,117},{8... | collective-permute-start | bytes 3244040 | tf_op jit(solution)/shard_map/nxt/ppermute | solution.py:54
  14.3 23.2 %collective-permute-start.2 = (bf16[264,1024]{1,0:T(8,128)(2,1)}, bf16[264,1024]{1,0:T(8,128)(2,1)S(1)}, u32[]{:S(2)}, u32[]{:S(2)}) collective-permute-start(bf16[264,1024]{1,0:T(8,128)(2,1)} %get-tuple-element.24), channel_id=1, source_target_pairs={{0,12},{1,13},{2,14},{3,15},{4,0},{5,1},{6,2},{7,3},{8,4},{9,5},{1... | collective-permute-start | bytes 1622024 | tf_op jit(solution)/shard_map/b01b/ppermute | solution.py:54
  16.1 1.2 %copy-start = (bf16[2,264,1024]{2,1,0:T(8,128)(2,1)S(1)}, bf16[2,264,1024]{2,1,0:T(8,128)(2,1)}, u32[]{:S(2)}) copy-start(bf16[2,264,1024]{2,1,0:T(8,128)(2,1)} %get-tuple-element.22.refs_2_) | copy-start | bytes 3244036
  22.4 15.9 %collective-permute-start.4 = (bf16[264,1024]{1,0:T(8,128)(2,1)S(1)}, bf16[264,1024]{1,0:T(8,128)(2,1)S(1)}, u32[]{:S(2)}, u32[]{:S(2)}) collective-permute-start(bf16[264,1024]{1,0:T(8,128)(2,1)S(1)} %collective-permute-done.3.refs_5_.b01a.refs_3_), channel_id=1, source_target_pairs={{0,16},{1,17},{2,18},{3,19},{4,20},{5,21},{6,22},{7,23},{8,24},{9,... | collective-permute-start | bytes 1622024 | tf_op jit(solution)/shard_map/prva/ppermute | solution.py:54
  31.7 14.0 %collective-permute-start.7 = (bf16[264,1024]{1,0:T(8,128)(2,1)S(1)}, bf16[264,1024]{1,0:T(8,128)(2,1)S(1)}, u32[]{:S(2)}, u32[]{:S(2)}) collective-permute-start(bf16[264,1024]{1,0:T(8,128)(2,1)S(1)} %slice_bitcast_fusion.1), channel_id=1, source_target_pairs={{0,2},{1,3},{2,0},{3,1},{4,6},{5,7},{6,4},{7,5},{8,10},{9,11},{10,... | collective-permute-start | bytes 1622024 | tf_op jit(solution)/shard_map/b13a/ppermute | solution.py:54
  33.3 14.9 %collective-permute-start.8 = (bf16[264,1024]{1,0:T(8,128)(2,1)S(1)}, bf16[264,1024]{1,0:T(8,128)(2,1)S(1)}, u32[]{:S(2)}, u32[]{:S(2)}) collective-permute-start(bf16[264,1024]{1,0:T(8,128)(2,1)S(1)} %slice_bitcast_fusion), channel_id=1, source_target_pairs={{0,4},{1,5},{2,6},{3,7},{4,8},{5,9},{6,10},{7,11},{8,12},{9,13},{1... | collective-permute-start | bytes 1622024 | tf_op jit(solution)/shard_map/b13b/ppermute | solution.py:54
  38.3 16.1 %collective-permute-start.10 = (bf16[264,1024]{1,0:T(8,128)(2,1)S(1)}, bf16[264,1024]{1,0:T(8,128)(2,1)S(1)}, u32[]{:S(2)}, u32[]{:S(2)}) collective-permute-start(bf16[264,1024]{1,0:T(8,128)(2,1)S(1)} %collective-permute-done.2.refs_6_.b01b.refs_4_), channel_id=1, source_target_pairs={{0,16},{1,17},{2,18},{3,19},{4,20},{5,21},{6,22},{7,23},{8,24},{9,... | collective-permute-start | bytes 1622024 | tf_op jit(solution)/shard_map/prvb/ppermute | solution.py:54
  38.5 15.9 %collective-permute-start.9 = (bf16[5,264,1024]{2,1,0:T(8,128)(2,1)S(1)}, bf16[5,264,1024]{2,1,0:T(8,128)(2,1)S(1)}, u32[]{:S(2)}, u32[]{:S(2)}) collective-permute-start(bf16[5,264,1024]{2,1,0:T(8,128)(2,1)S(1)} %bundle.1), channel_id=1, source_target_pairs={{0,1},{1,0},{2,3},{3,2},{4,5},{5,4},{6,7},{7,6},{8,9},{9,8},{10,11... | collective-permute-start | bytes 8110088 | tf_op jit(solution)/shard_map/cross/ppermute | solution.py:54
  54.4 5.8 %collective-permute-start.11 = (bf16[264,1024]{1,0:T(8,128)(2,1)S(1)}, bf16[264,1024]{1,0:T(8,128)(2,1)S(1)}, u32[]{:S(2)}, u32[]{:S(2)}) collective-permute-start(bf16[264,1024]{1,0:T(8,128)(2,1)S(1)} %collective-permute-done.10.refs_6_), channel_id=1, source_target_pairs={{0,1},{1,0},{2,3},{3,2},{4,5},{5,4},{6,7},{7,6},{8,9},{9,8},{10,11... | collective-permute-start | bytes 1622024 | tf_op jit(solution)/shard_map/prvbx/ppermute | solution.py:54
  59.6 6.9 %collective-permute-start.12 = (f32[4,256]{1,0:T(4,128)S(1)}, f32[4,256]{1,0:T(4,128)S(1)}, u32[]{:S(2)}, u32[]{:S(2)}) collective-permute-start(f32[4,256]{1,0:T(4,128)S(1)} %slice.24), channel_id=1, source_target_pairs={{0,1},{1,0},{2,3},{3,2},{4,5},{5,4},{6,7},{7,6},{8,9},{9,8},{10,11... | collective-permute-start | bytes 12296 | tf_op jit(solution)/shard_map/swapped/ppermute | solution.py:54
  60.2 6.3 %collective-permute-start.13 = (f32[8,256]{1,0:T(8,128)S(1)}, f32[8,256]{1,0:T(8,128)S(1)}, u32[]{:S(2)}, u32[]{:S(2)}) collective-permute-start(f32[8,256]{1,0:T(8,128)S(1)} %slice.25), channel_id=1, source_target_pairs={{0,2},{1,3},{2,0},{3,1},{4,6},{5,7},{6,4},{7,5},{8,10},{9,11},{10,... | collective-permute-start | bytes 24584 | tf_op jit(solution)/shard_map/side/ppermute | solution.py:54
  62.7 7.8 %collective-permute-start.16 = (f32[8,256]{1,0:T(8,128)S(1)}, f32[8,256]{1,0:T(8,128)S(1)}, u32[]{:S(2)}, u32[]{:S(2)}) collective-permute-start(f32[8,256]{1,0:T(8,128)S(1)} %get-tuple-element.43), channel_id=1, source_target_pairs={{0,118},{1,119},{2,116},{3,117},{4,122},{5,123},{6,120},{7,121},{8... | collective-permute-start | bytes 24584 | tf_op jit(solution)/shard_map/back_prv/ppermute | solution.py:54
  66.0 5.2 %collective-permute-start.17 = (f32[8,256]{1,0:T(8,128)S(1)}, f32[8,256]{1,0:T(8,128)S(1)}, u32[]{:S(2)}, u32[]{:S(2)}) collective-permute-start(f32[8,256]{1,0:T(8,128)S(1)} %get-tuple-element.42), channel_id=1, source_target_pairs={{0,119},{1,118},{2,117},{3,116},{4,123},{5,122},{6,121},{7,120},{8... | collective-permute-start | bytes 24584 | tf_op jit(solution)/shard_map/back_prvx/ppermute | solution.py:54
  67.1 5.0 %collective-permute-start.15 = (f32[6,256]{1,0:T(8,128)S(1)}, f32[6,256]{1,0:T(8,128)S(1)}, u32[]{:S(2)}, u32[]{:S(2)}) collective-permute-start(f32[6,256]{1,0:T(8,128)S(1)} %get-tuple-element.41), channel_id=1, source_target_pairs={{0,4},{1,5},{2,6},{3,7},{4,8},{5,9},{6,10},{7,11},{8,12},{9,13},{1... | collective-permute-start | bytes 18440 | tf_op jit(solution)/shard_map/back_01/ppermute | solution.py:54
  68.0 4.1 %collective-permute-start.14 = (f32[4,256]{1,0:T(4,128)S(1)}, f32[4,256]{1,0:T(4,128)S(1)}, u32[]{:S(2)}, u32[]{:S(2)}) collective-permute-start(f32[4,256]{1,0:T(4,128)S(1)} %get-tuple-element.40), channel_id=1, source_target_pairs={{0,12},{1,13},{2,14},{3,15},{4,0},{5,1},{6,2},{7,3},{8,4},{9,5},{1... | collective-permute-start | bytes 12296 | tf_op jit(solution)/shard_map/back_03/ppermute | solution.py:54

commit v4 on v3

--- a/solution.py
+++ b/solution.py
@@ -225,6 +225,7 @@
 
 W00, A00, KOWN, W03, A03, W10, A10 = 0, 2, 4, 6, 8, 10, 12
 W13, A13, W01, A01, K01, PRV, KOWNX, K01X, PRVX = 14, 16, 18, 20, 22, 24, 26, 28, 30
+REAL, FLOOR = 32, 34
 N_ROWS = 40
 
 
@@ -245,6 +246,12 @@
     keys = split(own) + split(ownx)
     put_ranks(ranks, keys)
     row_ref[...] = jnp.full(row_ref.shape, LOW, jnp.float32)
+    left = own_count(sizes_ref) - lax.axis_index("helper") * 2 * HALF
+    for h in range(2):
+        position = lax.broadcasted_iota(jnp.int32, (1, HALF), 1) + h * HALF
+        row_ref[REAL + h : REAL + h + 1, :] = jnp.where(position < left, 1.0, 0.0)
+    floor = jnp.where(own_count(sizes_ref, 1) < 2 * HALF * lax.axis_size("helper"), -1.0, LOW)
+    row_ref[FLOOR : FLOOR + 1, :] = jnp.full((1, HALF), floor, jnp.float32)
     pair_job(row_ref, [ranks.at[n] for n in range(4)], keys, split(own), both(W00), None)
 
 
@@ -287,7 +294,7 @@
     real_job(row_ref, real_rows(sizes_ref, 1, -1), b13, [prva], [PRV])
 
 
-def cross_kernel(row_ref, sizes_ref, own, b01a, b01b, b03, b10, b13a, b13b, cross):
+def cross_kernel(row_ref, sizes_ref, own, b01a, b01b, b03, b10, b13a, b13b, cross, prvbx):
     b13 = [b13a, b13b]
     queries = [*split(own), b01a, b01b, *split(b03), *split(b10), *b13]
     places = both(A00) + both(A01) + both(A03) + both(A10) + both(A13)
@@ -299,47 +306,43 @@
         row_ref, ranks, one, queries, both(W03) + both(W13), both(K01X), lambda k, q: (2 + k, q % 2) in SHARE
     )
     limits = real_rows(sizes_ref, 0, -1) + real_rows(sizes_ref, 1, 0) + real_rows(sizes_ref, 1, -1)
-    real_job(row_ref, limits, split(b03) + split(b10) + b13, [cross.at[4]], [PRVX])
-
-
-def end_kernel(row_ref, sizes_ref, b03, b10, b13a, b13b, prvb, prvbx):
+    real_job(row_ref, limits, split(b03) + split(b10) + b13, [cross.at[4], prvbx], both(PRVX))
+
+
+def end_kernel(row_ref, sizes_ref, b03, b10, b13a, b13b, prvb):
     limits = real_rows(sizes_ref, 1, -1) + real_rows(sizes_ref, 0, -1) + real_rows(sizes_ref, 1, 0)
-    real_job(row_ref, limits, [b13a, b13b, *split(b03), *split(b10)], [prvb, prvbx], [PRV + 1, PRVX + 1])
-
-
-def gather_kernel(sizes_ref, rows_ref, swapped_ref, side_ref, kept_ref, to03_ref, to01_ref):
-    left = own_count(sizes_ref) - lax.axis_index("helper") * 2 * HALF
-    floor = jnp.where(own_count(sizes_ref, 1) >= 2 * HALF * lax.axis_size("helper"), LOW, -1.0)
-    for h in range(2):
-        row = lambda ref, at: ref[at + h : at + h + 1, :]
-        real = lax.broadcasted_iota(jnp.int32, (1, HALF), 1) + h * HALF < left
-        within = jnp.maximum(row(rows_ref, W00), row(rows_ref, KOWN))
-        within = jnp.maximum(jnp.maximum(within, row(swapped_ref, 0)), jnp.maximum(row(side_ref, 0), -1.0))
-        adjacent = jnp.maximum(jnp.maximum(row(rows_ref, A00), row(side_ref, 2)), floor)
-        kept_ref[h : h + 1, :] = within
-        kept_ref[2 + h : 3 + h, :] = adjacent
-        kept_ref[4 + h : 5 + h, :] = jnp.where(real, 1.0, 0.0)
-    kept_ref[6:8, :] = jnp.zeros((2, HALF), jnp.float32)
+    real_job(row_ref, limits, [b13a, b13b, *split(b03), *split(b10)], [prvb], [PRV + 1])
+
+
+def gather_kernel(rows_ref, swapped_ref, side_ref, kept_ref, to03_ref, to01_ref, prv_ref):
+    within = jnp.maximum(rows_ref[W00 : W00 + 2, :], rows_ref[KOWN : KOWN + 2, :])
+    within = jnp.maximum(within, jnp.maximum(swapped_ref[0:2, :], side_ref[0:2, :]))
+    kept_ref[0:2, :] = jnp.maximum(within, -1.0)
+    kept_ref[2:4, :] = jnp.maximum(jnp.maximum(rows_ref[A00 : A00 + 2, :], side_ref[2:4, :]), rows_ref[FLOOR : FLOOR + 1, :])
+    kept_ref[4:6, :] = rows_ref[REAL : REAL + 2, :]
+    kept_ref[6:8, :] = rows_ref[REAL : REAL + 2, :]
     to03_ref[...] = jnp.maximum(rows_ref[W03 : W03 + 4, :], side_ref[4:8, :])
-    to01_ref[...] = rows_ref[W01 : W01 + 6, :]
+    to01_ref[0:4, :] = rows_ref[W01 : W01 + 4, :]
     to01_ref[4:6, :] = jnp.maximum(rows_ref[K01 : K01 + 2, :], swapped_ref[2:4, :])
-
-
-def final_kernel(kept, b03, b01, bprv, bprvx, within_ref, adjacent_ref):
+    prv_ref[0:2, :] = jnp.maximum(rows_ref[PRV : PRV + 2, :], swapped_ref[4:6, :])
+    prv_ref[2:8, :] = rows_ref[0:6, :]
+
+
+def final_kernel(kept, b03, b01, bprv, within_ref, adjacent_ref):
     for h in range(2):
         row = lambda ref, at: ref[at + h : at + h + 1, :]
         within = [row(kept, 0), row(b03, 0), row(b01, 0), row(b01, 4)]
-        adjacent = [row(kept, 2), row(b03, 2), row(b01, 2), row(bprv, 0), row(bprvx, 0)]
+        adjacent = [row(kept, 2), row(b03, 2), row(b01, 2), row(bprv, 0)]
         real = row(kept, 4) > 0
         place = slice(h * HALF, (h + 1) * HALF)
         within_ref[:, place] = jnp.where(real, functools.reduce(jnp.maximum, within), 0.0)
         adjacent_ref[:, place] = jnp.where(real, functools.reduce(jnp.maximum, adjacent), 0.0)
 
 
-def small_call(name, body, shapes, smem, arrays):
+def small_call(name, body, shapes, arrays):
     return pl.pallas_call(
         body,
-        in_specs=[SMEM] * smem + [VMEM] * (len(arrays) - smem),
+        in_specs=[VMEM] * len(arrays),
         out_specs=[VMEM] * len(shapes),
         out_shape=[jax.ShapeDtypeStruct(shape, jnp.float32) for shape in shapes],
         name=name,
@@ -362,11 +365,11 @@
     prva = send("prva", after(b01a, state), cluster=1)
     state = kernel_call("first", first_kernel, 0.5, state, sizes, [own, ownx, own_ranks, b01a])
 
+    prvb = send("prvb", after(b01b, state), cluster=1)
     b03, b10, state = lax.optimization_barrier((b03, b10, state))
     nxt, b01b, prva, state = lax.optimization_barrier((nxt, b01b, prva, state))
     b13a = send("b13a", b03[0], col=1)
     b13b = send("b13b", b10[1], row=1)
-    prvb = send("prvb", b01b, cluster=1)
     bundle = pl.pallas_call(
         bundle_kernel,
         in_specs=[VMEM] * 4,
@@ -380,26 +383,25 @@
         "same", same_kernel, 4.5, state, sizes,
         [own, ownx, own_ranks, b01a, b01b, b03, b10, nxt, prva], [rank_shape(2)],
     )
+    prvb, state = lax.optimization_barrier((prvb, state))
     state = kernel_call(
         "last", last_kernel, LONG, state, sizes,
         [own, ownx, own_ranks, b01a, b01b, ranks1, nxt, prva, b13a, b13b],
     )
-    prvbx = send("prvbx", after(prvb, state), core=1)
+    prvbx = send("prvbx", prvb, core=1)
     state = kernel_call(
-        "cross", cross_kernel, 4, state, sizes, [own, b01a, b01b, b03, b10, b13a, b13b, cross]
-    )
-
-    swapped = send("swapped", state[KOWNX : KOWNX + 4], core=1)
+        "cross", cross_kernel, 4, state, sizes, [own, b01a, b01b, b03, b10, b13a, b13b, cross, prvbx]
+    )
+
+    swapped = send("swapped", state[KOWNX : KOWNX + 6], core=1)
     side = send("side", state[W10 : W10 + 8], col=1)
-    state = kernel_call("end", end_kernel, 1.5, state, sizes, [b03, b10, b13a, b13b, prvb, prvbx])
-    shapes = [(8, HALF), (4, HALF), (6, HALF)]
-    kept, to_03, to_01 = small_call("gather", gather_kernel, shapes, 1, [sizes, state, swapped, side])
+    state = kernel_call("end", end_kernel, 1, state, sizes, [b03, b10, b13a, b13b, prvb])
+    shapes = [(8, HALF), (4, HALF), (6, HALF), (8, HALF)]
+    kept, to_03, to_01, to_prv = small_call("gather", gather_kernel, shapes, [state, swapped, side])
+    back_prv = send("back_prv", to_prv, cluster=-1, row=1)
+    back_01 = send("back_01", to_01, row=1)
     back_03 = send("back_03", to_03, row=-1)
-    back_01 = send("back_01", to_01, row=1)
-    back_prv = send("back_prv", state[PRV : PRV + 8], cluster=-1, row=1)
-    back_prvx = send("back_prvx", state[PRVX : PRVX + 8], cluster=-1, row=1, core=1)
-    arrays = [kept, back_03, back_01, back_prv, back_prvx]
-    return tuple(small_call("final", final_kernel, [(1, rows)] * 2, 0, arrays))
+    return tuple(small_call("final", final_kernel, [(1, rows)] * 2, [kept, back_03, back_01, back_prv]))
 
 
 def solution(mesh):

time: 73.7 us -> 72.1 us (0.978)
  waiting for transfers between devices: 21.2 us -> 20.1 us
    ppermute x18 -> x17, waiting for transfers between devices: 21.2 us -> 20.1 us  [send(): return lax.ppermute(value, AXES, pairs(**shift))]
    ppermute x18 -> x17, starting transfers between devices: 25.5 us -> 26.2 us  [send(): return lax.ppermute(value, AXES, pairs(**shift))]
  transfers between devices with their start and end apart: 18 -> 17, of which waited for: 9 -> 6; matrix products, arithmetic and copies ran while one was open for 0% -> 0% of each run, Pallas kernels for 28% -> 19%
where the time goes in v4:
time: 72.1 us; the launch traced here: 71.8 us
  starting transfers between devices  26.2 us (36%)
  Pallas kernels  23.4 us (32%)
  waiting for transfers between devices  20.1 us (28%)
  local copies, waits for them, and re-layouts  1.35 us (2%)
  between operations  0.76 us (1%)
    ppermute x17, starting transfers between devices, send(): return lax.ppermute(value, AXES, pairs(**shift))  26.2 us
    ppermute x17, waiting for transfers between devices, send(): return lax.ppermute(value, AXES, pairs(**shift))  20.1 us
    pallas_call x6, Pallas kernels, kernel_call(): pl.pallas_call(kernel, in_specs=[SMEM, VMEM] + [VMEM] * n, out_specs=[VME...  19.5 us
    pallas_call x1, Pallas kernels, packed(): pl.pallas_call(pack_kernel, in_specs=[pl.BlockSpec(memory_space=pltpu.HBM...  3.07 us
  transfers between devices with their start and end apart: 17, of which 6 were waited for; matrix products, arithmetic and copies ran while one was open for 0% of the time, Pallas kernels for 19%

profile of v4, /device:TPU:0, one launch (start us, length us, event | category | flops | bytes accessed | tf_op | source)
XLA Modules:
  0.0 71.8 jit_solution(2907036849762710792)
XLA Ops:
  0.6 3.1 %pack.1 = (bf16[2,264,1024]{2,1,0:T(8,128)(2,1)}, bf16[264,1024]{1,0:T(8,128)(2,1)}, bf16[264,1024]{1,0:T(8,128)(2,1)}) custom-call(s32[8]{0:T(128)} %refs_0_.11, f32[512,1024]{1,0:T(8,128)} %bitcast.5, s32[1,512]{1,0:T(1,128)} %rank_hbm.1), custom_call_target="tpu_custom_call" | custom-call | flops 2097152 | bytes 4194304 | tf_op jit(solution)/shard_map/pack/pallas_call | solution.py:111
  3.8 1.7 %collective-permute-start.6 = (bf16[2,264,1024]{2,1,0:T(8,128)(2,1)}, bf16[2,264,1024]{2,1,0:T(8,128)(2,1)S(1)}, u32[]{:S(2)}, u32[]{:S(2)}) collective-permute-start(bf16[2,264,1024]{2,1,0:T(8,128)(2,1)} %get-tuple-element.26.refs_2_), channel_id=1, source_target_pairs={{0,4},{1,5},{2,6},{3,7},{4,8},{5,9},{6,10},{7,11},{8,12},{9,13},{1... | collective-permute-start | bytes 3244040 | tf_op jit(solution)/shard_map/b03/ppermute | solution.py:54
  5.5 1.5 %collective-permute-start.7 = (bf16[2,264,1024]{2,1,0:T(8,128)(2,1)}, bf16[2,264,1024]{2,1,0:T(8,128)(2,1)S(1)}, u32[]{:S(2)}, u32[]{:S(2)}) collective-permute-start(bf16[2,264,1024]{2,1,0:T(8,128)(2,1)} %get-tuple-element.26.refs_2_), channel_id=1, source_target_pairs={{0,2},{1,3},{2,0},{3,1},{4,6},{5,7},{6,4},{7,5},{8,10},{9,11},{10,... | collective-permute-start | bytes 3244040 | tf_op jit(solution)/shard_map/b10/ppermute | solution.py:54
  7.0 1.7 %collective-permute-start.2 = (bf16[264,1024]{1,0:T(8,128)(2,1)}, bf16[264,1024]{1,0:T(8,128)(2,1)S(1)}, u32[]{:S(2)}, u32[]{:S(2)}) collective-permute-start(bf16[264,1024]{1,0:T(8,128)(2,1)} %get-tuple-element.30), channel_id=1, source_target_pairs={{0,12},{1,13},{2,14},{3,15},{4,0},{5,1},{6,2},{7,3},{8,4},{9,5},{1... | collective-permute-start | bytes 1622024 | tf_op jit(solution)/shard_map/b01a/ppermute | solution.py:54
  8.7 1.8 %collective-permute-start.1 = (bf16[264,1024]{1,0:T(8,128)(2,1)}, bf16[264,1024]{1,0:T(8,128)(2,1)S(1)}, u32[]{:S(2)}, u32[]{:S(2)}) collective-permute-start(bf16[264,1024]{1,0:T(8,128)(2,1)} %get-tuple-element.27), channel_id=1, source_target_pairs={{0,12},{1,13},{2,14},{3,15},{4,0},{5,1},{6,2},{7,3},{8,4},{9,5},{1... | collective-permute-start | bytes 1622024 | tf_op jit(solution)/shard_map/b01b/ppermute | solution.py:54
  10.5 5.6 %collective-permute-start.4 = (bf16[2,264,1024]{2,1,0:T(8,128)(2,1)}, bf16[2,264,1024]{2,1,0:T(8,128)(2,1)S(1)}, u32[]{:S(2)}, u32[]{:S(2)}) collective-permute-start(bf16[2,264,1024]{2,1,0:T(8,128)(2,1)} %get-tuple-element.26.refs_2_), channel_id=1, source_target_pairs={{0,114},{1,115},{2,112},{3,113},{4,118},{5,119},{6,116},{7,117},{8... | collective-permute-start | bytes 3244040 | tf_op jit(solution)/shard_map/nxt/ppermute | solution.py:54
  17.3 1.9 %self.1 = (f32[40,256]{1,0:T(8,128)S(1)}, f32[4,256,128]{2,1,0:T(8,128)S(1)}) custom-call(s32[8]{0:T(128)S(1)} %copy-done.1, f32[40,256]{1,0:T(8,128)S(1)} %broadcast_in_dim.3.refs_1_, bf16[2,264,1024]{2,1,0:T(8,128)(2,1)S(1)} %copy-done, bf16[2,264,1024]{2,1,0:T(8,128)(2,1)S(1)} %collective-permute-done.refs_3_), custom_call_target="tpu_custom_call" | custom-call | flops 1024 | bytes 1024 | tf_op jit(solution)/shard_map/self/pallas_call | solution.py:214
  19.2 3.2 %collective-permute-done.2.refs_5_.b01a.refs_3_ = bf16[264,1024]{1,0:T(8,128)(2,1)S(1)} collective-permute-done((bf16[264,1024]{1,0:T(8,128)(2,1)}, bf16[264,1024]{1,0:T(8,128)(2,1)S(1)}, u32[]{:S(2)}, u32[]{:S(2)}) %collective-permute-start.2) | collective-permute-done | bytes 540704 | tf_op jit(solution)/shard_map/b01a/ppermute | solution.py:54
  22.4 1.9 %collective-permute-start.5 = (bf16[264,1024]{1,0:T(8,128)(2,1)S(1)}, bf16[264,1024]{1,0:T(8,128)(2,1)S(1)}, u32[]{:S(2)}, u32[]{:S(2)}) collective-permute-start(bf16[264,1024]{1,0:T(8,128)(2,1)S(1)} %collective-permute-done.2.refs_5_.b01a.refs_3_), channel_id=1, source_target_pairs={{0,16},{1,17},{2,18},{3,19},{4,20},{5,21},{6,22},{7,23},{8,24},{9,... | collective-permute-start | bytes 1622024 | tf_op jit(solution)/shard_map/prva/ppermute | solution.py:54
  24.3 1.4 %first.1.refs_1_ = f32[40,256]{1,0:T(8,128)S(1)} custom-call(s32[8]{0:T(128)S(1)} %copy-done.1, f32[40,256]{1,0:T(8,128)S(1)} %get-tuple-element.28.refs_1_, bf16[2,264,1024]{2,1,0:T(8,128)(2,1)S(1)} %copy-done, bf16[2,264,1024]{2,1,0:T(8,128)(2,1)S(1)} %collective-permute-done.refs_3_, f32[4,256,128]{2,1,0:T(8,128)S(1)} %get-tuple-element.29.refs_4_, ...), custom_call_target="tpu_custom_call" | custom-call | flops 512 | bytes 1024 | tf_op jit(solution)/shard_map/first/pallas_call | solution.py:214
  25.7 5.9 %collective-permute-done.6.refs_7_.refs_5_.refs_2_ = bf16[2,264,1024]{2,1,0:T(8,128)(2,1)S(1)} collective-permute-done((bf16[2,264,1024]{2,1,0:T(8,128)(2,1)}, bf16[2,264,1024]{2,1,0:T(8,128)(2,1)S(1)}, u32[]{:S(2)}, u32[]{:S(2)}) %collective-permute-start.6) | collective-permute-done | bytes 1081376 | tf_op jit(solution)/shard_map/b03/ppermute | solution.py:54
  31.7 1.6 %collective-permute-start.8 = (bf16[264,1024]{1,0:T(8,128)(2,1)S(1)}, bf16[264,1024]{1,0:T(8,128)(2,1)S(1)}, u32[]{:S(2)}, u32[]{:S(2)}) collective-permute-start(bf16[264,1024]{1,0:T(8,128)(2,1)S(1)} %slice_bitcast_fusion.1), channel_id=1, source_target_pairs={{0,2},{1,3},{2,0},{3,1},{4,6},{5,7},{6,4},{7,5},{8,10},{9,11},{10,... | collective-permute-start | bytes 1622024 | tf_op jit(solution)/shard_map/b13a/ppermute | solution.py:54
  33.3 1.9 %collective-permute-start.3 = (bf16[264,1024]{1,0:T(8,128)(2,1)S(1)}, bf16[264,1024]{1,0:T(8,128)(2,1)S(1)}, u32[]{:S(2)}, u32[]{:S(2)}) collective-permute-start(bf16[264,1024]{1,0:T(8,128)(2,1)S(1)} %collective-permute-done.1.refs_6_.b01b.refs_4_), channel_id=1, source_target_pairs={{0,16},{1,17},{2,18},{3,19},{4,20},{5,21},{6,22},{7,23},{8,24},{9,... | collective-permute-start | bytes 1622024 | tf_op jit(solution)/shard_map/prvb/ppermute | solution.py:54
  35.2 1.6 %collective-permute-start.9 = (bf16[264,1024]{1,0:T(8,128)(2,1)S(1)}, bf16[264,1024]{1,0:T(8,128)(2,1)S(1)}, u32[]{:S(2)}, u32[]{:S(2)}) collective-permute-start(bf16[264,1024]{1,0:T(8,128)(2,1)S(1)} %slice_bitcast_fusion), channel_id=1, source_target_pairs={{0,4},{1,5},{2,6},{3,7},{4,8},{5,9},{6,10},{7,11},{8,12},{9,13},{1... | collective-permute-start | bytes 1622024 | tf_op jit(solution)/shard_map/b13b/ppermute | solution.py:54
  36.9 2.6 %collective-permute-done.4.refs_9_.refs_8_.nxt = bf16[2,264,1024]{2,1,0:T(8,128)(2,1)S(1)} collective-permute-done((bf16[2,264,1024]{2,1,0:T(8,128)(2,1)}, bf16[2,264,1024]{2,1,0:T(8,128)(2,1)S(1)}, u32[]{:S(2)}, u32[]{:S(2)}) %collective-permute-start.4) | collective-permute-done | bytes 1081376 | tf_op jit(solution)/shard_map/nxt/ppermute | solution.py:54
  39.8 5.4 %same.1 = (f32[40,256]{1,0:T(8,128)S(1)}, f32[2,256,128]{2,1,0:T(8,128)S(1)}) custom-call(s32[8]{0:T(128)S(1)} %copy-done.1, f32[40,256]{1,0:T(8,128)S(1)} %first.1.refs_1_, bf16[2,264,1024]{2,1,0:T(8,128)(2,1)S(1)} %copy-done, bf16[2,264,1024]{2,1,0:T(8,128)(2,1)S(1)} %collective-permute-done.refs_3_, f32[4,256,128]{2,1,0:T(8,128)S(1)} %get-tuple-element.29.refs_4_, ...), custom_call_target="tpu_custom_call" | custom-call | flops 4608 | bytes 1024 | tf_op jit(solution)/shard_map/same/pallas_call | solution.py:214
  45.2 5.5 %collective-permute-done.3.refs_6_ = bf16[264,1024]{1,0:T(8,128)(2,1)S(1)} collective-permute-done((bf16[264,1024]{1,0:T(8,128)(2,1)S(1)}, bf16[264,1024]{1,0:T(8,128)(2,1)S(1)}, u32[]{:S(2)}, u32[]{:S(2)}) %collective-permute-start.3) | collective-permute-done | bytes 540704 | tf_op jit(solution)/shard_map/prvb/ppermute | solution.py:54
  50.7 3.2 %last.1.refs_1_ = f32[40,256]{1,0:T(8,128)S(1)} custom-call(s32[8]{0:T(128)S(1)} %copy-done.1, f32[40,256]{1,0:T(8,128)S(1)} %get-tuple-element.41.refs_1_, bf16[2,264,1024]{2,1,0:T(8,128)(2,1)S(1)} %copy-done, bf16[2,264,1024]{2,1,0:T(8,128)(2,1)S(1)} %collective-permute-done.refs_3_, f32[4,256,128]{2,1,0:T(8,128)S(1)} %get-tuple-element.29.refs_4_, ...), custom_call_target="tpu_custom_call" | custom-call | flops 102400000000 | bytes 1024 | tf_op jit(solution)/shard_map/last/pallas_call | solution.py:214
  54.0 6.0 %cross.1.refs_1_ = f32[40,256]{1,0:T(8,128)S(1)} custom-call(s32[8]{0:T(128)S(1)} %copy-done.1, f32[40,256]{1,0:T(8,128)S(1)} %last.1.refs_1_, bf16[2,264,1024]{2,1,0:T(8,128)(2,1)S(1)} %copy-done, bf16[264,1024]{1,0:T(8,128)(2,1)S(1)} %collective-permute-done.2.refs_5_.b01a.refs_3_, bf16[264,1024]{1,0:T(8,128)(2,1)S(1)} %collective-permute-done.1.refs_6_.b01b.refs_4_, ...), custom_call_target="tpu_custom_call" | custom-call | flops 4096 | bytes 1024 | tf_op jit(solution)/shard_map/cross/pallas_call | solution.py:214
  60.9 1.6 %end.1.rows_ref = f32[40,256]{1,0:T(8,128)S(1)} custom-call(s32[8]{0:T(128)S(1)} %copy-done.1, f32[40,256]{1,0:T(8,128)S(1)} %cross.1.refs_1_, bf16[2,264,1024]{2,1,0:T(8,128)(2,1)S(1)} %collective-permute-done.6.refs_7_.refs_5_.refs_2_, bf16[2,264,1024]{2,1,0:T(8,128)(2,1)S(1)} %collective-permute-done.7.refs_8_.refs_6_.refs_3_, ...), custom_call_target="tpu_custom_call" | custom-call | flops 1024 | bytes 1024 | tf_op jit(solution)/shard_map/end/pallas_call | solution.py:214
  63.7 2.6 %collective-permute-start.16 = (f32[8,256]{1,0:T(8,128)S(1)}, f32[8,256]{1,0:T(8,128)S(1)}, u32[]{:S(2)}, u32[]{:S(2)}) collective-permute-start(f32[8,256]{1,0:T(8,128)S(1)} %get-tuple-element.47), channel_id=1, source_target_pairs={{0,118},{1,119},{2,116},{3,117},{4,122},{5,123},{6,120},{7,121},{8... | collective-permute-start | bytes 24584 | tf_op jit(solution)/shard_map/back_prv/ppermute | solution.py:54
  66.3 1.3 %collective-permute-start.15 = (f32[6,256]{1,0:T(8,128)S(1)}, f32[6,256]{1,0:T(8,128)S(1)}, u32[]{:S(2)}, u32[]{:S(2)}) collective-permute-start(f32[6,256]{1,0:T(8,128)S(1)} %get-tuple-element.46), channel_id=1, source_target_pairs={{0,4},{1,5},{2,6},{3,7},{4,8},{5,9},{6,10},{7,11},{8,12},{9,13},{1... | collective-permute-start | bytes 18440 | tf_op jit(solution)/shard_map/back_01/ppermute | solution.py:54
  67.6 1.9 %collective-permute-start.14 = (f32[4,256]{1,0:T(4,128)S(1)}, f32[4,256]{1,0:T(4,128)S(1)}, u32[]{:S(2)}, u32[]{:S(2)}) collective-permute-start(f32[4,256]{1,0:T(4,128)S(1)} %get-tuple-element.45), channel_id=1, source_target_pairs={{0,12},{1,13},{2,14},{3,15},{4,0},{5,1},{6,2},{7,3},{8,4},{9,5},{1... | collective-permute-start | bytes 12296 | tf_op jit(solution)/shard_map/back_03/ppermute | solution.py:54
  69.5 1.7 %collective-permute-done.14.b03 = f32[4,256]{1,0:T(4,128)S(1)} collective-permute-done((f32[4,256]{1,0:T(4,128)S(1)}, f32[4,256]{1,0:T(4,128)S(1)}, u32[]{:S(2)}, u32[]{:S(2)}) %collective-permute-start.14) | collective-permute-done | bytes 4128 | tf_op jit(solution)/shard_map/back_03/ppermute | solution.py:54
  (29 shorter events, 4.5 us)
Async XLA Ops:
  0.6 15.4 %copy-start.1 = (s32[8]{0:T(128)S(1)}, s32[8]{0:T(128)}, u32[]{:S(2)}) copy-start(s32[8]{0:T(128)} %refs_0_.11) | copy-start | bytes 100
  3.7 5.0 %collective-permute-start = (bf16[2,264,1024]{2,1,0:T(8,128)(2,1)}, bf16[2,264,1024]{2,1,0:T(8,128)(2,1)S(1)}, u32[]{:S(2)}, u32[]{:S(2)}) collective-permute-start(bf16[2,264,1024]{2,1,0:T(8,128)(2,1)} %get-tuple-element.26.refs_2_), channel_id=1, source_target_pairs={{0,1},{1,0},{2,3},{3,2},{4,5},{5,4},{6,7},{7,6},{8,9},{9,8},{10,11... | collective-permute-start | bytes 3244040 | tf_op jit(solution)/shard_map/ownx/ppermute | solution.py:54
  3.8 27.8 %collective-permute-start.6 = (bf16[2,264,1024]{2,1,0:T(8,128)(2,1)}, bf16[2,264,1024]{2,1,0:T(8,128)(2,1)S(1)}, u32[]{:S(2)}, u32[]{:S(2)}) collective-permute-start(bf16[2,264,1024]{2,1,0:T(8,128)(2,1)} %get-tuple-element.26.refs_2_), channel_id=1, source_target_pairs={{0,4},{1,5},{2,6},{3,7},{4,8},{5,9},{6,10},{7,11},{8,12},{9,13},{1... | collective-permute-start | bytes 3244040 | tf_op jit(solution)/shard_map/b03/ppermute | solution.py:54
  5.5 26.1 %collective-permute-start.7 = (bf16[2,264,1024]{2,1,0:T(8,128)(2,1)}, bf16[2,264,1024]{2,1,0:T(8,128)(2,1)S(1)}, u32[]{:S(2)}, u32[]{:S(2)}) collective-permute-start(bf16[2,264,1024]{2,1,0:T(8,128)(2,1)} %get-tuple-element.26.refs_2_), channel_id=1, source_target_pairs={{0,2},{1,3},{2,0},{3,1},{4,6},{5,7},{6,4},{7,5},{8,10},{9,11},{10,... | collective-permute-start | bytes 3244040 | tf_op jit(solution)/shard_map/b10/ppermute | solution.py:54
  7.0 15.4 %collective-permute-start.2 = (bf16[264,1024]{1,0:T(8,128)(2,1)}, bf16[264,1024]{1,0:T(8,128)(2,1)S(1)}, u32[]{:S(2)}, u32[]{:S(2)}) collective-permute-start(bf16[264,1024]{1,0:T(8,128)(2,1)} %get-tuple-element.30), channel_id=1, source_target_pairs={{0,12},{1,13},{2,14},{3,15},{4,0},{5,1},{6,2},{7,3},{8,4},{9,5},{1... | collective-permute-start | bytes 1622024 | tf_op jit(solution)/shard_map/b01a/ppermute | solution.py:54
  8.7 24.6 %collective-permute-start.1 = (bf16[264,1024]{1,0:T(8,128)(2,1)}, bf16[264,1024]{1,0:T(8,128)(2,1)S(1)}, u32[]{:S(2)}, u32[]{:S(2)}) collective-permute-start(bf16[264,1024]{1,0:T(8,128)(2,1)} %get-tuple-element.27), channel_id=1, source_target_pairs={{0,12},{1,13},{2,14},{3,15},{4,0},{5,1},{6,2},{7,3},{8,4},{9,5},{1... | collective-permute-start | bytes 1622024 | tf_op jit(solution)/shard_map/b01b/ppermute | solution.py:54
  10.5 29.0 %collective-permute-start.4 = (bf16[2,264,1024]{2,1,0:T(8,128)(2,1)}, bf16[2,264,1024]{2,1,0:T(8,128)(2,1)S(1)}, u32[]{:S(2)}, u32[]{:S(2)}) collective-permute-start(bf16[2,264,1024]{2,1,0:T(8,128)(2,1)} %get-tuple-element.26.refs_2_), channel_id=1, source_target_pairs={{0,114},{1,115},{2,112},{3,113},{4,118},{5,119},{6,116},{7,117},{8... | collective-permute-start | bytes 3244040 | tf_op jit(solution)/shard_map/nxt/ppermute | solution.py:54
  16.1 1.3 %copy-start = (bf16[2,264,1024]{2,1,0:T(8,128)(2,1)S(1)}, bf16[2,264,1024]{2,1,0:T(8,128)(2,1)}, u32[]{:S(2)}) copy-start(bf16[2,264,1024]{2,1,0:T(8,128)(2,1)} %get-tuple-element.26.refs_2_) | copy-start | bytes 3244036
  22.4 17.1 %collective-permute-start.5 = (bf16[264,1024]{1,0:T(8,128)(2,1)S(1)}, bf16[264,1024]{1,0:T(8,128)(2,1)S(1)}, u32[]{:S(2)}, u32[]{:S(2)}) collective-permute-start(bf16[264,1024]{1,0:T(8,128)(2,1)S(1)} %collective-permute-done.2.refs_5_.b01a.refs_3_), channel_id=1, source_target_pairs={{0,16},{1,17},{2,18},{3,19},{4,20},{5,21},{6,22},{7,23},{8,24},{9,... | collective-permute-start | bytes 1622024 | tf_op jit(solution)/shard_map/prva/ppermute | solution.py:54
  31.7 19.0 %collective-permute-start.8 = (bf16[264,1024]{1,0:T(8,128)(2,1)S(1)}, bf16[264,1024]{1,0:T(8,128)(2,1)S(1)}, u32[]{:S(2)}, u32[]{:S(2)}) collective-permute-start(bf16[264,1024]{1,0:T(8,128)(2,1)S(1)} %slice_bitcast_fusion.1), channel_id=1, source_target_pairs={{0,2},{1,3},{2,0},{3,1},{4,6},{5,7},{6,4},{7,5},{8,10},{9,11},{10,... | collective-permute-start | bytes 1622024 | tf_op jit(solution)/shard_map/b13a/ppermute | solution.py:54
  33.3 17.4 %collective-permute-start.3 = (bf16[264,1024]{1,0:T(8,128)(2,1)S(1)}, bf16[264,1024]{1,0:T(8,128)(2,1)S(1)}, u32[]{:S(2)}, u32[]{:S(2)}) collective-permute-start(bf16[264,1024]{1,0:T(8,128)(2,1)S(1)} %collective-permute-done.1.refs_6_.b01b.refs_4_), channel_id=1, source_target_pairs={{0,16},{1,17},{2,18},{3,19},{4,20},{5,21},{6,22},{7,23},{8,24},{9,... | collective-permute-start | bytes 1622024 | tf_op jit(solution)/shard_map/prvb/ppermute | solution.py:54
  35.2 15.5 %collective-permute-start.9 = (bf16[264,1024]{1,0:T(8,128)(2,1)S(1)}, bf16[264,1024]{1,0:T(8,128)(2,1)S(1)}, u32[]{:S(2)}, u32[]{:S(2)}) collective-permute-start(bf16[264,1024]{1,0:T(8,128)(2,1)S(1)} %slice_bitcast_fusion), channel_id=1, source_target_pairs={{0,4},{1,5},{2,6},{3,7},{4,8},{5,9},{6,10},{7,11},{8,12},{9,13},{1... | collective-permute-start | bytes 1622024 | tf_op jit(solution)/shard_map/b13b/ppermute | solution.py:54
  39.7 14.3 %collective-permute-start.10 = (bf16[5,264,1024]{2,1,0:T(8,128)(2,1)S(1)}, bf16[5,264,1024]{2,1,0:T(8,128)(2,1)S(1)}, u32[]{:S(2)}, u32[]{:S(2)}) collective-permute-start(bf16[5,264,1024]{2,1,0:T(8,128)(2,1)S(1)} %bundle.1), channel_id=1, source_target_pairs={{0,1},{1,0},{2,3},{3,2},{4,5},{5,4},{6,7},{7,6},{8,9},{9,8},{10,11... | collective-permute-start | bytes 8110088 | tf_op jit(solution)/shard_map/cross/ppermute | solution.py:54
  50.7 3.2 %collective-permute-start.11 = (bf16[264,1024]{1,0:T(8,128)(2,1)S(1)}, bf16[264,1024]{1,0:T(8,128)(2,1)S(1)}, u32[]{:S(2)}, u32[]{:S(2)}) collective-permute-start(bf16[264,1024]{1,0:T(8,128)(2,1)S(1)} %collective-permute-done.3.refs_6_), channel_id=1, source_target_pairs={{0,1},{1,0},{2,3},{3,2},{4,5},{5,4},{6,7},{7,6},{8,9},{9,8},{10,11... | collective-permute-start | bytes 1622024 | tf_op jit(solution)/shard_map/prvbx/ppermute | solution.py:54
  60.0 3.7 %collective-permute-start.13 = (f32[8,256]{1,0:T(8,128)S(1)}, f32[8,256]{1,0:T(8,128)S(1)}, u32[]{:S(2)}, u32[]{:S(2)}) collective-permute-start(f32[8,256]{1,0:T(8,128)S(1)} %slice.17), channel_id=1, source_target_pairs={{0,2},{1,3},{2,0},{3,1},{4,6},{5,7},{6,4},{7,5},{8,10},{9,11},{10,... | collective-permute-start | bytes 24584 | tf_op jit(solution)/shard_map/side/ppermute | solution.py:54
  60.7 1.8 %collective-permute-start.12 = (f32[6,256]{1,0:T(8,128)S(1)}, f32[6,256]{1,0:T(8,128)S(1)}, u32[]{:S(2)}, u32[]{:S(2)}) collective-permute-start(f32[6,256]{1,0:T(8,128)S(1)} %slice.16), channel_id=1, source_target_pairs={{0,1},{1,0},{2,3},{3,2},{4,5},{5,4},{6,7},{7,6},{8,9},{9,8},{10,11... | collective-permute-start | bytes 18440 | tf_op jit(solution)/shard_map/swapped/ppermute | solution.py:54
  63.7 7.5 %collective-permute-start.16 = (f32[8,256]{1,0:T(8,128)S(1)}, f32[8,256]{1,0:T(8,128)S(1)}, u32[]{:S(2)}, u32[]{:S(2)}) collective-permute-start(f32[8,256]{1,0:T(8,128)S(1)} %get-tuple-element.47), channel_id=1, source_target_pairs={{0,118},{1,119},{2,116},{3,117},{4,122},{5,123},{6,120},{7,121},{8... | collective-permute-start | bytes 24584 | tf_op jit(solution)/shard_map/back_prv/ppermute | solution.py:54
  66.3 4.9 %collective-permute-start.15 = (f32[6,256]{1,0:T(8,128)S(1)}, f32[6,256]{1,0:T(8,128)S(1)}, u32[]{:S(2)}, u32[]{:S(2)}) collective-permute-start(f32[6,256]{1,0:T(8,128)S(1)} %get-tuple-element.46), channel_id=1, source_target_pairs={{0,4},{1,5},{2,6},{3,7},{4,8},{5,9},{6,10},{7,11},{8,12},{9,13},{1... | collective-permute-start | bytes 18440 | tf_op jit(solution)/shard_map/back_01/ppermute | solution.py:54
  67.6 3.6 %collective-permute-start.14 = (f32[4,256]{1,0:T(4,128)S(1)}, f32[4,256]{1,0:T(4,128)S(1)}, u32[]{:S(2)}, u32[]{:S(2)}) collective-permute-start(f32[4,256]{1,0:T(4,128)S(1)} %get-tuple-element.45), channel_id=1, source_target_pairs={{0,12},{1,13},{2,14},{3,15},{4,0},{5,1},{6,2},{7,3},{8,4},{9,5},{1... | collective-permute-start | bytes 12296 | tf_op jit(solution)/shard_map/back_03/ppermute | solution.py:54

commit v5 on v4

--- a/solution.py
+++ b/solution.py
@@ -176,17 +176,19 @@
                     other = jnp.where(earlier, LOW, piece)
                     side = other if side is None else jnp.maximum(side, other)
             best[i] = jnp.maximum(best[i], jnp.concatenate(parts, axis=1))
-        sides.append(side)
+        if side is not None:
+            sides.append((k_at[n], side))
     keep(row_ref, q_at, best)
-    if k_at is not None:
-        keep(row_ref, k_at, [jnp.transpose(side) for side in sides])
+    for at, side in sides:
+        keep(row_ref, [at], [jnp.transpose(side)])
 
 
 def real_job(row_ref, limits, keys, queries, q_at):
     best = lowest(queries)
+    position = lax.broadcasted_iota(jnp.int32, (HALF, 128), 0).astype(jnp.float32)
     for n, key_ref in enumerate(keys):
         key = key_ref[:HALF, :]
-        real = lax.broadcasted_iota(jnp.int32, (HALF, 128), 0) < limits[n]
+        real = position < row_ref[limits[n] : limits[n] + 1, :128]
         for i, query in enumerate(queries):
             parts = [tops(jnp.where(real, piece, LOW)) for piece in pieces(inner(key, query[:HALF, :]))]
             best[i] = jnp.maximum(best[i], jnp.concatenate(parts, axis=1))
@@ -202,31 +204,31 @@
     return jax.ShapeDtypeStruct((halves, HALF, 128), jnp.float32)
 
 
-def kernel_call(name, body, tasks, rows, sizes, arrays, extra_out=()):
-    n = len(arrays)
-
-    def kernel(*refs):
-        sizes_ref, rows_in, ins = refs[0], refs[1], refs[2 : 2 + n]
-        row_ref, extra = refs[2 + n], refs[3 + n :]
+def kernel_call(name, body, tasks, rows, arrays, extra_out=(), scalars=()):
+    n = len(arrays) + len(scalars)
+
+    def kernel(rows_in, *refs):
+        row_ref = refs[n]
         row_ref[...] = rows_in[...]
-        body(row_ref, sizes_ref, *ins, *extra)
+        body(row_ref, *refs[:n], *refs[n + 1 :])
 
     out = pl.pallas_call(
         kernel,
-        in_specs=[SMEM, VMEM] + [VMEM] * n,
+        in_specs=[VMEM] * (1 + len(arrays)) + [SMEM] * len(scalars),
         out_specs=[VMEM] * (1 + len(extra_out)),
         out_shape=[jax.ShapeDtypeStruct((N_ROWS, HALF), jnp.float32), *extra_out],
         name=name,
         compiler_params=pltpu.CompilerParams(vmem_limit_bytes=14 * 2**20),
         cost_estimate=pl.CostEstimate(flops=int(tasks * 1024), bytes_accessed=1024, transcendentals=0),
-    )(sizes, rows, *arrays)
+    )(rows, *arrays, *scalars)
     return out if extra_out else out[0]
 
 
 W00, A00, KOWN, W03, A03, W10, A10 = 0, 2, 4, 6, 8, 10, 12
 W13, A13, W01, A01, K01, PRV, KOWNX, K01X, PRVX = 14, 16, 18, 20, 22, 24, 26, 28, 30
 REAL, FLOOR = 32, 34
-N_ROWS = 40
+L_NXT, L_NXTX, L_03, L_10, L_13 = 40, 42, 44, 46, 48
+N_ROWS = 56
 
 
 def both(at):
@@ -242,7 +244,7 @@
     return [start, start - HALF]
 
 
-def self_kernel(row_ref, sizes_ref, own, ownx, ranks):
+def self_kernel(row_ref, own, ownx, sizes_ref, ranks):
     keys = split(own) + split(ownx)
     put_ranks(ranks, keys)
     row_ref[...] = jnp.full(row_ref.shape, LOW, jnp.float32)
@@ -252,6 +254,11 @@
         row_ref[REAL + h : REAL + h + 1, :] = jnp.where(position < left, 1.0, 0.0)
     floor = jnp.where(own_count(sizes_ref, 1) < 2 * HALF * lax.axis_size("helper"), -1.0, LOW)
     row_ref[FLOOR : FLOOR + 1, :] = jnp.full((1, HALF), floor, jnp.float32)
+    limits = [(L_NXT, real_rows(sizes_ref, 0, 0, 0, 1)), (L_NXTX, real_rows(sizes_ref, 0, 0, 1, 1))]
+    limits += [(L_03, real_rows(sizes_ref, 0, -1)), (L_10, real_rows(sizes_ref, 1, 0)), (L_13, real_rows(sizes_ref, 1, -1))]
+    for at, counts in limits:
+        for h, count in enumerate(counts):
+            row_ref[at + h : at + h + 1, :] = jnp.full((1, HALF), count, jnp.int32).astype(jnp.float32)
     pair_job(row_ref, [ranks.at[n] for n in range(4)], keys, split(own), both(W00), None)
 
 
@@ -260,7 +267,7 @@
     pair_job(row_ref, [ranks.at[n] for n in range(4)], keys, queries, places, both(KOWN) + both(KOWNX), wanted)
 
 
-def first_kernel(row_ref, sizes_ref, own, ownx, ranks, b01a):
+def first_kernel(row_ref, own, ownx, ranks, b01a):
     own_job(row_ref, own, ownx, ranks, [b01a], [W01])
 
 
@@ -269,48 +276,47 @@
         bundle[n] = half[...]
 
 
-def same_kernel(row_ref, sizes_ref, own, ownx, own_ranks, b01a, b01b, b03, b10, nxt, prva, ranks):
+def same_kernel(row_ref, own, ownx, own_ranks, b01a, b01b, b03, b10, nxt, prva, ranks):
     places = [W01 + 1, W10, W10 + 1]
     own_job(row_ref, own, ownx, own_ranks, [b01b, *split(b10)], places, lambda k, q: q == 0 or (k, q - 1) in SHARE)
     queries = [*split(own), b01a, b01b, *split(b03), *split(b10)]
     places = both(A00) + both(A01) + both(A03) + both(A10)
-    real_job(row_ref, real_rows(sizes_ref, 0, 0, 0, 1), split(nxt), queries, places)
+    real_job(row_ref, both(L_NXT), split(nxt), queries, places)
     put_ranks(ranks, [b01a, b01b])
     pair_job(
         row_ref, [ranks.at[0], ranks.at[1]], [b01a, b01b], split(b03), both(W03), both(K01),
         lambda k, q: (k, q) in SHARE,
     )
-    limits = real_rows(sizes_ref, 0, -1) + real_rows(sizes_ref, 1, 0)
+    limits = both(L_03) + both(L_10)
     real_job(row_ref, limits, split(b03) + split(b10), [prva], [PRV])
 
 
-def last_kernel(row_ref, sizes_ref, own, ownx, ranks, b01a, b01b, ranks1, nxt, prva, b13a, b13b):
+def half_kernel(h, row_ref, own, ownx, ranks, b01a, b01b, ranks1, nxt, prva, b13):
+    own_job(row_ref, own, ownx, ranks, [b13], [W13 + h])
+    pair_job(
+        row_ref, [ranks1.at[0], ranks1.at[1]], [b01a, b01b], [b13], [W13 + h], both(K01), lambda k, q: (k, h) in SHARE
+    )
+    real_job(row_ref, both(L_NXT), split(nxt), [b13], [A13 + h])
+    real_job(row_ref, [L_13 + h], [b13], [prva], [PRV])
+
+
+def cross_kernel(row_ref, b03, b10, b13a, b13b, cross, prvbx):
     b13 = [b13a, b13b]
-    own_job(row_ref, own, ownx, ranks, b13, both(W13))
-    pair_job(
-        row_ref, [ranks1.at[0], ranks1.at[1]], [b01a, b01b], b13, both(W13), both(K01), lambda k, q: (k, q) in SHARE
-    )
-    real_job(row_ref, real_rows(sizes_ref, 0, 0, 0, 1), split(nxt), b13, both(A13))
-    real_job(row_ref, real_rows(sizes_ref, 1, -1), b13, [prva], [PRV])
-
-
-def cross_kernel(row_ref, sizes_ref, own, b01a, b01b, b03, b10, b13a, b13b, cross, prvbx):
-    b13 = [b13a, b13b]
-    queries = [*split(own), b01a, b01b, *split(b03), *split(b10), *b13]
-    places = both(A00) + both(A01) + both(A03) + both(A10) + both(A13)
-    real_job(row_ref, real_rows(sizes_ref, 0, 0, 1, 1), [cross.at[0], cross.at[1]], queries, places)
+    real_job(row_ref, both(L_NXTX), [cross.at[0], cross.at[1]], split(b10) + b13, both(A10) + both(A13))
     one = [cross.at[2], cross.at[3]]
     ranks = [rank_column(half[HALF:, : 2 * HALF]) for half in one]
-    queries = split(b03) + b13
     pair_job(
-        row_ref, ranks, one, queries, both(W03) + both(W13), both(K01X), lambda k, q: (2 + k, q % 2) in SHARE
-    )
-    limits = real_rows(sizes_ref, 0, -1) + real_rows(sizes_ref, 1, 0) + real_rows(sizes_ref, 1, -1)
+        row_ref, ranks, one, split(b03) + b13, both(W03) + both(W13), both(K01X),
+        lambda k, q: (2 + k, q % 2) in SHARE,
+    )
+    limits = both(L_03) + both(L_10) + both(L_13)
     real_job(row_ref, limits, split(b03) + split(b10) + b13, [cross.at[4], prvbx], both(PRVX))
 
 
-def end_kernel(row_ref, sizes_ref, b03, b10, b13a, b13b, prvb):
-    limits = real_rows(sizes_ref, 1, -1) + real_rows(sizes_ref, 0, -1) + real_rows(sizes_ref, 1, 0)
+def end_kernel(row_ref, own, b01a, b01b, b03, b10, b13a, b13b, cross, prvb):
+    queries = [*split(own), b01a, b01b, *split(b03)]
+    real_job(row_ref, both(L_NXTX), [cross.at[0], cross.at[1]], queries, both(A00) + both(A01) + both(A03))
+    limits = both(L_13) + both(L_03) + both(L_10)
     real_job(row_ref, limits, [b13a, b13b, *split(b03), *split(b10)], [prvb], [PRV + 1])
 
 
@@ -361,9 +367,9 @@
     ownx = send("ownx", own, core=1)
     b01b = send("b01b", after(own_b, ownx), row=-1)
     empty = jnp.zeros((N_ROWS, HALF), jnp.float32)
-    state, own_ranks = kernel_call("self", self_kernel, 1, empty, sizes, [own, ownx], [rank_shape(4)])
+    state, own_ranks = kernel_call("self", self_kernel, 1, empty, [own, ownx], [rank_shape(4)], [sizes])
     prva = send("prva", after(b01a, state), cluster=1)
-    state = kernel_call("first", first_kernel, 0.5, state, sizes, [own, ownx, own_ranks, b01a])
+    state = kernel_call("first", first_kernel, 0.5, state, [own, ownx, own_ranks, b01a])
 
     prvb = send("prvb", after(b01b, state), cluster=1)
     b03, b10, state = lax.optimization_barrier((b03, b10, state))
@@ -380,22 +386,21 @@
     )(b01a, b01b, nxt, prva)
     cross = send("cross", bundle, core=1)
     state, ranks1 = kernel_call(
-        "same", same_kernel, 4.5, state, sizes,
+        "same", same_kernel, 4.5, state,
         [own, ownx, own_ranks, b01a, b01b, b03, b10, nxt, prva], [rank_shape(2)],
     )
+    kept = [own, ownx, own_ranks, b01a, b01b, ranks1, nxt, prva]
+    state = kernel_call("left", functools.partial(half_kernel, 0), 1, state, [*kept, b13a])
     prvb, state = lax.optimization_barrier((prvb, state))
-    state = kernel_call(
-        "last", last_kernel, LONG, state, sizes,
-        [own, ownx, own_ranks, b01a, b01b, ranks1, nxt, prva, b13a, b13b],
-    )
+    state = kernel_call("right", functools.partial(half_kernel, 1), LONG, state, [*kept, b13b])
     prvbx = send("prvbx", prvb, core=1)
     state = kernel_call(
-        "cross", cross_kernel, 4, state, sizes, [own, b01a, b01b, b03, b10, b13a, b13b, cross, prvbx]
+        "cross", cross_kernel, 4, state, [b03, b10, b13a, b13b, cross, prvbx]
     )
 
     swapped = send("swapped", state[KOWNX : KOWNX + 6], core=1)
     side = send("side", state[W10 : W10 + 8], col=1)
-    state = kernel_call("end", end_kernel, 1, state, sizes, [b03, b10, b13a, b13b, prvb])
+    state = kernel_call("end", end_kernel, 1, state, [own, b01a, b01b, b03, b10, b13a, b13b, cross, prvb])
     shapes = [(8, HALF), (4, HALF), (6, HALF), (8, HALF)]
     kept, to_03, to_01, to_prv = small_call("gather", gather_kernel, shapes, [state, swapped, side])
     back_prv = send("back_prv", to_prv, cluster=-1, row=1)

time: 72.1 us -> 69.7 us (0.967)
  Pallas kernels: 23.4 us -> 20.7 us
  starting transfers between devices: 26.2 us -> 27.1 us
    pallas_call x6 -> x7, Pallas kernels: 19.5 us -> 16.8 us  [kernel_call(): pl.pallas_call(kernel, in_specs=[VMEM] * (1 + len(arrays)) + [SMEM] * len...]
    ppermute x17, starting transfers between devices: 26.2 us -> 27.1 us  [send(): return lax.ppermute(value, AXES, pairs(**shift))]
  transfers between devices with their start and end apart: 17 -> 17, of which waited for: 6 -> 8; matrix products, arithmetic and copies ran while one was open for 0% -> 0% of each run, Pallas kernels for 19% -> 19%
where the time goes in v5:
time: 69.7 us; the launch traced here: 69.4 us
  starting transfers between devices  27.1 us (39%)
  Pallas kernels  20.7 us (30%)
  waiting for transfers between devices  19.5 us (28%)
  local copies, waits for them, and re-layouts  1.35 us (2%)
  between operations  0.75 us (1%)
    ppermute x17, starting transfers between devices, send(): return lax.ppermute(value, AXES, pairs(**shift))  27.1 us
    ppermute x17, waiting for transfers between devices, send(): return lax.ppermute(value, AXES, pairs(**shift))  19.5 us
    pallas_call x7, Pallas kernels, kernel_call(): pl.pallas_call(kernel, in_specs=[VMEM] * (1 + len(arrays)) + [SMEM] * len...  16.8 us
    pallas_call x1, Pallas kernels, packed(): pl.pallas_call(pack_kernel, in_specs=[pl.BlockSpec(memory_space=pltpu.HBM...  3.08 us
  transfers between devices with their start and end apart: 17, of which 8 were waited for; matrix products, arithmetic and copies ran while one was open for 0% of the time, Pallas kernels for 19%

profile of v5, /device:TPU:0, one launch (start us, length us, event | category | flops | bytes accessed | tf_op | source)
XLA Modules:
  0.0 69.4 jit_solution(2961992279695806470)
XLA Ops:
  0.6 3.1 %pack.1 = (bf16[2,264,1024]{2,1,0:T(8,128)(2,1)}, bf16[264,1024]{1,0:T(8,128)(2,1)}, bf16[264,1024]{1,0:T(8,128)(2,1)}) custom-call(s32[8]{0:T(128)} %refs_2_.1, f32[512,1024]{1,0:T(8,128)} %bitcast.5, s32[1,512]{1,0:T(1,128)} %rank_hbm.1), custom_call_target="tpu_custom_call" | custom-call | flops 2097152 | bytes 4194304 | tf_op jit(solution)/shard_map/pack/pallas_call | solution.py:111
  3.8 1.7 %collective-permute-start.6 = (bf16[2,264,1024]{2,1,0:T(8,128)(2,1)}, bf16[2,264,1024]{2,1,0:T(8,128)(2,1)S(1)}, u32[]{:S(2)}, u32[]{:S(2)}) collective-permute-start(bf16[2,264,1024]{2,1,0:T(8,128)(2,1)} %get-tuple-element.26.refs_0_), channel_id=1, source_target_pairs={{0,4},{1,5},{2,6},{3,7},{4,8},{5,9},{6,10},{7,11},{8,12},{9,13},{1... | collective-permute-start | bytes 3244040 | tf_op jit(solution)/shard_map/b03/ppermute | solution.py:54
  5.5 1.5 %collective-permute-start.7 = (bf16[2,264,1024]{2,1,0:T(8,128)(2,1)}, bf16[2,264,1024]{2,1,0:T(8,128)(2,1)S(1)}, u32[]{:S(2)}, u32[]{:S(2)}) collective-permute-start(bf16[2,264,1024]{2,1,0:T(8,128)(2,1)} %get-tuple-element.26.refs_0_), channel_id=1, source_target_pairs={{0,2},{1,3},{2,0},{3,1},{4,6},{5,7},{6,4},{7,5},{8,10},{9,11},{10,... | collective-permute-start | bytes 3244040 | tf_op jit(solution)/shard_map/b10/ppermute | solution.py:54
  7.0 1.7 %collective-permute-start.2 = (bf16[264,1024]{1,0:T(8,128)(2,1)}, bf16[264,1024]{1,0:T(8,128)(2,1)S(1)}, u32[]{:S(2)}, u32[]{:S(2)}) collective-permute-start(bf16[264,1024]{1,0:T(8,128)(2,1)} %get-tuple-element.30), channel_id=1, source_target_pairs={{0,12},{1,13},{2,14},{3,15},{4,0},{5,1},{6,2},{7,3},{8,4},{9,5},{1... | collective-permute-start | bytes 1622024 | tf_op jit(solution)/shard_map/b01a/ppermute | solution.py:54
  8.7 1.8 %collective-permute-start.1 = (bf16[264,1024]{1,0:T(8,128)(2,1)}, bf16[264,1024]{1,0:T(8,128)(2,1)S(1)}, u32[]{:S(2)}, u32[]{:S(2)}) collective-permute-start(bf16[264,1024]{1,0:T(8,128)(2,1)} %get-tuple-element.27), channel_id=1, source_target_pairs={{0,12},{1,13},{2,14},{3,15},{4,0},{5,1},{6,2},{7,3},{8,4},{9,5},{1... | collective-permute-start | bytes 1622024 | tf_op jit(solution)/shard_map/b01b/ppermute | solution.py:54
  10.5 5.6 %collective-permute-start.4 = (bf16[2,264,1024]{2,1,0:T(8,128)(2,1)}, bf16[2,264,1024]{2,1,0:T(8,128)(2,1)S(1)}, u32[]{:S(2)}, u32[]{:S(2)}) collective-permute-start(bf16[2,264,1024]{2,1,0:T(8,128)(2,1)} %get-tuple-element.26.refs_0_), channel_id=1, source_target_pairs={{0,114},{1,115},{2,112},{3,113},{4,118},{5,119},{6,116},{7,117},{8... | collective-permute-start | bytes 3244040 | tf_op jit(solution)/shard_map/nxt/ppermute | solution.py:54
  17.3 1.8 %self.1 = (f32[56,256]{1,0:T(8,128)S(1)}, f32[4,256,128]{2,1,0:T(8,128)S(1)}) custom-call(f32[56,256]{1,0:T(8,128)S(1)} %broadcast_in_dim.3.rows_in, bf16[2,264,1024]{2,1,0:T(8,128)(2,1)S(1)} %copy-done, bf16[2,264,1024]{2,1,0:T(8,128)(2,1)S(1)} %collective-permute-done.refs_1_, s32[8]{0:T(128)S(1)} %copy-done.2), custom_call_target="tpu_custom_call" | custom-call | flops 1024 | bytes 1024 | tf_op jit(solution)/shard_map/self/pallas_call | solution.py:215
  19.2 3.2 %collective-permute-done.2.refs_3_.b01a.refs_1_ = bf16[264,1024]{1,0:T(8,128)(2,1)S(1)} collective-permute-done((bf16[264,1024]{1,0:T(8,128)(2,1)}, bf16[264,1024]{1,0:T(8,128)(2,1)S(1)}, u32[]{:S(2)}, u32[]{:S(2)}) %collective-permute-start.2) | collective-permute-done | bytes 540704 | tf_op jit(solution)/shard_map/b01a/ppermute | solution.py:54
  22.4 1.9 %collective-permute-start.5 = (bf16[264,1024]{1,0:T(8,128)(2,1)S(1)}, bf16[264,1024]{1,0:T(8,128)(2,1)S(1)}, u32[]{:S(2)}, u32[]{:S(2)}) collective-permute-start(bf16[264,1024]{1,0:T(8,128)(2,1)S(1)} %collective-permute-done.2.refs_3_.b01a.refs_1_), channel_id=1, source_target_pairs={{0,16},{1,17},{2,18},{3,19},{4,20},{5,21},{6,22},{7,23},{8,24},{9,... | collective-permute-start | bytes 1622024 | tf_op jit(solution)/shard_map/prva/ppermute | solution.py:54
  25.2 6.4 %collective-permute-done.6.refs_5_.refs_0_.refs_3_ = bf16[2,264,1024]{2,1,0:T(8,128)(2,1)S(1)} collective-permute-done((bf16[2,264,1024]{2,1,0:T(8,128)(2,1)}, bf16[2,264,1024]{2,1,0:T(8,128)(2,1)S(1)}, u32[]{:S(2)}, u32[]{:S(2)}) %collective-permute-start.6) | collective-permute-done | bytes 1081376 | tf_op jit(solution)/shard_map/b03/ppermute | solution.py:54
  31.7 1.6 %collective-permute-start.8 = (bf16[264,1024]{1,0:T(8,128)(2,1)S(1)}, bf16[264,1024]{1,0:T(8,128)(2,1)S(1)}, u32[]{:S(2)}, u32[]{:S(2)}) collective-permute-start(bf16[264,1024]{1,0:T(8,128)(2,1)S(1)} %slice_bitcast_fusion.1), channel_id=1, source_target_pairs={{0,2},{1,3},{2,0},{3,1},{4,6},{5,7},{6,4},{7,5},{8,10},{9,11},{10,... | collective-permute-start | bytes 1622024 | tf_op jit(solution)/shard_map/b13a/ppermute | solution.py:54
  33.3 1.9 %collective-permute-start.3 = (bf16[264,1024]{1,0:T(8,128)(2,1)S(1)}, bf16[264,1024]{1,0:T(8,128)(2,1)S(1)}, u32[]{:S(2)}, u32[]{:S(2)}) collective-permute-start(bf16[264,1024]{1,0:T(8,128)(2,1)S(1)} %collective-permute-done.1.refs_4_.b01b.refs_2_), channel_id=1, source_target_pairs={{0,16},{1,17},{2,18},{3,19},{4,20},{5,21},{6,22},{7,23},{8,24},{9,... | collective-permute-start | bytes 1622024 | tf_op jit(solution)/shard_map/prvb/ppermute | solution.py:54
  35.3 1.6 %collective-permute-start.9 = (bf16[264,1024]{1,0:T(8,128)(2,1)S(1)}, bf16[264,1024]{1,0:T(8,128)(2,1)S(1)}, u32[]{:S(2)}, u32[]{:S(2)}) collective-permute-start(bf16[264,1024]{1,0:T(8,128)(2,1)S(1)} %slice_bitcast_fusion), channel_id=1, source_target_pairs={{0,4},{1,5},{2,6},{3,7},{4,8},{5,9},{6,10},{7,11},{8,12},{9,13},{1... | collective-permute-start | bytes 1622024 | tf_op jit(solution)/shard_map/b13b/ppermute | solution.py:54
  36.9 2.6 %collective-permute-done.4.refs_7_.refs_6_.nxt = bf16[2,264,1024]{2,1,0:T(8,128)(2,1)S(1)} collective-permute-done((bf16[2,264,1024]{2,1,0:T(8,128)(2,1)}, bf16[2,264,1024]{2,1,0:T(8,128)(2,1)S(1)}, u32[]{:S(2)}, u32[]{:S(2)}) %collective-permute-start.4) | collective-permute-done | bytes 1081376 | tf_op jit(solution)/shard_map/nxt/ppermute | solution.py:54
  39.8 4.8 %same.1 = (f32[56,256]{1,0:T(8,128)S(1)}, f32[2,256,128]{2,1,0:T(8,128)S(1)}) custom-call(f32[56,256]{1,0:T(8,128)S(1)} %first.1.rows_in, bf16[2,264,1024]{2,1,0:T(8,128)(2,1)S(1)} %copy-done.1, bf16[2,264,1024]{2,1,0:T(8,128)(2,1)S(1)} %collective-permute-done.refs_1_, f32[4,256,128]{2,1,0:T(8,128)S(1)} %get-tuple-element.29.refs_2_, ...), custom_call_target="tpu_custom_call" | custom-call | flops 4608 | bytes 1024 | tf_op jit(solution)/shard_map/same/pallas_call | solution.py:215
  45.8 1.5 %left.1.rows_in = f32[56,256]{1,0:T(8,128)S(1)} custom-call(f32[56,256]{1,0:T(8,128)S(1)} %get-tuple-element.40.rows_in, bf16[2,264,1024]{2,1,0:T(8,128)(2,1)S(1)} %copy-done.1, bf16[2,264,1024]{2,1,0:T(8,128)(2,1)S(1)} %collective-permute-done.refs_1_, f32[4,256,128]{2,1,0:T(8,128)S(1)} %get-tuple-element.29.refs_2_, ...), custom_call_target="tpu_custom_call" | custom-call | flops 1024 | bytes 1024 | tf_op jit(solution)/shard_map/left/pallas_call | solution.py:215
  47.3 3.4 %collective-permute-done.3.refs_8_ = bf16[264,1024]{1,0:T(8,128)(2,1)S(1)} collective-permute-done((bf16[264,1024]{1,0:T(8,128)(2,1)S(1)}, bf16[264,1024]{1,0:T(8,128)(2,1)S(1)}, u32[]{:S(2)}, u32[]{:S(2)}) %collective-permute-start.3) | collective-permute-done | bytes 540704 | tf_op jit(solution)/shard_map/prvb/ppermute | solution.py:54
  50.7 1.3 %right.1.rows_in = f32[56,256]{1,0:T(8,128)S(1)} custom-call(f32[56,256]{1,0:T(8,128)S(1)} %left.1.rows_in, bf16[2,264,1024]{2,1,0:T(8,128)(2,1)S(1)} %copy-done.1, bf16[2,264,1024]{2,1,0:T(8,128)(2,1)S(1)} %collective-permute-done.refs_1_, f32[4,256,128]{2,1,0:T(8,128)S(1)} %get-tuple-element.29.refs_2_, ...), custom_call_target="tpu_custom_call" | custom-call | flops 102400000000 | bytes 1024 | tf_op jit(solution)/shard_map/right/pallas_call | solution.py:215
  52.6 3.8 %cross.1.rows_in = f32[56,256]{1,0:T(8,128)S(1)} custom-call(f32[56,256]{1,0:T(8,128)S(1)} %right.1.rows_in, bf16[2,264,1024]{2,1,0:T(8,128)(2,1)S(1)} %collective-permute-done.6.refs_5_.refs_0_.refs_3_, bf16[2,264,1024]{2,1,0:T(8,128)(2,1)S(1)} %collective-permute-done.7.refs_6_.refs_1_.refs_4_, ...), custom_call_target="tpu_custom_call" | custom-call | flops 4096 | bytes 1024 | tf_op jit(solution)/shard_map/cross/pallas_call | solution.py:215
  57.1 2.7 %end.1.rows_ref = f32[56,256]{1,0:T(8,128)S(1)} custom-call(f32[56,256]{1,0:T(8,128)S(1)} %cross.1.rows_in, bf16[2,264,1024]{2,1,0:T(8,128)(2,1)S(1)} %copy-done.1, bf16[264,1024]{1,0:T(8,128)(2,1)S(1)} %collective-permute-done.2.refs_3_.b01a.refs_1_, bf16[264,1024]{1,0:T(8,128)(2,1)S(1)} %collective-permute-done.1.refs_4_.b01b.refs_2_, ...), custom_call_target="tpu_custom_call" | custom-call | flops 1024 | bytes 1024 | tf_op jit(solution)/shard_map/end/pallas_call | solution.py:215
  60.2 3.7 %collective-permute-start.16 = (f32[8,256]{1,0:T(8,128)S(1)}, f32[8,256]{1,0:T(8,128)S(1)}, u32[]{:S(2)}, u32[]{:S(2)}) collective-permute-start(f32[8,256]{1,0:T(8,128)S(1)} %get-tuple-element.47), channel_id=1, source_target_pairs={{0,118},{1,119},{2,116},{3,117},{4,122},{5,123},{6,120},{7,121},{8... | collective-permute-start | bytes 24584 | tf_op jit(solution)/shard_map/back_prv/ppermute | solution.py:54
  63.9 1.3 %collective-permute-start.15 = (f32[6,256]{1,0:T(8,128)S(1)}, f32[6,256]{1,0:T(8,128)S(1)}, u32[]{:S(2)}, u32[]{:S(2)}) collective-permute-start(f32[6,256]{1,0:T(8,128)S(1)} %get-tuple-element.46), channel_id=1, source_target_pairs={{0,4},{1,5},{2,6},{3,7},{4,8},{5,9},{6,10},{7,11},{8,12},{9,13},{1... | collective-permute-start | bytes 18440 | tf_op jit(solution)/shard_map/back_01/ppermute | solution.py:54
  65.2 2.0 %collective-permute-start.14 = (f32[4,256]{1,0:T(4,128)S(1)}, f32[4,256]{1,0:T(4,128)S(1)}, u32[]{:S(2)}, u32[]{:S(2)}) collective-permute-start(f32[4,256]{1,0:T(4,128)S(1)} %get-tuple-element.45), channel_id=1, source_target_pairs={{0,12},{1,13},{2,14},{3,15},{4,0},{5,1},{6,2},{7,3},{8,4},{9,5},{1... | collective-permute-start | bytes 12296 | tf_op jit(solution)/shard_map/back_03/ppermute | solution.py:54
  67.2 1.7 %collective-permute-done.14.b03 = f32[4,256]{1,0:T(4,128)S(1)} collective-permute-done((f32[4,256]{1,0:T(4,128)S(1)}, f32[4,256]{1,0:T(4,128)S(1)}, u32[]{:S(2)}, u32[]{:S(2)}) %collective-permute-start.14) | collective-permute-done | bytes 4128 | tf_op jit(solution)/shard_map/back_03/ppermute | solution.py:54
  (32 shorter events, 6.0 us)
Async XLA Ops:
  0.6 15.5 %copy-start.2 = (s32[8]{0:T(128)S(1)}, s32[8]{0:T(128)}, u32[]{:S(2)}) copy-start(s32[8]{0:T(128)} %refs_2_.1) | copy-start | bytes 100
  3.7 5.0 %collective-permute-start = (bf16[2,264,1024]{2,1,0:T(8,128)(2,1)}, bf16[2,264,1024]{2,1,0:T(8,128)(2,1)S(1)}, u32[]{:S(2)}, u32[]{:S(2)}) collective-permute-start(bf16[2,264,1024]{2,1,0:T(8,128)(2,1)} %get-tuple-element.26.refs_0_), channel_id=1, source_target_pairs={{0,1},{1,0},{2,3},{3,2},{4,5},{5,4},{6,7},{7,6},{8,9},{9,8},{10,11... | collective-permute-start | bytes 3244040 | tf_op jit(solution)/shard_map/ownx/ppermute | solution.py:54
  3.8 27.8 %collective-permute-start.6 = (bf16[2,264,1024]{2,1,0:T(8,128)(2,1)}, bf16[2,264,1024]{2,1,0:T(8,128)(2,1)S(1)}, u32[]{:S(2)}, u32[]{:S(2)}) collective-permute-start(bf16[2,264,1024]{2,1,0:T(8,128)(2,1)} %get-tuple-element.26.refs_0_), channel_id=1, source_target_pairs={{0,4},{1,5},{2,6},{3,7},{4,8},{5,9},{6,10},{7,11},{8,12},{9,13},{1... | collective-permute-start | bytes 3244040 | tf_op jit(solution)/shard_map/b03/ppermute | solution.py:54
  5.5 26.1 %collective-permute-start.7 = (bf16[2,264,1024]{2,1,0:T(8,128)(2,1)}, bf16[2,264,1024]{2,1,0:T(8,128)(2,1)S(1)}, u32[]{:S(2)}, u32[]{:S(2)}) collective-permute-start(bf16[2,264,1024]{2,1,0:T(8,128)(2,1)} %get-tuple-element.26.refs_0_), channel_id=1, source_target_pairs={{0,2},{1,3},{2,0},{3,1},{4,6},{5,7},{6,4},{7,5},{8,10},{9,11},{10,... | collective-permute-start | bytes 3244040 | tf_op jit(solution)/shard_map/b10/ppermute | solution.py:54
  7.0 15.4 %collective-permute-start.2 = (bf16[264,1024]{1,0:T(8,128)(2,1)}, bf16[264,1024]{1,0:T(8,128)(2,1)S(1)}, u32[]{:S(2)}, u32[]{:S(2)}) collective-permute-start(bf16[264,1024]{1,0:T(8,128)(2,1)} %get-tuple-element.30), channel_id=1, source_target_pairs={{0,12},{1,13},{2,14},{3,15},{4,0},{5,1},{6,2},{7,3},{8,4},{9,5},{1... | collective-permute-start | bytes 1622024 | tf_op jit(solution)/shard_map/b01a/ppermute | solution.py:54
  8.7 24.6 %collective-permute-start.1 = (bf16[264,1024]{1,0:T(8,128)(2,1)}, bf16[264,1024]{1,0:T(8,128)(2,1)S(1)}, u32[]{:S(2)}, u32[]{:S(2)}) collective-permute-start(bf16[264,1024]{1,0:T(8,128)(2,1)} %get-tuple-element.27), channel_id=1, source_target_pairs={{0,12},{1,13},{2,14},{3,15},{4,0},{5,1},{6,2},{7,3},{8,4},{9,5},{1... | collective-permute-start | bytes 1622024 | tf_op jit(solution)/shard_map/b01b/ppermute | solution.py:54
  10.5 29.0 %collective-permute-start.4 = (bf16[2,264,1024]{2,1,0:T(8,128)(2,1)}, bf16[2,264,1024]{2,1,0:T(8,128)(2,1)S(1)}, u32[]{:S(2)}, u32[]{:S(2)}) collective-permute-start(bf16[2,264,1024]{2,1,0:T(8,128)(2,1)} %get-tuple-element.26.refs_0_), channel_id=1, source_target_pairs={{0,114},{1,115},{2,112},{3,113},{4,118},{5,119},{6,116},{7,117},{8... | collective-permute-start | bytes 3244040 | tf_op jit(solution)/shard_map/nxt/ppermute | solution.py:54
  16.1 1.3 %copy-start = (bf16[2,264,1024]{2,1,0:T(8,128)(2,1)S(1)}, bf16[2,264,1024]{2,1,0:T(8,128)(2,1)}, u32[]{:S(2)}) copy-start(bf16[2,264,1024]{2,1,0:T(8,128)(2,1)} %get-tuple-element.26.refs_0_) | copy-start | bytes 3244036
  17.3 7.0 %copy-start.1 = (bf16[2,264,1024]{2,1,0:T(8,128)(2,1)S(1)}, bf16[2,264,1024]{2,1,0:T(8,128)(2,1)}, u32[]{:S(2)}) copy-start(bf16[2,264,1024]{2,1,0:T(8,128)(2,1)} %get-tuple-element.26.refs_0_) | copy-start | bytes 3244036
  22.4 17.1 %collective-permute-start.5 = (bf16[264,1024]{1,0:T(8,128)(2,1)S(1)}, bf16[264,1024]{1,0:T(8,128)(2,1)S(1)}, u32[]{:S(2)}, u32[]{:S(2)}) collective-permute-start(bf16[264,1024]{1,0:T(8,128)(2,1)S(1)} %collective-permute-done.2.refs_3_.b01a.refs_1_), channel_id=1, source_target_pairs={{0,16},{1,17},{2,18},{3,19},{4,20},{5,21},{6,22},{7,23},{8,24},{9,... | collective-permute-start | bytes 1622024 | tf_op jit(solution)/shard_map/prva/ppermute | solution.py:54
  31.7 14.0 %collective-permute-start.8 = (bf16[264,1024]{1,0:T(8,128)(2,1)S(1)}, bf16[264,1024]{1,0:T(8,128)(2,1)S(1)}, u32[]{:S(2)}, u32[]{:S(2)}) collective-permute-start(bf16[264,1024]{1,0:T(8,128)(2,1)S(1)} %slice_bitcast_fusion.1), channel_id=1, source_target_pairs={{0,2},{1,3},{2,0},{3,1},{4,6},{5,7},{6,4},{7,5},{8,10},{9,11},{10,... | collective-permute-start | bytes 1622024 | tf_op jit(solution)/shard_map/b13a/ppermute | solution.py:54
  33.3 17.4 %collective-permute-start.3 = (bf16[264,1024]{1,0:T(8,128)(2,1)S(1)}, bf16[264,1024]{1,0:T(8,128)(2,1)S(1)}, u32[]{:S(2)}, u32[]{:S(2)}) collective-permute-start(bf16[264,1024]{1,0:T(8,128)(2,1)S(1)} %collective-permute-done.1.refs_4_.b01b.refs_2_), channel_id=1, source_target_pairs={{0,16},{1,17},{2,18},{3,19},{4,20},{5,21},{6,22},{7,23},{8,24},{9,... | collective-permute-start | bytes 1622024 | tf_op jit(solution)/shard_map/prvb/ppermute | solution.py:54
  35.3 15.5 %collective-permute-start.9 = (bf16[264,1024]{1,0:T(8,128)(2,1)S(1)}, bf16[264,1024]{1,0:T(8,128)(2,1)S(1)}, u32[]{:S(2)}, u32[]{:S(2)}) collective-permute-start(bf16[264,1024]{1,0:T(8,128)(2,1)S(1)} %slice_bitcast_fusion), channel_id=1, source_target_pairs={{0,4},{1,5},{2,6},{3,7},{4,8},{5,9},{6,10},{7,11},{8,12},{9,13},{1... | collective-permute-start | bytes 1622024 | tf_op jit(solution)/shard_map/b13b/ppermute | solution.py:54
  39.7 12.9 %collective-permute-start.10 = (bf16[5,264,1024]{2,1,0:T(8,128)(2,1)S(1)}, bf16[5,264,1024]{2,1,0:T(8,128)(2,1)S(1)}, u32[]{:S(2)}, u32[]{:S(2)}) collective-permute-start(bf16[5,264,1024]{2,1,0:T(8,128)(2,1)S(1)} %bundle.1), channel_id=1, source_target_pairs={{0,1},{1,0},{2,3},{3,2},{4,5},{5,4},{6,7},{7,6},{8,9},{9,8},{10,11... | collective-permute-start | bytes 8110088 | tf_op jit(solution)/shard_map/cross/ppermute | solution.py:54
  50.7 1.9 %collective-permute-start.11 = (bf16[264,1024]{1,0:T(8,128)(2,1)S(1)}, bf16[264,1024]{1,0:T(8,128)(2,1)S(1)}, u32[]{:S(2)}, u32[]{:S(2)}) collective-permute-start(bf16[264,1024]{1,0:T(8,128)(2,1)S(1)} %collective-permute-done.3.refs_8_), channel_id=1, source_target_pairs={{0,1},{1,0},{2,3},{3,2},{4,5},{5,4},{6,7},{7,6},{8,9},{9,8},{10,11... | collective-permute-start | bytes 1622024 | tf_op jit(solution)/shard_map/prvbx/ppermute | solution.py:54
  56.5 3.7 %collective-permute-start.13 = (f32[8,256]{1,0:T(8,128)S(1)}, f32[8,256]{1,0:T(8,128)S(1)}, u32[]{:S(2)}, u32[]{:S(2)}) collective-permute-start(f32[8,256]{1,0:T(8,128)S(1)} %slice.17), channel_id=1, source_target_pairs={{0,2},{1,3},{2,0},{3,1},{4,6},{5,7},{6,4},{7,5},{8,10},{9,11},{10,... | collective-permute-start | bytes 24584 | tf_op jit(solution)/shard_map/side/ppermute | solution.py:54
  57.1 2.7 %collective-permute-start.12 = (f32[6,256]{1,0:T(8,128)S(1)}, f32[6,256]{1,0:T(8,128)S(1)}, u32[]{:S(2)}, u32[]{:S(2)}) collective-permute-start(f32[6,256]{1,0:T(8,128)S(1)} %slice.16), channel_id=1, source_target_pairs={{0,1},{1,0},{2,3},{3,2},{4,5},{5,4},{6,7},{7,6},{8,9},{9,8},{10,11... | collective-permute-start | bytes 18440 | tf_op jit(solution)/shard_map/swapped/ppermute | solution.py:54
  60.2 8.6 %collective-permute-start.16 = (f32[8,256]{1,0:T(8,128)S(1)}, f32[8,256]{1,0:T(8,128)S(1)}, u32[]{:S(2)}, u32[]{:S(2)}) collective-permute-start(f32[8,256]{1,0:T(8,128)S(1)} %get-tuple-element.47), channel_id=1, source_target_pairs={{0,118},{1,119},{2,116},{3,117},{4,122},{5,123},{6,120},{7,121},{8... | collective-permute-start | bytes 24584 | tf_op jit(solution)/shard_map/back_prv/ppermute | solution.py:54
  63.9 4.9 %collective-permute-start.15 = (f32[6,256]{1,0:T(8,128)S(1)}, f32[6,256]{1,0:T(8,128)S(1)}, u32[]{:S(2)}, u32[]{:S(2)}) collective-permute-start(f32[6,256]{1,0:T(8,128)S(1)} %get-tuple-element.46), channel_id=1, source_target_pairs={{0,4},{1,5},{2,6},{3,7},{4,8},{5,9},{6,10},{7,11},{8,12},{9,13},{1... | collective-permute-start | bytes 18440 | tf_op jit(solution)/shard_map/back_01/ppermute | solution.py:54
  65.2 3.6 %collective-permute-start.14 = (f32[4,256]{1,0:T(4,128)S(1)}, f32[4,256]{1,0:T(4,128)S(1)}, u32[]{:S(2)}, u32[]{:S(2)}) collective-permute-start(f32[4,256]{1,0:T(4,128)S(1)} %get-tuple-element.45), channel_id=1, source_target_pairs={{0,12},{1,13},{2,14},{3,15},{4,0},{5,1},{6,2},{7,3},{8,4},{9,5},{1... | collective-permute-start | bytes 12296 | tf_op jit(solution)/shard_map/back_03/ppermute | solution.py:54

commit v6 on v5

--- a/solution.py
+++ b/solution.py
@@ -65,7 +65,7 @@
 
 
 PARTS = 4
-PACK_MIB = 60
+PACK_MIB = 56
 LONG = 10**8
 
 
@@ -73,7 +73,7 @@
     return sizes_ref[lax.rem(lax.axis_index("group") + step, lax.axis_size("group"))]
 
 
-def pack_kernel(sizes_hbm, rows_hbm, rank_hbm, pay_ref, a_ref, b_ref, rows_ref, rank_ref, sizes_ref, sem):
+def pack_kernel(sizes_hbm, rows_hbm, rank_hbm, pay_hbm, a_hbm, b_hbm, rows_ref, rank_ref, pay_ref, sizes_ref, sem, out_sem):
     part = 2 * HALF // PARTS
     copies = [
         pltpu.make_async_copy(rows_hbm.at[pl.ds(i * part, part)], rows_ref.at[pl.ds(i * part, part)], sem.at[i])
@@ -81,29 +81,32 @@
     ]
     rank_copy = pltpu.make_async_copy(rank_hbm, rank_ref, sem.at[PARTS])
     sizes_copy = pltpu.make_async_copy(sizes_hbm, sizes_ref, sem.at[PARTS + 1])
-    for copy in [*copies, rank_copy, sizes_copy]:
+    for copy in [rank_copy, sizes_copy, *copies]:
         copy.start()
-    for i, copy in enumerate(copies):
-        copy.wait()
-        half, at = divmod(i * part, HALF)
-        rows = rows_ref[i * part : (i + 1) * part, :]
-        scale = lax.rsqrt(jnp.mean(rows * rows, axis=-1, keepdims=True) + 1e-06) / math.sqrt(D)
-        unit = (rows * scale).astype(jnp.bfloat16)
-        pay_ref[half, at : at + part, :] = unit
-        (a_ref, b_ref)[half][at : at + part, :] = unit
     rank_copy.wait()
     sizes_copy.wait()
     left = own_count(sizes_ref) - lax.axis_index("helper") * 2 * HALF
-    for half, half_ref in enumerate((a_ref, b_ref)):
+    outs = []
+    for half, half_hbm in enumerate((a_hbm, b_hbm)):
         rank = rank_ref[:, half * HALF : (half + 1) * HALF]
         position = lax.broadcasted_iota(jnp.int32, (1, HALF), 1) + half * HALF
         real = position < left
         high = jnp.where(real, rank // BASE, int(FAR) // BASE).astype(jnp.float32)
         low = jnp.where(real, rank % BASE, 0).astype(jnp.float32)
-        both = jnp.concatenate([high, low, jnp.zeros((1, D - 2 * HALF), jnp.float32)], axis=1)
-        tail = jnp.broadcast_to(both, (EXTRA, D)).astype(jnp.bfloat16)
-        pay_ref[half, HALF:, :] = tail
-        half_ref[HALF:, :] = tail
+        row = jnp.concatenate([high, low, jnp.zeros((1, D - 2 * HALF), jnp.float32)], axis=1)
+        pay_ref[half, HALF:, :] = jnp.broadcast_to(row, (EXTRA, D)).astype(jnp.bfloat16)
+        for i in range(half * PARTS // 2, (half + 1) * PARTS // 2):
+            copies[i].wait()
+            rows = rows_ref[i * part : (i + 1) * part, :]
+            scale = lax.rsqrt(jnp.mean(rows * rows, axis=-1, keepdims=True) + 1e-06) / math.sqrt(D)
+            at = i * part - half * HALF
+            pay_ref[half, at : at + part, :] = (rows * scale).astype(jnp.bfloat16)
+        outs.append(pltpu.make_async_copy(pay_ref.at[half], pay_hbm.at[half], out_sem.at[2 * half]))
+        outs.append(pltpu.make_async_copy(pay_ref.at[half], half_hbm, out_sem.at[2 * half + 1]))
+        for out in outs[2 * half :]:
+            out.start()
+    for out in outs:
+        out.wait()
 
 
 def packed(rows, ranks, sizes):
@@ -111,13 +114,15 @@
     return pl.pallas_call(
         pack_kernel,
         in_specs=[pl.BlockSpec(memory_space=pltpu.HBM)] * 3,
-        out_specs=[VMEM] * 3,
+        out_specs=[pl.BlockSpec(memory_space=pltpu.HBM)] * 3,
         out_shape=[jax.ShapeDtypeStruct((2, PAY, D), jnp.bfloat16), half, half],
         scratch_shapes=[
             pltpu.VMEM((2 * HALF, D), jnp.float32),
             pltpu.VMEM((1, 2 * HALF), jnp.int32),
+            pltpu.VMEM((2, PAY, D), jnp.bfloat16),
             pltpu.SMEM(sizes.shape, jnp.int32),
             pltpu.SemaphoreType.DMA((PARTS + 2,)),
+            pltpu.SemaphoreType.DMA((4,)),
         ],
         name="pack",
         compiler_params=pltpu.CompilerParams(vmem_limit_bytes=PACK_MIB * 2**20),
@@ -219,7 +224,7 @@
         out_shape=[jax.ShapeDtypeStruct((N_ROWS, HALF), jnp.float32), *extra_out],
         name=name,
         compiler_params=pltpu.CompilerParams(vmem_limit_bytes=14 * 2**20),
-        cost_estimate=pl.CostEstimate(flops=int(tasks * 1024), bytes_accessed=1024, transcendentals=0),
+        cost_estimate=pl.CostEstimate(flops=int(tasks * 1024) if tasks == LONG else 0, bytes_accessed=0, transcendentals=0),
     )(rows, *arrays, *scalars)
     return out if extra_out else out[0]
 
@@ -271,8 +276,10 @@
     own_job(row_ref, own, ownx, ranks, [b01a], [W01])
 
 
-def bundle_kernel(b01a, b01b, nxt, prva, bundle):
-    for n, half in enumerate([nxt.at[0], nxt.at[1], b01a, b01b, prva]):
+def bundle_kernel(b01a, b01b, nxt, prva, bundle, nxta, nxtb):
+    nxta[...] = nxt[0, :HALF, :]
+    nxtb[...] = nxt[1, :HALF, :]
+    for n, half in enumerate([b01a, b01b, prva]):
         bundle[n] = half[...]
 
 
@@ -300,22 +307,26 @@
     real_job(row_ref, [L_13 + h], [b13], [prva], [PRV])
 
 
-def cross_kernel(row_ref, b03, b10, b13a, b13b, cross, prvbx):
+def other_kernel(row_ref, own, b01a, b01b, b03, b10, nxtax, nxtbx):
+    queries = [*split(own), b01a, b01b, *split(b03), *split(b10)]
+    places = both(A00) + both(A01) + both(A03) + both(A10)
+    real_job(row_ref, both(L_NXTX), [nxtax, nxtbx], queries, places)
+
+
+def cross_kernel(row_ref, b03, b10, b13a, b13b, nxtax, nxtbx, cross, prvbx):
     b13 = [b13a, b13b]
-    real_job(row_ref, both(L_NXTX), [cross.at[0], cross.at[1]], split(b10) + b13, both(A10) + both(A13))
-    one = [cross.at[2], cross.at[3]]
+    real_job(row_ref, both(L_NXTX), [nxtax, nxtbx], b13, both(A13))
+    one = [cross.at[0], cross.at[1]]
     ranks = [rank_column(half[HALF:, : 2 * HALF]) for half in one]
     pair_job(
         row_ref, ranks, one, split(b03) + b13, both(W03) + both(W13), both(K01X),
         lambda k, q: (2 + k, q % 2) in SHARE,
     )
     limits = both(L_03) + both(L_10) + both(L_13)
-    real_job(row_ref, limits, split(b03) + split(b10) + b13, [cross.at[4], prvbx], both(PRVX))
-
-
-def end_kernel(row_ref, own, b01a, b01b, b03, b10, b13a, b13b, cross, prvb):
-    queries = [*split(own), b01a, b01b, *split(b03)]
-    real_job(row_ref, both(L_NXTX), [cross.at[0], cross.at[1]], queries, both(A00) + both(A01) + both(A03))
+    real_job(row_ref, limits, split(b03) + split(b10) + b13, [cross.at[2], prvbx], both(PRVX))
+
+
+def end_kernel(row_ref, b03, b10, b13a, b13b, prvb):
     limits = both(L_13) + both(L_03) + both(L_10)
     real_job(row_ref, limits, [b13a, b13b, *split(b03), *split(b10)], [prvb], [PRV + 1])
 
@@ -376,31 +387,35 @@
     nxt, b01b, prva, state = lax.optimization_barrier((nxt, b01b, prva, state))
     b13a = send("b13a", b03[0], col=1)
     b13b = send("b13b", b10[1], row=1)
-    bundle = pl.pallas_call(
+    half = jax.ShapeDtypeStruct((HALF, D), jnp.bfloat16)
+    bundle, nxta, nxtb = pl.pallas_call(
         bundle_kernel,
         in_specs=[VMEM] * 4,
-        out_specs=VMEM,
-        out_shape=jax.ShapeDtypeStruct((5, PAY, D), jnp.bfloat16),
+        out_specs=[VMEM] * 3,
+        out_shape=[jax.ShapeDtypeStruct((3, PAY, D), jnp.bfloat16), half, half],
         name="bundle",
         compiler_params=pltpu.CompilerParams(vmem_limit_bytes=8 * 2**20),
     )(b01a, b01b, nxt, prva)
-    cross = send("cross", bundle, core=1)
+    nxtax = send("nxtax", nxta, core=1)
+    nxtbx = send("nxtbx", nxtb, core=1)
     state, ranks1 = kernel_call(
         "same", same_kernel, 4.5, state,
         [own, ownx, own_ranks, b01a, b01b, b03, b10, nxt, prva], [rank_shape(2)],
     )
+    state = kernel_call("other", other_kernel, 0, state, [own, b01a, b01b, b03, b10, nxtax, nxtbx])
+    cross = send("cross", after(bundle, state), core=1)
     kept = [own, ownx, own_ranks, b01a, b01b, ranks1, nxt, prva]
     state = kernel_call("left", functools.partial(half_kernel, 0), 1, state, [*kept, b13a])
     prvb, state = lax.optimization_barrier((prvb, state))
     state = kernel_call("right", functools.partial(half_kernel, 1), LONG, state, [*kept, b13b])
     prvbx = send("prvbx", prvb, core=1)
     state = kernel_call(
-        "cross", cross_kernel, 4, state, [b03, b10, b13a, b13b, cross, prvbx]
+        "cross", cross_kernel, 4, state, [b03, b10, b13a, b13b, nxtax, nxtbx, cross, prvbx]
     )
 
     swapped = send("swapped", state[KOWNX : KOWNX + 6], core=1)
     side = send("side", state[W10 : W10 + 8], col=1)
-    state = kernel_call("end", end_kernel, 1, state, [own, b01a, b01b, b03, b10, b13a, b13b, cross, prvb])
+    state = kernel_call("end", end_kernel, 1, state, [b03, b10, b13a, b13b, prvb])
     shapes = [(8, HALF), (4, HALF), (6, HALF), (8, HALF)]
     kept, to_03, to_01, to_prv = small_call("gather", gather_kernel, shapes, [state, swapped, side])
     back_prv = send("back_prv", to_prv, cluster=-1, row=1)

time: 69.7 us -> 68.1 us (0.977)
  starting transfers between devices: 27.1 us -> 24.3 us
  waiting for transfers between devices: 19.5 us -> 20.9 us
    ppermute x17 -> x19, starting transfers between devices: 27.1 us -> 24.3 us  [send(): return lax.ppermute(value, AXES, pairs(**shift))]
    ppermute x17 -> x19, waiting for transfers between devices: 19.5 us -> 20.9 us  [send(): return lax.ppermute(value, AXES, pairs(**shift))]
    pallas_call x7 -> x8, Pallas kernels: 16.8 us -> 17 us  [kernel_call(): pl.pallas_call(kernel, in_specs=[VMEM] * (1 + len(arrays)) + [SMEM] * len...]
  transfers between devices with their start and end apart: 17 -> 19, of which waited for: 8 -> 10; matrix products, arithmetic and copies ran while one was open for 0% -> 0% of each run, Pallas kernels for 19% -> 21%
where the time goes in v6:
time: 68.1 us; the launch traced here: 67.9 us
  starting transfers between devices  24.3 us (36%)
  waiting for transfers between devices  20.9 us (31%)
  Pallas kernels  20.6 us (30%)
  local copies, waits for them, and re-layouts  1.33 us (2%)
  between operations  0.77 us (1%)
    ppermute x19, starting transfers between devices, send(): return lax.ppermute(value, AXES, pairs(**shift))  24.3 us
    ppermute x19, waiting for transfers between devices, send(): return lax.ppermute(value, AXES, pairs(**shift))  20.9 us
    pallas_call x8, Pallas kernels, kernel_call(): pl.pallas_call(kernel, in_specs=[VMEM] * (1 + len(arrays)) + [SMEM] * len...  17 us
    pallas_call x1, Pallas kernels, packed(): pl.pallas_call(pack_kernel, in_specs=[pl.BlockSpec(memory_space=pltpu.HBM...  2.8 us
  transfers between devices with their start and end apart: 19, of which 10 were waited for; matrix products, arithmetic and copies ran while one was open for 0% of the time, Pallas kernels for 21%

profile of v6, /device:TPU:0, one launch (start us, length us, event | category | flops | bytes accessed | tf_op | source)
XLA Modules:
  0.0 67.9 jit_solution(13282827677018374191)
XLA Ops:
  0.6 2.8 %pack.1 = (bf16[2,264,1024]{2,1,0:T(8,128)(2,1)}, bf16[264,1024]{1,0:T(8,128)(2,1)}, bf16[264,1024]{1,0:T(8,128)(2,1)}) custom-call(s32[8]{0:T(128)} %refs_2_.1, f32[512,1024]{1,0:T(8,128)} %bitcast.5, s32[1,512]{1,0:T(1,128)} %rank_hbm.1), custom_call_target="tpu_custom_call" | custom-call | flops 2097152 | bytes 4194304 | tf_op jit(solution)/shard_map/pack/pallas_call | solution.py:114
  3.5 1.7 %collective-permute-start.7 = (bf16[2,264,1024]{2,1,0:T(8,128)(2,1)}, bf16[2,264,1024]{2,1,0:T(8,128)(2,1)S(1)}, u32[]{:S(2)}, u32[]{:S(2)}) collective-permute-start(bf16[2,264,1024]{2,1,0:T(8,128)(2,1)} %get-tuple-element.30.refs_0_), channel_id=1, source_target_pairs={{0,2},{1,3},{2,0},{3,1},{4,6},{5,7},{6,4},{7,5},{8,10},{9,11},{10,... | collective-permute-start | bytes 3244040 | tf_op jit(solution)/shard_map/b10/ppermute | solution.py:54
  5.2 1.6 %collective-permute-start.6 = (bf16[2,264,1024]{2,1,0:T(8,128)(2,1)}, bf16[2,264,1024]{2,1,0:T(8,128)(2,1)S(1)}, u32[]{:S(2)}, u32[]{:S(2)}) collective-permute-start(bf16[2,264,1024]{2,1,0:T(8,128)(2,1)} %get-tuple-element.30.refs_0_), channel_id=1, source_target_pairs={{0,4},{1,5},{2,6},{3,7},{4,8},{5,9},{6,10},{7,11},{8,12},{9,13},{1... | collective-permute-start | bytes 3244040 | tf_op jit(solution)/shard_map/b03/ppermute | solution.py:54
  6.8 1.7 %collective-permute-start.2 = (bf16[264,1024]{1,0:T(8,128)(2,1)}, bf16[264,1024]{1,0:T(8,128)(2,1)S(1)}, u32[]{:S(2)}, u32[]{:S(2)}) collective-permute-start(bf16[264,1024]{1,0:T(8,128)(2,1)} %get-tuple-element.34), channel_id=1, source_target_pairs={{0,12},{1,13},{2,14},{3,15},{4,0},{5,1},{6,2},{7,3},{8,4},{9,5},{1... | collective-permute-start | bytes 1622024 | tf_op jit(solution)/shard_map/b01a/ppermute | solution.py:54
  8.4 5.6 %collective-permute-start.4 = (bf16[2,264,1024]{2,1,0:T(8,128)(2,1)}, bf16[2,264,1024]{2,1,0:T(8,128)(2,1)S(1)}, u32[]{:S(2)}, u32[]{:S(2)}) collective-permute-start(bf16[2,264,1024]{2,1,0:T(8,128)(2,1)} %get-tuple-element.30.refs_0_), channel_id=1, source_target_pairs={{0,114},{1,115},{2,112},{3,113},{4,118},{5,119},{6,116},{7,117},{8... | collective-permute-start | bytes 3244040 | tf_op jit(solution)/shard_map/nxt/ppermute | solution.py:54
  14.0 1.8 %collective-permute-start.1 = (bf16[264,1024]{1,0:T(8,128)(2,1)}, bf16[264,1024]{1,0:T(8,128)(2,1)S(1)}, u32[]{:S(2)}, u32[]{:S(2)}) collective-permute-start(bf16[264,1024]{1,0:T(8,128)(2,1)} %get-tuple-element.31), channel_id=1, source_target_pairs={{0,12},{1,13},{2,14},{3,15},{4,0},{5,1},{6,2},{7,3},{8,4},{9,5},{1... | collective-permute-start | bytes 1622024 | tf_op jit(solution)/shard_map/b01b/ppermute | solution.py:54
  15.8 1.2 %copy-done = bf16[2,264,1024]{2,1,0:T(8,128)(2,1)S(1)} copy-done((bf16[2,264,1024]{2,1,0:T(8,128)(2,1)S(1)}, bf16[2,264,1024]{2,1,0:T(8,128)(2,1)}, u32[]{:S(2)}) %copy-start) | copy-done | bytes 1081368
  17.1 1.8 %self.1 = (f32[56,256]{1,0:T(8,128)S(1)}, f32[4,256,128]{2,1,0:T(8,128)S(1)}) custom-call(f32[56,256]{1,0:T(8,128)S(1)} %broadcast_in_dim.3.rows_in, bf16[2,264,1024]{2,1,0:T(8,128)(2,1)S(1)} %copy-done, bf16[2,264,1024]{2,1,0:T(8,128)(2,1)S(1)} %collective-permute-done.refs_1_, s32[8]{0:T(128)S(1)} %copy-done.2), custom_call_target="tpu_custom_call" | custom-call | tf_op jit(solution)/shard_map/self/pallas_call | solution.py:220
  18.9 3.2 %collective-permute-done.2.refs_3_.b01a.refs_1_ = bf16[264,1024]{1,0:T(8,128)(2,1)S(1)} collective-permute-done((bf16[264,1024]{1,0:T(8,128)(2,1)}, bf16[264,1024]{1,0:T(8,128)(2,1)S(1)}, u32[]{:S(2)}, u32[]{:S(2)}) %collective-permute-start.2) | collective-permute-done | bytes 540704 | tf_op jit(solution)/shard_map/b01a/ppermute | solution.py:54
  22.1 1.9 %collective-permute-start.5 = (bf16[264,1024]{1,0:T(8,128)(2,1)S(1)}, bf16[264,1024]{1,0:T(8,128)(2,1)S(1)}, u32[]{:S(2)}, u32[]{:S(2)}) collective-permute-start(bf16[264,1024]{1,0:T(8,128)(2,1)S(1)} %collective-permute-done.2.refs_3_.b01a.refs_1_), channel_id=1, source_target_pairs={{0,16},{1,17},{2,18},{3,19},{4,20},{5,21},{6,22},{7,23},{8,24},{9,... | collective-permute-start | bytes 1622024 | tf_op jit(solution)/shard_map/prva/ppermute | solution.py:54
  25.0 5.1 %collective-permute-done.7.refs_6_.refs_4_.refs_1_ = bf16[2,264,1024]{2,1,0:T(8,128)(2,1)S(1)} collective-permute-done((bf16[2,264,1024]{2,1,0:T(8,128)(2,1)}, bf16[2,264,1024]{2,1,0:T(8,128)(2,1)S(1)}, u32[]{:S(2)}, u32[]{:S(2)}) %collective-permute-start.7) | collective-permute-done | bytes 1081376 | tf_op jit(solution)/shard_map/b10/ppermute | solution.py:54
  30.0 2.6 %collective-permute-done.6.refs_5_.refs_3_.refs_0_ = bf16[2,264,1024]{2,1,0:T(8,128)(2,1)S(1)} collective-permute-done((bf16[2,264,1024]{2,1,0:T(8,128)(2,1)}, bf16[2,264,1024]{2,1,0:T(8,128)(2,1)S(1)}, u32[]{:S(2)}, u32[]{:S(2)}) %collective-permute-start.6) | collective-permute-done | bytes 1081376 | tf_op jit(solution)/shard_map/b03/ppermute | solution.py:54
  33.3 1.9 %collective-permute-start.3 = (bf16[264,1024]{1,0:T(8,128)(2,1)S(1)}, bf16[264,1024]{1,0:T(8,128)(2,1)S(1)}, u32[]{:S(2)}, u32[]{:S(2)}) collective-permute-start(bf16[264,1024]{1,0:T(8,128)(2,1)S(1)} %collective-permute-done.1.refs_4_.b01b.refs_2_), channel_id=1, source_target_pairs={{0,16},{1,17},{2,18},{3,19},{4,20},{5,21},{6,22},{7,23},{8,24},{9,... | collective-permute-start | bytes 1622024 | tf_op jit(solution)/shard_map/prvb/ppermute | solution.py:54
  38.8 4.8 %same.1 = (f32[56,256]{1,0:T(8,128)S(1)}, f32[2,256,128]{2,1,0:T(8,128)S(1)}) custom-call(f32[56,256]{1,0:T(8,128)S(1)} %first.1.rows_in, bf16[2,264,1024]{2,1,0:T(8,128)(2,1)S(1)} %copy-done.1, bf16[2,264,1024]{2,1,0:T(8,128)(2,1)S(1)} %collective-permute-done.refs_1_, f32[4,256,128]{2,1,0:T(8,128)S(1)} %get-tuple-element.33.refs_2_, ...), custom_call_target="tpu_custom_call" | custom-call | tf_op jit(solution)/shard_map/same/pallas_call | solution.py:220
  43.7 2.4 %other.1.rows_in = f32[56,256]{1,0:T(8,128)S(1)} custom-call(f32[56,256]{1,0:T(8,128)S(1)} %get-tuple-element.44.rows_in, bf16[2,264,1024]{2,1,0:T(8,128)(2,1)S(1)} %copy-done.1, bf16[264,1024]{1,0:T(8,128)(2,1)S(1)} %collective-permute-done.2.refs_3_.b01a.refs_1_, bf16[264,1024]{1,0:T(8,128)(2,1)S(1)} %collective-permute-done.1.refs_4_.b01b.refs_2_, ...), custom_call_target="tpu_custom_call" | custom-call | tf_op jit(solution)/shard_map/other/pallas_call | solution.py:220
  46.4 1.5 %left.1.rows_in = f32[56,256]{1,0:T(8,128)S(1)} custom-call(f32[56,256]{1,0:T(8,128)S(1)} %other.1.rows_in, bf16[2,264,1024]{2,1,0:T(8,128)(2,1)S(1)} %copy-done.1, bf16[2,264,1024]{2,1,0:T(8,128)(2,1)S(1)} %collective-permute-done.refs_1_, f32[4,256,128]{2,1,0:T(8,128)S(1)} %get-tuple-element.33.refs_2_, ...), custom_call_target="tpu_custom_call" | custom-call | tf_op jit(solution)/shard_map/left/pallas_call | solution.py:220
  47.9 3.2 %collective-permute-done.3.refs_4_ = bf16[264,1024]{1,0:T(8,128)(2,1)S(1)} collective-permute-done((bf16[264,1024]{1,0:T(8,128)(2,1)S(1)}, bf16[264,1024]{1,0:T(8,128)(2,1)S(1)}, u32[]{:S(2)}, u32[]{:S(2)}) %collective-permute-start.3) | collective-permute-done | bytes 540704 | tf_op jit(solution)/shard_map/prvb/ppermute | solution.py:54
  51.1 1.3 %right.1.rows_in = f32[56,256]{1,0:T(8,128)S(1)} custom-call(f32[56,256]{1,0:T(8,128)S(1)} %left.1.rows_in, bf16[2,264,1024]{2,1,0:T(8,128)(2,1)S(1)} %copy-done.1, bf16[2,264,1024]{2,1,0:T(8,128)(2,1)S(1)} %collective-permute-done.refs_1_, f32[4,256,128]{2,1,0:T(8,128)S(1)} %get-tuple-element.33.refs_2_, ...), custom_call_target="tpu_custom_call" | custom-call | flops 102400000000 | tf_op jit(solution)/shard_map/right/pallas_call | solution.py:220
  53.0 3.3 %cross.1.rows_in = f32[56,256]{1,0:T(8,128)S(1)} custom-call(f32[56,256]{1,0:T(8,128)S(1)} %right.1.rows_in, bf16[2,264,1024]{2,1,0:T(8,128)(2,1)S(1)} %collective-permute-done.6.refs_5_.refs_3_.refs_0_, bf16[2,264,1024]{2,1,0:T(8,128)(2,1)S(1)} %collective-permute-done.7.refs_6_.refs_4_.refs_1_, ...), custom_call_target="tpu_custom_call" | custom-call | tf_op jit(solution)/shard_map/cross/pallas_call | solution.py:220
  57.8 2.2 %collective-permute-done.15.side_ref = f32[8,256]{1,0:T(8,128)S(1)} collective-permute-done((f32[8,256]{1,0:T(8,128)S(1)}, f32[8,256]{1,0:T(8,128)S(1)}, u32[]{:S(2)}, u32[]{:S(2)}) %collective-permute-start.15) | collective-permute-done | bytes 8224 | tf_op jit(solution)/shard_map/side/ppermute | solution.py:54
  60.1 2.1 %collective-permute-start.18 = (f32[8,256]{1,0:T(8,128)S(1)}, f32[8,256]{1,0:T(8,128)S(1)}, u32[]{:S(2)}, u32[]{:S(2)}) collective-permute-start(f32[8,256]{1,0:T(8,128)S(1)} %get-tuple-element.55), channel_id=1, source_target_pairs={{0,118},{1,119},{2,116},{3,117},{4,122},{5,123},{6,120},{7,121},{8... | collective-permute-start | bytes 24584 | tf_op jit(solution)/shard_map/back_prv/ppermute | solution.py:54
  62.1 1.6 %collective-permute-start.17 = (f32[6,256]{1,0:T(8,128)S(1)}, f32[6,256]{1,0:T(8,128)S(1)}, u32[]{:S(2)}, u32[]{:S(2)}) collective-permute-start(f32[6,256]{1,0:T(8,128)S(1)} %get-tuple-element.54), channel_id=1, source_target_pairs={{0,4},{1,5},{2,6},{3,7},{4,8},{5,9},{6,10},{7,11},{8,12},{9,13},{1... | collective-permute-start | bytes 18440 | tf_op jit(solution)/shard_map/back_01/ppermute | solution.py:54
  63.7 1.7 %collective-permute-start.16 = (f32[4,256]{1,0:T(4,128)S(1)}, f32[4,256]{1,0:T(4,128)S(1)}, u32[]{:S(2)}, u32[]{:S(2)}) collective-permute-start(f32[4,256]{1,0:T(4,128)S(1)} %get-tuple-element.53), channel_id=1, source_target_pairs={{0,12},{1,13},{2,14},{3,15},{4,0},{5,1},{6,2},{7,3},{8,4},{9,5},{1... | collective-permute-start | bytes 12296 | tf_op jit(solution)/shard_map/back_03/ppermute | solution.py:54
  65.4 1.9 %collective-permute-done.16.b03 = f32[4,256]{1,0:T(4,128)S(1)} collective-permute-done((f32[4,256]{1,0:T(4,128)S(1)}, f32[4,256]{1,0:T(4,128)S(1)}, u32[]{:S(2)}, u32[]{:S(2)}) %collective-permute-start.16) | collective-permute-done | bytes 4128 | tf_op jit(solution)/shard_map/back_03/ppermute | solution.py:54
  (37 shorter events, 8.3 us)
Async XLA Ops:
  0.6 15.2 %copy-start.2 = (s32[8]{0:T(128)S(1)}, s32[8]{0:T(128)}, u32[]{:S(2)}) copy-start(s32[8]{0:T(128)} %refs_2_.1) | copy-start | bytes 100
  3.5 10.6 %collective-permute-start = (bf16[2,264,1024]{2,1,0:T(8,128)(2,1)}, bf16[2,264,1024]{2,1,0:T(8,128)(2,1)S(1)}, u32[]{:S(2)}, u32[]{:S(2)}) collective-permute-start(bf16[2,264,1024]{2,1,0:T(8,128)(2,1)} %get-tuple-element.30.refs_0_), channel_id=1, source_target_pairs={{0,1},{1,0},{2,3},{3,2},{4,5},{5,4},{6,7},{7,6},{8,9},{9,8},{10,11... | collective-permute-start | bytes 3244040 | tf_op jit(solution)/shard_map/ownx/ppermute | solution.py:54
  3.5 26.5 %collective-permute-start.7 = (bf16[2,264,1024]{2,1,0:T(8,128)(2,1)}, bf16[2,264,1024]{2,1,0:T(8,128)(2,1)S(1)}, u32[]{:S(2)}, u32[]{:S(2)}) collective-permute-start(bf16[2,264,1024]{2,1,0:T(8,128)(2,1)} %get-tuple-element.30.refs_0_), channel_id=1, source_target_pairs={{0,2},{1,3},{2,0},{3,1},{4,6},{5,7},{6,4},{7,5},{8,10},{9,11},{10,... | collective-permute-start | bytes 3244040 | tf_op jit(solution)/shard_map/b10/ppermute | solution.py:54
  5.2 27.4 %collective-permute-start.6 = (bf16[2,264,1024]{2,1,0:T(8,128)(2,1)}, bf16[2,264,1024]{2,1,0:T(8,128)(2,1)S(1)}, u32[]{:S(2)}, u32[]{:S(2)}) collective-permute-start(bf16[2,264,1024]{2,1,0:T(8,128)(2,1)} %get-tuple-element.30.refs_0_), channel_id=1, source_target_pairs={{0,4},{1,5},{2,6},{3,7},{4,8},{5,9},{6,10},{7,11},{8,12},{9,13},{1... | collective-permute-start | bytes 3244040 | tf_op jit(solution)/shard_map/b03/ppermute | solution.py:54
  6.8 15.4 %collective-permute-start.2 = (bf16[264,1024]{1,0:T(8,128)(2,1)}, bf16[264,1024]{1,0:T(8,128)(2,1)S(1)}, u32[]{:S(2)}, u32[]{:S(2)}) collective-permute-start(bf16[264,1024]{1,0:T(8,128)(2,1)} %get-tuple-element.34), channel_id=1, source_target_pairs={{0,12},{1,13},{2,14},{3,15},{4,0},{5,1},{6,2},{7,3},{8,4},{9,5},{1... | collective-permute-start | bytes 1622024 | tf_op jit(solution)/shard_map/b01a/ppermute | solution.py:54
  8.4 28.8 %collective-permute-start.4 = (bf16[2,264,1024]{2,1,0:T(8,128)(2,1)}, bf16[2,264,1024]{2,1,0:T(8,128)(2,1)S(1)}, u32[]{:S(2)}, u32[]{:S(2)}) collective-permute-start(bf16[2,264,1024]{2,1,0:T(8,128)(2,1)} %get-tuple-element.30.refs_0_), channel_id=1, source_target_pairs={{0,114},{1,115},{2,112},{3,113},{4,118},{5,119},{6,116},{7,117},{8... | collective-permute-start | bytes 3244040 | tf_op jit(solution)/shard_map/nxt/ppermute | solution.py:54
  14.0 19.3 %collective-permute-start.1 = (bf16[264,1024]{1,0:T(8,128)(2,1)}, bf16[264,1024]{1,0:T(8,128)(2,1)S(1)}, u32[]{:S(2)}, u32[]{:S(2)}) collective-permute-start(bf16[264,1024]{1,0:T(8,128)(2,1)} %get-tuple-element.31), channel_id=1, source_target_pairs={{0,12},{1,13},{2,14},{3,15},{4,0},{5,1},{6,2},{7,3},{8,4},{9,5},{1... | collective-permute-start | bytes 1622024 | tf_op jit(solution)/shard_map/b01b/ppermute | solution.py:54
  15.8 1.2 %copy-start = (bf16[2,264,1024]{2,1,0:T(8,128)(2,1)S(1)}, bf16[2,264,1024]{2,1,0:T(8,128)(2,1)}, u32[]{:S(2)}) copy-start(bf16[2,264,1024]{2,1,0:T(8,128)(2,1)} %get-tuple-element.30.refs_0_) | copy-start | bytes 3244036
  17.1 7.0 %copy-start.1 = (bf16[2,264,1024]{2,1,0:T(8,128)(2,1)S(1)}, bf16[2,264,1024]{2,1,0:T(8,128)(2,1)}, u32[]{:S(2)}) copy-start(bf16[2,264,1024]{2,1,0:T(8,128)(2,1)} %get-tuple-element.30.refs_0_) | copy-start | bytes 3244036
  22.1 15.9 %collective-permute-start.5 = (bf16[264,1024]{1,0:T(8,128)(2,1)S(1)}, bf16[264,1024]{1,0:T(8,128)(2,1)S(1)}, u32[]{:S(2)}, u32[]{:S(2)}) collective-permute-start(bf16[264,1024]{1,0:T(8,128)(2,1)S(1)} %collective-permute-done.2.refs_3_.b01a.refs_1_), channel_id=1, source_target_pairs={{0,16},{1,17},{2,18},{3,19},{4,20},{5,21},{6,22},{7,23},{8,24},{9,... | collective-permute-start | bytes 1622024 | tf_op jit(solution)/shard_map/prva/ppermute | solution.py:54
  32.7 13.7 %collective-permute-start.10 = (bf16[264,1024]{1,0:T(8,128)(2,1)S(1)}, bf16[264,1024]{1,0:T(8,128)(2,1)S(1)}, u32[]{:S(2)}, u32[]{:S(2)}) collective-permute-start(bf16[264,1024]{1,0:T(8,128)(2,1)S(1)} %slice_bitcast_fusion.1), channel_id=1, source_target_pairs={{0,2},{1,3},{2,0},{3,1},{4,6},{5,7},{6,4},{7,5},{8,10},{9,11},{10,... | collective-permute-start | bytes 1622024 | tf_op jit(solution)/shard_map/b13a/ppermute | solution.py:54
  33.3 17.8 %collective-permute-start.3 = (bf16[264,1024]{1,0:T(8,128)(2,1)S(1)}, bf16[264,1024]{1,0:T(8,128)(2,1)S(1)}, u32[]{:S(2)}, u32[]{:S(2)}) collective-permute-start(bf16[264,1024]{1,0:T(8,128)(2,1)S(1)} %collective-permute-done.1.refs_4_.b01b.refs_2_), channel_id=1, source_target_pairs={{0,16},{1,17},{2,18},{3,19},{4,20},{5,21},{6,22},{7,23},{8,24},{9,... | collective-permute-start | bytes 1622024 | tf_op jit(solution)/shard_map/prvb/ppermute | solution.py:54
  35.2 15.9 %collective-permute-start.11 = (bf16[264,1024]{1,0:T(8,128)(2,1)S(1)}, bf16[264,1024]{1,0:T(8,128)(2,1)S(1)}, u32[]{:S(2)}, u32[]{:S(2)}) collective-permute-start(bf16[264,1024]{1,0:T(8,128)(2,1)S(1)} %slice_bitcast_fusion), channel_id=1, source_target_pairs={{0,4},{1,5},{2,6},{3,7},{4,8},{5,9},{6,10},{7,11},{8,12},{9,13},{1... | collective-permute-start | bytes 1622024 | tf_op jit(solution)/shard_map/b13b/ppermute | solution.py:54
  38.2 5.4 %collective-permute-start.8 = (bf16[256,1024]{1,0:T(8,128)(2,1)S(1)}, bf16[256,1024]{1,0:T(8,128)(2,1)S(1)}, u32[]{:S(2)}, u32[]{:S(2)}) collective-permute-start(bf16[256,1024]{1,0:T(8,128)(2,1)S(1)} %get-tuple-element.45), channel_id=1, source_target_pairs={{0,1},{1,0},{2,3},{3,2},{4,5},{5,4},{6,7},{7,6},{8,9},{9,8},{10,11... | collective-permute-start | bytes 1572872 | tf_op jit(solution)/shard_map/nxtax/ppermute | solution.py:54
  38.3 5.3 %collective-permute-start.9 = (bf16[256,1024]{1,0:T(8,128)(2,1)S(1)}, bf16[256,1024]{1,0:T(8,128)(2,1)S(1)}, u32[]{:S(2)}, u32[]{:S(2)}) collective-permute-start(bf16[256,1024]{1,0:T(8,128)(2,1)S(1)} %get-tuple-element.46), channel_id=1, source_target_pairs={{0,1},{1,0},{2,3},{3,2},{4,5},{5,4},{6,7},{7,6},{8,9},{9,8},{10,11... | collective-permute-start | bytes 1572872 | tf_op jit(solution)/shard_map/nxtbx/ppermute | solution.py:54
  46.1 7.0 %collective-permute-start.12 = (bf16[3,264,1024]{2,1,0:T(8,128)(2,1)S(1)}, bf16[3,264,1024]{2,1,0:T(8,128)(2,1)S(1)}, u32[]{:S(2)}, u32[]{:S(2)}) collective-permute-start(bf16[3,264,1024]{2,1,0:T(8,128)(2,1)S(1)} %get-tuple-element.50), channel_id=1, source_target_pairs={{0,1},{1,0},{2,3},{3,2},{4,5},{5,4},{6,7},{7,6},{8,9},{9,8},{10,11... | collective-permute-start | bytes 4866056 | tf_op jit(solution)/shard_map/cross/ppermute | solution.py:54
  51.1 1.9 %collective-permute-start.13 = (bf16[264,1024]{1,0:T(8,128)(2,1)S(1)}, bf16[264,1024]{1,0:T(8,128)(2,1)S(1)}, u32[]{:S(2)}, u32[]{:S(2)}) collective-permute-start(bf16[264,1024]{1,0:T(8,128)(2,1)S(1)} %collective-permute-done.3.refs_4_), channel_id=1, source_target_pairs={{0,1},{1,0},{2,3},{3,2},{4,5},{5,4},{6,7},{7,6},{8,9},{9,8},{10,11... | collective-permute-start | bytes 1622024 | tf_op jit(solution)/shard_map/prvbx/ppermute | solution.py:54
  56.3 3.7 %collective-permute-start.15 = (f32[8,256]{1,0:T(8,128)S(1)}, f32[8,256]{1,0:T(8,128)S(1)}, u32[]{:S(2)}, u32[]{:S(2)}) collective-permute-start(f32[8,256]{1,0:T(8,128)S(1)} %slice.17), channel_id=1, source_target_pairs={{0,2},{1,3},{2,0},{3,1},{4,6},{5,7},{6,4},{7,5},{8,10},{9,11},{10,... | collective-permute-start | bytes 24584 | tf_op jit(solution)/shard_map/side/ppermute | solution.py:54
  56.6 1.2 %collective-permute-start.14 = (f32[6,256]{1,0:T(8,128)S(1)}, f32[6,256]{1,0:T(8,128)S(1)}, u32[]{:S(2)}, u32[]{:S(2)}) collective-permute-start(f32[6,256]{1,0:T(8,128)S(1)} %slice.16), channel_id=1, source_target_pairs={{0,1},{1,0},{2,3},{3,2},{4,5},{5,4},{6,7},{7,6},{8,9},{9,8},{10,11... | collective-permute-start | bytes 18440 | tf_op jit(solution)/shard_map/swapped/ppermute | solution.py:54
  60.1 7.3 %collective-permute-start.18 = (f32[8,256]{1,0:T(8,128)S(1)}, f32[8,256]{1,0:T(8,128)S(1)}, u32[]{:S(2)}, u32[]{:S(2)}) collective-permute-start(f32[8,256]{1,0:T(8,128)S(1)} %get-tuple-element.55), channel_id=1, source_target_pairs={{0,118},{1,119},{2,116},{3,117},{4,122},{5,123},{6,120},{7,121},{8... | collective-permute-start | bytes 24584 | tf_op jit(solution)/shard_map/back_prv/ppermute | solution.py:54
  62.1 5.2 %collective-permute-start.17 = (f32[6,256]{1,0:T(8,128)S(1)}, f32[6,256]{1,0:T(8,128)S(1)}, u32[]{:S(2)}, u32[]{:S(2)}) collective-permute-start(f32[6,256]{1,0:T(8,128)S(1)} %get-tuple-element.54), channel_id=1, source_target_pairs={{0,4},{1,5},{2,6},{3,7},{4,8},{5,9},{6,10},{7,11},{8,12},{9,13},{1... | collective-permute-start | bytes 18440 | tf_op jit(solution)/shard_map/back_01/ppermute | solution.py:54
  63.7 3.6 %collective-permute-start.16 = (f32[4,256]{1,0:T(4,128)S(1)}, f32[4,256]{1,0:T(4,128)S(1)}, u32[]{:S(2)}, u32[]{:S(2)}) collective-permute-start(f32[4,256]{1,0:T(4,128)S(1)} %get-tuple-element.53), channel_id=1, source_target_pairs={{0,12},{1,13},{2,14},{3,15},{4,0},{5,1},{6,2},{7,3},{8,4},{9,5},{1... | collective-permute-start | bytes 12296 | tf_op jit(solution)/shard_map/back_03/ppermute | solution.py:54

commit v7 on v6

--- a/solution.py
+++ b/solution.py
@@ -313,7 +313,7 @@
     real_job(row_ref, both(L_NXTX), [nxtax, nxtbx], queries, places)
 
 
-def cross_kernel(row_ref, b03, b10, b13a, b13b, nxtax, nxtbx, cross, prvbx):
+def cross_kernel(row_ref, b03, b13a, b13b, nxtax, nxtbx, cross):
     b13 = [b13a, b13b]
     real_job(row_ref, both(L_NXTX), [nxtax, nxtbx], b13, both(A13))
     one = [cross.at[0], cross.at[1]]
@@ -322,8 +322,11 @@
         row_ref, ranks, one, split(b03) + b13, both(W03) + both(W13), both(K01X),
         lambda k, q: (2 + k, q % 2) in SHARE,
     )
+
+
+def prev_kernel(row_ref, b03, b10, b13a, b13b, cross, prvbx):
     limits = both(L_03) + both(L_10) + both(L_13)
-    real_job(row_ref, limits, split(b03) + split(b10) + b13, [cross.at[2], prvbx], both(PRVX))
+    real_job(row_ref, limits, [*split(b03), *split(b10), b13a, b13b], [cross.at[2], prvbx], both(PRVX))
 
 
 def end_kernel(row_ref, b03, b10, b13a, b13b, prvb):
@@ -409,12 +412,11 @@
     prvb, state = lax.optimization_barrier((prvb, state))
     state = kernel_call("right", functools.partial(half_kernel, 1), LONG, state, [*kept, b13b])
     prvbx = send("prvbx", prvb, core=1)
-    state = kernel_call(
-        "cross", cross_kernel, 4, state, [b03, b10, b13a, b13b, nxtax, nxtbx, cross, prvbx]
-    )
-
+    state = kernel_call("cross", cross_kernel, 0, state, [b03, b13a, b13b, nxtax, nxtbx, cross])
+
+    side = send("side", state[W10 : W10 + 8], col=1)
+    state = kernel_call("prev", prev_kernel, 0, state, [b03, b10, b13a, b13b, cross, prvbx])
     swapped = send("swapped", state[KOWNX : KOWNX + 6], core=1)
-    side = send("side", state[W10 : W10 + 8], col=1)
     state = kernel_call("end", end_kernel, 1, state, [b03, b10, b13a, b13b, prvb])
     shapes = [(8, HALF), (4, HALF), (6, HALF), (8, HALF)]
     kept, to_03, to_01, to_prv = small_call("gather", gather_kernel, shapes, [state, swapped, side])

time: 68.1 us -> 67 us (0.984)
  waiting for transfers between devices: 20.9 us -> 18 us
  starting transfers between devices: 24.3 us -> 25.8 us
    ppermute x19, waiting for transfers between devices: 20.9 us -> 18 us  [send(): return lax.ppermute(value, AXES, pairs(**shift))]
    ppermute x19, starting transfers between devices: 24.3 us -> 25.8 us  [send(): return lax.ppermute(value, AXES, pairs(**shift))]
    pallas_call x8 -> x9, Pallas kernels: 17 us -> 17.3 us  [kernel_call(): pl.pallas_call(kernel, in_specs=[VMEM] * (1 + len(arrays)) + [SMEM] * len...]
  transfers between devices with their start and end apart: 19 -> 19, of which waited for: 10 -> 8; matrix products, arithmetic and copies ran while one was open for 0% -> 0% of each run, Pallas kernels for 21% -> 26%
where the time goes in v7:
time: 67 us; the launch traced here: 66.8 us
  starting transfers between devices  25.8 us (39%)
  Pallas kernels  20.9 us (31%)
  waiting for transfers between devices  18 us (27%)
  local copies, waits for them, and re-layouts  1.33 us (2%)
  between operations  0.8 us (1%)
    ppermute x19, starting transfers between devices, send(): return lax.ppermute(value, AXES, pairs(**shift))  25.8 us
    ppermute x19, waiting for transfers between devices, send(): return lax.ppermute(value, AXES, pairs(**shift))  18 us
    pallas_call x9, Pallas kernels, kernel_call(): pl.pallas_call(kernel, in_specs=[VMEM] * (1 + len(arrays)) + [SMEM] * len...  17.3 us
    pallas_call x1, Pallas kernels, packed(): pl.pallas_call(pack_kernel, in_specs=[pl.BlockSpec(memory_space=pltpu.HBM...  2.8 us
  transfers between devices with their start and end apart: 19, of which 8 were waited for; matrix products, arithmetic and copies ran while one was open for 0% of the time, Pallas kernels for 26%

profile of v7, /device:TPU:0, one launch (start us, length us, event | category | flops | bytes accessed | tf_op | source)
XLA Modules:
  0.0 66.8 jit_solution(12279866054988170346)
XLA Ops:
  0.6 2.8 %pack.1 = (bf16[2,264,1024]{2,1,0:T(8,128)(2,1)}, bf16[264,1024]{1,0:T(8,128)(2,1)}, bf16[264,1024]{1,0:T(8,128)(2,1)}) custom-call(s32[8]{0:T(128)} %refs_2_.1, f32[512,1024]{1,0:T(8,128)} %bitcast.5, s32[1,512]{1,0:T(1,128)} %rank_hbm.1), custom_call_target="tpu_custom_call" | custom-call | flops 2097152 | bytes 4194304 | tf_op jit(solution)/shard_map/pack/pallas_call | solution.py:114
  3.5 1.7 %collective-permute-start.7 = (bf16[2,264,1024]{2,1,0:T(8,128)(2,1)}, bf16[2,264,1024]{2,1,0:T(8,128)(2,1)S(1)}, u32[]{:S(2)}, u32[]{:S(2)}) collective-permute-start(bf16[2,264,1024]{2,1,0:T(8,128)(2,1)} %get-tuple-element.30.refs_0_), channel_id=1, source_target_pairs={{0,2},{1,3},{2,0},{3,1},{4,6},{5,7},{6,4},{7,5},{8,10},{9,11},{10,... | collective-permute-start | bytes 3244040 | tf_op jit(solution)/shard_map/b10/ppermute | solution.py:54
  5.2 1.6 %collective-permute-start.6 = (bf16[2,264,1024]{2,1,0:T(8,128)(2,1)}, bf16[2,264,1024]{2,1,0:T(8,128)(2,1)S(1)}, u32[]{:S(2)}, u32[]{:S(2)}) collective-permute-start(bf16[2,264,1024]{2,1,0:T(8,128)(2,1)} %get-tuple-element.30.refs_0_), channel_id=1, source_target_pairs={{0,4},{1,5},{2,6},{3,7},{4,8},{5,9},{6,10},{7,11},{8,12},{9,13},{1... | collective-permute-start | bytes 3244040 | tf_op jit(solution)/shard_map/b03/ppermute | solution.py:54
  6.8 1.7 %collective-permute-start.2 = (bf16[264,1024]{1,0:T(8,128)(2,1)}, bf16[264,1024]{1,0:T(8,128)(2,1)S(1)}, u32[]{:S(2)}, u32[]{:S(2)}) collective-permute-start(bf16[264,1024]{1,0:T(8,128)(2,1)} %get-tuple-element.34), channel_id=1, source_target_pairs={{0,12},{1,13},{2,14},{3,15},{4,0},{5,1},{6,2},{7,3},{8,4},{9,5},{1... | collective-permute-start | bytes 1622024 | tf_op jit(solution)/shard_map/b01a/ppermute | solution.py:54
  8.4 5.6 %collective-permute-start.4 = (bf16[2,264,1024]{2,1,0:T(8,128)(2,1)}, bf16[2,264,1024]{2,1,0:T(8,128)(2,1)S(1)}, u32[]{:S(2)}, u32[]{:S(2)}) collective-permute-start(bf16[2,264,1024]{2,1,0:T(8,128)(2,1)} %get-tuple-element.30.refs_0_), channel_id=1, source_target_pairs={{0,114},{1,115},{2,112},{3,113},{4,118},{5,119},{6,116},{7,117},{8... | collective-permute-start | bytes 3244040 | tf_op jit(solution)/shard_map/nxt/ppermute | solution.py:54
  14.0 1.8 %collective-permute-start.1 = (bf16[264,1024]{1,0:T(8,128)(2,1)}, bf16[264,1024]{1,0:T(8,128)(2,1)S(1)}, u32[]{:S(2)}, u32[]{:S(2)}) collective-permute-start(bf16[264,1024]{1,0:T(8,128)(2,1)} %get-tuple-element.31), channel_id=1, source_target_pairs={{0,12},{1,13},{2,14},{3,15},{4,0},{5,1},{6,2},{7,3},{8,4},{9,5},{1... | collective-permute-start | bytes 1622024 | tf_op jit(solution)/shard_map/b01b/ppermute | solution.py:54
  15.8 1.2 %copy-done = bf16[2,264,1024]{2,1,0:T(8,128)(2,1)S(1)} copy-done((bf16[2,264,1024]{2,1,0:T(8,128)(2,1)S(1)}, bf16[2,264,1024]{2,1,0:T(8,128)(2,1)}, u32[]{:S(2)}) %copy-start) | copy-done | bytes 1081368
  17.1 1.8 %self.1 = (f32[56,256]{1,0:T(8,128)S(1)}, f32[4,256,128]{2,1,0:T(8,128)S(1)}) custom-call(f32[56,256]{1,0:T(8,128)S(1)} %broadcast_in_dim.3.rows_in, bf16[2,264,1024]{2,1,0:T(8,128)(2,1)S(1)} %copy-done, bf16[2,264,1024]{2,1,0:T(8,128)(2,1)S(1)} %collective-permute-done.refs_1_, s32[8]{0:T(128)S(1)} %copy-done.2), custom_call_target="tpu_custom_call" | custom-call | tf_op jit(solution)/shard_map/self/pallas_call | solution.py:220
  18.9 3.2 %collective-permute-done.2.refs_3_.b01a.refs_1_ = bf16[264,1024]{1,0:T(8,128)(2,1)S(1)} collective-permute-done((bf16[264,1024]{1,0:T(8,128)(2,1)}, bf16[264,1024]{1,0:T(8,128)(2,1)S(1)}, u32[]{:S(2)}, u32[]{:S(2)}) %collective-permute-start.2) | collective-permute-done | bytes 540704 | tf_op jit(solution)/shard_map/b01a/ppermute | solution.py:54
  22.1 1.9 %collective-permute-start.5 = (bf16[264,1024]{1,0:T(8,128)(2,1)S(1)}, bf16[264,1024]{1,0:T(8,128)(2,1)S(1)}, u32[]{:S(2)}, u32[]{:S(2)}) collective-permute-start(bf16[264,1024]{1,0:T(8,128)(2,1)S(1)} %collective-permute-done.2.refs_3_.b01a.refs_1_), channel_id=1, source_target_pairs={{0,16},{1,17},{2,18},{3,19},{4,20},{5,21},{6,22},{7,23},{8,24},{9,... | collective-permute-start | bytes 1622024 | tf_op jit(solution)/shard_map/prva/ppermute | solution.py:54
  25.0 5.1 %collective-permute-done.7.refs_6_.refs_4_.refs_1_ = bf16[2,264,1024]{2,1,0:T(8,128)(2,1)S(1)} collective-permute-done((bf16[2,264,1024]{2,1,0:T(8,128)(2,1)}, bf16[2,264,1024]{2,1,0:T(8,128)(2,1)S(1)}, u32[]{:S(2)}, u32[]{:S(2)}) %collective-permute-start.7) | collective-permute-done | bytes 1081376 | tf_op jit(solution)/shard_map/b10/ppermute | solution.py:54
  30.0 2.6 %collective-permute-done.6.refs_5_.refs_3_.refs_0_ = bf16[2,264,1024]{2,1,0:T(8,128)(2,1)S(1)} collective-permute-done((bf16[2,264,1024]{2,1,0:T(8,128)(2,1)}, bf16[2,264,1024]{2,1,0:T(8,128)(2,1)S(1)}, u32[]{:S(2)}, u32[]{:S(2)}) %collective-permute-start.6) | collective-permute-done | bytes 1081376 | tf_op jit(solution)/shard_map/b03/ppermute | solution.py:54
  33.3 1.9 %collective-permute-start.3 = (bf16[264,1024]{1,0:T(8,128)(2,1)S(1)}, bf16[264,1024]{1,0:T(8,128)(2,1)S(1)}, u32[]{:S(2)}, u32[]{:S(2)}) collective-permute-start(bf16[264,1024]{1,0:T(8,128)(2,1)S(1)} %collective-permute-done.1.refs_4_.b01b.refs_2_), channel_id=1, source_target_pairs={{0,16},{1,17},{2,18},{3,19},{4,20},{5,21},{6,22},{7,23},{8,24},{9,... | collective-permute-start | bytes 1622024 | tf_op jit(solution)/shard_map/prvb/ppermute | solution.py:54
  38.8 4.8 %same.1 = (f32[56,256]{1,0:T(8,128)S(1)}, f32[2,256,128]{2,1,0:T(8,128)S(1)}) custom-call(f32[56,256]{1,0:T(8,128)S(1)} %first.1.rows_in, bf16[2,264,1024]{2,1,0:T(8,128)(2,1)S(1)} %copy-done.1, bf16[2,264,1024]{2,1,0:T(8,128)(2,1)S(1)} %collective-permute-done.refs_1_, f32[4,256,128]{2,1,0:T(8,128)S(1)} %get-tuple-element.33.refs_2_, ...), custom_call_target="tpu_custom_call" | custom-call | tf_op jit(solution)/shard_map/same/pallas_call | solution.py:220
  43.7 2.4 %other.1.rows_in = f32[56,256]{1,0:T(8,128)S(1)} custom-call(f32[56,256]{1,0:T(8,128)S(1)} %get-tuple-element.44.rows_in, bf16[2,264,1024]{2,1,0:T(8,128)(2,1)S(1)} %copy-done.1, bf16[264,1024]{1,0:T(8,128)(2,1)S(1)} %collective-permute-done.2.refs_3_.b01a.refs_1_, bf16[264,1024]{1,0:T(8,128)(2,1)S(1)} %collective-permute-done.1.refs_4_.b01b.refs_2_, ...), custom_call_target="tpu_custom_call" | custom-call | tf_op jit(solution)/shard_map/other/pallas_call | solution.py:220
  46.4 1.5 %left.1.rows_in = f32[56,256]{1,0:T(8,128)S(1)} custom-call(f32[56,256]{1,0:T(8,128)S(1)} %other.1.rows_in, bf16[2,264,1024]{2,1,0:T(8,128)(2,1)S(1)} %copy-done.1, bf16[2,264,1024]{2,1,0:T(8,128)(2,1)S(1)} %collective-permute-done.refs_1_, f32[4,256,128]{2,1,0:T(8,128)S(1)} %get-tuple-element.33.refs_2_, ...), custom_call_target="tpu_custom_call" | custom-call | tf_op jit(solution)/shard_map/left/pallas_call | solution.py:220
  47.9 3.2 %collective-permute-done.3.refs_4_ = bf16[264,1024]{1,0:T(8,128)(2,1)S(1)} collective-permute-done((bf16[264,1024]{1,0:T(8,128)(2,1)S(1)}, bf16[264,1024]{1,0:T(8,128)(2,1)S(1)}, u32[]{:S(2)}, u32[]{:S(2)}) %collective-permute-start.3) | collective-permute-done | bytes 540704 | tf_op jit(solution)/shard_map/prvb/ppermute | solution.py:54
  51.1 1.3 %right.1.rows_in = f32[56,256]{1,0:T(8,128)S(1)} custom-call(f32[56,256]{1,0:T(8,128)S(1)} %left.1.rows_in, bf16[2,264,1024]{2,1,0:T(8,128)(2,1)S(1)} %copy-done.1, bf16[2,264,1024]{2,1,0:T(8,128)(2,1)S(1)} %collective-permute-done.refs_1_, f32[4,256,128]{2,1,0:T(8,128)S(1)} %get-tuple-element.33.refs_2_, ...), custom_call_target="tpu_custom_call" | custom-call | flops 102400000000 | tf_op jit(solution)/shard_map/right/pallas_call | solution.py:220
  52.5 1.7 %cross.1.rows_in = f32[56,256]{1,0:T(8,128)S(1)} custom-call(f32[56,256]{1,0:T(8,128)S(1)} %right.1.rows_in, bf16[2,264,1024]{2,1,0:T(8,128)(2,1)S(1)} %collective-permute-done.6.refs_5_.refs_3_.refs_0_, bf16[264,1024]{1,0:T(8,128)(2,1)S(1)} %collective-permute-done.10.refs_8_.refs_1_.refs_2_, ...), custom_call_target="tpu_custom_call" | custom-call | tf_op jit(solution)/shard_map/cross/pallas_call | solution.py:220
  54.7 1.8 %prev.1.rows_in = f32[56,256]{1,0:T(8,128)S(1)} custom-call(f32[56,256]{1,0:T(8,128)S(1)} %cross.1.rows_in, bf16[2,264,1024]{2,1,0:T(8,128)(2,1)S(1)} %collective-permute-done.6.refs_5_.refs_3_.refs_0_, bf16[2,264,1024]{2,1,0:T(8,128)(2,1)S(1)} %collective-permute-done.7.refs_6_.refs_4_.refs_1_, ...), custom_call_target="tpu_custom_call" | custom-call | tf_op jit(solution)/shard_map/prev/pallas_call | solution.py:220
  58.1 2.9 %collective-permute-start.18 = (f32[8,256]{1,0:T(8,128)S(1)}, f32[8,256]{1,0:T(8,128)S(1)}, u32[]{:S(2)}, u32[]{:S(2)}) collective-permute-start(f32[8,256]{1,0:T(8,128)S(1)} %get-tuple-element.55), channel_id=1, source_target_pairs={{0,118},{1,119},{2,116},{3,117},{4,122},{5,123},{6,120},{7,121},{8... | collective-permute-start | bytes 24584 | tf_op jit(solution)/shard_map/back_prv/ppermute | solution.py:54
  61.0 1.6 %collective-permute-start.17 = (f32[6,256]{1,0:T(8,128)S(1)}, f32[6,256]{1,0:T(8,128)S(1)}, u32[]{:S(2)}, u32[]{:S(2)}) collective-permute-start(f32[6,256]{1,0:T(8,128)S(1)} %get-tuple-element.54), channel_id=1, source_target_pairs={{0,4},{1,5},{2,6},{3,7},{4,8},{5,9},{6,10},{7,11},{8,12},{9,13},{1... | collective-permute-start | bytes 18440 | tf_op jit(solution)/shard_map/back_01/ppermute | solution.py:54
  62.6 1.7 %collective-permute-start.16 = (f32[4,256]{1,0:T(4,128)S(1)}, f32[4,256]{1,0:T(4,128)S(1)}, u32[]{:S(2)}, u32[]{:S(2)}) collective-permute-start(f32[4,256]{1,0:T(4,128)S(1)} %get-tuple-element.53), channel_id=1, source_target_pairs={{0,12},{1,13},{2,14},{3,15},{4,0},{5,1},{6,2},{7,3},{8,4},{9,5},{1... | collective-permute-start | bytes 12296 | tf_op jit(solution)/shard_map/back_03/ppermute | solution.py:54
  64.2 1.9 %collective-permute-done.16.b03 = f32[4,256]{1,0:T(4,128)S(1)} collective-permute-done((f32[4,256]{1,0:T(4,128)S(1)}, f32[4,256]{1,0:T(4,128)S(1)}, u32[]{:S(2)}, u32[]{:S(2)}) %collective-permute-start.16) | collective-permute-done | bytes 4128 | tf_op jit(solution)/shard_map/back_03/ppermute | solution.py:54
  (38 shorter events, 8.3 us)
Async XLA Ops:
  0.6 15.2 %copy-start.2 = (s32[8]{0:T(128)S(1)}, s32[8]{0:T(128)}, u32[]{:S(2)}) copy-start(s32[8]{0:T(128)} %refs_2_.1) | copy-start | bytes 100
  3.5 10.6 %collective-permute-start = (bf16[2,264,1024]{2,1,0:T(8,128)(2,1)}, bf16[2,264,1024]{2,1,0:T(8,128)(2,1)S(1)}, u32[]{:S(2)}, u32[]{:S(2)}) collective-permute-start(bf16[2,264,1024]{2,1,0:T(8,128)(2,1)} %get-tuple-element.30.refs_0_), channel_id=1, source_target_pairs={{0,1},{1,0},{2,3},{3,2},{4,5},{5,4},{6,7},{7,6},{8,9},{9,8},{10,11... | collective-permute-start | bytes 3244040 | tf_op jit(solution)/shard_map/ownx/ppermute | solution.py:54
  3.5 26.5 %collective-permute-start.7 = (bf16[2,264,1024]{2,1,0:T(8,128)(2,1)}, bf16[2,264,1024]{2,1,0:T(8,128)(2,1)S(1)}, u32[]{:S(2)}, u32[]{:S(2)}) collective-permute-start(bf16[2,264,1024]{2,1,0:T(8,128)(2,1)} %get-tuple-element.30.refs_0_), channel_id=1, source_target_pairs={{0,2},{1,3},{2,0},{3,1},{4,6},{5,7},{6,4},{7,5},{8,10},{9,11},{10,... | collective-permute-start | bytes 3244040 | tf_op jit(solution)/shard_map/b10/ppermute | solution.py:54
  5.2 27.4 %collective-permute-start.6 = (bf16[2,264,1024]{2,1,0:T(8,128)(2,1)}, bf16[2,264,1024]{2,1,0:T(8,128)(2,1)S(1)}, u32[]{:S(2)}, u32[]{:S(2)}) collective-permute-start(bf16[2,264,1024]{2,1,0:T(8,128)(2,1)} %get-tuple-element.30.refs_0_), channel_id=1, source_target_pairs={{0,4},{1,5},{2,6},{3,7},{4,8},{5,9},{6,10},{7,11},{8,12},{9,13},{1... | collective-permute-start | bytes 3244040 | tf_op jit(solution)/shard_map/b03/ppermute | solution.py:54
  6.8 15.4 %collective-permute-start.2 = (bf16[264,1024]{1,0:T(8,128)(2,1)}, bf16[264,1024]{1,0:T(8,128)(2,1)S(1)}, u32[]{:S(2)}, u32[]{:S(2)}) collective-permute-start(bf16[264,1024]{1,0:T(8,128)(2,1)} %get-tuple-element.34), channel_id=1, source_target_pairs={{0,12},{1,13},{2,14},{3,15},{4,0},{5,1},{6,2},{7,3},{8,4},{9,5},{1... | collective-permute-start | bytes 1622024 | tf_op jit(solution)/shard_map/b01a/ppermute | solution.py:54
  8.4 28.8 %collective-permute-start.4 = (bf16[2,264,1024]{2,1,0:T(8,128)(2,1)}, bf16[2,264,1024]{2,1,0:T(8,128)(2,1)S(1)}, u32[]{:S(2)}, u32[]{:S(2)}) collective-permute-start(bf16[2,264,1024]{2,1,0:T(8,128)(2,1)} %get-tuple-element.30.refs_0_), channel_id=1, source_target_pairs={{0,114},{1,115},{2,112},{3,113},{4,118},{5,119},{6,116},{7,117},{8... | collective-permute-start | bytes 3244040 | tf_op jit(solution)/shard_map/nxt/ppermute | solution.py:54
  14.0 19.3 %collective-permute-start.1 = (bf16[264,1024]{1,0:T(8,128)(2,1)}, bf16[264,1024]{1,0:T(8,128)(2,1)S(1)}, u32[]{:S(2)}, u32[]{:S(2)}) collective-permute-start(bf16[264,1024]{1,0:T(8,128)(2,1)} %get-tuple-element.31), channel_id=1, source_target_pairs={{0,12},{1,13},{2,14},{3,15},{4,0},{5,1},{6,2},{7,3},{8,4},{9,5},{1... | collective-permute-start | bytes 1622024 | tf_op jit(solution)/shard_map/b01b/ppermute | solution.py:54
  15.8 1.2 %copy-start = (bf16[2,264,1024]{2,1,0:T(8,128)(2,1)S(1)}, bf16[2,264,1024]{2,1,0:T(8,128)(2,1)}, u32[]{:S(2)}) copy-start(bf16[2,264,1024]{2,1,0:T(8,128)(2,1)} %get-tuple-element.30.refs_0_) | copy-start | bytes 3244036
  17.1 7.0 %copy-start.1 = (bf16[2,264,1024]{2,1,0:T(8,128)(2,1)S(1)}, bf16[2,264,1024]{2,1,0:T(8,128)(2,1)}, u32[]{:S(2)}) copy-start(bf16[2,264,1024]{2,1,0:T(8,128)(2,1)} %get-tuple-element.30.refs_0_) | copy-start | bytes 3244036
  22.1 15.9 %collective-permute-start.5 = (bf16[264,1024]{1,0:T(8,128)(2,1)S(1)}, bf16[264,1024]{1,0:T(8,128)(2,1)S(1)}, u32[]{:S(2)}, u32[]{:S(2)}) collective-permute-start(bf16[264,1024]{1,0:T(8,128)(2,1)S(1)} %collective-permute-done.2.refs_3_.b01a.refs_1_), channel_id=1, source_target_pairs={{0,16},{1,17},{2,18},{3,19},{4,20},{5,21},{6,22},{7,23},{8,24},{9,... | collective-permute-start | bytes 1622024 | tf_op jit(solution)/shard_map/prva/ppermute | solution.py:54
  32.7 13.7 %collective-permute-start.10 = (bf16[264,1024]{1,0:T(8,128)(2,1)S(1)}, bf16[264,1024]{1,0:T(8,128)(2,1)S(1)}, u32[]{:S(2)}, u32[]{:S(2)}) collective-permute-start(bf16[264,1024]{1,0:T(8,128)(2,1)S(1)} %slice_bitcast_fusion.1), channel_id=1, source_target_pairs={{0,2},{1,3},{2,0},{3,1},{4,6},{5,7},{6,4},{7,5},{8,10},{9,11},{10,... | collective-permute-start | bytes 1622024 | tf_op jit(solution)/shard_map/b13a/ppermute | solution.py:54
  33.3 17.8 %collective-permute-start.3 = (bf16[264,1024]{1,0:T(8,128)(2,1)S(1)}, bf16[264,1024]{1,0:T(8,128)(2,1)S(1)}, u32[]{:S(2)}, u32[]{:S(2)}) collective-permute-start(bf16[264,1024]{1,0:T(8,128)(2,1)S(1)} %collective-permute-done.1.refs_4_.b01b.refs_2_), channel_id=1, source_target_pairs={{0,16},{1,17},{2,18},{3,19},{4,20},{5,21},{6,22},{7,23},{8,24},{9,... | collective-permute-start | bytes 1622024 | tf_op jit(solution)/shard_map/prvb/ppermute | solution.py:54
  35.2 15.9 %collective-permute-start.11 = (bf16[264,1024]{1,0:T(8,128)(2,1)S(1)}, bf16[264,1024]{1,0:T(8,128)(2,1)S(1)}, u32[]{:S(2)}, u32[]{:S(2)}) collective-permute-start(bf16[264,1024]{1,0:T(8,128)(2,1)S(1)} %slice_bitcast_fusion), channel_id=1, source_target_pairs={{0,4},{1,5},{2,6},{3,7},{4,8},{5,9},{6,10},{7,11},{8,12},{9,13},{1... | collective-permute-start | bytes 1622024 | tf_op jit(solution)/shard_map/b13b/ppermute | solution.py:54
  38.2 5.4 %collective-permute-start.8 = (bf16[256,1024]{1,0:T(8,128)(2,1)S(1)}, bf16[256,1024]{1,0:T(8,128)(2,1)S(1)}, u32[]{:S(2)}, u32[]{:S(2)}) collective-permute-start(bf16[256,1024]{1,0:T(8,128)(2,1)S(1)} %get-tuple-element.45), channel_id=1, source_target_pairs={{0,1},{1,0},{2,3},{3,2},{4,5},{5,4},{6,7},{7,6},{8,9},{9,8},{10,11... | collective-permute-start | bytes 1572872 | tf_op jit(solution)/shard_map/nxtax/ppermute | solution.py:54
  38.3 5.3 %collective-permute-start.9 = (bf16[256,1024]{1,0:T(8,128)(2,1)S(1)}, bf16[256,1024]{1,0:T(8,128)(2,1)S(1)}, u32[]{:S(2)}, u32[]{:S(2)}) collective-permute-start(bf16[256,1024]{1,0:T(8,128)(2,1)S(1)} %get-tuple-element.46), channel_id=1, source_target_pairs={{0,1},{1,0},{2,3},{3,2},{4,5},{5,4},{6,7},{7,6},{8,9},{9,8},{10,11... | collective-permute-start | bytes 1572872 | tf_op jit(solution)/shard_map/nxtbx/ppermute | solution.py:54
  46.1 6.4 %collective-permute-start.12 = (bf16[3,264,1024]{2,1,0:T(8,128)(2,1)S(1)}, bf16[3,264,1024]{2,1,0:T(8,128)(2,1)S(1)}, u32[]{:S(2)}, u32[]{:S(2)}) collective-permute-start(bf16[3,264,1024]{2,1,0:T(8,128)(2,1)S(1)} %get-tuple-element.50), channel_id=1, source_target_pairs={{0,1},{1,0},{2,3},{3,2},{4,5},{5,4},{6,7},{7,6},{8,9},{9,8},{10,11... | collective-permute-start | bytes 4866056 | tf_op jit(solution)/shard_map/cross/ppermute | solution.py:54
  51.1 3.6 %collective-permute-start.13 = (bf16[264,1024]{1,0:T(8,128)(2,1)S(1)}, bf16[264,1024]{1,0:T(8,128)(2,1)S(1)}, u32[]{:S(2)}, u32[]{:S(2)}) collective-permute-start(bf16[264,1024]{1,0:T(8,128)(2,1)S(1)} %collective-permute-done.3.refs_4_), channel_id=1, source_target_pairs={{0,1},{1,0},{2,3},{3,2},{4,5},{5,4},{6,7},{7,6},{8,9},{9,8},{10,11... | collective-permute-start | bytes 1622024 | tf_op jit(solution)/shard_map/prvbx/ppermute | solution.py:54
  54.2 4.0 %collective-permute-start.15 = (f32[8,256]{1,0:T(8,128)S(1)}, f32[8,256]{1,0:T(8,128)S(1)}, u32[]{:S(2)}, u32[]{:S(2)}) collective-permute-start(f32[8,256]{1,0:T(8,128)S(1)} %slice.17), channel_id=1, source_target_pairs={{0,2},{1,3},{2,0},{3,1},{4,6},{5,7},{6,4},{7,5},{8,10},{9,11},{10,... | collective-permute-start | bytes 24584 | tf_op jit(solution)/shard_map/side/ppermute | solution.py:54
  56.6 1.4 %collective-permute-start.14 = (f32[6,256]{1,0:T(8,128)S(1)}, f32[6,256]{1,0:T(8,128)S(1)}, u32[]{:S(2)}, u32[]{:S(2)}) collective-permute-start(f32[6,256]{1,0:T(8,128)S(1)} %slice.16), channel_id=1, source_target_pairs={{0,1},{1,0},{2,3},{3,2},{4,5},{5,4},{6,7},{7,6},{8,9},{9,8},{10,11... | collective-permute-start | bytes 18440 | tf_op jit(solution)/shard_map/swapped/ppermute | solution.py:54
  58.1 8.0 %collective-permute-start.18 = (f32[8,256]{1,0:T(8,128)S(1)}, f32[8,256]{1,0:T(8,128)S(1)}, u32[]{:S(2)}, u32[]{:S(2)}) collective-permute-start(f32[8,256]{1,0:T(8,128)S(1)} %get-tuple-element.55), channel_id=1, source_target_pairs={{0,118},{1,119},{2,116},{3,117},{4,122},{5,123},{6,120},{7,121},{8... | collective-permute-start | bytes 24584 | tf_op jit(solution)/shard_map/back_prv/ppermute | solution.py:54
  61.0 5.2 %collective-permute-start.17 = (f32[6,256]{1,0:T(8,128)S(1)}, f32[6,256]{1,0:T(8,128)S(1)}, u32[]{:S(2)}, u32[]{:S(2)}) collective-permute-start(f32[6,256]{1,0:T(8,128)S(1)} %get-tuple-element.54), channel_id=1, source_target_pairs={{0,4},{1,5},{2,6},{3,7},{4,8},{5,9},{6,10},{7,11},{8,12},{9,13},{1... | collective-permute-start | bytes 18440 | tf_op jit(solution)/shard_map/back_01/ppermute | solution.py:54
  62.6 3.6 %collective-permute-start.16 = (f32[4,256]{1,0:T(4,128)S(1)}, f32[4,256]{1,0:T(4,128)S(1)}, u32[]{:S(2)}, u32[]{:S(2)}) collective-permute-start(f32[4,256]{1,0:T(4,128)S(1)} %get-tuple-element.53), channel_id=1, source_target_pairs={{0,12},{1,13},{2,14},{3,15},{4,0},{5,1},{6,2},{7,3},{8,4},{9,5},{1... | collective-permute-start | bytes 12296 | tf_op jit(solution)/shard_map/back_03/ppermute | solution.py:54

commit v8 on v7

--- a/solution.py
+++ b/solution.py
@@ -10,7 +10,7 @@
 
 D = 1024
 HALF = 256
-EXTRA = 8
+EXTRA = 16
 PAY = HALF + EXTRA
 BASE = 64
 FAR = 8192.0

time: 67 us -> 68 us (1.015)
  waiting for transfers between devices: 18 us -> 19.1 us
    ppermute x19, waiting for transfers between devices: 18 us -> 19.1 us  [send(): return lax.ppermute(value, AXES, pairs(**shift))]
  transfers between devices with their start and end apart: 19 -> 19, of which waited for: 8 -> 9; matrix products, arithmetic and copies ran while one was open for 0% -> 0% of each run, Pallas kernels for 26% -> 26%
where the time goes in v8:
time: 68 us; the launch traced here: 67.8 us
  starting transfers between devices  25.7 us (38%)
  Pallas kernels  20.9 us (31%)
  waiting for transfers between devices  19.1 us (28%)
  local copies, waits for them, and re-layouts  1.34 us (2%)
  between operations  0.8 us (1%)
    ppermute x19, starting transfers between devices, send(): return lax.ppermute(value, AXES, pairs(**shift))  25.7 us
    ppermute x19, waiting for transfers between devices, send(): return lax.ppermute(value, AXES, pairs(**shift))  19.1 us
    pallas_call x9, Pallas kernels, kernel_call(): pl.pallas_call(kernel, in_specs=[VMEM] * (1 + len(arrays)) + [SMEM] * len...  17.3 us
    pallas_call x1, Pallas kernels, packed(): pl.pallas_call(pack_kernel, in_specs=[pl.BlockSpec(memory_space=pltpu.HBM...  2.82 us
  transfers between devices with their start and end apart: 19, of which 9 were waited for; matrix products, arithmetic and copies ran while one was open for 0% of the time, Pallas kernels for 26%

profile of v8, /device:TPU:0, one launch (start us, length us, event | category | flops | bytes accessed | tf_op | source)
XLA Modules:
  0.0 67.8 jit_solution(2477295538738046052)
XLA Ops:
  0.6 2.8 %pack.1 = (bf16[2,272,1024]{2,1,0:T(8,128)(2,1)}, bf16[272,1024]{1,0:T(8,128)(2,1)}, bf16[272,1024]{1,0:T(8,128)(2,1)}) custom-call(s32[8]{0:T(128)} %refs_2_.1, f32[512,1024]{1,0:T(8,128)} %bitcast.5, s32[1,512]{1,0:T(1,128)} %rank_hbm.1), custom_call_target="tpu_custom_call" | custom-call | flops 2097152 | bytes 4194304 | tf_op jit(solution)/shard_map/pack/pallas_call | solution.py:114
  3.6 1.7 %collective-permute-start.7 = (bf16[2,272,1024]{2,1,0:T(8,128)(2,1)}, bf16[2,272,1024]{2,1,0:T(8,128)(2,1)S(1)}, u32[]{:S(2)}, u32[]{:S(2)}) collective-permute-start(bf16[2,272,1024]{2,1,0:T(8,128)(2,1)} %get-tuple-element.30.refs_0_), channel_id=1, source_target_pairs={{0,2},{1,3},{2,0},{3,1},{4,6},{5,7},{6,4},{7,5},{8,10},{9,11},{10,... | collective-permute-start | bytes 3342344 | tf_op jit(solution)/shard_map/b10/ppermute | solution.py:54
  5.2 1.6 %collective-permute-start.6 = (bf16[2,272,1024]{2,1,0:T(8,128)(2,1)}, bf16[2,272,1024]{2,1,0:T(8,128)(2,1)S(1)}, u32[]{:S(2)}, u32[]{:S(2)}) collective-permute-start(bf16[2,272,1024]{2,1,0:T(8,128)(2,1)} %get-tuple-element.30.refs_0_), channel_id=1, source_target_pairs={{0,4},{1,5},{2,6},{3,7},{4,8},{5,9},{6,10},{7,11},{8,12},{9,13},{1... | collective-permute-start | bytes 3342344 | tf_op jit(solution)/shard_map/b03/ppermute | solution.py:54
  6.8 1.7 %collective-permute-start.2 = (bf16[272,1024]{1,0:T(8,128)(2,1)}, bf16[272,1024]{1,0:T(8,128)(2,1)S(1)}, u32[]{:S(2)}, u32[]{:S(2)}) collective-permute-start(bf16[272,1024]{1,0:T(8,128)(2,1)} %get-tuple-element.34), channel_id=1, source_target_pairs={{0,12},{1,13},{2,14},{3,15},{4,0},{5,1},{6,2},{7,3},{8,4},{9,5},{1... | collective-permute-start | bytes 1671176 | tf_op jit(solution)/shard_map/b01a/ppermute | solution.py:54
  8.5 5.6 %collective-permute-start.4 = (bf16[2,272,1024]{2,1,0:T(8,128)(2,1)}, bf16[2,272,1024]{2,1,0:T(8,128)(2,1)S(1)}, u32[]{:S(2)}, u32[]{:S(2)}) collective-permute-start(bf16[2,272,1024]{2,1,0:T(8,128)(2,1)} %get-tuple-element.30.refs_0_), channel_id=1, source_target_pairs={{0,114},{1,115},{2,112},{3,113},{4,118},{5,119},{6,116},{7,117},{8... | collective-permute-start | bytes 3342344 | tf_op jit(solution)/shard_map/nxt/ppermute | solution.py:54
  14.0 1.8 %collective-permute-start.1 = (bf16[272,1024]{1,0:T(8,128)(2,1)}, bf16[272,1024]{1,0:T(8,128)(2,1)S(1)}, u32[]{:S(2)}, u32[]{:S(2)}) collective-permute-start(bf16[272,1024]{1,0:T(8,128)(2,1)} %get-tuple-element.31), channel_id=1, source_target_pairs={{0,12},{1,13},{2,14},{3,15},{4,0},{5,1},{6,2},{7,3},{8,4},{9,5},{1... | collective-permute-start | bytes 1671176 | tf_op jit(solution)/shard_map/b01b/ppermute | solution.py:54
  15.8 1.2 %copy-done = bf16[2,272,1024]{2,1,0:T(8,128)(2,1)S(1)} copy-done((bf16[2,272,1024]{2,1,0:T(8,128)(2,1)S(1)}, bf16[2,272,1024]{2,1,0:T(8,128)(2,1)}, u32[]{:S(2)}) %copy-start) | copy-done | bytes 1114136
  17.1 1.8 %self.1 = (f32[56,256]{1,0:T(8,128)S(1)}, f32[4,256,128]{2,1,0:T(8,128)S(1)}) custom-call(f32[56,256]{1,0:T(8,128)S(1)} %broadcast_in_dim.3.rows_in, bf16[2,272,1024]{2,1,0:T(8,128)(2,1)S(1)} %copy-done, bf16[2,272,1024]{2,1,0:T(8,128)(2,1)S(1)} %collective-permute-done.refs_1_, s32[8]{0:T(128)S(1)} %copy-done.2), custom_call_target="tpu_custom_call" | custom-call | tf_op jit(solution)/shard_map/self/pallas_call | solution.py:220
  18.9 3.6 %collective-permute-done.2.refs_3_.b01a.refs_1_ = bf16[272,1024]{1,0:T(8,128)(2,1)S(1)} collective-permute-done((bf16[272,1024]{1,0:T(8,128)(2,1)}, bf16[272,1024]{1,0:T(8,128)(2,1)S(1)}, u32[]{:S(2)}, u32[]{:S(2)}) %collective-permute-start.2) | collective-permute-done | bytes 557088 | tf_op jit(solution)/shard_map/b01a/ppermute | solution.py:54
  22.5 1.9 %collective-permute-start.5 = (bf16[272,1024]{1,0:T(8,128)(2,1)S(1)}, bf16[272,1024]{1,0:T(8,128)(2,1)S(1)}, u32[]{:S(2)}, u32[]{:S(2)}) collective-permute-start(bf16[272,1024]{1,0:T(8,128)(2,1)S(1)} %collective-permute-done.2.refs_3_.b01a.refs_1_), channel_id=1, source_target_pairs={{0,16},{1,17},{2,18},{3,19},{4,20},{5,21},{6,22},{7,23},{8,24},{9,... | collective-permute-start | bytes 1671176 | tf_op jit(solution)/shard_map/prva/ppermute | solution.py:54
  25.3 5.4 %collective-permute-done.7.refs_6_.refs_4_.refs_1_ = bf16[2,272,1024]{2,1,0:T(8,128)(2,1)S(1)} collective-permute-done((bf16[2,272,1024]{2,1,0:T(8,128)(2,1)}, bf16[2,272,1024]{2,1,0:T(8,128)(2,1)S(1)}, u32[]{:S(2)}, u32[]{:S(2)}) %collective-permute-start.7) | collective-permute-done | bytes 1114144 | tf_op jit(solution)/shard_map/b10/ppermute | solution.py:54
  30.8 2.6 %collective-permute-done.6.refs_5_.refs_3_.refs_0_ = bf16[2,272,1024]{2,1,0:T(8,128)(2,1)S(1)} collective-permute-done((bf16[2,272,1024]{2,1,0:T(8,128)(2,1)}, bf16[2,272,1024]{2,1,0:T(8,128)(2,1)S(1)}, u32[]{:S(2)}, u32[]{:S(2)}) %collective-permute-start.6) | collective-permute-done | bytes 1114144 | tf_op jit(solution)/shard_map/b03/ppermute | solution.py:54
  34.0 1.9 %collective-permute-start.3 = (bf16[272,1024]{1,0:T(8,128)(2,1)S(1)}, bf16[272,1024]{1,0:T(8,128)(2,1)S(1)}, u32[]{:S(2)}, u32[]{:S(2)}) collective-permute-start(bf16[272,1024]{1,0:T(8,128)(2,1)S(1)} %collective-permute-done.1.refs_4_.b01b.refs_2_), channel_id=1, source_target_pairs={{0,16},{1,17},{2,18},{3,19},{4,20},{5,21},{6,22},{7,23},{8,24},{9,... | collective-permute-start | bytes 1671176 | tf_op jit(solution)/shard_map/prvb/ppermute | solution.py:54
  39.5 4.8 %same.1 = (f32[56,256]{1,0:T(8,128)S(1)}, f32[2,256,128]{2,1,0:T(8,128)S(1)}) custom-call(f32[56,256]{1,0:T(8,128)S(1)} %first.1.rows_in, bf16[2,272,1024]{2,1,0:T(8,128)(2,1)S(1)} %copy-done.1, bf16[2,272,1024]{2,1,0:T(8,128)(2,1)S(1)} %collective-permute-done.refs_1_, f32[4,256,128]{2,1,0:T(8,128)S(1)} %get-tuple-element.33.refs_2_, ...), custom_call_target="tpu_custom_call" | custom-call | tf_op jit(solution)/shard_map/same/pallas_call | solution.py:220
  44.4 2.4 %other.1.rows_in = f32[56,256]{1,0:T(8,128)S(1)} custom-call(f32[56,256]{1,0:T(8,128)S(1)} %get-tuple-element.44.rows_in, bf16[2,272,1024]{2,1,0:T(8,128)(2,1)S(1)} %copy-done.1, bf16[272,1024]{1,0:T(8,128)(2,1)S(1)} %collective-permute-done.2.refs_3_.b01a.refs_1_, bf16[272,1024]{1,0:T(8,128)(2,1)S(1)} %collective-permute-done.1.refs_4_.b01b.refs_2_, ...), custom_call_target="tpu_custom_call" | custom-call | tf_op jit(solution)/shard_map/other/pallas_call | solution.py:220
  47.4 1.5 %left.1.rows_in = f32[56,256]{1,0:T(8,128)S(1)} custom-call(f32[56,256]{1,0:T(8,128)S(1)} %other.1.rows_in, bf16[2,272,1024]{2,1,0:T(8,128)(2,1)S(1)} %copy-done.1, bf16[2,272,1024]{2,1,0:T(8,128)(2,1)S(1)} %collective-permute-done.refs_1_, f32[4,256,128]{2,1,0:T(8,128)S(1)} %get-tuple-element.33.refs_2_, ...), custom_call_target="tpu_custom_call" | custom-call | tf_op jit(solution)/shard_map/left/pallas_call | solution.py:220
  48.9 3.3 %collective-permute-done.3.refs_4_ = bf16[272,1024]{1,0:T(8,128)(2,1)S(1)} collective-permute-done((bf16[272,1024]{1,0:T(8,128)(2,1)S(1)}, bf16[272,1024]{1,0:T(8,128)(2,1)S(1)}, u32[]{:S(2)}, u32[]{:S(2)}) %collective-permute-start.3) | collective-permute-done | bytes 557088 | tf_op jit(solution)/shard_map/prvb/ppermute | solution.py:54
  52.2 1.3 %right.1.rows_in = f32[56,256]{1,0:T(8,128)S(1)} custom-call(f32[56,256]{1,0:T(8,128)S(1)} %left.1.rows_in, bf16[2,272,1024]{2,1,0:T(8,128)(2,1)S(1)} %copy-done.1, bf16[2,272,1024]{2,1,0:T(8,128)(2,1)S(1)} %collective-permute-done.refs_1_, f32[4,256,128]{2,1,0:T(8,128)S(1)} %get-tuple-element.33.refs_2_, ...), custom_call_target="tpu_custom_call" | custom-call | flops 102400000000 | tf_op jit(solution)/shard_map/right/pallas_call | solution.py:220
  53.5 1.7 %cross.1.rows_in = f32[56,256]{1,0:T(8,128)S(1)} custom-call(f32[56,256]{1,0:T(8,128)S(1)} %right.1.rows_in, bf16[2,272,1024]{2,1,0:T(8,128)(2,1)S(1)} %collective-permute-done.6.refs_5_.refs_3_.refs_0_, bf16[272,1024]{1,0:T(8,128)(2,1)S(1)} %collective-permute-done.10.refs_8_.refs_1_.refs_2_, ...), custom_call_target="tpu_custom_call" | custom-call | tf_op jit(solution)/shard_map/cross/pallas_call | solution.py:220
  55.8 1.8 %prev.1.rows_in = f32[56,256]{1,0:T(8,128)S(1)} custom-call(f32[56,256]{1,0:T(8,128)S(1)} %cross.1.rows_in, bf16[2,272,1024]{2,1,0:T(8,128)(2,1)S(1)} %collective-permute-done.6.refs_5_.refs_3_.refs_0_, bf16[2,272,1024]{2,1,0:T(8,128)(2,1)S(1)} %collective-permute-done.7.refs_6_.refs_4_.refs_1_, ...), custom_call_target="tpu_custom_call" | custom-call | tf_op jit(solution)/shard_map/prev/pallas_call | solution.py:220
  59.2 2.8 %collective-permute-start.18 = (f32[8,256]{1,0:T(8,128)S(1)}, f32[8,256]{1,0:T(8,128)S(1)}, u32[]{:S(2)}, u32[]{:S(2)}) collective-permute-start(f32[8,256]{1,0:T(8,128)S(1)} %get-tuple-element.55), channel_id=1, source_target_pairs={{0,118},{1,119},{2,116},{3,117},{4,122},{5,123},{6,120},{7,121},{8... | collective-permute-start | bytes 24584 | tf_op jit(solution)/shard_map/back_prv/ppermute | solution.py:54
  62.1 1.6 %collective-permute-start.17 = (f32[6,256]{1,0:T(8,128)S(1)}, f32[6,256]{1,0:T(8,128)S(1)}, u32[]{:S(2)}, u32[]{:S(2)}) collective-permute-start(f32[6,256]{1,0:T(8,128)S(1)} %get-tuple-element.54), channel_id=1, source_target_pairs={{0,4},{1,5},{2,6},{3,7},{4,8},{5,9},{6,10},{7,11},{8,12},{9,13},{1... | collective-permute-start | bytes 18440 | tf_op jit(solution)/shard_map/back_01/ppermute | solution.py:54
  63.6 1.7 %collective-permute-start.16 = (f32[4,256]{1,0:T(4,128)S(1)}, f32[4,256]{1,0:T(4,128)S(1)}, u32[]{:S(2)}, u32[]{:S(2)}) collective-permute-start(f32[4,256]{1,0:T(4,128)S(1)} %get-tuple-element.53), channel_id=1, source_target_pairs={{0,12},{1,13},{2,14},{3,15},{4,0},{5,1},{6,2},{7,3},{8,4},{9,5},{1... | collective-permute-start | bytes 12296 | tf_op jit(solution)/shard_map/back_03/ppermute | solution.py:54
  65.3 1.9 %collective-permute-done.16.b03 = f32[4,256]{1,0:T(4,128)S(1)} collective-permute-done((f32[4,256]{1,0:T(4,128)S(1)}, f32[4,256]{1,0:T(4,128)S(1)}, u32[]{:S(2)}, u32[]{:S(2)}) %collective-permute-start.16) | collective-permute-done | bytes 4128 | tf_op jit(solution)/shard_map/back_03/ppermute | solution.py:54
  (38 shorter events, 8.6 us)
Async XLA Ops:
  0.6 15.2 %copy-start.2 = (s32[8]{0:T(128)S(1)}, s32[8]{0:T(128)}, u32[]{:S(2)}) copy-start(s32[8]{0:T(128)} %refs_2_.1) | copy-start | bytes 100
  3.5 10.6 %collective-permute-start = (bf16[2,272,1024]{2,1,0:T(8,128)(2,1)}, bf16[2,272,1024]{2,1,0:T(8,128)(2,1)S(1)}, u32[]{:S(2)}, u32[]{:S(2)}) collective-permute-start(bf16[2,272,1024]{2,1,0:T(8,128)(2,1)} %get-tuple-element.30.refs_0_), channel_id=1, source_target_pairs={{0,1},{1,0},{2,3},{3,2},{4,5},{5,4},{6,7},{7,6},{8,9},{9,8},{10,11... | collective-permute-start | bytes 3342344 | tf_op jit(solution)/shard_map/ownx/ppermute | solution.py:54
  3.6 27.2 %collective-permute-start.7 = (bf16[2,272,1024]{2,1,0:T(8,128)(2,1)}, bf16[2,272,1024]{2,1,0:T(8,128)(2,1)S(1)}, u32[]{:S(2)}, u32[]{:S(2)}) collective-permute-start(bf16[2,272,1024]{2,1,0:T(8,128)(2,1)} %get-tuple-element.30.refs_0_), channel_id=1, source_target_pairs={{0,2},{1,3},{2,0},{3,1},{4,6},{5,7},{6,4},{7,5},{8,10},{9,11},{10,... | collective-permute-start | bytes 3342344 | tf_op jit(solution)/shard_map/b10/ppermute | solution.py:54
  5.2 28.1 %collective-permute-start.6 = (bf16[2,272,1024]{2,1,0:T(8,128)(2,1)}, bf16[2,272,1024]{2,1,0:T(8,128)(2,1)S(1)}, u32[]{:S(2)}, u32[]{:S(2)}) collective-permute-start(bf16[2,272,1024]{2,1,0:T(8,128)(2,1)} %get-tuple-element.30.refs_0_), channel_id=1, source_target_pairs={{0,4},{1,5},{2,6},{3,7},{4,8},{5,9},{6,10},{7,11},{8,12},{9,13},{1... | collective-permute-start | bytes 3342344 | tf_op jit(solution)/shard_map/b03/ppermute | solution.py:54
  6.8 15.7 %collective-permute-start.2 = (bf16[272,1024]{1,0:T(8,128)(2,1)}, bf16[272,1024]{1,0:T(8,128)(2,1)S(1)}, u32[]{:S(2)}, u32[]{:S(2)}) collective-permute-start(bf16[272,1024]{1,0:T(8,128)(2,1)} %get-tuple-element.34), channel_id=1, source_target_pairs={{0,12},{1,13},{2,14},{3,15},{4,0},{5,1},{6,2},{7,3},{8,4},{9,5},{1... | collective-permute-start | bytes 1671176 | tf_op jit(solution)/shard_map/b01a/ppermute | solution.py:54
  8.5 29.5 %collective-permute-start.4 = (bf16[2,272,1024]{2,1,0:T(8,128)(2,1)}, bf16[2,272,1024]{2,1,0:T(8,128)(2,1)S(1)}, u32[]{:S(2)}, u32[]{:S(2)}) collective-permute-start(bf16[2,272,1024]{2,1,0:T(8,128)(2,1)} %get-tuple-element.30.refs_0_), channel_id=1, source_target_pairs={{0,114},{1,115},{2,112},{3,113},{4,118},{5,119},{6,116},{7,117},{8... | collective-permute-start | bytes 3342344 | tf_op jit(solution)/shard_map/nxt/ppermute | solution.py:54
  14.0 20.0 %collective-permute-start.1 = (bf16[272,1024]{1,0:T(8,128)(2,1)}, bf16[272,1024]{1,0:T(8,128)(2,1)S(1)}, u32[]{:S(2)}, u32[]{:S(2)}) collective-permute-start(bf16[272,1024]{1,0:T(8,128)(2,1)} %get-tuple-element.31), channel_id=1, source_target_pairs={{0,12},{1,13},{2,14},{3,15},{4,0},{5,1},{6,2},{7,3},{8,4},{9,5},{1... | collective-permute-start | bytes 1671176 | tf_op jit(solution)/shard_map/b01b/ppermute | solution.py:54
  15.8 1.2 %copy-start = (bf16[2,272,1024]{2,1,0:T(8,128)(2,1)S(1)}, bf16[2,272,1024]{2,1,0:T(8,128)(2,1)}, u32[]{:S(2)}) copy-start(bf16[2,272,1024]{2,1,0:T(8,128)(2,1)} %get-tuple-element.30.refs_0_) | copy-start | bytes 3342340
  17.1 7.3 %copy-start.1 = (bf16[2,272,1024]{2,1,0:T(8,128)(2,1)S(1)}, bf16[2,272,1024]{2,1,0:T(8,128)(2,1)}, u32[]{:S(2)}) copy-start(bf16[2,272,1024]{2,1,0:T(8,128)(2,1)} %get-tuple-element.30.refs_0_) | copy-start | bytes 3342340
  22.5 16.3 %collective-permute-start.5 = (bf16[272,1024]{1,0:T(8,128)(2,1)S(1)}, bf16[272,1024]{1,0:T(8,128)(2,1)S(1)}, u32[]{:S(2)}, u32[]{:S(2)}) collective-permute-start(bf16[272,1024]{1,0:T(8,128)(2,1)S(1)} %collective-permute-done.2.refs_3_.b01a.refs_1_), channel_id=1, source_target_pairs={{0,16},{1,17},{2,18},{3,19},{4,20},{5,21},{6,22},{7,23},{8,24},{9,... | collective-permute-start | bytes 1671176 | tf_op jit(solution)/shard_map/prva/ppermute | solution.py:54
  33.4 14.0 %collective-permute-start.10 = (bf16[272,1024]{1,0:T(8,128)(2,1)S(1)}, bf16[272,1024]{1,0:T(8,128)(2,1)S(1)}, u32[]{:S(2)}, u32[]{:S(2)}) collective-permute-start(bf16[272,1024]{1,0:T(8,128)(2,1)S(1)} %slice_bitcast_fusion.1), channel_id=1, source_target_pairs={{0,2},{1,3},{2,0},{3,1},{4,6},{5,7},{6,4},{7,5},{8,10},{9,11},{10,... | collective-permute-start | bytes 1671176 | tf_op jit(solution)/shard_map/b13a/ppermute | solution.py:54
  34.0 18.2 %collective-permute-start.3 = (bf16[272,1024]{1,0:T(8,128)(2,1)S(1)}, bf16[272,1024]{1,0:T(8,128)(2,1)S(1)}, u32[]{:S(2)}, u32[]{:S(2)}) collective-permute-start(bf16[272,1024]{1,0:T(8,128)(2,1)S(1)} %collective-permute-done.1.refs_4_.b01b.refs_2_), channel_id=1, source_target_pairs={{0,16},{1,17},{2,18},{3,19},{4,20},{5,21},{6,22},{7,23},{8,24},{9,... | collective-permute-start | bytes 1671176 | tf_op jit(solution)/shard_map/prvb/ppermute | solution.py:54
  36.0 16.2 %collective-permute-start.11 = (bf16[272,1024]{1,0:T(8,128)(2,1)S(1)}, bf16[272,1024]{1,0:T(8,128)(2,1)S(1)}, u32[]{:S(2)}, u32[]{:S(2)}) collective-permute-start(bf16[272,1024]{1,0:T(8,128)(2,1)S(1)} %slice_bitcast_fusion), channel_id=1, source_target_pairs={{0,4},{1,5},{2,6},{3,7},{4,8},{5,9},{6,10},{7,11},{8,12},{9,13},{1... | collective-permute-start | bytes 1671176 | tf_op jit(solution)/shard_map/b13b/ppermute | solution.py:54
  38.9 5.4 %collective-permute-start.8 = (bf16[256,1024]{1,0:T(8,128)(2,1)S(1)}, bf16[256,1024]{1,0:T(8,128)(2,1)S(1)}, u32[]{:S(2)}, u32[]{:S(2)}) collective-permute-start(bf16[256,1024]{1,0:T(8,128)(2,1)S(1)} %get-tuple-element.45), channel_id=1, source_target_pairs={{0,1},{1,0},{2,3},{3,2},{4,5},{5,4},{6,7},{7,6},{8,9},{9,8},{10,11... | collective-permute-start | bytes 1572872 | tf_op jit(solution)/shard_map/nxtax/ppermute | solution.py:54
  39.0 5.3 %collective-permute-start.9 = (bf16[256,1024]{1,0:T(8,128)(2,1)S(1)}, bf16[256,1024]{1,0:T(8,128)(2,1)S(1)}, u32[]{:S(2)}, u32[]{:S(2)}) collective-permute-start(bf16[256,1024]{1,0:T(8,128)(2,1)S(1)} %get-tuple-element.46), channel_id=1, source_target_pairs={{0,1},{1,0},{2,3},{3,2},{4,5},{5,4},{6,7},{7,6},{8,9},{9,8},{10,11... | collective-permute-start | bytes 1572872 | tf_op jit(solution)/shard_map/nxtbx/ppermute | solution.py:54
  46.8 6.8 %collective-permute-start.12 = (bf16[3,272,1024]{2,1,0:T(8,128)(2,1)S(1)}, bf16[3,272,1024]{2,1,0:T(8,128)(2,1)S(1)}, u32[]{:S(2)}, u32[]{:S(2)}) collective-permute-start(bf16[3,272,1024]{2,1,0:T(8,128)(2,1)S(1)} %get-tuple-element.50), channel_id=1, source_target_pairs={{0,1},{1,0},{2,3},{3,2},{4,5},{5,4},{6,7},{7,6},{8,9},{9,8},{10,11... | collective-permute-start | bytes 5013512 | tf_op jit(solution)/shard_map/cross/ppermute | solution.py:54
  52.2 3.6 %collective-permute-start.13 = (bf16[272,1024]{1,0:T(8,128)(2,1)S(1)}, bf16[272,1024]{1,0:T(8,128)(2,1)S(1)}, u32[]{:S(2)}, u32[]{:S(2)}) collective-permute-start(bf16[272,1024]{1,0:T(8,128)(2,1)S(1)} %collective-permute-done.3.refs_4_), channel_id=1, source_target_pairs={{0,1},{1,0},{2,3},{3,2},{4,5},{5,4},{6,7},{7,6},{8,9},{9,8},{10,11... | collective-permute-start | bytes 1671176 | tf_op jit(solution)/shard_map/prvbx/ppermute | solution.py:54
  55.2 4.0 %collective-permute-start.15 = (f32[8,256]{1,0:T(8,128)S(1)}, f32[8,256]{1,0:T(8,128)S(1)}, u32[]{:S(2)}, u32[]{:S(2)}) collective-permute-start(f32[8,256]{1,0:T(8,128)S(1)} %slice.17), channel_id=1, source_target_pairs={{0,2},{1,3},{2,0},{3,1},{4,6},{5,7},{6,4},{7,5},{8,10},{9,11},{10,... | collective-permute-start | bytes 24584 | tf_op jit(solution)/shard_map/side/ppermute | solution.py:54
  57.6 1.4 %collective-permute-start.14 = (f32[6,256]{1,0:T(8,128)S(1)}, f32[6,256]{1,0:T(8,128)S(1)}, u32[]{:S(2)}, u32[]{:S(2)}) collective-permute-start(f32[6,256]{1,0:T(8,128)S(1)} %slice.16), channel_id=1, source_target_pairs={{0,1},{1,0},{2,3},{3,2},{4,5},{5,4},{6,7},{7,6},{8,9},{9,8},{10,11... | collective-permute-start | bytes 18440 | tf_op jit(solution)/shard_map/swapped/ppermute | solution.py:54
  59.2 8.0 %collective-permute-start.18 = (f32[8,256]{1,0:T(8,128)S(1)}, f32[8,256]{1,0:T(8,128)S(1)}, u32[]{:S(2)}, u32[]{:S(2)}) collective-permute-start(f32[8,256]{1,0:T(8,128)S(1)} %get-tuple-element.55), channel_id=1, source_target_pairs={{0,118},{1,119},{2,116},{3,117},{4,122},{5,123},{6,120},{7,121},{8... | collective-permute-start | bytes 24584 | tf_op jit(solution)/shard_map/back_prv/ppermute | solution.py:54
  62.1 5.2 %collective-permute-start.17 = (f32[6,256]{1,0:T(8,128)S(1)}, f32[6,256]{1,0:T(8,128)S(1)}, u32[]{:S(2)}, u32[]{:S(2)}) collective-permute-start(f32[6,256]{1,0:T(8,128)S(1)} %get-tuple-element.54), channel_id=1, source_target_pairs={{0,4},{1,5},{2,6},{3,7},{4,8},{5,9},{6,10},{7,11},{8,12},{9,13},{1... | collective-permute-start | bytes 18440 | tf_op jit(solution)/shard_map/back_01/ppermute | solution.py:54
  63.6 3.6 %collective-permute-start.16 = (f32[4,256]{1,0:T(4,128)S(1)}, f32[4,256]{1,0:T(4,128)S(1)}, u32[]{:S(2)}, u32[]{:S(2)}) collective-permute-start(f32[4,256]{1,0:T(4,128)S(1)} %get-tuple-element.53), channel_id=1, source_target_pairs={{0,12},{1,13},{2,14},{3,15},{4,0},{5,1},{6,2},{7,3},{8,4},{9,5},{1... | collective-permute-start | bytes 12296 | tf_op jit(solution)/shard_map/back_03/ppermute | solution.py:54

commit v9 on v7

--- a/solution.py
+++ b/solution.py
@@ -65,7 +65,7 @@
 
 
 PARTS = 4
-PACK_MIB = 56
+PACK_MIB = 60
 LONG = 10**8
 
 
@@ -73,7 +73,7 @@
     return sizes_ref[lax.rem(lax.axis_index("group") + step, lax.axis_size("group"))]
 
 
-def pack_kernel(sizes_hbm, rows_hbm, rank_hbm, pay_hbm, a_hbm, b_hbm, rows_ref, rank_ref, pay_ref, sizes_ref, sem, out_sem):
+def pack_kernel(sizes_hbm, rows_hbm, rank_hbm, pay_ref, a_ref, b_ref, rows_ref, rank_ref, sizes_ref, sem):
     part = 2 * HALF // PARTS
     copies = [
         pltpu.make_async_copy(rows_hbm.at[pl.ds(i * part, part)], rows_ref.at[pl.ds(i * part, part)], sem.at[i])
@@ -81,32 +81,29 @@
     ]
     rank_copy = pltpu.make_async_copy(rank_hbm, rank_ref, sem.at[PARTS])
     sizes_copy = pltpu.make_async_copy(sizes_hbm, sizes_ref, sem.at[PARTS + 1])
-    for copy in [rank_copy, sizes_copy, *copies]:
+    for copy in [*copies, rank_copy, sizes_copy]:
         copy.start()
+    for i, copy in enumerate(copies):
+        copy.wait()
+        half, at = divmod(i * part, HALF)
+        rows = rows_ref[i * part : (i + 1) * part, :]
+        scale = lax.rsqrt(jnp.mean(rows * rows, axis=-1, keepdims=True) + 1e-06) / math.sqrt(D)
+        unit = (rows * scale).astype(jnp.bfloat16)
+        pay_ref[half, at : at + part, :] = unit
+        (a_ref, b_ref)[half][at : at + part, :] = unit
     rank_copy.wait()
     sizes_copy.wait()
     left = own_count(sizes_ref) - lax.axis_index("helper") * 2 * HALF
-    outs = []
-    for half, half_hbm in enumerate((a_hbm, b_hbm)):
+    for half, half_ref in enumerate((a_ref, b_ref)):
         rank = rank_ref[:, half * HALF : (half + 1) * HALF]
         position = lax.broadcasted_iota(jnp.int32, (1, HALF), 1) + half * HALF
         real = position < left
         high = jnp.where(real, rank // BASE, int(FAR) // BASE).astype(jnp.float32)
         low = jnp.where(real, rank % BASE, 0).astype(jnp.float32)
-        row = jnp.concatenate([high, low, jnp.zeros((1, D - 2 * HALF), jnp.float32)], axis=1)
-        pay_ref[half, HALF:, :] = jnp.broadcast_to(row, (EXTRA, D)).astype(jnp.bfloat16)
-        for i in range(half * PARTS // 2, (half + 1) * PARTS // 2):
-            copies[i].wait()
-            rows = rows_ref[i * part : (i + 1) * part, :]
-            scale = lax.rsqrt(jnp.mean(rows * rows, axis=-1, keepdims=True) + 1e-06) / math.sqrt(D)
-            at = i * part - half * HALF
-            pay_ref[half, at : at + part, :] = (rows * scale).astype(jnp.bfloat16)
-        outs.append(pltpu.make_async_copy(pay_ref.at[half], pay_hbm.at[half], out_sem.at[2 * half]))
-        outs.append(pltpu.make_async_copy(pay_ref.at[half], half_hbm, out_sem.at[2 * half + 1]))
-        for out in outs[2 * half :]:
-            out.start()
-    for out in outs:
-        out.wait()
+        both = jnp.concatenate([high, low, jnp.zeros((1, D - 2 * HALF), jnp.float32)], axis=1)
+        tail = jnp.broadcast_to(both, (EXTRA, D)).astype(jnp.bfloat16)
+        pay_ref[half, HALF:, :] = tail
+        half_ref[HALF:, :] = tail
 
 
 def packed(rows, ranks, sizes):
@@ -114,15 +111,13 @@
     return pl.pallas_call(
         pack_kernel,
         in_specs=[pl.BlockSpec(memory_space=pltpu.HBM)] * 3,
-        out_specs=[pl.BlockSpec(memory_space=pltpu.HBM)] * 3,
+        out_specs=[VMEM] * 3,
         out_shape=[jax.ShapeDtypeStruct((2, PAY, D), jnp.bfloat16), half, half],
         scratch_shapes=[
             pltpu.VMEM((2 * HALF, D), jnp.float32),
             pltpu.VMEM((1, 2 * HALF), jnp.int32),
-            pltpu.VMEM((2, PAY, D), jnp.bfloat16),
             pltpu.SMEM(sizes.shape, jnp.int32),
             pltpu.SemaphoreType.DMA((PARTS + 2,)),
-            pltpu.SemaphoreType.DMA((4,)),
         ],
         name="pack",
         compiler_params=pltpu.CompilerParams(vmem_limit_bytes=PACK_MIB * 2**20),

time: 67 us -> 67.2 us (level)
  no operation moved by 1% of the time
where the time goes in v9:
time: 67.2 us; the launch traced here: 67 us
  starting transfers between devices  25.7 us (38%)
  Pallas kernels  21.1 us (31%)
  waiting for transfers between devices  18 us (27%)
  local copies, waits for them, and re-layouts  1.33 us (2%)
  between operations  0.8 us (1%)
    ppermute x19, starting transfers between devices, send(): return lax.ppermute(value, AXES, pairs(**shift))  25.7 us
    ppermute x19, waiting for transfers between devices, send(): return lax.ppermute(value, AXES, pairs(**shift))  18 us
    pallas_call x9, Pallas kernels, kernel_call(): pl.pallas_call(kernel, in_specs=[VMEM] * (1 + len(arrays)) + [SMEM] * len...  17.3 us
    pallas_call x1, Pallas kernels, packed(): pl.pallas_call(pack_kernel, in_specs=[pl.BlockSpec(memory_space=pltpu.HBM...  3.07 us
  transfers between devices with their start and end apart: 19, of which 8 were waited for; matrix products, arithmetic and copies ran while one was open for 0% of the time, Pallas kernels for 26%

profile of v9, /device:TPU:0, one launch (start us, length us, event | category | flops | bytes accessed | tf_op | source)
XLA Modules:
  0.0 67.0 jit_solution(18247413020683631202)
XLA Ops:
  0.6 3.1 %pack.1 = (bf16[2,264,1024]{2,1,0:T(8,128)(2,1)}, bf16[264,1024]{1,0:T(8,128)(2,1)}, bf16[264,1024]{1,0:T(8,128)(2,1)}) custom-call(s32[8]{0:T(128)} %refs_2_.1, f32[512,1024]{1,0:T(8,128)} %bitcast.5, s32[1,512]{1,0:T(1,128)} %rank_hbm.1), custom_call_target="tpu_custom_call" | custom-call | flops 2097152 | bytes 4194304 | tf_op jit(solution)/shard_map/pack/pallas_call | solution.py:111
  3.8 1.7 %collective-permute-start.7 = (bf16[2,264,1024]{2,1,0:T(8,128)(2,1)}, bf16[2,264,1024]{2,1,0:T(8,128)(2,1)S(1)}, u32[]{:S(2)}, u32[]{:S(2)}) collective-permute-start(bf16[2,264,1024]{2,1,0:T(8,128)(2,1)} %get-tuple-element.30.refs_0_), channel_id=1, source_target_pairs={{0,2},{1,3},{2,0},{3,1},{4,6},{5,7},{6,4},{7,5},{8,10},{9,11},{10,... | collective-permute-start | bytes 3244040 | tf_op jit(solution)/shard_map/b10/ppermute | solution.py:54
  5.5 1.6 %collective-permute-start.6 = (bf16[2,264,1024]{2,1,0:T(8,128)(2,1)}, bf16[2,264,1024]{2,1,0:T(8,128)(2,1)S(1)}, u32[]{:S(2)}, u32[]{:S(2)}) collective-permute-start(bf16[2,264,1024]{2,1,0:T(8,128)(2,1)} %get-tuple-element.30.refs_0_), channel_id=1, source_target_pairs={{0,4},{1,5},{2,6},{3,7},{4,8},{5,9},{6,10},{7,11},{8,12},{9,13},{1... | collective-permute-start | bytes 3244040 | tf_op jit(solution)/shard_map/b03/ppermute | solution.py:54
  7.0 1.7 %collective-permute-start.2 = (bf16[264,1024]{1,0:T(8,128)(2,1)}, bf16[264,1024]{1,0:T(8,128)(2,1)S(1)}, u32[]{:S(2)}, u32[]{:S(2)}) collective-permute-start(bf16[264,1024]{1,0:T(8,128)(2,1)} %get-tuple-element.34), channel_id=1, source_target_pairs={{0,12},{1,13},{2,14},{3,15},{4,0},{5,1},{6,2},{7,3},{8,4},{9,5},{1... | collective-permute-start | bytes 1622024 | tf_op jit(solution)/shard_map/b01a/ppermute | solution.py:54
  8.7 5.6 %collective-permute-start.4 = (bf16[2,264,1024]{2,1,0:T(8,128)(2,1)}, bf16[2,264,1024]{2,1,0:T(8,128)(2,1)S(1)}, u32[]{:S(2)}, u32[]{:S(2)}) collective-permute-start(bf16[2,264,1024]{2,1,0:T(8,128)(2,1)} %get-tuple-element.30.refs_0_), channel_id=1, source_target_pairs={{0,114},{1,115},{2,112},{3,113},{4,118},{5,119},{6,116},{7,117},{8... | collective-permute-start | bytes 3244040 | tf_op jit(solution)/shard_map/nxt/ppermute | solution.py:54
  14.3 1.8 %collective-permute-start.1 = (bf16[264,1024]{1,0:T(8,128)(2,1)}, bf16[264,1024]{1,0:T(8,128)(2,1)S(1)}, u32[]{:S(2)}, u32[]{:S(2)}) collective-permute-start(bf16[264,1024]{1,0:T(8,128)(2,1)} %get-tuple-element.31), channel_id=1, source_target_pairs={{0,12},{1,13},{2,14},{3,15},{4,0},{5,1},{6,2},{7,3},{8,4},{9,5},{1... | collective-permute-start | bytes 1622024 | tf_op jit(solution)/shard_map/b01b/ppermute | solution.py:54
  16.1 1.2 %copy-done = bf16[2,264,1024]{2,1,0:T(8,128)(2,1)S(1)} copy-done((bf16[2,264,1024]{2,1,0:T(8,128)(2,1)S(1)}, bf16[2,264,1024]{2,1,0:T(8,128)(2,1)}, u32[]{:S(2)}) %copy-start) | copy-done | bytes 1081368
  17.3 1.8 %self.1 = (f32[56,256]{1,0:T(8,128)S(1)}, f32[4,256,128]{2,1,0:T(8,128)S(1)}) custom-call(f32[56,256]{1,0:T(8,128)S(1)} %broadcast_in_dim.3.rows_in, bf16[2,264,1024]{2,1,0:T(8,128)(2,1)S(1)} %copy-done, bf16[2,264,1024]{2,1,0:T(8,128)(2,1)S(1)} %collective-permute-done.refs_1_, s32[8]{0:T(128)S(1)} %copy-done.2), custom_call_target="tpu_custom_call" | custom-call | tf_op jit(solution)/shard_map/self/pallas_call | solution.py:215
  19.2 3.2 %collective-permute-done.2.refs_3_.b01a.refs_1_ = bf16[264,1024]{1,0:T(8,128)(2,1)S(1)} collective-permute-done((bf16[264,1024]{1,0:T(8,128)(2,1)}, bf16[264,1024]{1,0:T(8,128)(2,1)S(1)}, u32[]{:S(2)}, u32[]{:S(2)}) %collective-permute-start.2) | collective-permute-done | bytes 540704 | tf_op jit(solution)/shard_map/b01a/ppermute | solution.py:54
  22.4 1.9 %collective-permute-start.5 = (bf16[264,1024]{1,0:T(8,128)(2,1)S(1)}, bf16[264,1024]{1,0:T(8,128)(2,1)S(1)}, u32[]{:S(2)}, u32[]{:S(2)}) collective-permute-start(bf16[264,1024]{1,0:T(8,128)(2,1)S(1)} %collective-permute-done.2.refs_3_.b01a.refs_1_), channel_id=1, source_target_pairs={{0,16},{1,17},{2,18},{3,19},{4,20},{5,21},{6,22},{7,23},{8,24},{9,... | collective-permute-start | bytes 1622024 | tf_op jit(solution)/shard_map/prva/ppermute | solution.py:54
  25.2 5.1 %collective-permute-done.7.refs_6_.refs_4_.refs_1_ = bf16[2,264,1024]{2,1,0:T(8,128)(2,1)S(1)} collective-permute-done((bf16[2,264,1024]{2,1,0:T(8,128)(2,1)}, bf16[2,264,1024]{2,1,0:T(8,128)(2,1)S(1)}, u32[]{:S(2)}, u32[]{:S(2)}) %collective-permute-start.7) | collective-permute-done | bytes 1081376 | tf_op jit(solution)/shard_map/b10/ppermute | solution.py:54
  30.3 2.6 %collective-permute-done.6.refs_5_.refs_3_.refs_0_ = bf16[2,264,1024]{2,1,0:T(8,128)(2,1)S(1)} collective-permute-done((bf16[2,264,1024]{2,1,0:T(8,128)(2,1)}, bf16[2,264,1024]{2,1,0:T(8,128)(2,1)S(1)}, u32[]{:S(2)}, u32[]{:S(2)}) %collective-permute-start.6) | collective-permute-done | bytes 1081376 | tf_op jit(solution)/shard_map/b03/ppermute | solution.py:54
  33.6 1.9 %collective-permute-start.3 = (bf16[264,1024]{1,0:T(8,128)(2,1)S(1)}, bf16[264,1024]{1,0:T(8,128)(2,1)S(1)}, u32[]{:S(2)}, u32[]{:S(2)}) collective-permute-start(bf16[264,1024]{1,0:T(8,128)(2,1)S(1)} %collective-permute-done.1.refs_4_.b01b.refs_2_), channel_id=1, source_target_pairs={{0,16},{1,17},{2,18},{3,19},{4,20},{5,21},{6,22},{7,23},{8,24},{9,... | collective-permute-start | bytes 1622024 | tf_op jit(solution)/shard_map/prvb/ppermute | solution.py:54
  39.1 4.8 %same.1 = (f32[56,256]{1,0:T(8,128)S(1)}, f32[2,256,128]{2,1,0:T(8,128)S(1)}) custom-call(f32[56,256]{1,0:T(8,128)S(1)} %first.1.rows_in, bf16[2,264,1024]{2,1,0:T(8,128)(2,1)S(1)} %copy-done.1, bf16[2,264,1024]{2,1,0:T(8,128)(2,1)S(1)} %collective-permute-done.refs_1_, f32[4,256,128]{2,1,0:T(8,128)S(1)} %get-tuple-element.33.refs_2_, ...), custom_call_target="tpu_custom_call" | custom-call | tf_op jit(solution)/shard_map/same/pallas_call | solution.py:215
  43.9 2.4 %other.1.rows_in = f32[56,256]{1,0:T(8,128)S(1)} custom-call(f32[56,256]{1,0:T(8,128)S(1)} %get-tuple-element.44.rows_in, bf16[2,264,1024]{2,1,0:T(8,128)(2,1)S(1)} %copy-done.1, bf16[264,1024]{1,0:T(8,128)(2,1)S(1)} %collective-permute-done.2.refs_3_.b01a.refs_1_, bf16[264,1024]{1,0:T(8,128)(2,1)S(1)} %collective-permute-done.1.refs_4_.b01b.refs_2_, ...), custom_call_target="tpu_custom_call" | custom-call | tf_op jit(solution)/shard_map/other/pallas_call | solution.py:215
  46.7 1.5 %left.1.rows_in = f32[56,256]{1,0:T(8,128)S(1)} custom-call(f32[56,256]{1,0:T(8,128)S(1)} %other.1.rows_in, bf16[2,264,1024]{2,1,0:T(8,128)(2,1)S(1)} %copy-done.1, bf16[2,264,1024]{2,1,0:T(8,128)(2,1)S(1)} %collective-permute-done.refs_1_, f32[4,256,128]{2,1,0:T(8,128)S(1)} %get-tuple-element.33.refs_2_, ...), custom_call_target="tpu_custom_call" | custom-call | tf_op jit(solution)/shard_map/left/pallas_call | solution.py:215
  48.1 3.2 %collective-permute-done.3.refs_4_ = bf16[264,1024]{1,0:T(8,128)(2,1)S(1)} collective-permute-done((bf16[264,1024]{1,0:T(8,128)(2,1)S(1)}, bf16[264,1024]{1,0:T(8,128)(2,1)S(1)}, u32[]{:S(2)}, u32[]{:S(2)}) %collective-permute-start.3) | collective-permute-done | bytes 540704 | tf_op jit(solution)/shard_map/prvb/ppermute | solution.py:54
  51.4 1.3 %right.1.rows_in = f32[56,256]{1,0:T(8,128)S(1)} custom-call(f32[56,256]{1,0:T(8,128)S(1)} %left.1.rows_in, bf16[2,264,1024]{2,1,0:T(8,128)(2,1)S(1)} %copy-done.1, bf16[2,264,1024]{2,1,0:T(8,128)(2,1)S(1)} %collective-permute-done.refs_1_, f32[4,256,128]{2,1,0:T(8,128)S(1)} %get-tuple-element.33.refs_2_, ...), custom_call_target="tpu_custom_call" | custom-call | flops 102400000000 | tf_op jit(solution)/shard_map/right/pallas_call | solution.py:215
  52.7 1.7 %cross.1.rows_in = f32[56,256]{1,0:T(8,128)S(1)} custom-call(f32[56,256]{1,0:T(8,128)S(1)} %right.1.rows_in, bf16[2,264,1024]{2,1,0:T(8,128)(2,1)S(1)} %collective-permute-done.6.refs_5_.refs_3_.refs_0_, bf16[264,1024]{1,0:T(8,128)(2,1)S(1)} %collective-permute-done.10.refs_8_.refs_1_.refs_2_, ...), custom_call_target="tpu_custom_call" | custom-call | tf_op jit(solution)/shard_map/cross/pallas_call | solution.py:215
  55.0 1.8 %prev.1.rows_in = f32[56,256]{1,0:T(8,128)S(1)} custom-call(f32[56,256]{1,0:T(8,128)S(1)} %cross.1.rows_in, bf16[2,264,1024]{2,1,0:T(8,128)(2,1)S(1)} %collective-permute-done.6.refs_5_.refs_3_.refs_0_, bf16[2,264,1024]{2,1,0:T(8,128)(2,1)S(1)} %collective-permute-done.7.refs_6_.refs_4_.refs_1_, ...), custom_call_target="tpu_custom_call" | custom-call | tf_op jit(solution)/shard_map/prev/pallas_call | solution.py:215
  58.4 2.8 %collective-permute-start.18 = (f32[8,256]{1,0:T(8,128)S(1)}, f32[8,256]{1,0:T(8,128)S(1)}, u32[]{:S(2)}, u32[]{:S(2)}) collective-permute-start(f32[8,256]{1,0:T(8,128)S(1)} %get-tuple-element.55), channel_id=1, source_target_pairs={{0,118},{1,119},{2,116},{3,117},{4,122},{5,123},{6,120},{7,121},{8... | collective-permute-start | bytes 24584 | tf_op jit(solution)/shard_map/back_prv/ppermute | solution.py:54
  61.2 1.6 %collective-permute-start.17 = (f32[6,256]{1,0:T(8,128)S(1)}, f32[6,256]{1,0:T(8,128)S(1)}, u32[]{:S(2)}, u32[]{:S(2)}) collective-permute-start(f32[6,256]{1,0:T(8,128)S(1)} %get-tuple-element.54), channel_id=1, source_target_pairs={{0,4},{1,5},{2,6},{3,7},{4,8},{5,9},{6,10},{7,11},{8,12},{9,13},{1... | collective-permute-start | bytes 18440 | tf_op jit(solution)/shard_map/back_01/ppermute | solution.py:54
  62.8 1.7 %collective-permute-start.16 = (f32[4,256]{1,0:T(4,128)S(1)}, f32[4,256]{1,0:T(4,128)S(1)}, u32[]{:S(2)}, u32[]{:S(2)}) collective-permute-start(f32[4,256]{1,0:T(4,128)S(1)} %get-tuple-element.53), channel_id=1, source_target_pairs={{0,12},{1,13},{2,14},{3,15},{4,0},{5,1},{6,2},{7,3},{8,4},{9,5},{1... | collective-permute-start | bytes 12296 | tf_op jit(solution)/shard_map/back_03/ppermute | solution.py:54
  64.5 1.9 %collective-permute-done.16.b03 = f32[4,256]{1,0:T(4,128)S(1)} collective-permute-done((f32[4,256]{1,0:T(4,128)S(1)}, f32[4,256]{1,0:T(4,128)S(1)}, u32[]{:S(2)}, u32[]{:S(2)}) %collective-permute-start.16) | collective-permute-done | bytes 4128 | tf_op jit(solution)/shard_map/back_03/ppermute | solution.py:54
  (38 shorter events, 8.3 us)
Async XLA Ops:
  0.6 15.5 %copy-start.2 = (s32[8]{0:T(128)S(1)}, s32[8]{0:T(128)}, u32[]{:S(2)}) copy-start(s32[8]{0:T(128)} %refs_2_.1) | copy-start | bytes 100
  3.7 10.6 %collective-permute-start = (bf16[2,264,1024]{2,1,0:T(8,128)(2,1)}, bf16[2,264,1024]{2,1,0:T(8,128)(2,1)S(1)}, u32[]{:S(2)}, u32[]{:S(2)}) collective-permute-start(bf16[2,264,1024]{2,1,0:T(8,128)(2,1)} %get-tuple-element.30.refs_0_), channel_id=1, source_target_pairs={{0,1},{1,0},{2,3},{3,2},{4,5},{5,4},{6,7},{7,6},{8,9},{9,8},{10,11... | collective-permute-start | bytes 3244040 | tf_op jit(solution)/shard_map/ownx/ppermute | solution.py:54
  3.8 26.5 %collective-permute-start.7 = (bf16[2,264,1024]{2,1,0:T(8,128)(2,1)}, bf16[2,264,1024]{2,1,0:T(8,128)(2,1)S(1)}, u32[]{:S(2)}, u32[]{:S(2)}) collective-permute-start(bf16[2,264,1024]{2,1,0:T(8,128)(2,1)} %get-tuple-element.30.refs_0_), channel_id=1, source_target_pairs={{0,2},{1,3},{2,0},{3,1},{4,6},{5,7},{6,4},{7,5},{8,10},{9,11},{10,... | collective-permute-start | bytes 3244040 | tf_op jit(solution)/shard_map/b10/ppermute | solution.py:54
  5.5 27.4 %collective-permute-start.6 = (bf16[2,264,1024]{2,1,0:T(8,128)(2,1)}, bf16[2,264,1024]{2,1,0:T(8,128)(2,1)S(1)}, u32[]{:S(2)}, u32[]{:S(2)}) collective-permute-start(bf16[2,264,1024]{2,1,0:T(8,128)(2,1)} %get-tuple-element.30.refs_0_), channel_id=1, source_target_pairs={{0,4},{1,5},{2,6},{3,7},{4,8},{5,9},{6,10},{7,11},{8,12},{9,13},{1... | collective-permute-start | bytes 3244040 | tf_op jit(solution)/shard_map/b03/ppermute | solution.py:54
  7.0 15.4 %collective-permute-start.2 = (bf16[264,1024]{1,0:T(8,128)(2,1)}, bf16[264,1024]{1,0:T(8,128)(2,1)S(1)}, u32[]{:S(2)}, u32[]{:S(2)}) collective-permute-start(bf16[264,1024]{1,0:T(8,128)(2,1)} %get-tuple-element.34), channel_id=1, source_target_pairs={{0,12},{1,13},{2,14},{3,15},{4,0},{5,1},{6,2},{7,3},{8,4},{9,5},{1... | collective-permute-start | bytes 1622024 | tf_op jit(solution)/shard_map/b01a/ppermute | solution.py:54
  8.7 28.8 %collective-permute-start.4 = (bf16[2,264,1024]{2,1,0:T(8,128)(2,1)}, bf16[2,264,1024]{2,1,0:T(8,128)(2,1)S(1)}, u32[]{:S(2)}, u32[]{:S(2)}) collective-permute-start(bf16[2,264,1024]{2,1,0:T(8,128)(2,1)} %get-tuple-element.30.refs_0_), channel_id=1, source_target_pairs={{0,114},{1,115},{2,112},{3,113},{4,118},{5,119},{6,116},{7,117},{8... | collective-permute-start | bytes 3244040 | tf_op jit(solution)/shard_map/nxt/ppermute | solution.py:54
  14.3 19.3 %collective-permute-start.1 = (bf16[264,1024]{1,0:T(8,128)(2,1)}, bf16[264,1024]{1,0:T(8,128)(2,1)S(1)}, u32[]{:S(2)}, u32[]{:S(2)}) collective-permute-start(bf16[264,1024]{1,0:T(8,128)(2,1)} %get-tuple-element.31), channel_id=1, source_target_pairs={{0,12},{1,13},{2,14},{3,15},{4,0},{5,1},{6,2},{7,3},{8,4},{9,5},{1... | collective-permute-start | bytes 1622024 | tf_op jit(solution)/shard_map/b01b/ppermute | solution.py:54
  16.1 1.2 %copy-start = (bf16[2,264,1024]{2,1,0:T(8,128)(2,1)S(1)}, bf16[2,264,1024]{2,1,0:T(8,128)(2,1)}, u32[]{:S(2)}) copy-start(bf16[2,264,1024]{2,1,0:T(8,128)(2,1)} %get-tuple-element.30.refs_0_) | copy-start | bytes 3244036
  17.3 7.0 %copy-start.1 = (bf16[2,264,1024]{2,1,0:T(8,128)(2,1)S(1)}, bf16[2,264,1024]{2,1,0:T(8,128)(2,1)}, u32[]{:S(2)}) copy-start(bf16[2,264,1024]{2,1,0:T(8,128)(2,1)} %get-tuple-element.30.refs_0_) | copy-start | bytes 3244036
  22.4 15.9 %collective-permute-start.5 = (bf16[264,1024]{1,0:T(8,128)(2,1)S(1)}, bf16[264,1024]{1,0:T(8,128)(2,1)S(1)}, u32[]{:S(2)}, u32[]{:S(2)}) collective-permute-start(bf16[264,1024]{1,0:T(8,128)(2,1)S(1)} %collective-permute-done.2.refs_3_.b01a.refs_1_), channel_id=1, source_target_pairs={{0,16},{1,17},{2,18},{3,19},{4,20},{5,21},{6,22},{7,23},{8,24},{9,... | collective-permute-start | bytes 1622024 | tf_op jit(solution)/shard_map/prva/ppermute | solution.py:54
  32.9 13.7 %collective-permute-start.10 = (bf16[264,1024]{1,0:T(8,128)(2,1)S(1)}, bf16[264,1024]{1,0:T(8,128)(2,1)S(1)}, u32[]{:S(2)}, u32[]{:S(2)}) collective-permute-start(bf16[264,1024]{1,0:T(8,128)(2,1)S(1)} %slice_bitcast_fusion.1), channel_id=1, source_target_pairs={{0,2},{1,3},{2,0},{3,1},{4,6},{5,7},{6,4},{7,5},{8,10},{9,11},{10,... | collective-permute-start | bytes 1622024 | tf_op jit(solution)/shard_map/b13a/ppermute | solution.py:54
  33.6 17.8 %collective-permute-start.3 = (bf16[264,1024]{1,0:T(8,128)(2,1)S(1)}, bf16[264,1024]{1,0:T(8,128)(2,1)S(1)}, u32[]{:S(2)}, u32[]{:S(2)}) collective-permute-start(bf16[264,1024]{1,0:T(8,128)(2,1)S(1)} %collective-permute-done.1.refs_4_.b01b.refs_2_), channel_id=1, source_target_pairs={{0,16},{1,17},{2,18},{3,19},{4,20},{5,21},{6,22},{7,23},{8,24},{9,... | collective-permute-start | bytes 1622024 | tf_op jit(solution)/shard_map/prvb/ppermute | solution.py:54
  35.5 15.9 %collective-permute-start.11 = (bf16[264,1024]{1,0:T(8,128)(2,1)S(1)}, bf16[264,1024]{1,0:T(8,128)(2,1)S(1)}, u32[]{:S(2)}, u32[]{:S(2)}) collective-permute-start(bf16[264,1024]{1,0:T(8,128)(2,1)S(1)} %slice_bitcast_fusion), channel_id=1, source_target_pairs={{0,4},{1,5},{2,6},{3,7},{4,8},{5,9},{6,10},{7,11},{8,12},{9,13},{1... | collective-permute-start | bytes 1622024 | tf_op jit(solution)/shard_map/b13b/ppermute | solution.py:54
  38.5 5.4 %collective-permute-start.8 = (bf16[256,1024]{1,0:T(8,128)(2,1)S(1)}, bf16[256,1024]{1,0:T(8,128)(2,1)S(1)}, u32[]{:S(2)}, u32[]{:S(2)}) collective-permute-start(bf16[256,1024]{1,0:T(8,128)(2,1)S(1)} %get-tuple-element.45), channel_id=1, source_target_pairs={{0,1},{1,0},{2,3},{3,2},{4,5},{5,4},{6,7},{7,6},{8,9},{9,8},{10,11... | collective-permute-start | bytes 1572872 | tf_op jit(solution)/shard_map/nxtax/ppermute | solution.py:54
  38.6 5.3 %collective-permute-start.9 = (bf16[256,1024]{1,0:T(8,128)(2,1)S(1)}, bf16[256,1024]{1,0:T(8,128)(2,1)S(1)}, u32[]{:S(2)}, u32[]{:S(2)}) collective-permute-start(bf16[256,1024]{1,0:T(8,128)(2,1)S(1)} %get-tuple-element.46), channel_id=1, source_target_pairs={{0,1},{1,0},{2,3},{3,2},{4,5},{5,4},{6,7},{7,6},{8,9},{9,8},{10,11... | collective-permute-start | bytes 1572872 | tf_op jit(solution)/shard_map/nxtbx/ppermute | solution.py:54
  46.3 6.4 %collective-permute-start.12 = (bf16[3,264,1024]{2,1,0:T(8,128)(2,1)S(1)}, bf16[3,264,1024]{2,1,0:T(8,128)(2,1)S(1)}, u32[]{:S(2)}, u32[]{:S(2)}) collective-permute-start(bf16[3,264,1024]{2,1,0:T(8,128)(2,1)S(1)} %get-tuple-element.50), channel_id=1, source_target_pairs={{0,1},{1,0},{2,3},{3,2},{4,5},{5,4},{6,7},{7,6},{8,9},{9,8},{10,11... | collective-permute-start | bytes 4866056 | tf_op jit(solution)/shard_map/cross/ppermute | solution.py:54
  51.4 3.6 %collective-permute-start.13 = (bf16[264,1024]{1,0:T(8,128)(2,1)S(1)}, bf16[264,1024]{1,0:T(8,128)(2,1)S(1)}, u32[]{:S(2)}, u32[]{:S(2)}) collective-permute-start(bf16[264,1024]{1,0:T(8,128)(2,1)S(1)} %collective-permute-done.3.refs_4_), channel_id=1, source_target_pairs={{0,1},{1,0},{2,3},{3,2},{4,5},{5,4},{6,7},{7,6},{8,9},{9,8},{10,11... | collective-permute-start | bytes 1622024 | tf_op jit(solution)/shard_map/prvbx/ppermute | solution.py:54
  54.4 4.0 %collective-permute-start.15 = (f32[8,256]{1,0:T(8,128)S(1)}, f32[8,256]{1,0:T(8,128)S(1)}, u32[]{:S(2)}, u32[]{:S(2)}) collective-permute-start(f32[8,256]{1,0:T(8,128)S(1)} %slice.17), channel_id=1, source_target_pairs={{0,2},{1,3},{2,0},{3,1},{4,6},{5,7},{6,4},{7,5},{8,10},{9,11},{10,... | collective-permute-start | bytes 24584 | tf_op jit(solution)/shard_map/side/ppermute | solution.py:54
  56.8 1.4 %collective-permute-start.14 = (f32[6,256]{1,0:T(8,128)S(1)}, f32[6,256]{1,0:T(8,128)S(1)}, u32[]{:S(2)}, u32[]{:S(2)}) collective-permute-start(f32[6,256]{1,0:T(8,128)S(1)} %slice.16), channel_id=1, source_target_pairs={{0,1},{1,0},{2,3},{3,2},{4,5},{5,4},{6,7},{7,6},{8,9},{9,8},{10,11... | collective-permute-start | bytes 18440 | tf_op jit(solution)/shard_map/swapped/ppermute | solution.py:54
  58.4 8.0 %collective-permute-start.18 = (f32[8,256]{1,0:T(8,128)S(1)}, f32[8,256]{1,0:T(8,128)S(1)}, u32[]{:S(2)}, u32[]{:S(2)}) collective-permute-start(f32[8,256]{1,0:T(8,128)S(1)} %get-tuple-element.55), channel_id=1, source_target_pairs={{0,118},{1,119},{2,116},{3,117},{4,122},{5,123},{6,120},{7,121},{8... | collective-permute-start | bytes 24584 | tf_op jit(solution)/shard_map/back_prv/ppermute | solution.py:54
  61.2 5.2 %collective-permute-start.17 = (f32[6,256]{1,0:T(8,128)S(1)}, f32[6,256]{1,0:T(8,128)S(1)}, u32[]{:S(2)}, u32[]{:S(2)}) collective-permute-start(f32[6,256]{1,0:T(8,128)S(1)} %get-tuple-element.54), channel_id=1, source_target_pairs={{0,4},{1,5},{2,6},{3,7},{4,8},{5,9},{6,10},{7,11},{8,12},{9,13},{1... | collective-permute-start | bytes 18440 | tf_op jit(solution)/shard_map/back_01/ppermute | solution.py:54
  62.8 3.6 %collective-permute-start.16 = (f32[4,256]{1,0:T(4,128)S(1)}, f32[4,256]{1,0:T(4,128)S(1)}, u32[]{:S(2)}, u32[]{:S(2)}) collective-permute-start(f32[4,256]{1,0:T(4,128)S(1)} %get-tuple-element.53), channel_id=1, source_target_pairs={{0,12},{1,13},{2,14},{3,15},{4,0},{5,1},{6,2},{7,3},{8,4},{9,5},{1... | collective-permute-start | bytes 12296 | tf_op jit(solution)/shard_map/back_03/ppermute | solution.py:54

commit v10 on v9

--- a/solution.py
+++ b/solution.py
@@ -403,9 +403,9 @@
     state = kernel_call("other", other_kernel, 0, state, [own, b01a, b01b, b03, b10, nxtax, nxtbx])
     cross = send("cross", after(bundle, state), core=1)
     kept = [own, ownx, own_ranks, b01a, b01b, ranks1, nxt, prva]
-    state = kernel_call("left", functools.partial(half_kernel, 0), 1, state, [*kept, b13a])
+    state = kernel_call("left", functools.partial(half_kernel, 1), 1, state, [*kept, b13b])
     prvb, state = lax.optimization_barrier((prvb, state))
-    state = kernel_call("right", functools.partial(half_kernel, 1), LONG, state, [*kept, b13b])
+    state = kernel_call("right", functools.partial(half_kernel, 0), LONG, state, [*kept, b13a])
     prvbx = send("prvbx", prvb, core=1)
     state = kernel_call("cross", cross_kernel, 0, state, [b03, b13a, b13b, nxtax, nxtbx, cross])
 

time: 67.2 us -> 68.1 us (1.013)
  starting transfers between devices: 25.7 us -> 26.9 us
    ppermute x19, starting transfers between devices: 25.7 us -> 26.9 us  [send(): return lax.ppermute(value, AXES, pairs(**shift))]
  transfers between devices with their start and end apart: 19 -> 19, of which waited for: 8 -> 9; matrix products, arithmetic and copies ran while one was open for 0% -> 0% of each run, Pallas kernels for 26% -> 26%
where the time goes in v10:
time: 68.1 us; the launch traced here: 67.7 us
  starting transfers between devices  26.9 us (40%)
  Pallas kernels  21.1 us (31%)
  waiting for transfers between devices  17.6 us (26%)
  local copies, waits for them, and re-layouts  1.33 us (2%)
  between operations  0.81 us (1%)
    ppermute x19, starting transfers between devices, send(): return lax.ppermute(value, AXES, pairs(**shift))  26.9 us
    ppermute x19, waiting for transfers between devices, send(): return lax.ppermute(value, AXES, pairs(**shift))  17.6 us
    pallas_call x9, Pallas kernels, kernel_call(): pl.pallas_call(kernel, in_specs=[VMEM] * (1 + len(arrays)) + [SMEM] * len...  17.3 us
    pallas_call x1, Pallas kernels, packed(): pl.pallas_call(pack_kernel, in_specs=[pl.BlockSpec(memory_space=pltpu.HBM...  3.07 us
  transfers between devices with their start and end apart: 19, of which 9 were waited for; matrix products, arithmetic and copies ran while one was open for 0% of the time, Pallas kernels for 26%

profile of v10, /device:TPU:0, one launch (start us, length us, event | category | flops | bytes accessed | tf_op | source)
XLA Modules:
  0.0 67.7 jit_solution(8690318613950401807)
XLA Ops:
  0.6 3.1 %pack.1 = (bf16[2,264,1024]{2,1,0:T(8,128)(2,1)}, bf16[264,1024]{1,0:T(8,128)(2,1)}, bf16[264,1024]{1,0:T(8,128)(2,1)}) custom-call(s32[8]{0:T(128)} %refs_2_.1, f32[512,1024]{1,0:T(8,128)} %bitcast.5, s32[1,512]{1,0:T(1,128)} %rank_hbm.1), custom_call_target="tpu_custom_call" | custom-call | flops 2097152 | bytes 4194304 | tf_op jit(solution)/shard_map/pack/pallas_call | solution.py:111
  3.8 1.7 %collective-permute-start.7 = (bf16[2,264,1024]{2,1,0:T(8,128)(2,1)}, bf16[2,264,1024]{2,1,0:T(8,128)(2,1)S(1)}, u32[]{:S(2)}, u32[]{:S(2)}) collective-permute-start(bf16[2,264,1024]{2,1,0:T(8,128)(2,1)} %get-tuple-element.30.refs_0_), channel_id=1, source_target_pairs={{0,2},{1,3},{2,0},{3,1},{4,6},{5,7},{6,4},{7,5},{8,10},{9,11},{10,... | collective-permute-start | bytes 3244040 | tf_op jit(solution)/shard_map/b10/ppermute | solution.py:54
  5.5 1.6 %collective-permute-start.6 = (bf16[2,264,1024]{2,1,0:T(8,128)(2,1)}, bf16[2,264,1024]{2,1,0:T(8,128)(2,1)S(1)}, u32[]{:S(2)}, u32[]{:S(2)}) collective-permute-start(bf16[2,264,1024]{2,1,0:T(8,128)(2,1)} %get-tuple-element.30.refs_0_), channel_id=1, source_target_pairs={{0,4},{1,5},{2,6},{3,7},{4,8},{5,9},{6,10},{7,11},{8,12},{9,13},{1... | collective-permute-start | bytes 3244040 | tf_op jit(solution)/shard_map/b03/ppermute | solution.py:54
  7.0 1.7 %collective-permute-start.2 = (bf16[264,1024]{1,0:T(8,128)(2,1)}, bf16[264,1024]{1,0:T(8,128)(2,1)S(1)}, u32[]{:S(2)}, u32[]{:S(2)}) collective-permute-start(bf16[264,1024]{1,0:T(8,128)(2,1)} %get-tuple-element.34), channel_id=1, source_target_pairs={{0,12},{1,13},{2,14},{3,15},{4,0},{5,1},{6,2},{7,3},{8,4},{9,5},{1... | collective-permute-start | bytes 1622024 | tf_op jit(solution)/shard_map/b01a/ppermute | solution.py:54
  8.7 5.6 %collective-permute-start.4 = (bf16[2,264,1024]{2,1,0:T(8,128)(2,1)}, bf16[2,264,1024]{2,1,0:T(8,128)(2,1)S(1)}, u32[]{:S(2)}, u32[]{:S(2)}) collective-permute-start(bf16[2,264,1024]{2,1,0:T(8,128)(2,1)} %get-tuple-element.30.refs_0_), channel_id=1, source_target_pairs={{0,114},{1,115},{2,112},{3,113},{4,118},{5,119},{6,116},{7,117},{8... | collective-permute-start | bytes 3244040 | tf_op jit(solution)/shard_map/nxt/ppermute | solution.py:54
  14.3 1.8 %collective-permute-start.1 = (bf16[264,1024]{1,0:T(8,128)(2,1)}, bf16[264,1024]{1,0:T(8,128)(2,1)S(1)}, u32[]{:S(2)}, u32[]{:S(2)}) collective-permute-start(bf16[264,1024]{1,0:T(8,128)(2,1)} %get-tuple-element.31), channel_id=1, source_target_pairs={{0,12},{1,13},{2,14},{3,15},{4,0},{5,1},{6,2},{7,3},{8,4},{9,5},{1... | collective-permute-start | bytes 1622024 | tf_op jit(solution)/shard_map/b01b/ppermute | solution.py:54
  17.3 1.8 %self.1 = (f32[56,256]{1,0:T(8,128)S(1)}, f32[4,256,128]{2,1,0:T(8,128)S(1)}) custom-call(f32[56,256]{1,0:T(8,128)S(1)} %broadcast_in_dim.3.rows_in, bf16[2,264,1024]{2,1,0:T(8,128)(2,1)S(1)} %copy-done, bf16[2,264,1024]{2,1,0:T(8,128)(2,1)S(1)} %collective-permute-done.refs_1_, s32[8]{0:T(128)S(1)} %copy-done.2), custom_call_target="tpu_custom_call" | custom-call | tf_op jit(solution)/shard_map/self/pallas_call | solution.py:215
  19.2 3.2 %collective-permute-done.2.refs_3_.b01a.refs_1_ = bf16[264,1024]{1,0:T(8,128)(2,1)S(1)} collective-permute-done((bf16[264,1024]{1,0:T(8,128)(2,1)}, bf16[264,1024]{1,0:T(8,128)(2,1)S(1)}, u32[]{:S(2)}, u32[]{:S(2)}) %collective-permute-start.2) | collective-permute-done | bytes 540704 | tf_op jit(solution)/shard_map/b01a/ppermute | solution.py:54
  22.4 1.9 %collective-permute-start.5 = (bf16[264,1024]{1,0:T(8,128)(2,1)S(1)}, bf16[264,1024]{1,0:T(8,128)(2,1)S(1)}, u32[]{:S(2)}, u32[]{:S(2)}) collective-permute-start(bf16[264,1024]{1,0:T(8,128)(2,1)S(1)} %collective-permute-done.2.refs_3_.b01a.refs_1_), channel_id=1, source_target_pairs={{0,16},{1,17},{2,18},{3,19},{4,20},{5,21},{6,22},{7,23},{8,24},{9,... | collective-permute-start | bytes 1622024 | tf_op jit(solution)/shard_map/prva/ppermute | solution.py:54
  25.2 5.1 %collective-permute-done.7.refs_6_.refs_4_.refs_1_ = bf16[2,264,1024]{2,1,0:T(8,128)(2,1)S(1)} collective-permute-done((bf16[2,264,1024]{2,1,0:T(8,128)(2,1)}, bf16[2,264,1024]{2,1,0:T(8,128)(2,1)S(1)}, u32[]{:S(2)}, u32[]{:S(2)}) %collective-permute-start.7) | collective-permute-done | bytes 1081376 | tf_op jit(solution)/shard_map/b10/ppermute | solution.py:54
  30.3 2.6 %collective-permute-done.6.refs_5_.refs_3_.refs_0_ = bf16[2,264,1024]{2,1,0:T(8,128)(2,1)S(1)} collective-permute-done((bf16[2,264,1024]{2,1,0:T(8,128)(2,1)}, bf16[2,264,1024]{2,1,0:T(8,128)(2,1)S(1)}, u32[]{:S(2)}, u32[]{:S(2)}) %collective-permute-start.6) | collective-permute-done | bytes 1081376 | tf_op jit(solution)/shard_map/b03/ppermute | solution.py:54
  33.3 1.9 %collective-permute-start.3 = (bf16[264,1024]{1,0:T(8,128)(2,1)S(1)}, bf16[264,1024]{1,0:T(8,128)(2,1)S(1)}, u32[]{:S(2)}, u32[]{:S(2)}) collective-permute-start(bf16[264,1024]{1,0:T(8,128)(2,1)S(1)} %collective-permute-done.1.refs_4_.b01b.refs_2_), channel_id=1, source_target_pairs={{0,16},{1,17},{2,18},{3,19},{4,20},{5,21},{6,22},{7,23},{8,24},{9,... | collective-permute-start | bytes 1622024 | tf_op jit(solution)/shard_map/prvb/ppermute | solution.py:54
  35.9 1.7 %collective-permute-done.4.refs_7_.nxt.refs_6_ = bf16[2,264,1024]{2,1,0:T(8,128)(2,1)S(1)} collective-permute-done((bf16[2,264,1024]{2,1,0:T(8,128)(2,1)}, bf16[2,264,1024]{2,1,0:T(8,128)(2,1)S(1)}, u32[]{:S(2)}, u32[]{:S(2)}) %collective-permute-start.4) | collective-permute-done | bytes 1081376 | tf_op jit(solution)/shard_map/nxt/ppermute | solution.py:54
  39.1 4.8 %same.1 = (f32[56,256]{1,0:T(8,128)S(1)}, f32[2,256,128]{2,1,0:T(8,128)S(1)}) custom-call(f32[56,256]{1,0:T(8,128)S(1)} %first.1.rows_in, bf16[2,264,1024]{2,1,0:T(8,128)(2,1)S(1)} %copy-done.1, bf16[2,264,1024]{2,1,0:T(8,128)(2,1)S(1)} %collective-permute-done.refs_1_, f32[4,256,128]{2,1,0:T(8,128)S(1)} %get-tuple-element.33.refs_2_, ...), custom_call_target="tpu_custom_call" | custom-call | tf_op jit(solution)/shard_map/same/pallas_call | solution.py:215
  43.9 2.4 %other.1.rows_in = f32[56,256]{1,0:T(8,128)S(1)} custom-call(f32[56,256]{1,0:T(8,128)S(1)} %get-tuple-element.44.rows_in, bf16[2,264,1024]{2,1,0:T(8,128)(2,1)S(1)} %copy-done.1, bf16[264,1024]{1,0:T(8,128)(2,1)S(1)} %collective-permute-done.2.refs_3_.b01a.refs_1_, bf16[264,1024]{1,0:T(8,128)(2,1)S(1)} %collective-permute-done.1.refs_4_.b01b.refs_2_, ...), custom_call_target="tpu_custom_call" | custom-call | tf_op jit(solution)/shard_map/other/pallas_call | solution.py:215
  47.8 1.3 %left.1.rows_in = f32[56,256]{1,0:T(8,128)S(1)} custom-call(f32[56,256]{1,0:T(8,128)S(1)} %other.1.rows_in, bf16[2,264,1024]{2,1,0:T(8,128)(2,1)S(1)} %copy-done.1, bf16[2,264,1024]{2,1,0:T(8,128)(2,1)S(1)} %collective-permute-done.refs_1_, f32[4,256,128]{2,1,0:T(8,128)S(1)} %get-tuple-element.33.refs_2_, ...), custom_call_target="tpu_custom_call" | custom-call | tf_op jit(solution)/shard_map/left/pallas_call | solution.py:215
  49.2 1.4 %collective-permute-done.3.refs_4_ = bf16[264,1024]{1,0:T(8,128)(2,1)S(1)} collective-permute-done((bf16[264,1024]{1,0:T(8,128)(2,1)S(1)}, bf16[264,1024]{1,0:T(8,128)(2,1)S(1)}, u32[]{:S(2)}, u32[]{:S(2)}) %collective-permute-start.3) | collective-permute-done | bytes 540704 | tf_op jit(solution)/shard_map/prvb/ppermute | solution.py:54
  50.5 1.5 %right.1.rows_in = f32[56,256]{1,0:T(8,128)S(1)} custom-call(f32[56,256]{1,0:T(8,128)S(1)} %left.1.rows_in, bf16[2,264,1024]{2,1,0:T(8,128)(2,1)S(1)} %copy-done.1, bf16[2,264,1024]{2,1,0:T(8,128)(2,1)S(1)} %collective-permute-done.refs_1_, f32[4,256,128]{2,1,0:T(8,128)S(1)} %get-tuple-element.33.refs_2_, ...), custom_call_target="tpu_custom_call" | custom-call | flops 102400000000 | tf_op jit(solution)/shard_map/right/pallas_call | solution.py:215
  52.0 1.7 %cross.1.rows_in = f32[56,256]{1,0:T(8,128)S(1)} custom-call(f32[56,256]{1,0:T(8,128)S(1)} %right.1.rows_in, bf16[2,264,1024]{2,1,0:T(8,128)(2,1)S(1)} %collective-permute-done.6.refs_5_.refs_3_.refs_0_, bf16[264,1024]{1,0:T(8,128)(2,1)S(1)} %collective-permute-done.11.refs_8_.refs_1_.refs_2_, ...), custom_call_target="tpu_custom_call" | custom-call | tf_op jit(solution)/shard_map/cross/pallas_call | solution.py:215
  54.6 1.8 %prev.1.rows_in = f32[56,256]{1,0:T(8,128)S(1)} custom-call(f32[56,256]{1,0:T(8,128)S(1)} %cross.1.rows_in, bf16[2,264,1024]{2,1,0:T(8,128)(2,1)S(1)} %collective-permute-done.6.refs_5_.refs_3_.refs_0_, bf16[2,264,1024]{2,1,0:T(8,128)(2,1)S(1)} %collective-permute-done.7.refs_6_.refs_4_.refs_1_, ...), custom_call_target="tpu_custom_call" | custom-call | tf_op jit(solution)/shard_map/prev/pallas_call | solution.py:215
  57.9 3.5 %collective-permute-start.18 = (f32[8,256]{1,0:T(8,128)S(1)}, f32[8,256]{1,0:T(8,128)S(1)}, u32[]{:S(2)}, u32[]{:S(2)}) collective-permute-start(f32[8,256]{1,0:T(8,128)S(1)} %get-tuple-element.55), channel_id=1, source_target_pairs={{0,118},{1,119},{2,116},{3,117},{4,122},{5,123},{6,120},{7,121},{8... | collective-permute-start | bytes 24584 | tf_op jit(solution)/shard_map/back_prv/ppermute | solution.py:54
  61.4 1.5 %collective-permute-start.17 = (f32[6,256]{1,0:T(8,128)S(1)}, f32[6,256]{1,0:T(8,128)S(1)}, u32[]{:S(2)}, u32[]{:S(2)}) collective-permute-start(f32[6,256]{1,0:T(8,128)S(1)} %get-tuple-element.54), channel_id=1, source_target_pairs={{0,4},{1,5},{2,6},{3,7},{4,8},{5,9},{6,10},{7,11},{8,12},{9,13},{1... | collective-permute-start | bytes 18440 | tf_op jit(solution)/shard_map/back_01/ppermute | solution.py:54
  62.8 2.7 %collective-permute-start.16 = (f32[4,256]{1,0:T(4,128)S(1)}, f32[4,256]{1,0:T(4,128)S(1)}, u32[]{:S(2)}, u32[]{:S(2)}) collective-permute-start(f32[4,256]{1,0:T(4,128)S(1)} %get-tuple-element.53), channel_id=1, source_target_pairs={{0,12},{1,13},{2,14},{3,15},{4,0},{5,1},{6,2},{7,3},{8,4},{9,5},{1... | collective-permute-start | bytes 12296 | tf_op jit(solution)/shard_map/back_03/ppermute | solution.py:54
  65.5 1.3 %collective-permute-done.16.b03 = f32[4,256]{1,0:T(4,128)S(1)} collective-permute-done((f32[4,256]{1,0:T(4,128)S(1)}, f32[4,256]{1,0:T(4,128)S(1)}, u32[]{:S(2)}, u32[]{:S(2)}) %collective-permute-start.16) | collective-permute-done | bytes 4128 | tf_op jit(solution)/shard_map/back_03/ppermute | solution.py:54
  (38 shorter events, 9.5 us)
Async XLA Ops:
  0.6 15.5 %copy-start.2 = (s32[8]{0:T(128)S(1)}, s32[8]{0:T(128)}, u32[]{:S(2)}) copy-start(s32[8]{0:T(128)} %refs_2_.1) | copy-start | bytes 100
  3.7 10.6 %collective-permute-start = (bf16[2,264,1024]{2,1,0:T(8,128)(2,1)}, bf16[2,264,1024]{2,1,0:T(8,128)(2,1)S(1)}, u32[]{:S(2)}, u32[]{:S(2)}) collective-permute-start(bf16[2,264,1024]{2,1,0:T(8,128)(2,1)} %get-tuple-element.30.refs_0_), channel_id=1, source_target_pairs={{0,1},{1,0},{2,3},{3,2},{4,5},{5,4},{6,7},{7,6},{8,9},{9,8},{10,11... | collective-permute-start | bytes 3244040 | tf_op jit(solution)/shard_map/ownx/ppermute | solution.py:54
  3.8 26.5 %collective-permute-start.7 = (bf16[2,264,1024]{2,1,0:T(8,128)(2,1)}, bf16[2,264,1024]{2,1,0:T(8,128)(2,1)S(1)}, u32[]{:S(2)}, u32[]{:S(2)}) collective-permute-start(bf16[2,264,1024]{2,1,0:T(8,128)(2,1)} %get-tuple-element.30.refs_0_), channel_id=1, source_target_pairs={{0,2},{1,3},{2,0},{3,1},{4,6},{5,7},{6,4},{7,5},{8,10},{9,11},{10,... | collective-permute-start | bytes 3244040 | tf_op jit(solution)/shard_map/b10/ppermute | solution.py:54
  5.5 27.4 %collective-permute-start.6 = (bf16[2,264,1024]{2,1,0:T(8,128)(2,1)}, bf16[2,264,1024]{2,1,0:T(8,128)(2,1)S(1)}, u32[]{:S(2)}, u32[]{:S(2)}) collective-permute-start(bf16[2,264,1024]{2,1,0:T(8,128)(2,1)} %get-tuple-element.30.refs_0_), channel_id=1, source_target_pairs={{0,4},{1,5},{2,6},{3,7},{4,8},{5,9},{6,10},{7,11},{8,12},{9,13},{1... | collective-permute-start | bytes 3244040 | tf_op jit(solution)/shard_map/b03/ppermute | solution.py:54
  7.0 15.4 %collective-permute-start.2 = (bf16[264,1024]{1,0:T(8,128)(2,1)}, bf16[264,1024]{1,0:T(8,128)(2,1)S(1)}, u32[]{:S(2)}, u32[]{:S(2)}) collective-permute-start(bf16[264,1024]{1,0:T(8,128)(2,1)} %get-tuple-element.34), channel_id=1, source_target_pairs={{0,12},{1,13},{2,14},{3,15},{4,0},{5,1},{6,2},{7,3},{8,4},{9,5},{1... | collective-permute-start | bytes 1622024 | tf_op jit(solution)/shard_map/b01a/ppermute | solution.py:54
  8.7 28.8 %collective-permute-start.4 = (bf16[2,264,1024]{2,1,0:T(8,128)(2,1)}, bf16[2,264,1024]{2,1,0:T(8,128)(2,1)S(1)}, u32[]{:S(2)}, u32[]{:S(2)}) collective-permute-start(bf16[2,264,1024]{2,1,0:T(8,128)(2,1)} %get-tuple-element.30.refs_0_), channel_id=1, source_target_pairs={{0,114},{1,115},{2,112},{3,113},{4,118},{5,119},{6,116},{7,117},{8... | collective-permute-start | bytes 3244040 | tf_op jit(solution)/shard_map/nxt/ppermute | solution.py:54
  14.3 19.0 %collective-permute-start.1 = (bf16[264,1024]{1,0:T(8,128)(2,1)}, bf16[264,1024]{1,0:T(8,128)(2,1)S(1)}, u32[]{:S(2)}, u32[]{:S(2)}) collective-permute-start(bf16[264,1024]{1,0:T(8,128)(2,1)} %get-tuple-element.31), channel_id=1, source_target_pairs={{0,12},{1,13},{2,14},{3,15},{4,0},{5,1},{6,2},{7,3},{8,4},{9,5},{1... | collective-permute-start | bytes 1622024 | tf_op jit(solution)/shard_map/b01b/ppermute | solution.py:54
  16.1 1.2 %copy-start = (bf16[2,264,1024]{2,1,0:T(8,128)(2,1)S(1)}, bf16[2,264,1024]{2,1,0:T(8,128)(2,1)}, u32[]{:S(2)}) copy-start(bf16[2,264,1024]{2,1,0:T(8,128)(2,1)} %get-tuple-element.30.refs_0_) | copy-start | bytes 3244036
  17.3 7.0 %copy-start.1 = (bf16[2,264,1024]{2,1,0:T(8,128)(2,1)S(1)}, bf16[2,264,1024]{2,1,0:T(8,128)(2,1)}, u32[]{:S(2)}) copy-start(bf16[2,264,1024]{2,1,0:T(8,128)(2,1)} %get-tuple-element.30.refs_0_) | copy-start | bytes 3244036
  22.4 15.9 %collective-permute-start.5 = (bf16[264,1024]{1,0:T(8,128)(2,1)S(1)}, bf16[264,1024]{1,0:T(8,128)(2,1)S(1)}, u32[]{:S(2)}, u32[]{:S(2)}) collective-permute-start(bf16[264,1024]{1,0:T(8,128)(2,1)S(1)} %collective-permute-done.2.refs_3_.b01a.refs_1_), channel_id=1, source_target_pairs={{0,16},{1,17},{2,18},{3,19},{4,20},{5,21},{6,22},{7,23},{8,24},{9,... | collective-permute-start | bytes 1622024 | tf_op jit(solution)/shard_map/prva/ppermute | solution.py:54
  32.9 14.9 %collective-permute-start.10 = (bf16[264,1024]{1,0:T(8,128)(2,1)S(1)}, bf16[264,1024]{1,0:T(8,128)(2,1)S(1)}, u32[]{:S(2)}, u32[]{:S(2)}) collective-permute-start(bf16[264,1024]{1,0:T(8,128)(2,1)S(1)} %slice_bitcast_fusion.1), channel_id=1, source_target_pairs={{0,4},{1,5},{2,6},{3,7},{4,8},{5,9},{6,10},{7,11},{8,12},{9,13},{1... | collective-permute-start | bytes 1622024 | tf_op jit(solution)/shard_map/b13b/ppermute | solution.py:54
  33.3 17.2 %collective-permute-start.3 = (bf16[264,1024]{1,0:T(8,128)(2,1)S(1)}, bf16[264,1024]{1,0:T(8,128)(2,1)S(1)}, u32[]{:S(2)}, u32[]{:S(2)}) collective-permute-start(bf16[264,1024]{1,0:T(8,128)(2,1)S(1)} %collective-permute-done.1.refs_4_.b01b.refs_2_), channel_id=1, source_target_pairs={{0,16},{1,17},{2,18},{3,19},{4,20},{5,21},{6,22},{7,23},{8,24},{9,... | collective-permute-start | bytes 1622024 | tf_op jit(solution)/shard_map/prvb/ppermute | solution.py:54
  35.2 15.3 %collective-permute-start.11 = (bf16[264,1024]{1,0:T(8,128)(2,1)S(1)}, bf16[264,1024]{1,0:T(8,128)(2,1)S(1)}, u32[]{:S(2)}, u32[]{:S(2)}) collective-permute-start(bf16[264,1024]{1,0:T(8,128)(2,1)S(1)} %slice_bitcast_fusion), channel_id=1, source_target_pairs={{0,2},{1,3},{2,0},{3,1},{4,6},{5,7},{6,4},{7,5},{8,10},{9,11},{10,... | collective-permute-start | bytes 1622024 | tf_op jit(solution)/shard_map/b13a/ppermute | solution.py:54
  38.5 5.4 %collective-permute-start.8 = (bf16[256,1024]{1,0:T(8,128)(2,1)S(1)}, bf16[256,1024]{1,0:T(8,128)(2,1)S(1)}, u32[]{:S(2)}, u32[]{:S(2)}) collective-permute-start(bf16[256,1024]{1,0:T(8,128)(2,1)S(1)} %get-tuple-element.45), channel_id=1, source_target_pairs={{0,1},{1,0},{2,3},{3,2},{4,5},{5,4},{6,7},{7,6},{8,9},{9,8},{10,11... | collective-permute-start | bytes 1572872 | tf_op jit(solution)/shard_map/nxtax/ppermute | solution.py:54
  38.6 5.3 %collective-permute-start.9 = (bf16[256,1024]{1,0:T(8,128)(2,1)S(1)}, bf16[256,1024]{1,0:T(8,128)(2,1)S(1)}, u32[]{:S(2)}, u32[]{:S(2)}) collective-permute-start(bf16[256,1024]{1,0:T(8,128)(2,1)S(1)} %get-tuple-element.46), channel_id=1, source_target_pairs={{0,1},{1,0},{2,3},{3,2},{4,5},{5,4},{6,7},{7,6},{8,9},{9,8},{10,11... | collective-permute-start | bytes 1572872 | tf_op jit(solution)/shard_map/nxtbx/ppermute | solution.py:54
  46.3 5.7 %collective-permute-start.12 = (bf16[3,264,1024]{2,1,0:T(8,128)(2,1)S(1)}, bf16[3,264,1024]{2,1,0:T(8,128)(2,1)S(1)}, u32[]{:S(2)}, u32[]{:S(2)}) collective-permute-start(bf16[3,264,1024]{2,1,0:T(8,128)(2,1)S(1)} %get-tuple-element.50), channel_id=1, source_target_pairs={{0,1},{1,0},{2,3},{3,2},{4,5},{5,4},{6,7},{7,6},{8,9},{9,8},{10,11... | collective-permute-start | bytes 4866056 | tf_op jit(solution)/shard_map/cross/ppermute | solution.py:54
  50.5 4.1 %collective-permute-start.13 = (bf16[264,1024]{1,0:T(8,128)(2,1)S(1)}, bf16[264,1024]{1,0:T(8,128)(2,1)S(1)}, u32[]{:S(2)}, u32[]{:S(2)}) collective-permute-start(bf16[264,1024]{1,0:T(8,128)(2,1)S(1)} %collective-permute-done.3.refs_4_), channel_id=1, source_target_pairs={{0,1},{1,0},{2,3},{3,2},{4,5},{5,4},{6,7},{7,6},{8,9},{9,8},{10,11... | collective-permute-start | bytes 1622024 | tf_op jit(solution)/shard_map/prvbx/ppermute | solution.py:54
  53.7 4.1 %collective-permute-start.15 = (f32[8,256]{1,0:T(8,128)S(1)}, f32[8,256]{1,0:T(8,128)S(1)}, u32[]{:S(2)}, u32[]{:S(2)}) collective-permute-start(f32[8,256]{1,0:T(8,128)S(1)} %slice.17), channel_id=1, source_target_pairs={{0,2},{1,3},{2,0},{3,1},{4,6},{5,7},{6,4},{7,5},{8,10},{9,11},{10,... | collective-permute-start | bytes 24584 | tf_op jit(solution)/shard_map/side/ppermute | solution.py:54
  56.5 1.3 %collective-permute-start.14 = (f32[6,256]{1,0:T(8,128)S(1)}, f32[6,256]{1,0:T(8,128)S(1)}, u32[]{:S(2)}, u32[]{:S(2)}) collective-permute-start(f32[6,256]{1,0:T(8,128)S(1)} %slice.16), channel_id=1, source_target_pairs={{0,1},{1,0},{2,3},{3,2},{4,5},{5,4},{6,7},{7,6},{8,9},{9,8},{10,11... | collective-permute-start | bytes 18440 | tf_op jit(solution)/shard_map/swapped/ppermute | solution.py:54
  57.9 9.3 %collective-permute-start.18 = (f32[8,256]{1,0:T(8,128)S(1)}, f32[8,256]{1,0:T(8,128)S(1)}, u32[]{:S(2)}, u32[]{:S(2)}) collective-permute-start(f32[8,256]{1,0:T(8,128)S(1)} %get-tuple-element.55), channel_id=1, source_target_pairs={{0,118},{1,119},{2,116},{3,117},{4,122},{5,123},{6,120},{7,121},{8... | collective-permute-start | bytes 24584 | tf_op jit(solution)/shard_map/back_prv/ppermute | solution.py:54
  61.4 5.8 %collective-permute-start.17 = (f32[6,256]{1,0:T(8,128)S(1)}, f32[6,256]{1,0:T(8,128)S(1)}, u32[]{:S(2)}, u32[]{:S(2)}) collective-permute-start(f32[6,256]{1,0:T(8,128)S(1)} %get-tuple-element.54), channel_id=1, source_target_pairs={{0,4},{1,5},{2,6},{3,7},{4,8},{5,9},{6,10},{7,11},{8,12},{9,13},{1... | collective-permute-start | bytes 18440 | tf_op jit(solution)/shard_map/back_01/ppermute | solution.py:54
  62.8 4.0 %collective-permute-start.16 = (f32[4,256]{1,0:T(4,128)S(1)}, f32[4,256]{1,0:T(4,128)S(1)}, u32[]{:S(2)}, u32[]{:S(2)}) collective-permute-start(f32[4,256]{1,0:T(4,128)S(1)} %get-tuple-element.53), channel_id=1, source_target_pairs={{0,12},{1,13},{2,14},{3,15},{4,0},{5,1},{6,2},{7,3},{8,4},{9,5},{1... | collective-permute-start | bytes 12296 | tf_op jit(solution)/shard_map/back_03/ppermute | solution.py:54

commit v11 on v9

--- a/solution.py
+++ b/solution.py
@@ -370,9 +370,9 @@
     own, own_a, own_b = packed(embeddings[0], ranks, sizes)
 
     b01a = send("b01a", own_a, row=-1)
+    b10 = send("b10", own, col=1)
+    nxt = send("nxt", own, cluster=-1)
     b03 = send("b03", own, row=1)
-    nxt = send("nxt", own, cluster=-1)
-    b10 = send("b10", own, col=1)
     ownx = send("ownx", own, core=1)
     b01b = send("b01b", after(own_b, ownx), row=-1)
     empty = jnp.zeros((N_ROWS, HALF), jnp.float32)
@@ -381,7 +381,7 @@
     state = kernel_call("first", first_kernel, 0.5, state, [own, ownx, own_ranks, b01a])
 
     prvb = send("prvb", after(b01b, state), cluster=1)
-    b03, b10, state = lax.optimization_barrier((b03, b10, state))
+    b10, b03, state = lax.optimization_barrier((b10, b03, state))
     nxt, b01b, prva, state = lax.optimization_barrier((nxt, b01b, prva, state))
     b13a = send("b13a", b03[0], col=1)
     b13b = send("b13b", b10[1], row=1)

time: 67.2 us -> 67.4 us (level)
  starting transfers between devices: 25.7 us -> 28.5 us
  waiting for transfers between devices: 18 us -> 15.3 us
    ppermute x19, starting transfers between devices: 25.7 us -> 28.5 us  [send(): return lax.ppermute(value, AXES, pairs(**shift))]
    ppermute x19, waiting for transfers between devices: 18 us -> 15.3 us  [send(): return lax.ppermute(value, AXES, pairs(**shift))]
  transfers between devices with their start and end apart: 19 -> 19, of which waited for: 8 -> 6; matrix products, arithmetic and copies ran while one was open for 0% -> 0% of each run, Pallas kernels for 26% -> 26%
where the time goes in v11:
time: 67.4 us; the launch traced here: 67.1 us
  starting transfers between devices  28.5 us (42%)
  Pallas kernels  21.2 us (31%)
  waiting for transfers between devices  15.3 us (23%)
  local copies, waits for them, and re-layouts  1.33 us (2%)
  between operations  0.81 us (1%)
    ppermute x19, starting transfers between devices, send(): return lax.ppermute(value, AXES, pairs(**shift))  28.5 us
    pallas_call x9, Pallas kernels, kernel_call(): pl.pallas_call(kernel, in_specs=[VMEM] * (1 + len(arrays)) + [SMEM] * len...  17.3 us
    ppermute x19, waiting for transfers between devices, send(): return lax.ppermute(value, AXES, pairs(**shift))  15.3 us
    pallas_call x1, Pallas kernels, packed(): pl.pallas_call(pack_kernel, in_specs=[pl.BlockSpec(memory_space=pltpu.HBM...  3.07 us
  transfers between devices with their start and end apart: 19, of which 6 were waited for; matrix products, arithmetic and copies ran while one was open for 0% of the time, Pallas kernels for 26%

profile of v11, /device:TPU:0, one launch (start us, length us, event | category | flops | bytes accessed | tf_op | source)
XLA Modules:
  0.0 67.1 jit_solution(10764127342290491641)
XLA Ops:
  0.6 3.1 %pack.1 = (bf16[2,264,1024]{2,1,0:T(8,128)(2,1)}, bf16[264,1024]{1,0:T(8,128)(2,1)}, bf16[264,1024]{1,0:T(8,128)(2,1)}) custom-call(s32[8]{0:T(128)} %refs_2_.1, f32[512,1024]{1,0:T(8,128)} %bitcast.5, s32[1,512]{1,0:T(1,128)} %rank_hbm.1), custom_call_target="tpu_custom_call" | custom-call | flops 2097152 | bytes 4194304 | tf_op jit(solution)/shard_map/pack/pallas_call | solution.py:111
  3.8 1.7 %collective-permute-start.7 = (bf16[2,264,1024]{2,1,0:T(8,128)(2,1)}, bf16[2,264,1024]{2,1,0:T(8,128)(2,1)S(1)}, u32[]{:S(2)}, u32[]{:S(2)}) collective-permute-start(bf16[2,264,1024]{2,1,0:T(8,128)(2,1)} %get-tuple-element.30.refs_0_), channel_id=1, source_target_pairs={{0,4},{1,5},{2,6},{3,7},{4,8},{5,9},{6,10},{7,11},{8,12},{9,13},{1... | collective-permute-start | bytes 3244040 | tf_op jit(solution)/shard_map/b03/ppermute | solution.py:54
  5.5 1.5 %collective-permute-start.6 = (bf16[2,264,1024]{2,1,0:T(8,128)(2,1)}, bf16[2,264,1024]{2,1,0:T(8,128)(2,1)S(1)}, u32[]{:S(2)}, u32[]{:S(2)}) collective-permute-start(bf16[2,264,1024]{2,1,0:T(8,128)(2,1)} %get-tuple-element.30.refs_0_), channel_id=1, source_target_pairs={{0,2},{1,3},{2,0},{3,1},{4,6},{5,7},{6,4},{7,5},{8,10},{9,11},{10,... | collective-permute-start | bytes 3244040 | tf_op jit(solution)/shard_map/b10/ppermute | solution.py:54
  7.0 1.7 %collective-permute-start.2 = (bf16[264,1024]{1,0:T(8,128)(2,1)}, bf16[264,1024]{1,0:T(8,128)(2,1)S(1)}, u32[]{:S(2)}, u32[]{:S(2)}) collective-permute-start(bf16[264,1024]{1,0:T(8,128)(2,1)} %get-tuple-element.34), channel_id=1, source_target_pairs={{0,12},{1,13},{2,14},{3,15},{4,0},{5,1},{6,2},{7,3},{8,4},{9,5},{1... | collective-permute-start | bytes 1622024 | tf_op jit(solution)/shard_map/b01a/ppermute | solution.py:54
  8.7 5.6 %collective-permute-start.4 = (bf16[2,264,1024]{2,1,0:T(8,128)(2,1)}, bf16[2,264,1024]{2,1,0:T(8,128)(2,1)S(1)}, u32[]{:S(2)}, u32[]{:S(2)}) collective-permute-start(bf16[2,264,1024]{2,1,0:T(8,128)(2,1)} %get-tuple-element.30.refs_0_), channel_id=1, source_target_pairs={{0,114},{1,115},{2,112},{3,113},{4,118},{5,119},{6,116},{7,117},{8... | collective-permute-start | bytes 3244040 | tf_op jit(solution)/shard_map/nxt/ppermute | solution.py:54
  14.3 1.8 %collective-permute-start.1 = (bf16[264,1024]{1,0:T(8,128)(2,1)}, bf16[264,1024]{1,0:T(8,128)(2,1)S(1)}, u32[]{:S(2)}, u32[]{:S(2)}) collective-permute-start(bf16[264,1024]{1,0:T(8,128)(2,1)} %get-tuple-element.31), channel_id=1, source_target_pairs={{0,12},{1,13},{2,14},{3,15},{4,0},{5,1},{6,2},{7,3},{8,4},{9,5},{1... | collective-permute-start | bytes 1622024 | tf_op jit(solution)/shard_map/b01b/ppermute | solution.py:54
  17.3 1.8 %self.1 = (f32[56,256]{1,0:T(8,128)S(1)}, f32[4,256,128]{2,1,0:T(8,128)S(1)}) custom-call(f32[56,256]{1,0:T(8,128)S(1)} %broadcast_in_dim.3.rows_in, bf16[2,264,1024]{2,1,0:T(8,128)(2,1)S(1)} %copy-done, bf16[2,264,1024]{2,1,0:T(8,128)(2,1)S(1)} %collective-permute-done.refs_1_, s32[8]{0:T(128)S(1)} %copy-done.2), custom_call_target="tpu_custom_call" | custom-call | tf_op jit(solution)/shard_map/self/pallas_call | solution.py:215
  19.2 3.2 %collective-permute-done.2.refs_3_.b01a.refs_1_ = bf16[264,1024]{1,0:T(8,128)(2,1)S(1)} collective-permute-done((bf16[264,1024]{1,0:T(8,128)(2,1)}, bf16[264,1024]{1,0:T(8,128)(2,1)S(1)}, u32[]{:S(2)}, u32[]{:S(2)}) %collective-permute-start.2) | collective-permute-done | bytes 540704 | tf_op jit(solution)/shard_map/b01a/ppermute | solution.py:54
  22.4 1.9 %collective-permute-start.5 = (bf16[264,1024]{1,0:T(8,128)(2,1)S(1)}, bf16[264,1024]{1,0:T(8,128)(2,1)S(1)}, u32[]{:S(2)}, u32[]{:S(2)}) collective-permute-start(bf16[264,1024]{1,0:T(8,128)(2,1)S(1)} %collective-permute-done.2.refs_3_.b01a.refs_1_), channel_id=1, source_target_pairs={{0,16},{1,17},{2,18},{3,19},{4,20},{5,21},{6,22},{7,23},{8,24},{9,... | collective-permute-start | bytes 1622024 | tf_op jit(solution)/shard_map/prva/ppermute | solution.py:54
  25.2 6.4 %collective-permute-done.7.refs_5_.refs_3_.refs_0_ = bf16[2,264,1024]{2,1,0:T(8,128)(2,1)S(1)} collective-permute-done((bf16[2,264,1024]{2,1,0:T(8,128)(2,1)}, bf16[2,264,1024]{2,1,0:T(8,128)(2,1)S(1)}, u32[]{:S(2)}, u32[]{:S(2)}) %collective-permute-start.7) | collective-permute-done | bytes 1081376 | tf_op jit(solution)/shard_map/b03/ppermute | solution.py:54
  31.7 1.6 %collective-permute-start.10 = (bf16[264,1024]{1,0:T(8,128)(2,1)S(1)}, bf16[264,1024]{1,0:T(8,128)(2,1)S(1)}, u32[]{:S(2)}, u32[]{:S(2)}) collective-permute-start(bf16[264,1024]{1,0:T(8,128)(2,1)S(1)} %slice_bitcast_fusion.1), channel_id=1, source_target_pairs={{0,2},{1,3},{2,0},{3,1},{4,6},{5,7},{6,4},{7,5},{8,10},{9,11},{10,... | collective-permute-start | bytes 1622024 | tf_op jit(solution)/shard_map/b13a/ppermute | solution.py:54
  33.3 1.9 %collective-permute-start.3 = (bf16[264,1024]{1,0:T(8,128)(2,1)S(1)}, bf16[264,1024]{1,0:T(8,128)(2,1)S(1)}, u32[]{:S(2)}, u32[]{:S(2)}) collective-permute-start(bf16[264,1024]{1,0:T(8,128)(2,1)S(1)} %collective-permute-done.1.refs_4_.b01b.refs_2_), channel_id=1, source_target_pairs={{0,16},{1,17},{2,18},{3,19},{4,20},{5,21},{6,22},{7,23},{8,24},{9,... | collective-permute-start | bytes 1622024 | tf_op jit(solution)/shard_map/prvb/ppermute | solution.py:54
  35.2 1.6 %collective-permute-start.11 = (bf16[264,1024]{1,0:T(8,128)(2,1)S(1)}, bf16[264,1024]{1,0:T(8,128)(2,1)S(1)}, u32[]{:S(2)}, u32[]{:S(2)}) collective-permute-start(bf16[264,1024]{1,0:T(8,128)(2,1)S(1)} %slice_bitcast_fusion), channel_id=1, source_target_pairs={{0,4},{1,5},{2,6},{3,7},{4,8},{5,9},{6,10},{7,11},{8,12},{9,13},{1... | collective-permute-start | bytes 1622024 | tf_op jit(solution)/shard_map/b13b/ppermute | solution.py:54
  39.1 4.8 %same.1 = (f32[56,256]{1,0:T(8,128)S(1)}, f32[2,256,128]{2,1,0:T(8,128)S(1)}) custom-call(f32[56,256]{1,0:T(8,128)S(1)} %first.1.rows_in, bf16[2,264,1024]{2,1,0:T(8,128)(2,1)S(1)} %copy-done.1, bf16[2,264,1024]{2,1,0:T(8,128)(2,1)S(1)} %collective-permute-done.refs_1_, f32[4,256,128]{2,1,0:T(8,128)S(1)} %get-tuple-element.33.refs_2_, ...), custom_call_target="tpu_custom_call" | custom-call | tf_op jit(solution)/shard_map/same/pallas_call | solution.py:215
  43.9 2.4 %other.1.rows_in = f32[56,256]{1,0:T(8,128)S(1)} custom-call(f32[56,256]{1,0:T(8,128)S(1)} %get-tuple-element.44.rows_in, bf16[2,264,1024]{2,1,0:T(8,128)(2,1)S(1)} %copy-done.1, bf16[264,1024]{1,0:T(8,128)(2,1)S(1)} %collective-permute-done.2.refs_3_.b01a.refs_1_, bf16[264,1024]{1,0:T(8,128)(2,1)S(1)} %collective-permute-done.1.refs_4_.b01b.refs_2_, ...), custom_call_target="tpu_custom_call" | custom-call | tf_op jit(solution)/shard_map/other/pallas_call | solution.py:215
  46.7 1.5 %left.1.rows_in = f32[56,256]{1,0:T(8,128)S(1)} custom-call(f32[56,256]{1,0:T(8,128)S(1)} %other.1.rows_in, bf16[2,264,1024]{2,1,0:T(8,128)(2,1)S(1)} %copy-done.1, bf16[2,264,1024]{2,1,0:T(8,128)(2,1)S(1)} %collective-permute-done.refs_1_, f32[4,256,128]{2,1,0:T(8,128)S(1)} %get-tuple-element.33.refs_2_, ...), custom_call_target="tpu_custom_call" | custom-call | tf_op jit(solution)/shard_map/left/pallas_call | solution.py:215
  48.2 2.5 %collective-permute-done.3.refs_4_ = bf16[264,1024]{1,0:T(8,128)(2,1)S(1)} collective-permute-done((bf16[264,1024]{1,0:T(8,128)(2,1)S(1)}, bf16[264,1024]{1,0:T(8,128)(2,1)S(1)}, u32[]{:S(2)}, u32[]{:S(2)}) %collective-permute-start.3) | collective-permute-done | bytes 540704 | tf_op jit(solution)/shard_map/prvb/ppermute | solution.py:54
  50.7 1.3 %right.1.rows_in = f32[56,256]{1,0:T(8,128)S(1)} custom-call(f32[56,256]{1,0:T(8,128)S(1)} %left.1.rows_in, bf16[2,264,1024]{2,1,0:T(8,128)(2,1)S(1)} %copy-done.1, bf16[2,264,1024]{2,1,0:T(8,128)(2,1)S(1)} %collective-permute-done.refs_1_, f32[4,256,128]{2,1,0:T(8,128)S(1)} %get-tuple-element.33.refs_2_, ...), custom_call_target="tpu_custom_call" | custom-call | flops 102400000000 | tf_op jit(solution)/shard_map/right/pallas_call | solution.py:215
  52.1 1.7 %cross.1.rows_in = f32[56,256]{1,0:T(8,128)S(1)} custom-call(f32[56,256]{1,0:T(8,128)S(1)} %right.1.rows_in, bf16[2,264,1024]{2,1,0:T(8,128)(2,1)S(1)} %collective-permute-done.7.refs_5_.refs_3_.refs_0_, bf16[264,1024]{1,0:T(8,128)(2,1)S(1)} %collective-permute-done.10.refs_8_.refs_1_.refs_2_, ...), custom_call_target="tpu_custom_call" | custom-call | tf_op jit(solution)/shard_map/cross/pallas_call | solution.py:215
  54.7 1.8 %prev.1.rows_in = f32[56,256]{1,0:T(8,128)S(1)} custom-call(f32[56,256]{1,0:T(8,128)S(1)} %cross.1.rows_in, bf16[2,264,1024]{2,1,0:T(8,128)(2,1)S(1)} %collective-permute-done.7.refs_5_.refs_3_.refs_0_, bf16[2,264,1024]{2,1,0:T(8,128)(2,1)S(1)} %collective-permute-done.6.refs_6_.refs_4_.refs_1_, ...), custom_call_target="tpu_custom_call" | custom-call | tf_op jit(solution)/shard_map/prev/pallas_call | solution.py:215
  57.9 3.7 %collective-permute-start.18 = (f32[8,256]{1,0:T(8,128)S(1)}, f32[8,256]{1,0:T(8,128)S(1)}, u32[]{:S(2)}, u32[]{:S(2)}) collective-permute-start(f32[8,256]{1,0:T(8,128)S(1)} %get-tuple-element.55), channel_id=1, source_target_pairs={{0,118},{1,119},{2,116},{3,117},{4,122},{5,123},{6,120},{7,121},{8... | collective-permute-start | bytes 24584 | tf_op jit(solution)/shard_map/back_prv/ppermute | solution.py:54
  61.6 1.3 %collective-permute-start.17 = (f32[6,256]{1,0:T(8,128)S(1)}, f32[6,256]{1,0:T(8,128)S(1)}, u32[]{:S(2)}, u32[]{:S(2)}) collective-permute-start(f32[6,256]{1,0:T(8,128)S(1)} %get-tuple-element.54), channel_id=1, source_target_pairs={{0,4},{1,5},{2,6},{3,7},{4,8},{5,9},{6,10},{7,11},{8,12},{9,13},{1... | collective-permute-start | bytes 18440 | tf_op jit(solution)/shard_map/back_01/ppermute | solution.py:54
  62.9 2.0 %collective-permute-start.16 = (f32[4,256]{1,0:T(4,128)S(1)}, f32[4,256]{1,0:T(4,128)S(1)}, u32[]{:S(2)}, u32[]{:S(2)}) collective-permute-start(f32[4,256]{1,0:T(4,128)S(1)} %get-tuple-element.53), channel_id=1, source_target_pairs={{0,12},{1,13},{2,14},{3,15},{4,0},{5,1},{6,2},{7,3},{8,4},{9,5},{1... | collective-permute-start | bytes 12296 | tf_op jit(solution)/shard_map/back_03/ppermute | solution.py:54
  64.9 1.7 %collective-permute-done.16.b03 = f32[4,256]{1,0:T(4,128)S(1)} collective-permute-done((f32[4,256]{1,0:T(4,128)S(1)}, f32[4,256]{1,0:T(4,128)S(1)}, u32[]{:S(2)}, u32[]{:S(2)}) %collective-permute-start.16) | collective-permute-done | bytes 4128 | tf_op jit(solution)/shard_map/back_03/ppermute | solution.py:54
  (38 shorter events, 7.7 us)
Async XLA Ops:
  0.6 15.4 %copy-start.2 = (s32[8]{0:T(128)S(1)}, s32[8]{0:T(128)}, u32[]{:S(2)}) copy-start(s32[8]{0:T(128)} %refs_2_.1) | copy-start | bytes 100
  3.7 10.5 %collective-permute-start = (bf16[2,264,1024]{2,1,0:T(8,128)(2,1)}, bf16[2,264,1024]{2,1,0:T(8,128)(2,1)S(1)}, u32[]{:S(2)}, u32[]{:S(2)}) collective-permute-start(bf16[2,264,1024]{2,1,0:T(8,128)(2,1)} %get-tuple-element.30.refs_0_), channel_id=1, source_target_pairs={{0,1},{1,0},{2,3},{3,2},{4,5},{5,4},{6,7},{7,6},{8,9},{9,8},{10,11... | collective-permute-start | bytes 3244040 | tf_op jit(solution)/shard_map/ownx/ppermute | solution.py:54
  3.8 27.8 %collective-permute-start.7 = (bf16[2,264,1024]{2,1,0:T(8,128)(2,1)}, bf16[2,264,1024]{2,1,0:T(8,128)(2,1)S(1)}, u32[]{:S(2)}, u32[]{:S(2)}) collective-permute-start(bf16[2,264,1024]{2,1,0:T(8,128)(2,1)} %get-tuple-element.30.refs_0_), channel_id=1, source_target_pairs={{0,4},{1,5},{2,6},{3,7},{4,8},{5,9},{6,10},{7,11},{8,12},{9,13},{1... | collective-permute-start | bytes 3244040 | tf_op jit(solution)/shard_map/b03/ppermute | solution.py:54
  5.5 26.1 %collective-permute-start.6 = (bf16[2,264,1024]{2,1,0:T(8,128)(2,1)}, bf16[2,264,1024]{2,1,0:T(8,128)(2,1)S(1)}, u32[]{:S(2)}, u32[]{:S(2)}) collective-permute-start(bf16[2,264,1024]{2,1,0:T(8,128)(2,1)} %get-tuple-element.30.refs_0_), channel_id=1, source_target_pairs={{0,2},{1,3},{2,0},{3,1},{4,6},{5,7},{6,4},{7,5},{8,10},{9,11},{10,... | collective-permute-start | bytes 3244040 | tf_op jit(solution)/shard_map/b10/ppermute | solution.py:54
  7.0 15.4 %collective-permute-start.2 = (bf16[264,1024]{1,0:T(8,128)(2,1)}, bf16[264,1024]{1,0:T(8,128)(2,1)S(1)}, u32[]{:S(2)}, u32[]{:S(2)}) collective-permute-start(bf16[264,1024]{1,0:T(8,128)(2,1)} %get-tuple-element.34), channel_id=1, source_target_pairs={{0,12},{1,13},{2,14},{3,15},{4,0},{5,1},{6,2},{7,3},{8,4},{9,5},{1... | collective-permute-start | bytes 1622024 | tf_op jit(solution)/shard_map/b01a/ppermute | solution.py:54
  8.7 28.8 %collective-permute-start.4 = (bf16[2,264,1024]{2,1,0:T(8,128)(2,1)}, bf16[2,264,1024]{2,1,0:T(8,128)(2,1)S(1)}, u32[]{:S(2)}, u32[]{:S(2)}) collective-permute-start(bf16[2,264,1024]{2,1,0:T(8,128)(2,1)} %get-tuple-element.30.refs_0_), channel_id=1, source_target_pairs={{0,114},{1,115},{2,112},{3,113},{4,118},{5,119},{6,116},{7,117},{8... | collective-permute-start | bytes 3244040 | tf_op jit(solution)/shard_map/nxt/ppermute | solution.py:54
  14.3 19.0 %collective-permute-start.1 = (bf16[264,1024]{1,0:T(8,128)(2,1)}, bf16[264,1024]{1,0:T(8,128)(2,1)S(1)}, u32[]{:S(2)}, u32[]{:S(2)}) collective-permute-start(bf16[264,1024]{1,0:T(8,128)(2,1)} %get-tuple-element.31), channel_id=1, source_target_pairs={{0,12},{1,13},{2,14},{3,15},{4,0},{5,1},{6,2},{7,3},{8,4},{9,5},{1... | collective-permute-start | bytes 1622024 | tf_op jit(solution)/shard_map/b01b/ppermute | solution.py:54
  16.1 1.2 %copy-start = (bf16[2,264,1024]{2,1,0:T(8,128)(2,1)S(1)}, bf16[2,264,1024]{2,1,0:T(8,128)(2,1)}, u32[]{:S(2)}) copy-start(bf16[2,264,1024]{2,1,0:T(8,128)(2,1)} %get-tuple-element.30.refs_0_) | copy-start | bytes 3244036
  17.3 7.0 %copy-start.1 = (bf16[2,264,1024]{2,1,0:T(8,128)(2,1)S(1)}, bf16[2,264,1024]{2,1,0:T(8,128)(2,1)}, u32[]{:S(2)}) copy-start(bf16[2,264,1024]{2,1,0:T(8,128)(2,1)} %get-tuple-element.30.refs_0_) | copy-start | bytes 3244036
  22.4 15.9 %collective-permute-start.5 = (bf16[264,1024]{1,0:T(8,128)(2,1)S(1)}, bf16[264,1024]{1,0:T(8,128)(2,1)S(1)}, u32[]{:S(2)}, u32[]{:S(2)}) collective-permute-start(bf16[264,1024]{1,0:T(8,128)(2,1)S(1)} %collective-permute-done.2.refs_3_.b01a.refs_1_), channel_id=1, source_target_pairs={{0,16},{1,17},{2,18},{3,19},{4,20},{5,21},{6,22},{7,23},{8,24},{9,... | collective-permute-start | bytes 1622024 | tf_op jit(solution)/shard_map/prva/ppermute | solution.py:54
  31.7 15.0 %collective-permute-start.10 = (bf16[264,1024]{1,0:T(8,128)(2,1)S(1)}, bf16[264,1024]{1,0:T(8,128)(2,1)S(1)}, u32[]{:S(2)}, u32[]{:S(2)}) collective-permute-start(bf16[264,1024]{1,0:T(8,128)(2,1)S(1)} %slice_bitcast_fusion.1), channel_id=1, source_target_pairs={{0,2},{1,3},{2,0},{3,1},{4,6},{5,7},{6,4},{7,5},{8,10},{9,11},{10,... | collective-permute-start | bytes 1622024 | tf_op jit(solution)/shard_map/b13a/ppermute | solution.py:54
  33.3 17.4 %collective-permute-start.3 = (bf16[264,1024]{1,0:T(8,128)(2,1)S(1)}, bf16[264,1024]{1,0:T(8,128)(2,1)S(1)}, u32[]{:S(2)}, u32[]{:S(2)}) collective-permute-start(bf16[264,1024]{1,0:T(8,128)(2,1)S(1)} %collective-permute-done.1.refs_4_.b01b.refs_2_), channel_id=1, source_target_pairs={{0,16},{1,17},{2,18},{3,19},{4,20},{5,21},{6,22},{7,23},{8,24},{9,... | collective-permute-start | bytes 1622024 | tf_op jit(solution)/shard_map/prvb/ppermute | solution.py:54
  35.2 15.4 %collective-permute-start.11 = (bf16[264,1024]{1,0:T(8,128)(2,1)S(1)}, bf16[264,1024]{1,0:T(8,128)(2,1)S(1)}, u32[]{:S(2)}, u32[]{:S(2)}) collective-permute-start(bf16[264,1024]{1,0:T(8,128)(2,1)S(1)} %slice_bitcast_fusion), channel_id=1, source_target_pairs={{0,4},{1,5},{2,6},{3,7},{4,8},{5,9},{6,10},{7,11},{8,12},{9,13},{1... | collective-permute-start | bytes 1622024 | tf_op jit(solution)/shard_map/b13b/ppermute | solution.py:54
  38.5 5.4 %collective-permute-start.8 = (bf16[256,1024]{1,0:T(8,128)(2,1)S(1)}, bf16[256,1024]{1,0:T(8,128)(2,1)S(1)}, u32[]{:S(2)}, u32[]{:S(2)}) collective-permute-start(bf16[256,1024]{1,0:T(8,128)(2,1)S(1)} %get-tuple-element.45), channel_id=1, source_target_pairs={{0,1},{1,0},{2,3},{3,2},{4,5},{5,4},{6,7},{7,6},{8,9},{9,8},{10,11... | collective-permute-start | bytes 1572872 | tf_op jit(solution)/shard_map/nxtax/ppermute | solution.py:54
  38.6 5.3 %collective-permute-start.9 = (bf16[256,1024]{1,0:T(8,128)(2,1)S(1)}, bf16[256,1024]{1,0:T(8,128)(2,1)S(1)}, u32[]{:S(2)}, u32[]{:S(2)}) collective-permute-start(bf16[256,1024]{1,0:T(8,128)(2,1)S(1)} %get-tuple-element.46), channel_id=1, source_target_pairs={{0,1},{1,0},{2,3},{3,2},{4,5},{5,4},{6,7},{7,6},{8,9},{9,8},{10,11... | collective-permute-start | bytes 1572872 | tf_op jit(solution)/shard_map/nxtbx/ppermute | solution.py:54
  46.3 5.7 %collective-permute-start.12 = (bf16[3,264,1024]{2,1,0:T(8,128)(2,1)S(1)}, bf16[3,264,1024]{2,1,0:T(8,128)(2,1)S(1)}, u32[]{:S(2)}, u32[]{:S(2)}) collective-permute-start(bf16[3,264,1024]{2,1,0:T(8,128)(2,1)S(1)} %get-tuple-element.50), channel_id=1, source_target_pairs={{0,1},{1,0},{2,3},{3,2},{4,5},{5,4},{6,7},{7,6},{8,9},{9,8},{10,11... | collective-permute-start | bytes 4866056 | tf_op jit(solution)/shard_map/cross/ppermute | solution.py:54
  50.7 4.0 %collective-permute-start.13 = (bf16[264,1024]{1,0:T(8,128)(2,1)S(1)}, bf16[264,1024]{1,0:T(8,128)(2,1)S(1)}, u32[]{:S(2)}, u32[]{:S(2)}) collective-permute-start(bf16[264,1024]{1,0:T(8,128)(2,1)S(1)} %collective-permute-done.3.refs_4_), channel_id=1, source_target_pairs={{0,1},{1,0},{2,3},{3,2},{4,5},{5,4},{6,7},{7,6},{8,9},{9,8},{10,11... | collective-permute-start | bytes 1622024 | tf_op jit(solution)/shard_map/prvbx/ppermute | solution.py:54
  53.8 4.1 %collective-permute-start.15 = (f32[8,256]{1,0:T(8,128)S(1)}, f32[8,256]{1,0:T(8,128)S(1)}, u32[]{:S(2)}, u32[]{:S(2)}) collective-permute-start(f32[8,256]{1,0:T(8,128)S(1)} %slice.17), channel_id=1, source_target_pairs={{0,2},{1,3},{2,0},{3,1},{4,6},{5,7},{6,4},{7,5},{8,10},{9,11},{10,... | collective-permute-start | bytes 24584 | tf_op jit(solution)/shard_map/side/ppermute | solution.py:54
  56.5 1.3 %collective-permute-start.14 = (f32[6,256]{1,0:T(8,128)S(1)}, f32[6,256]{1,0:T(8,128)S(1)}, u32[]{:S(2)}, u32[]{:S(2)}) collective-permute-start(f32[6,256]{1,0:T(8,128)S(1)} %slice.16), channel_id=1, source_target_pairs={{0,1},{1,0},{2,3},{3,2},{4,5},{5,4},{6,7},{7,6},{8,9},{9,8},{10,11... | collective-permute-start | bytes 18440 | tf_op jit(solution)/shard_map/swapped/ppermute | solution.py:54
  57.9 8.6 %collective-permute-start.18 = (f32[8,256]{1,0:T(8,128)S(1)}, f32[8,256]{1,0:T(8,128)S(1)}, u32[]{:S(2)}, u32[]{:S(2)}) collective-permute-start(f32[8,256]{1,0:T(8,128)S(1)} %get-tuple-element.55), channel_id=1, source_target_pairs={{0,118},{1,119},{2,116},{3,117},{4,122},{5,123},{6,120},{7,121},{8... | collective-permute-start | bytes 24584 | tf_op jit(solution)/shard_map/back_prv/ppermute | solution.py:54
  61.6 4.9 %collective-permute-start.17 = (f32[6,256]{1,0:T(8,128)S(1)}, f32[6,256]{1,0:T(8,128)S(1)}, u32[]{:S(2)}, u32[]{:S(2)}) collective-permute-start(f32[6,256]{1,0:T(8,128)S(1)} %get-tuple-element.54), channel_id=1, source_target_pairs={{0,4},{1,5},{2,6},{3,7},{4,8},{5,9},{6,10},{7,11},{8,12},{9,13},{1... | collective-permute-start | bytes 18440 | tf_op jit(solution)/shard_map/back_01/ppermute | solution.py:54
  62.9 3.6 %collective-permute-start.16 = (f32[4,256]{1,0:T(4,128)S(1)}, f32[4,256]{1,0:T(4,128)S(1)}, u32[]{:S(2)}, u32[]{:S(2)}) collective-permute-start(f32[4,256]{1,0:T(4,128)S(1)} %get-tuple-element.53), channel_id=1, source_target_pairs={{0,12},{1,13},{2,14},{3,15},{4,0},{5,1},{6,2},{7,3},{8,4},{9,5},{1... | collective-permute-start | bytes 12296 | tf_op jit(solution)/shard_map/back_03/ppermute | solution.py:54
